TPU v7x, 256 devices: a whole 4x4x8 slice. The times are simulated.
256 devices in a mesh: span: 32 (over z, y_lo, core), mp: 4 (over x), phase: 2 (over y_hi).
Axes of the slice: x: 4, y: 4 (y_hi: 2, y_lo: 2; y = y_hi * 2 + y_lo), z: 8, core: 2. Of those that a mesh axis runs over, the one named last changes fastest.
Arguments:
- latents: bfloat16 [32768, 2560], P(('span', 'phase')), may hold values from -6 to 6
- w_qkv: bfloat16 [2560, 3, 1536], P(None, None, 'mp'), may hold values from -0.125 to 0.125
- w_out: bfloat16 [1536, 2560], P('mp'), may hold values from -0.15625 to 0.15625
- decay: float32 [32, 2, 12], P('span', None, 'mp'), may hold values from 0.4 to 0.999, as said below
- frame_ids: int32 [32, 1024], P('span'), may hold values from 0 to 15, never falling along the last dimension, each value on 1 to 256 neighbouring positions
- memory_mask: int32 [32, 17], P('span'), may hold values 0 or 1
Outputs:
- refined: bfloat16 [32768, 2560], P(('span', 'phase'), 'mp')
Inputs may be any that keep to these rules, and one draw needn't show every extreme that they name: `frame_ids`: along each span's 1024 tokens the frame numbers never fall, and every frame from 0 on holds 1 to 256 tokens. `decay`: every entry lies strictly between 0 and 1.
All inputs are finite; a program needn't handle non-finite values. No bound on the sum of `memory_mask` on one device may be relied on, other than what follows from the above.
Results may differ from a plain program's by a relative error of at most 0.004.
Values may be sent and summed in bfloat16 or wider, within the bound.
No kernel may reach another device: no remote copies, remote signals or barrier semaphores. Data moves between devices by JAX's collectives and lax.ppermute only.
A program may use at most 128 MiB of HBM per device.

v0:
```python
import jax
import jax.numpy as jnp
from jax import lax
from jax.sharding import Mesh
from jax.sharding import PartitionSpec as P

HD = 128
WIN = 64
MEM = 256
SPAN = ("span_0", "span_1", "span_2")
SPAN_PHASE = ("span_0", "span_1", "span_2", "phase")


outside_frame = 1048576
epsilon = 1e-06


def extended_2(x, sides, width):
    for axis, dim in sides:
        size, length = (lax.axis_size(axis), x.shape[dim])
        up = [(i, (i + 1) % size) for i in range(size - 1)]
        down = [(j, i) for i, j in up]
        last = lax.slice_in_dim(x, length - width, length, axis=dim)
        first = lax.slice_in_dim(x, 0, width, axis=dim)
        before = lax.ppermute(last, axis, up)
        after = lax.ppermute(first, axis, down)
        x = jnp.concatenate([before, x, after], axis=dim)
    return x


def from_partner(x, axis, bit):
    return lax.ppermute(x, axis, [(i, i ^ 1 << bit) for i in range(lax.axis_size(axis))])


def nothing_yet(x, identity):
    return jax.tree.map(
        lambda part, zero: jnp.zeros_like(part) + jnp.asarray(zero, part.dtype), x, identity
    )


def entering(x, axes, combine, identity):
    before = start = nothing_yet(x, identity)
    subtotal = x
    for axis in reversed(axes):
        length, mine = (lax.axis_size(axis), lax.axis_index(axis))
        pieces = jax.tree.map(lambda part: lax.all_gather(part, axis), subtotal)
        inside, subtotal = (start, start)
        for k in range(length):
            passed = k < mine
            subtotal = combine(subtotal, jax.tree.map(lambda part: part[k], pieces))
            inside = jax.tree.map(lambda new, old: jnp.where(passed, new, old), subtotal, inside)
        before = combine(inside, before)
    return before


def cut_along(x, dim, length):
    before, after = (x.shape[:dim], x.shape[dim + 1 :])
    return jnp.moveaxis(x.reshape(*before, length, -1, *after), dim, 0)


def sum_at_owner(x, axis, dim):
    blocks = cut_along(x, dim, lax.axis_size(axis))
    arrived = lax.all_to_all(blocks, axis, split_axis=0, concat_axis=0, tiled=True)
    return arrived.astype(jnp.float32).sum(axis=0)


def head_normed(raw):
    count = raw.shape[0]
    grouped = raw.reshape(count, -1, HD)
    scaled = grouped * lax.rsqrt(jnp.mean(grouped * grouped, axis=-1, keepdims=True) + epsilon)
    return scaled.reshape(count, -1).astype(jnp.bfloat16)


def chain_step(earlier, later):
    return (earlier[0] * later[0], later[0] * earlier[1] + later[1])


def window_attend(
    queries_pad, keys_ext, values_ext, frames_ext, memory_keys, memory_values, memory_open
):
    total_rows, width = queries_pad.shape
    heads = width // HD
    count = total_rows // WIN
    score_scale = HD ** (-0.5)
    window_query = queries_pad.reshape(count, WIN, heads, HD)
    key_win = keys_ext.reshape(count, WIN, heads, HD)
    value_win = values_ext.reshape(count, WIN, heads, HD)
    memory_key_rows = memory_keys.reshape(MEM, heads, HD)
    memory_value_rows = memory_values.reshape(MEM, heads, HD)
    score_win = (
        jnp.einsum("wqhd,wkhd->whqk", window_query, key_win, preferred_element_type=jnp.float32)
        * score_scale
    )
    memory_score = (
        jnp.einsum(
            "bntu,atu->btna", window_query, memory_key_rows, preferred_element_type=jnp.float32
        )
        * score_scale
    )
    frame_win = frames_ext.reshape(count, WIN)
    allowed = frame_win[:, None, None, :] <= frame_win[:, None, :, None]
    exp_win = jnp.where(allowed, jnp.exp(score_win), 0.0)
    exp_mem = jnp.where((memory_open == 1)[:, None, None, None], jnp.exp(memory_score), 0.0)
    denom = jnp.sum(exp_win, axis=-1, keepdims=True) + jnp.sum(exp_mem, axis=-1, keepdims=True)
    weight_win = (exp_win / denom).astype(jnp.bfloat16)
    memory_weight = (exp_mem / denom).astype(jnp.bfloat16)
    refined_output = jnp.einsum(
        "whqk,wkhd->wqhd", weight_win, value_win, preferred_element_type=jnp.float32
    )
    refined_output = refined_output + jnp.einsum(
        "bykl,lyp->bkyp", memory_weight, memory_value_rows, preferred_element_type=jnp.float32
    )
    return refined_output.reshape(total_rows, width).astype(jnp.bfloat16)


def local(latents, w_qkv, w_out, decay, frame_ids, memory_mask):
    rows, width = latents.shape
    columns = w_qkv.shape[2]
    half_win = WIN // 2
    phase = lax.axis_index("phase")
    mixed = jnp.dot(latents, w_qkv.reshape(width, 3 * columns), preferred_element_type=jnp.float32)
    queries = head_normed(mixed[:, :columns])
    keys = head_normed(mixed[:, columns : 2 * columns])
    values = mixed[:, 2 * columns :].astype(jnp.bfloat16)
    joined = jnp.concatenate([keys, values], axis=1)
    extended = extended_2(joined, (("phase", 0),), half_win)
    keys_ext = extended[:, :columns]
    values_ext = extended[:, columns:]
    rate_rows = decay[0]
    own_rate = jnp.repeat(lax.dynamic_index_in_dim(rate_rows, phase, 0, keepdims=False), HD)
    tail_keys = keys[rows - MEM :].astype(jnp.float32)
    tail_values = values[rows - MEM :].astype(jnp.float32)
    terms = jnp.stack(
        [(1.0 - own_rate) * tail_keys, jnp.sqrt(1.0 - own_rate * own_rate) * tail_values]
    )
    identity = (jnp.ones((columns,), jnp.float32), jnp.zeros((2, MEM, columns), jnp.float32))
    partner = from_partner(terms, "phase", 0)
    first = phase == 0
    lower = (jnp.repeat(rate_rows[0], HD), jnp.where(first, terms, partner))
    upper = (jnp.repeat(rate_rows[1], HD), jnp.where(first, partner, terms))
    span_prefix = entering(chain_step(lower, upper), SPAN, chain_step, identity)
    memory = jnp.where(first, span_prefix[1], chain_step(span_prefix, lower)[1])
    memory_keys = memory[0].astype(jnp.bfloat16)
    memory_values = memory[1].astype(jnp.bfloat16)
    frames_pad = jnp.pad(frame_ids[0], (half_win, half_win), constant_values=outside_frame)
    frames_ext = lax.dynamic_slice_in_dim(frames_pad, phase * rows, rows + WIN)
    window_count = rows // WIN + 1
    opened = lax.dynamic_slice_in_dim(memory_mask[0], phase * (rows // WIN), window_count)
    queries_pad = jnp.pad(queries, ((half_win, half_win), (0, 0)))
    attended = window_attend(
        queries_pad, keys_ext, values_ext, frames_ext, memory_keys, memory_values, opened
    )[half_win : half_win + rows]
    partial_sum = jnp.dot(attended, w_out, preferred_element_type=jnp.float32)
    summed = sum_at_owner(partial_sum.astype(jnp.bfloat16), "mp", 1)
    share = summed.shape[1]
    own_columns = lax.dynamic_slice_in_dim(latents, lax.axis_index("mp") * share, share, 1)
    return (own_columns.astype(jnp.float32) + summed).astype(jnp.bfloat16)


def solution(mesh):
    finer = Mesh(
        mesh.devices.reshape(8, 2, 2, mesh.shape["mp"], mesh.shape["phase"]),
        ("span_0", "span_1", "span_2", "mp", "phase"),
    )
    placed = (
        P(SPAN_PHASE, None),
        P(None, None, "mp"),
        P("mp", None),
        P(SPAN, None, "mp"),
        P(SPAN, None),
        P(SPAN, None),
    )
    return jax.shard_map(
        local, mesh=finer, in_specs=placed, out_specs=P(SPAN_PHASE, "mp"), check_vma=False
    )
```

profile of v0, /device:TPU:32, one launch (start us, length us, event | category | flops | bytes accessed | tf_op | source)
XLA Modules:
  0.0 248.0 jit_solution(18020618885181132543)
XLA Ops:
  6.5 9.0 %copy.51 = bf16[2560,3,384]{0,2,1:T(8,128)(2,1)} copy(bf16[2560,3,384]{2,0,1:T(8,128)(2,1)} %param.7) | data formatting | bytes 11796480 | tf_op args[1]
  15.6 8.1 %fusion.30 = (bf16[512,1152]{1,0:T(8,128)(2,1)}, f32[512,1152]{1,0:T(8,128)S(1)}) fusion(bf16[512,2560]{1,0:T(8,128)(2,1)} %param.6, bf16[2560,1152]{0,1:T(8,128)(2,1)} %bitcast.155), kind=kOutput, calls=%fused_computation.102 | convolution fusion | flops 3020488704 | bytes 12058624 | tf_op jit(solution)/shard_map/dot_general | solution.py:121
  23.6 1.4 copy-done.4
  25.0 1.0 slice_multiply_fusion
  26.0 1.4 copy.54
  27.4 0.1 reduce_sum.46
  27.5 0.1 mul.301
  27.6 1.2 copy.55
  28.8 0.3 copy.52
  29.1 0.1 reduce_sum.45
  29.2 0.1 mul.295
  29.2 1.2 copy.53
  30.4 2.0 multiply_convert_fusion
  32.4 0.5 slice_bitcast_fusion.9
  33.0 1.0 multiply_bitcast_fusion
  34.0 1.0 pad_maximum_fusion.1
  35.1 3.2 %collective-permute-start.2 = (f32[2,256,384]{2,1,0:T(8,128)}, f32[2,256,384]{2,1,0:T(8,128)}, u32[]{:S(2)}, u32[]{:S(2)}) collective-permute-start(f32[2,256,384]{2,1,0:T(8,128)} %pad_maximum_fusion.1), channel_id=1, source_target_pairs={{0,1},{1,0},{2,3},{3,2},{4,5},{5,4},{6,7},{7,6},{8,9},{9,8},{10,11... | collective-permute-start | bytes 2359304 | tf_op jit(solution)/shard_map/ppermute | solution.py:32
  38.3 17.8 %collective-permute-done.2 = f32[2,256,384]{2,1,0:T(8,128)} collective-permute-done((f32[2,256,384]{2,1,0:T(8,128)}, f32[2,256,384]{2,1,0:T(8,128)}, u32[]{:S(2)}, u32[]{:S(2)}) %collective-permute-start.2) | collective-permute-done | bytes 786464 | tf_op jit(solution)/shard_map/ppermute | solution.py:32
  56.1 2.1 select_add_fusion
  58.4 0.1 broadcast_in_dim.56
  58.5 1.8 all-gather.1
  60.3 4.3 %all-gather.2 = f32[2,1,384]{2,1,0:T(1,128)S(1)} all-gather(f32[1,1,384]{2,1,0:T(1,128)S(1)} %get-tuple-element.30), channel_id=1, replica_groups=mesh['span_0'=8,'span_1'=2,'span_2'=2,'mp'=4,'phase'=2] {'span_1'}, dimensions={0}, use_global_device_ids=true | all-gather | bytes 4608 | tf_op jit(solution)/shard_map/all_gather | solution.py:46
  64.6 0.6 select_multiply_fusion
  65.2 11.0 %all-gather.12.cloned.1.call-done = f32[4,256,384]{2,1,0:T(8,128)} async-done(((f32[2,256,384]{2,1,0:T(8,128)}), f32[4,256,384]{2,1,0:T(8,128)}) %all-gather.12.cloned.1.call-update) | async-done | bytes 1572880 | tf_op jit(solution)/shard_map/all_gather | solution.py:46
  76.2 2.3 bitcast_add_fusion.2
  78.6 33.7 %all-gather.8.cloned.1.call-done = f32[2,2,256,384]{3,2,1,0:T(8,128)} async-done(((f32[1,2,256,384]{3,2,1,0:T(8,128)}), f32[2,2,256,384]{3,2,1,0:T(8,128)}) %all-gather.8.cloned.1.call-update) | async-done | bytes 1572880 | tf_op jit(solution)/shard_map/all_gather | solution.py:46
  112.3 2.4 multiply_add_fusion
  114.7 1.1 slice.173
  115.8 1.3 collective-permute-start.1
  117.1 6.1 %collective-permute-start = (bf16[32,768]{1,0:T(8,128)(2,1)S(1)}, bf16[32,768]{1,0:T(8,128)(2,1)S(1)}, u32[]{:S(2)}, u32[]{:S(2)}) collective-permute-start(bf16[32,768]{1,0:T(8,128)(2,1)S(1)} %get-tuple-element.25), channel_id=1, source_target_pairs={{0,1},{2,3},{4,5},{6,7},{8,9},{10,11},{12,13},{14,15},{16,17},{18,... | collective-permute-start | bytes 147464 | tf_op jit(solution)/shard_map/ppermute | solution.py:25
  123.2 0.1 pad_dynamic-slice_fusion
  123.3 0.1 le.20
  123.4 22.5 %all-gather.3 = f32[8,1,384]{2,1,0:T(1,128)S(1)} all-gather(f32[1,1,384]{2,1,0:T(1,128)S(1)} %get-tuple-element.29), channel_id=1, replica_groups=mesh['span_0'=8,'span_1'=2,'span_2'=2,'mp'=4,'phase'=2] {'span_0'}, dimensions={0}, use_global_device_ids=true | all-gather | bytes 13824 | tf_op jit(solution)/shard_map/all_gather | solution.py:46
  145.9 0.6 slice_reduce_fusion.6
  146.5 0.7 broadcast_bitcast_fusion
  147.2 0.8 broadcast_compare_fusion
  147.9 0.6 compare_bitcast_fusion
  148.6 0.8 pad.9
  149.4 2.1 reshape.175
  151.5 1.9 copy.60
  153.4 0.1 pad_maximum_fusion
  153.5 0.9 fusion.28
  154.4 0.9 reshape.176
  155.3 2.2 reshape.174
  157.5 3.2 %fusion.31 = (f32[9,3,64]{2,1,0:T(4,128)}, f32[9,3,64,64]{2,3,1,0:T(8,128)}) fusion(bf16[9,64,3,128]{3,2,1,0:T(4,128)(2,1)} %reshape.176, bf16[9,64,3,128]{3,2,1,0:T(4,128)(2,1)} %reshape.175, pred[9,64,64]{1,2,0:T(8,128)(4,1)} %broadcast_compare_fusion), kind=kOutput, calls=%fused_computation.103 | convolution fusion | flops 28641600 | bytes 1370880 | tf_op jit(solution)/shard_map/wqhd,wkhd->whqk/dot_general | solution.py:91
  160.7 27.9 %all-gather.10.cloned.1.call-done = f32[8,2,256,384]{3,2,1,0:T(8,128)} async-done(((f32[1,2,256,384]{3,2,1,0:T(8,128)}), f32[8,2,256,384]{3,2,1,0:T(8,128)}) %all-gather.10.cloned.1.call-update) | async-done | bytes 6291472 | tf_op jit(solution)/shard_map/all_gather | solution.py:46
  188.6 4.6 %select_convert_fusion = bf16[2,256,384]{2,1,0:T(8,128)(2,1)S(1)} fusion(f32[8,2,256,384]{3,2,1,0:T(8,128)} %all-gather.10.cloned.1.call-done, f32[2,2,256,384]{3,2,1,0:T(8,128)} %all-gather.8.cloned.1.call-done, f32[4,256,384]{2,1,0:T(8,128)S(1)} %copy-done.1, f32[384]{0:T(512)} %broadcast_bitcast_fusion, f32[384]{0:T(512)S(1)} %get-tuple-element.31, ...), kind=kLoop, calls=%fused_computation.46 | loop fusion | flops 8454144 | bytes 11426317 | tf_op jit(solution)/shard_map/convert.1
  193.2 0.1 copy.58
  193.4 0.1 copy.64
  193.5 0.6 copy-done.5
  194.2 0.4 fusion.32
  194.6 0.4 bitcast_reduce_fusion
  195.0 0.3 copy-done.6
  195.3 0.3 copy-done.13
  195.6 0.3 convolution_bitcast_fusion.1
  195.9 0.6 fusion.4
  196.5 0.4 copy.68
  196.9 0.1 copy.92
  197.0 1.5 convolution_convert_fusion
  198.5 1.8 copy.91
  200.2 4.5 %all-to-all-start = ((bf16[4,512,640]{2,1,0:T(8,128)(2,1)}), bf16[4,512,640]{2,1,0:T(8,128)(2,1)}, u32[]{:S(2)}, u32[]{:S(2)}) async-start(bf16[4,512,640]{2,1,0:T(8,128)(2,1)} %bitcast.151), calls=%async_computation | async-start | bytes 5242880 | tf_op jit(solution)/shard_map/all_to_all | solution.py:63
  204.8 32.3 %all-to-all-done = bf16[4,512,640]{2,1,0:T(8,128)(2,1)} async-done(((bf16[4,512,640]{2,1,0:T(8,128)(2,1)}), bf16[4,512,640]{2,1,0:T(8,128)(2,1)}, u32[]{:S(2)}, u32[]{:S(2)}) %all-to-all-start) | async-done | bytes 2621472 | tf_op jit(solution)/shard_map/all_to_all | solution.py:63
  237.1 2.3 convert_reduce_fusion
  239.4 2.1 add_convert_fusion
  (45 shorter events, 0.5 us)
Async XLA Ops:
  6.5 190.4 %copy-start = (bf16[384,2560]{1,0:T(8,128)(2,1)S(1)}, bf16[384,2560]{1,0:T(8,128)(2,1)}, u32[]{:S(2)}) copy-start(bf16[384,2560]{1,0:T(8,128)(2,1)} %param.8) | copy-start | bytes 5898244
  6.5 69.7 %all-gather.12.cloned.1.call-start = ((), (), s32[]{:S(2)}) async-start(), calls=%async_computation.3 | async-start | bytes 2359296 | tf_op jit(solution)/shard_map/all_gather | solution.py:46
  23.6 1.4 copy-start.4
  30.4 2.0 copy-start.9
  34.0 24.3 %copy-start.2 = (f32[1,256,384]{2,1,0:T(8,128)}, f32[1,256,384]{2,1,0:T(8,128)S(1)}, u32[]{:S(2)}) copy-start(f32[1,256,384]{2,1,0:T(8,128)S(1)} %multiply_bitcast_fusion) | copy-start | bytes 1179652
  34.0 24.3 %copy-start.3 = (f32[1,256,384]{2,1,0:T(8,128)}, f32[1,256,384]{2,1,0:T(8,128)S(1)}, u32[]{:S(2)}) copy-start(f32[1,256,384]{2,1,0:T(8,128)S(1)} %multiply_bitcast_fusion.1) | copy-start | bytes 1179652
  35.1 21.1 %collective-permute-start.2 = (f32[2,256,384]{2,1,0:T(8,128)}, f32[2,256,384]{2,1,0:T(8,128)}, u32[]{:S(2)}, u32[]{:S(2)}) collective-permute-start(f32[2,256,384]{2,1,0:T(8,128)} %pad_maximum_fusion.1), channel_id=1, source_target_pairs={{0,1},{1,0},{2,3},{3,2},{4,5},{5,4},{6,7},{7,6},{8,9},{9,8},{10,11... | collective-permute-start | bytes 2359304 | tf_op jit(solution)/shard_map/ppermute | solution.py:32
  58.3 54.0 %all-gather.8.cloned.1.call-start = ((), (), s32[]{:S(2)}) async-start(), calls=%async_computation.1 | async-start | bytes 2359296 | tf_op jit(solution)/shard_map/all_gather | solution.py:46
  78.6 110.0 %all-gather.10.cloned.1.call-start = ((), (), s32[]{:S(2)}) async-start(), calls=%async_computation.2 | async-start | bytes 7077888 | tf_op jit(solution)/shard_map/all_gather | solution.py:46
  114.7 8.5 %copy-start.8 = (s32[1,1024]{1,0:T(1,128)S(1)}, s32[1,1024]{1,0:T(1,128)}, u32[]{:S(2)}) copy-start(s32[1,1024]{1,0:T(1,128)} %param.10) | copy-start | bytes 12292
  114.7 31.8 %copy-start.10 = (f32[3]{0:T(128)S(1)}, f32[3]{0:T(128)}, u32[]{:S(2)}) copy-start(f32[3]{0:T(128)} %get-tuple-element.33) | copy-start | bytes 40
  114.7 33.2 %copy-start.12 = (s32[1,17]{1,0:T(1,128)S(1)}, s32[1,17]{1,0:T(1,128)}, u32[]{:S(2)}) copy-start(s32[1,17]{1,0:T(1,128)} %param.11) | copy-start | bytes 208
  115.8 37.6 %collective-permute-start.1 = (bf16[32,768]{1,0:T(8,128)(2,1)S(1)}, bf16[32,768]{1,0:T(8,128)(2,1)S(1)}, u32[]{:S(2)}, u32[]{:S(2)}) collective-permute-start(bf16[32,768]{1,0:T(8,128)(2,1)S(1)} %get-tuple-element.26), channel_id=1, source_target_pairs={{1,0},{3,2},{5,4},{7,6},{9,8},{11,10},{13,12},{15,14},{17,16},{19,... | collective-permute-start | bytes 147464 | tf_op jit(solution)/shard_map/ppermute | solution.py:26
  117.1 36.3 %collective-permute-start = (bf16[32,768]{1,0:T(8,128)(2,1)S(1)}, bf16[32,768]{1,0:T(8,128)(2,1)S(1)}, u32[]{:S(2)}, u32[]{:S(2)}) collective-permute-start(bf16[32,768]{1,0:T(8,128)(2,1)S(1)} %get-tuple-element.25), channel_id=1, source_target_pairs={{0,1},{2,3},{4,5},{6,7},{8,9},{10,11},{12,13},{14,15},{16,17},{18,... | collective-permute-start | bytes 147464 | tf_op jit(solution)/shard_map/ppermute | solution.py:25
  155.3 33.3 %copy-start.1 = (f32[4,256,384]{2,1,0:T(8,128)S(1)}, f32[4,256,384]{2,1,0:T(8,128)}, u32[]{:S(2)}) copy-start(f32[4,256,384]{2,1,0:T(8,128)} %all-gather.12.cloned.1.call-done) | copy-start | bytes 4718596
  193.2 1.0 copy-start.5
  193.2 1.3 copy-start.11
  194.2 0.8 copy-start.7
  194.2 1.1 copy-start.6
  194.2 1.4 copy-start.13
  200.2 36.8 %all-to-all-start = ((bf16[4,512,640]{2,1,0:T(8,128)(2,1)}), bf16[4,512,640]{2,1,0:T(8,128)(2,1)}, u32[]{:S(2)}, u32[]{:S(2)}) async-start(bf16[4,512,640]{2,1,0:T(8,128)(2,1)} %bitcast.151), calls=%async_computation | async-start | bytes 5242880 | tf_op jit(solution)/shard_map/all_to_all | solution.py:63
Sparse Core Ops, SparseCore 0:
  58.4 17.7 all-gather.11
  78.7 33.5 all-gather.7
  114.9 73.6 all-gather.9
where the time goes:
time: 251 us; the launch traced here: 248 us
  waiting for transfers between devices  123 us (49%)
  local copies, waits for them, and re-layouts  29.3 us (12%)
  blocking collectives  28.6 us (11%)
  other arithmetic  24.7 us (10%)
  starting transfers between devices  15.1 us (6%)
  matrix products  14.1 us (6%)
  between operations  13.4 us (5%)
    all_gather x3, waiting for transfers between devices, entering(): pieces = jax.tree.map(lambda part: lax.all_gather(part, axis), subtotal)  72.6 us
    all_to_all x1, waiting for transfers between devices, sum_at_owner(): lax.all_to_all(blocks, axis, split_axis=0, concat_axis=0, tiled=True)  32.3 us
    all_gather x3, blocking collectives, entering(): pieces = jax.tree.map(lambda part: lax.all_gather(part, axis), subtotal)  28.6 us
    ppermute x1, waiting for transfers between devices, from_partner(): lax.ppermute(x, axis, [(i, i ^ 1 << bit) for i in range(lax.axis_size(axi...  17.8 us
    unnamed x31, local copies, waits for them, and re-layouts  11.8 us
    dot_general x1, matrix products, local(): jnp.dot(latents, w_qkv.reshape(width, 3 * columns), preferred_element_typ...  8.07 us
    add x3, other arithmetic, chain_step(): return (earlier[0] * later[0], later[0] * earlier[1] + later[1])  6.85 us
    ppermute x1, starting transfers between devices, extended_2(): before = lax.ppermute(last, axis, up)  6.05 us
  transfers between devices with their start and end apart: 7, of which 5 were waited for; matrix products, arithmetic and copies ran while one was open for 7% of the time, Pallas kernels for 0%

commit v1 on v0

v1 whole, which is shorter than its diff:
```python
import functools

import jax
import jax.numpy as jnp
from jax import lax
from jax.experimental import pallas as pl
from jax.experimental.pallas import tpu as pltpu
from jax.sharding import Mesh
from jax.sharding import PartitionSpec as P

HD = 128
WIN = 64
HALF_WIN = 32
MEM = 256
ROWS = 512
EXT = ROWS + WIN
HEADS = 3
COLS = HEADS * HD
PARTS = 8
PART = MEM // PARTS
PAYLOAD = 2 * PART + 16
DEPTH = 512
BLOCK = 192
SPAN = ("z", "y", "core")
PLANE = ("y", "core", "phase")

outside_frame = 1048576
epsilon = 1e-06
F32 = jnp.float32
BF16 = jnp.bfloat16
SCALE2 = HD ** (-0.5) * 1.4426950408889634


def shape(dims, dtype):
    return jax.ShapeDtypeStruct(dims, dtype)


def normed(x):
    heads = []
    for h in range(HEADS):
        part = x[:, h * HD : (h + 1) * HD]
        square = jnp.mean(part * part, axis=-1, keepdims=True)
        heads.append(part * lax.rsqrt(square + epsilon))
    return jnp.concatenate(heads, axis=1).astype(BF16)


def pieces_of(row):
    full = jnp.broadcast_to(row, (16, COLS))
    high = full.astype(BF16).astype(F32)
    middle = (full - high).astype(BF16).astype(F32)
    low = full - high - middle
    at = lax.broadcasted_iota(jnp.int32, (16, COLS), 0)
    return jnp.where(at == 0, high, jnp.where(at == 1, middle, jnp.where(at == 2, low, 0.0))).astype(BF16)


def row_of(pieces):
    wide = pieces.astype(F32)
    return wide[0:1] + wide[1:2] + wide[2:3]


def tail_kernel(phase, decay, lat, wk, wv, out, acc):
    k = pl.program_id(0)

    @pl.when(k == 0)
    def _():
        acc[...] = jnp.zeros_like(acc)

    x = lat[...]
    acc[:, :COLS] += jnp.dot(x, wk[0], preferred_element_type=F32)
    acc[:, COLS:] += jnp.dot(x, wv[0], preferred_element_type=F32)

    @pl.when(k == pl.num_programs(0) - 1)
    def _():
        keys = normed(acc[:, :COLS])
        values = acc[:, COLS:].astype(BF16)
        first = phase[0] == 0
        rates = [jnp.where(first, decay[0, h], decay[1, h]) for h in range(HEADS)]
        lane = lax.broadcasted_iota(jnp.int32, (1, COLS), 1)
        row = jnp.where(lane < HD, rates[0], jnp.where(lane < 2 * HD, rates[1], rates[2]))
        tile = pieces_of(row)
        for d in range(PARTS):
            out[d, :PART] = keys[d * PART : (d + 1) * PART]
            out[d, PART : 2 * PART] = values[d * PART : (d + 1) * PART]
            out[d, 2 * PART :] = tile


def tails(phase, decay, latents, w3):
    depth = latents.shape[1]
    smem = pl.BlockSpec(memory_space=pltpu.SMEM)
    return pl.pallas_call(
        tail_kernel,
        grid=(depth // DEPTH,),
        out_shape=shape((PARTS, PAYLOAD, COLS), BF16),
        in_specs=[
            smem,
            smem,
            pl.BlockSpec((MEM, DEPTH), lambda k: (1, k)),
            pl.BlockSpec((1, DEPTH, COLS), lambda k: (1, k, 0)),
            pl.BlockSpec((1, DEPTH, COLS), lambda k: (2, k, 0)),
        ],
        out_specs=pl.BlockSpec((PARTS, PAYLOAD, COLS), lambda k: (0, 0, 0)),
        scratch_shapes=[pltpu.VMEM((MEM, 2 * COLS), F32)],
        cost_estimate=pl.CostEstimate(flops=2 * MEM * depth * 2 * COLS, bytes_accessed=5500000, transcendentals=0),
        name="tail_projection",
    )(phase, decay, latents, w3, w3)


def rest_kernel(phase, lat, wq, wk, wv, tail, q_out, kv_out, halo, accq, acc):
    k = pl.program_id(0)

    @pl.when(k == 0)
    def _():
        accq[...] = jnp.zeros_like(accq)
        acc[...] = jnp.zeros_like(acc)

    accq[...] += jnp.dot(lat[...], wq[0], preferred_element_type=F32)
    x = lat[:MEM]
    acc[:, :COLS] += jnp.dot(x, wk[0], preferred_element_type=F32)
    acc[:, COLS:] += jnp.dot(x, wv[0], preferred_element_type=F32)

    @pl.when(k == pl.num_programs(0) - 1)
    def _():
        q_out[...] = normed(accq[...])
        keys = normed(acc[:, :COLS])
        values = acc[:, COLS:].astype(BF16)
        kv_out[:, :COLS] = keys
        kv_out[:, COLS:] = values
        first = phase[0] == 0
        halo[:PART] = jnp.where(first, tail[0, :PART], keys[:PART])
        halo[PART:] = jnp.where(first, tail[0, PART : 2 * PART], values[:PART])


def rest(phase, latents, w3, payload):
    depth = latents.shape[1]
    smem = pl.BlockSpec(memory_space=pltpu.SMEM)
    weight = [pl.BlockSpec((1, DEPTH, COLS), lambda k, j=j: (j, k, 0)) for j in range(3)]
    return pl.pallas_call(
        rest_kernel,
        grid=(depth // DEPTH,),
        out_shape=(shape((ROWS, COLS), BF16), shape((MEM, 2 * COLS), BF16), shape((2 * PART, COLS), BF16)),
        in_specs=[
            smem,
            pl.BlockSpec((ROWS, DEPTH), lambda k: (0, k)),
            *weight,
            pl.BlockSpec((1, PAYLOAD, COLS), lambda k: (PARTS - 1, 0, 0)),
        ],
        out_specs=(
            pl.BlockSpec((ROWS, COLS), lambda k: (0, 0)),
            pl.BlockSpec((MEM, 2 * COLS), lambda k: (0, 0)),
            pl.BlockSpec((2 * PART, COLS), lambda k: (0, 0)),
        ),
        scratch_shapes=[pltpu.VMEM((ROWS, COLS), F32), pltpu.VMEM((MEM, 2 * COLS), F32)],
        cost_estimate=pl.CostEstimate(flops=4 * ROWS * depth * COLS, bytes_accessed=9000000, transcendentals=0),
        name="rest_projection",
    )(phase, latents, w3, w3, w3, payload)


def vmem_call(kernel, outs, name, flops, args, smem=0, scratch=()):
    specs = [pl.BlockSpec(memory_space=pltpu.SMEM)] * smem
    specs += [pl.BlockSpec(memory_space=pltpu.VMEM)] * (len(args) - smem)
    single = not isinstance(outs, tuple)
    out_spec = pl.BlockSpec(memory_space=pltpu.VMEM)
    nbytes = sum(a.size * a.dtype.itemsize for a in args)
    return pl.pallas_call(
        kernel,
        out_shape=outs,
        in_specs=specs,
        out_specs=out_spec if single else tuple(out_spec for _ in outs),
        scratch_shapes=list(scratch),
        cost_estimate=pl.CostEstimate(flops=flops, bytes_accessed=nbytes, transcendentals=0),
        compiler_params=pltpu.CompilerParams(vmem_limit_bytes=32 * 1024 * 1024),
        name=name,
    )(*args)


def window_kernel(q, head_rows, tail_rows, halo, frame_row, frame_column, top, bottom, qx, kx, vx):
    edge = jnp.zeros((HALF_WIN, COLS), BF16)
    qx[:HALF_WIN] = edge
    qx[HALF_WIN + ROWS :] = edge
    qx[HALF_WIN : HALF_WIN + ROWS] = q[...]
    for ext, columns, rows in ((kx, slice(0, COLS), slice(0, PART)), (vx, slice(COLS, 2 * COLS), slice(PART, 2 * PART))):
        ext[:HALF_WIN] = halo[rows]
        ext[HALF_WIN + ROWS :] = halo[rows]
        ext[HALF_WIN : HALF_WIN + MEM] = head_rows[:, columns]
        for d in range(PARTS):
            at = HALF_WIN + MEM + d * PART
            ext[at : at + PART] = tail_rows[d, rows]
    ones = jnp.ones((BLOCK, HD), BF16)
    window_a = lax.broadcasted_iota(jnp.int32, (BLOCK, BLOCK), 0) // WIN
    window_b = lax.broadcasted_iota(jnp.int32, (BLOCK, BLOCK), 1) // WIN
    for b in range(EXT // BLOCK):
        rows = slice(b * BLOCK, (b + 1) * BLOCK)
        allowed = (window_a == window_b) & (frame_row[b] <= frame_column[rows, :1])
        low, high = max(b * BLOCK, HALF_WIN), min((b + 1) * BLOCK, HALF_WIN + ROWS)
        for h in range(HEADS):
            c = slice(h * HD, (h + 1) * HD)
            score = lax.dot_general(qx[rows, c], kx[rows, c], (((1,), (1,)), ((), ())), preferred_element_type=F32)
            weight = jnp.where(allowed, jnp.exp2(score * SCALE2), 0.0).astype(BF16)
            both = jnp.concatenate([vx[rows, c], ones], axis=1)
            result = jnp.dot(weight, both, preferred_element_type=F32)
            cut = result[low - b * BLOCK : high - b * BLOCK]
            top[low - HALF_WIN : high - HALF_WIN, c] = cut[:, :HD]
            bottom[low - HALF_WIN : high - HALF_WIN, c] = cut[:, HD:]


def coefficients(rate):
    return 1.0 - rate, jnp.sqrt(1.0 - rate * rate)


def pack(out, state, row):
    out[: 2 * PART] = state.astype(BF16)
    out[2 * PART :] = pieces_of(row)


def keep(out, state, row):
    out[: 2 * PART] = state
    out[2 * PART :] = jnp.broadcast_to(row, (8, COLS))


def plane_step(keys, values, rate, tail_keys, tail_values):
    for_keys, for_values = coefficients(rate)
    return (
        rate * keys + for_keys * tail_keys.astype(F32),
        rate * values + for_values * tail_values.astype(F32),
    )


def plane_kernel(arrived, state, payload):
    keys = values = jnp.zeros((PART, COLS), F32)
    total = jnp.ones((1, COLS), F32)
    for i in range(PARTS):
        rate = row_of(arrived[i, 2 * PART :])
        keys, values = plane_step(keys, values, rate, arrived[i, :PART], arrived[i, PART : 2 * PART])
        total = total * rate
    both = jnp.concatenate([keys, values], axis=0)
    keep(state, both, total)
    pack(payload, both, total)


def first_kernel(own, got, before, payload):
    entering, rate = got[: 2 * PART].astype(F32), row_of(got[2 * PART :])
    keep(before, entering, rate)
    own_rate = own[2 * PART : 2 * PART + 1]
    pack(payload, own[: 2 * PART] + own_rate * entering, own_rate * rate)


def next_kernel(own, earlier, got, before, payload):
    rate = earlier[2 * PART : 2 * PART + 1]
    entering = earlier[: 2 * PART] + rate * got[: 2 * PART].astype(F32)
    rate = rate * row_of(got[2 * PART :])
    keep(before, entering, rate)
    own_rate = own[2 * PART : 2 * PART + 1]
    pack(payload, own[: 2 * PART] + own_rate * entering, own_rate * rate)


def memory_kernel(earlier, got, arrived, out):
    rate = earlier[2 * PART : 2 * PART + 1]
    entering = earlier[: 2 * PART] + rate * got[: 2 * PART].astype(F32)
    keys, values = entering[:PART], entering[PART:]
    for i in range(PARTS):
        out[i, :PART] = keys.astype(BF16)
        out[i, PART:] = values.astype(BF16)
        if i < PARTS - 1:
            rate = row_of(arrived[i, 2 * PART :])
            keys, values = plane_step(keys, values, rate, arrived[i, :PART], arrived[i, PART : 2 * PART])


def attend_kernel(phase, opened, q, memory, top, bottom, out):
    start = phase[0] * (ROWS // WIN)
    row = lax.broadcasted_iota(jnp.int32, (ROWS, HD), 0)
    window = (row + HALF_WIN) // WIN
    is_open = jnp.zeros((ROWS, HD), F32)
    for w in range(ROWS // WIN + 1):
        flag = jnp.where(opened[0, start + w] == 1, 1.0, 0.0)
        is_open = jnp.where(window == w, flag, is_open)
    ones = jnp.ones((MEM, HD), BF16)
    for h in range(HEADS):
        c = slice(h * HD, (h + 1) * HD)
        keys = memory[:, :PART, c].reshape(MEM, HD)
        values = memory[:, PART:, c].reshape(MEM, HD)
        score = lax.dot_general(q[:, c], keys, (((1,), (1,)), ((), ())), preferred_element_type=F32)
        weight = jnp.exp2(score * SCALE2).astype(BF16)
        result = jnp.dot(weight, jnp.concatenate([values, ones], axis=1), preferred_element_type=F32)
        above = top[:, c] + is_open * result[:, :HD]
        below = bottom[:, c] + is_open * result[:, HD:]
        out[:, c] = (above / below).astype(BF16)


def final_kernel(column, lat, *refs):
    out = refs[-1]
    attended, weights = refs[:4], refs[4:8]
    total = lat[...].astype(F32)
    for a, w in zip(attended, weights):
        total = total + jnp.dot(a[...], w[...], preferred_element_type=F32).astype(BF16).astype(F32)
    out[...] = total.astype(BF16)


def final(column, latents, attended, weights):
    share = weights[0].shape[1]
    rows = 256
    whole = pl.BlockSpec((COLS, share), lambda i, col: (0, 0))
    return pl.pallas_call(
        final_kernel,
        grid_spec=pltpu.PrefetchScalarGridSpec(
            num_scalar_prefetch=1,
            grid=(ROWS // rows,),
            in_specs=[pl.BlockSpec((rows, share), lambda i, col: (i, col[0]))]
            + [pl.BlockSpec((rows, COLS), lambda i, col: (i, 0))] * 4
            + [whole] * 4,
            out_specs=pl.BlockSpec((rows, share), lambda i, col: (i, 0)),
        ),
        out_shape=shape((ROWS, share), BF16),
        cost_estimate=pl.CostEstimate(flops=2 * ROWS * 4 * COLS * share, bytes_accessed=4000000, transcendentals=0),
        name="output_projection",
    )(column, latents, *attended, *weights)


def moved(x, axis, by, wrap=True):
    size = lax.axis_size(axis)
    pairs = [(i, (i + by) % size) for i in range(size) if wrap or 0 <= i + by < size]
    return lax.ppermute(x, axis, pairs)


def local(latents, w_qkv, w_out, decay, frame_ids, memory_mask):
    phase = lax.axis_index("phase")
    mp = lax.axis_index("mp")
    phase_ref = phase.reshape(1).astype(jnp.int32)
    w3 = jnp.transpose(w_qkv, (1, 0, 2))

    payload = tails(phase_ref, decay[0], latents, w3)
    arrived = lax.all_to_all(payload, PLANE, 0, 0, tiled=True)

    queries, head_rows, halo = rest(phase_ref, latents, w3, payload)
    halo = lax.ppermute(halo, "phase", [(0, 1), (1, 0)])

    share = w_out.shape[1] // 4
    offsets = (0, 1, -1, 2)
    weights = []
    for by in offsets:
        piece = lax.dynamic_slice_in_dim(w_out, (mp + by) % 4 * share, share, 1)
        weights.append(moved(piece, "mp", by) if by else piece)

    frames_pad = jnp.pad(frame_ids[0], (HALF_WIN, HALF_WIN), constant_values=outside_frame)
    frames = lax.dynamic_slice_in_dim(frames_pad, phase * ROWS, EXT)
    frame_row = frames.reshape(EXT // BLOCK, 1, BLOCK)
    frame_column = jnp.broadcast_to(frames[:, None], (EXT, HD))
    top, bottom = vmem_call(
        window_kernel,
        (shape((ROWS, COLS), F32), shape((ROWS, COLS), F32)),
        "window_attention",
        4 * EXT * BLOCK * COLS * 2,
        (queries, head_rows, payload, halo, frame_row, frame_column),
        scratch=[pltpu.VMEM((EXT, COLS), BF16)] * 3,
    )

    wide = shape((2 * PART + 8, COLS), F32)
    packed = shape((PAYLOAD, COLS), BF16)
    own, sent = vmem_call(plane_kernel, (wide, packed), "plane_total", 1000000, (arrived,))
    got = moved(sent, "z", 1, wrap=False)
    before, sent = vmem_call(first_kernel, (wide, packed), "before_1", 100000, (own, got))
    got = moved(sent, "z", 2, wrap=False)
    before, sent = vmem_call(next_kernel, (wide, packed), "before_3", 100000, (own, before, got))
    got = moved(sent, "z", 4, wrap=False)
    memory = vmem_call(
        memory_kernel, shape((PARTS, 2 * PART, COLS), BF16), "section_memory", 1000000, (before, got, arrived)
    )
    memory = lax.all_to_all(memory, PLANE, 0, 0, tiled=True)

    attended = vmem_call(
        attend_kernel,
        shape((ROWS, COLS), BF16),
        "memory_attention",
        4 * ROWS * MEM * COLS * 2,
        (phase_ref, memory_mask, queries, memory, top, bottom),
        smem=2,
    )
    gathered = [moved(attended, "mp", by) if by else attended for by in offsets]
    return final(mp.reshape(1).astype(jnp.int32), latents, gathered, weights)


def solution(mesh):
    finer = Mesh(
        mesh.devices.reshape(8, 2, 2, mesh.shape["mp"], mesh.shape["phase"]),
        ("z", "y", "core", "mp", "phase"),
    )
    placed = (
        P((*SPAN, "phase"), None),
        P(None, None, "mp"),
        P("mp", None),
        P(SPAN, None, "mp"),
        P(SPAN, None),
        P(SPAN, None),
    )
    return jax.shard_map(
        local, mesh=finer, in_specs=placed, out_specs=P((*SPAN, "phase"), "mp"), check_vma=False
    )
```

time: 251 us -> 99.7 us (0.40)
  the two profiles are of different devices: /device:TPU:32 before, /device:TPU:6 now
where the time goes in v1:
time: 99.7 us; the launch traced here: 99.1 us
  starting transfers between devices  35.3 us (35%)
  waiting for transfers between devices  22.7 us (23%)
  Pallas kernels  22 us (22%)
  blocking collectives  13.6 us (14%)
  local copies, waits for them, and re-layouts  5.37 us (5%)
    ppermute x9, starting transfers between devices, moved(): return lax.ppermute(x, axis, pairs)  28.5 us
    ppermute x9, waiting for transfers between devices, moved(): return lax.ppermute(x, axis, pairs)  22.4 us
    all_to_all x1, blocking collectives, local(): arrived = lax.all_to_all(payload, PLANE, 0, 0, tiled=True)  13.6 us
    pallas_call x1, Pallas kernels, rest(): pl.pallas_call(rest_kernel, grid=(depth // DEPTH,), out_shape=(shape((ROW...  7.94 us
    pallas_call x1, Pallas kernels, tails(): pl.pallas_call(tail_kernel, grid=(depth // DEPTH,), out_shape=shape((PART...  6.1 us
    pallas_call x1, Pallas kernels, final(): pl.pallas_call(final_kernel, grid_spec=pltpu.PrefetchScalarGridSpec(num_s...  4.65 us
    unnamed x22, local copies, waits for them, and re-layouts  3.9 us
    all_to_all x1, starting transfers between devices, local(): memory = lax.all_to_all(memory, PLANE, 0, 0, tiled=True)  3.45 us
  transfers between devices with their start and end apart: 11, of which 6 were waited for; matrix products, arithmetic and copies ran while one was open for 1% of the time, Pallas kernels for 11%

profile of v1, /device:TPU:6, one launch (start us, length us, event | category | flops | bytes accessed | tf_op | source)
XLA Modules:
  0.0 99.1 jit_solution(5127585292554452475)
XLA Ops:
  0.0 0.0 copy-start.6
  0.0 6.1 %tail_projection.1.tail.tail_rows = bf16[8,80,384]{2,1,0:T(8,128)(2,1)} custom-call(s32[1]{0:T(128)} %bitcast.1.phase, f32[2,3]{1,0:T(2,128)} %bitcast.11, bf16[512,2560]{1,0:T(8,128)(2,1)} %lat.5, bf16[3,2560,384]{2,1,0:T(8,128)(2,1)} %bitcast.5, bf16[3,2560,384]{2,1,0:T(8,128)(2,1)} %bitcast.6), custom_call_target="tpu_custom_call" | custom-call | flops 1006632960 | bytes 5500000 | tf_op jit(solution)/shard_map/tail_projection/pallas_call | solution.py:90
  6.1 13.6 %all_to_all.10.arrived = bf16[8,80,384]{2,1,0:T(8,128)(2,1)S(1)} all-to-all(bf16[8,80,384]{2,1,0:T(8,128)(2,1)} %tail_projection.1.tail.tail_rows), channel_id=1, replica_groups=mesh['z'=8,'y'=2,'core'=2,'mp'=4,'phase'=2] {'y','core','phase'}, dimensions={0} | all-to-all | bytes 983040 | tf_op jit(solution)/shard_map/all_to_all | solution.py:331
  19.7 0.2 plane_total.1
  19.8 3.8 %collective-permute-start = (bf16[80,384]{1,0:T(8,128)(2,1)S(1)}, bf16[80,384]{1,0:T(8,128)(2,1)S(1)}, u32[]{:S(2)}, u32[]{:S(2)}) collective-permute-start(bf16[80,384]{1,0:T(8,128)(2,1)S(1)} %get-tuple-element.18), channel_id=1, source_target_pairs={{0,32},{32,64},{64,96},{96,128},{128,160},{160,192},{192,224},{1,3... | collective-permute-start | bytes 184328 | tf_op jit(solution)/shard_map/ppermute | solution.py:321
  23.7 1.8 %collective-permute-done.got = bf16[80,384]{1,0:T(8,128)(2,1)S(1)} collective-permute-done((bf16[80,384]{1,0:T(8,128)(2,1)S(1)}, bf16[80,384]{1,0:T(8,128)(2,1)S(1)}, u32[]{:S(2)}, u32[]{:S(2)}) %collective-permute-start) | collective-permute-done | bytes 61472 | tf_op jit(solution)/shard_map/ppermute | solution.py:321
  25.5 5.7 %collective-permute-start.1 = (bf16[80,384]{1,0:T(8,128)(2,1)S(1)}, bf16[80,384]{1,0:T(8,128)(2,1)S(1)}, u32[]{:S(2)}, u32[]{:S(2)}) collective-permute-start(bf16[80,384]{1,0:T(8,128)(2,1)S(1)} %get-tuple-element.20), channel_id=1, source_target_pairs={{0,64},{32,96},{64,128},{96,160},{128,192},{160,224},{1,65},{33,97... | collective-permute-start | bytes 184328 | tf_op jit(solution)/shard_map/ppermute | solution.py:321
  31.3 0.0 copy-done.6
  31.3 1.2 %constant_dynamic-slice_fusion = (bf16[384,640]{1,0:T(8,128)(2,1)}, bf16[384,640]{1,0:T(8,128)(2,1)}, bf16[384,640]{1,0:T(8,128)(2,1)}, bf16[384,640]{1,0:T(8,128)(2,1)S(1)}) fusion(bf16[384,2560]{1,0:T(8,128)(2,1)S(1)} %copy-done.6, s32[]{:T(128)S(6)} %select_n.42, s32[]{:T(128)S(6)} %select_n.38, s32[]{:T(128)S(6)} %select_n.36, s32[]{:T(128)S(6)} %select_n.40), kind=kLoop, calls=%fused_computation.1 | loop fusion | bytes 3932176 | tf_op jit(solution)/shard_map/dynamic_slice | solution.py:340
  32.5 1.4 %collective-permute-start.9 = (bf16[384,640]{1,0:T(8,128)(2,1)}, bf16[384,640]{1,0:T(8,128)(2,1)}, u32[]{:S(2)}, u32[]{:S(2)}) collective-permute-start(bf16[384,640]{1,0:T(8,128)(2,1)} %get-tuple-element.27), channel_id=1, source_target_pairs={{0,4},{2,6},{4,0},{6,2},{1,5},{3,7},{5,1},{7,3},{8,12},{10,14},{12... | collective-permute-start | bytes 1474568 | tf_op jit(solution)/shard_map/ppermute | solution.py:321
  33.9 0.0 collective-permute-done.1.got
  33.9 10.7 %collective-permute-start.2 = (bf16[80,384]{1,0:T(8,128)(2,1)S(1)}, bf16[80,384]{1,0:T(8,128)(2,1)S(1)}, u32[]{:S(2)}, u32[]{:S(2)}) collective-permute-start(bf16[80,384]{1,0:T(8,128)(2,1)S(1)} %get-tuple-element.22), channel_id=1, source_target_pairs={{0,128},{32,160},{64,192},{96,224},{1,129},{33,161},{65,193},{97,2... | collective-permute-start | bytes 184328 | tf_op jit(solution)/shard_map/ppermute | solution.py:321
  44.7 1.8 %collective-permute-done.2.got = bf16[80,384]{1,0:T(8,128)(2,1)S(1)} collective-permute-done((bf16[80,384]{1,0:T(8,128)(2,1)S(1)}, bf16[80,384]{1,0:T(8,128)(2,1)S(1)}, u32[]{:S(2)}, u32[]{:S(2)}) %collective-permute-start.2) | collective-permute-done | bytes 61472 | tf_op jit(solution)/shard_map/ppermute | solution.py:321
  46.5 0.9 section_memory.1
  47.5 3.5 %all-to-all-start.1 = ((bf16[8,64,384]{2,1,0:T(8,128)(2,1)}), bf16[8,64,384]{2,1,0:T(8,128)(2,1)S(1)}, u32[]{:S(2)}, u32[]{:S(2)}) async-start(bf16[8,64,384]{2,1,0:T(8,128)(2,1)} %section_memory.1), calls=%async_computation.1 | async-start | bytes 786432 | tf_op jit(solution)/shard_map/all_to_all | solution.py:367
  50.9 0.0 copy-start.10
  50.9 0.0 copy-start
  51.0 0.0 copy-start.5
  51.0 7.9 %rest_projection.1 = (bf16[512,384]{1,0:T(8,128)(2,1)}, bf16[256,768]{1,0:T(8,128)(2,1)}, bf16[64,384]{1,0:T(8,128)(2,1)}) custom-call(s32[1]{0:T(128)} %bitcast.1.phase, bf16[512,2560]{1,0:T(8,128)(2,1)} %lat.5, bf16[3,2560,384]{2,1,0:T(8,128)(2,1)} %bitcast.7, bf16[3,2560,384]{2,1,0:T(8,128)(2,1)} %bitcast.8, bf16[3,2560,384]{2,1,0:T(8,128)(2,1)} %bitcast.9, ...), custom_call_target="tpu_custom_call" | custom-call | flops 2013265920 | bytes 9000000 | tf_op jit(solution)/shard_map/rest_projection/pallas_call | solution.py:137
  58.9 3.4 %collective-permute-start.3 = (bf16[64,384]{1,0:T(8,128)(2,1)}, bf16[64,384]{1,0:T(8,128)(2,1)S(1)}, u32[]{:S(2)}, u32[]{:S(2)}) collective-permute-start(bf16[64,384]{1,0:T(8,128)(2,1)} %get-tuple-element.24), channel_id=1, source_target_pairs={{0,1},{1,0},{2,3},{3,2},{4,5},{5,4},{6,7},{7,6},{8,9},{9,8},{10,11... | collective-permute-start | bytes 147464 | tf_op jit(solution)/shard_map/ppermute | solution.py:334
  62.3 0.5 collective-permute-start.7
  62.8 1.5 %collective-permute-start.8 = (bf16[384,640]{1,0:T(8,128)(2,1)S(1)}, bf16[384,640]{1,0:T(8,128)(2,1)}, u32[]{:S(2)}, u32[]{:S(2)}) collective-permute-start(bf16[384,640]{1,0:T(8,128)(2,1)S(1)} %get-tuple-element.30), channel_id=1, source_target_pairs={{0,6},{2,0},{4,2},{6,4},{1,7},{3,1},{5,3},{7,5},{8,14},{10,8},{12,... | collective-permute-start | bytes 1474568 | tf_op jit(solution)/shard_map/ppermute | solution.py:321
  64.3 0.0 copy-done.10
  64.3 0.1 pad_dynamic-slice_fusion
  64.4 0.1 reshape.12.frame_row
  64.5 0.2 collective-permute-done.3.halo
  64.7 0.1 broadcast_in_dim.2.frame_column
  64.9 0.0 copy-done
  64.9 0.0 copy-start.1
  64.9 1.0 copy-done.1
  65.9 0.0 copy-start.4
  65.9 1.0 %copy-done.4 = bf16[256,768]{1,0:T(8,128)(2,1)S(1)} copy-done((bf16[256,768]{1,0:T(8,128)(2,1)S(1)}, bf16[256,768]{1,0:T(8,128)(2,1)}, u32[]{:S(2)}) %copy-start.4) | copy-done | bytes 393240
  66.9 0.9 window_attention.1
  67.8 0.0 all-to-all-done.1.memory
  67.8 0.0 copy-done.5
  67.8 0.0 copy-start.2
  67.8 1.0 copy-done.2
  68.8 1.2 %memory_attention.1.refs_0_ = bf16[512,384]{1,0:T(8,128)(2,1)S(1)} custom-call(s32[1]{0:T(128)} %bitcast.1.phase, s32[1,17]{1,0:T(1,128)S(1)} %copy-done.5, bf16[512,384]{1,0:T(8,128)(2,1)S(1)} %copy-done.2, bf16[8,64,384]{2,1,0:T(8,128)(2,1)S(1)} %all-to-all-done.1.memory, f32[512,384]{1,0:T(8,128)S(1)} %get-tuple-element.25.top, ...), custom_call_target="tpu_custom_call" | custom-call | flops 402653184 | bytes 2359368 | tf_op jit(solution)/shard_map/memory_attention/pallas_call | solution.py:164
  70.0 0.0 copy-start.3
  70.0 1.5 %collective-permute-start.6 = (bf16[512,384]{1,0:T(8,128)(2,1)S(1)}, bf16[512,384]{1,0:T(8,128)(2,1)S(1)}, u32[]{:S(2)}, u32[]{:S(2)}) collective-permute-start(bf16[512,384]{1,0:T(8,128)(2,1)S(1)} %memory_attention.1.refs_0_), channel_id=1, source_target_pairs={{0,4},{2,6},{4,0},{6,2},{1,5},{3,7},{5,1},{7,3},{8,12},{10,14},{12... | collective-permute-start | bytes 1179656 | tf_op jit(solution)/shard_map/ppermute | solution.py:321
  71.5 0.9 collective-permute-start.5
  72.4 0.0 collective-permute-done.9.refs_7_
  72.4 2.3 %collective-permute-start.4 = (bf16[512,384]{1,0:T(8,128)(2,1)S(1)}, bf16[512,384]{1,0:T(8,128)(2,1)S(1)}, u32[]{:S(2)}, u32[]{:S(2)}) collective-permute-start(bf16[512,384]{1,0:T(8,128)(2,1)S(1)} %memory_attention.1.refs_0_), channel_id=1, source_target_pairs={{0,2},{2,4},{4,6},{6,0},{1,3},{3,5},{5,7},{7,1},{8,10},{10,12},{12... | collective-permute-start | bytes 1179656 | tf_op jit(solution)/shard_map/ppermute | solution.py:321
  74.8 2.0 %collective-permute-done.7.refs_5_ = bf16[384,640]{1,0:T(8,128)(2,1)} collective-permute-done((bf16[384,640]{1,0:T(8,128)(2,1)}, bf16[384,640]{1,0:T(8,128)(2,1)}, u32[]{:S(2)}, u32[]{:S(2)}) %collective-permute-start.7) | collective-permute-done | bytes 491552 | tf_op jit(solution)/shard_map/ppermute | solution.py:321
  76.7 9.9 %collective-permute-done.8.refs_6_ = bf16[384,640]{1,0:T(8,128)(2,1)} collective-permute-done((bf16[384,640]{1,0:T(8,128)(2,1)S(1)}, bf16[384,640]{1,0:T(8,128)(2,1)}, u32[]{:S(2)}, u32[]{:S(2)}) %collective-permute-start.8) | collective-permute-done | bytes 491552 | tf_op jit(solution)/shard_map/ppermute | solution.py:321
  86.7 0.0 collective-permute-done.6.refs_3_
  86.7 0.0 copy-start.7
  86.7 6.9 %collective-permute-done.5.refs_2_ = bf16[512,384]{1,0:T(8,128)(2,1)S(1)} collective-permute-done((bf16[512,384]{1,0:T(8,128)(2,1)S(1)}, bf16[512,384]{1,0:T(8,128)(2,1)S(1)}, u32[]{:S(2)}, u32[]{:S(2)}) %collective-permute-start.5) | collective-permute-done | bytes 393248 | tf_op jit(solution)/shard_map/ppermute | solution.py:321
  93.6 0.0 copy-start.8
  93.6 0.0 collective-permute-done.4.refs_1_
  93.6 0.0 copy-start.9
  93.6 0.0 copy-done.3
  93.6 0.0 copy-done.7
  93.6 0.7 copy-done.8
  94.3 0.2 copy-done.9
  94.5 4.7 %output_projection.1 = bf16[512,640]{1,0:T(8,128)(2,1)} custom-call(s32[1]{0:T(128)} %bitcast.column, bf16[512,2560]{1,0:T(8,128)(2,1)} %lat.5, bf16[512,384]{1,0:T(8,128)(2,1)} %copy-done.3, bf16[512,384]{1,0:T(8,128)(2,1)} %copy-done.9, bf16[512,384]{1,0:T(8,128)(2,1)} %copy-done.8, bf16[512,384]{1,0:T(8,128)(2,1)} %copy-done.7, ...), custom_call_target="tpu_custom_call" | custom-call | flops 1006632960 | bytes 4000000 | tf_op jit(solution)/shard_map/output_projection/pallas_call | solution.py:302
  (2 shorter events, 0.1 us)
Async XLA Ops:
  0.0 31.3 %copy-start.6 = (bf16[384,2560]{1,0:T(8,128)(2,1)S(1)}, bf16[384,2560]{1,0:T(8,128)(2,1)}, u32[]{:S(2)}) copy-start(bf16[384,2560]{1,0:T(8,128)(2,1)} %param.8) | copy-start | bytes 5898244
  19.8 5.7 %collective-permute-start = (bf16[80,384]{1,0:T(8,128)(2,1)S(1)}, bf16[80,384]{1,0:T(8,128)(2,1)S(1)}, u32[]{:S(2)}, u32[]{:S(2)}) collective-permute-start(bf16[80,384]{1,0:T(8,128)(2,1)S(1)} %get-tuple-element.18), channel_id=1, source_target_pairs={{0,32},{32,64},{64,96},{96,128},{128,160},{160,192},{192,224},{1,3... | collective-permute-start | bytes 184328 | tf_op jit(solution)/shard_map/ppermute | solution.py:321
  25.5 8.4 %collective-permute-start.1 = (bf16[80,384]{1,0:T(8,128)(2,1)S(1)}, bf16[80,384]{1,0:T(8,128)(2,1)S(1)}, u32[]{:S(2)}, u32[]{:S(2)}) collective-permute-start(bf16[80,384]{1,0:T(8,128)(2,1)S(1)} %get-tuple-element.20), channel_id=1, source_target_pairs={{0,64},{32,96},{64,128},{96,160},{128,192},{160,224},{1,65},{33,97... | collective-permute-start | bytes 184328 | tf_op jit(solution)/shard_map/ppermute | solution.py:321
  32.5 39.9 %collective-permute-start.9 = (bf16[384,640]{1,0:T(8,128)(2,1)}, bf16[384,640]{1,0:T(8,128)(2,1)}, u32[]{:S(2)}, u32[]{:S(2)}) collective-permute-start(bf16[384,640]{1,0:T(8,128)(2,1)} %get-tuple-element.27), channel_id=1, source_target_pairs={{0,4},{2,6},{4,0},{6,2},{1,5},{3,7},{5,1},{7,3},{8,12},{10,14},{12... | collective-permute-start | bytes 1474568 | tf_op jit(solution)/shard_map/ppermute | solution.py:321
  33.9 12.6 %collective-permute-start.2 = (bf16[80,384]{1,0:T(8,128)(2,1)S(1)}, bf16[80,384]{1,0:T(8,128)(2,1)S(1)}, u32[]{:S(2)}, u32[]{:S(2)}) collective-permute-start(bf16[80,384]{1,0:T(8,128)(2,1)S(1)} %get-tuple-element.22), channel_id=1, source_target_pairs={{0,128},{32,160},{64,192},{96,224},{1,129},{33,161},{65,193},{97,2... | collective-permute-start | bytes 184328 | tf_op jit(solution)/shard_map/ppermute | solution.py:321
  47.5 20.3 %all-to-all-start.1 = ((bf16[8,64,384]{2,1,0:T(8,128)(2,1)}), bf16[8,64,384]{2,1,0:T(8,128)(2,1)S(1)}, u32[]{:S(2)}, u32[]{:S(2)}) async-start(bf16[8,64,384]{2,1,0:T(8,128)(2,1)} %section_memory.1), calls=%async_computation.1 | async-start | bytes 786432 | tf_op jit(solution)/shard_map/all_to_all | solution.py:367
  50.9 13.4 %copy-start.10 = (s32[1,1024]{1,0:T(1,128)S(1)}, s32[1,1024]{1,0:T(1,128)}, u32[]{:S(2)}) copy-start(s32[1,1024]{1,0:T(1,128)} %param.10) | copy-start | bytes 12292
  50.9 13.9 %copy-start = (bf16[8,80,384]{2,1,0:T(8,128)(2,1)S(1)}, bf16[8,80,384]{2,1,0:T(8,128)(2,1)}, u32[]{:S(2)}) copy-start(bf16[8,80,384]{2,1,0:T(8,128)(2,1)} %tail_projection.1.tail.tail_rows) | copy-start | bytes 1474564
  51.0 16.8 %copy-start.5 = (s32[1,17]{1,0:T(1,128)S(1)}, s32[1,17]{1,0:T(1,128)}, u32[]{:S(2)}) copy-start(s32[1,17]{1,0:T(1,128)} %opened.1) | copy-start | bytes 208
  58.9 5.8 %collective-permute-start.3 = (bf16[64,384]{1,0:T(8,128)(2,1)}, bf16[64,384]{1,0:T(8,128)(2,1)S(1)}, u32[]{:S(2)}, u32[]{:S(2)}) collective-permute-start(bf16[64,384]{1,0:T(8,128)(2,1)} %get-tuple-element.24), channel_id=1, source_target_pairs={{0,1},{1,0},{2,3},{3,2},{4,5},{5,4},{6,7},{7,6},{8,9},{9,8},{10,11... | collective-permute-start | bytes 147464 | tf_op jit(solution)/shard_map/ppermute | solution.py:334
  62.3 14.4 %collective-permute-start.7 = (bf16[384,640]{1,0:T(8,128)(2,1)}, bf16[384,640]{1,0:T(8,128)(2,1)}, u32[]{:S(2)}, u32[]{:S(2)}) collective-permute-start(bf16[384,640]{1,0:T(8,128)(2,1)} %get-tuple-element.28), channel_id=1, source_target_pairs={{0,2},{2,4},{4,6},{6,0},{1,3},{3,5},{5,7},{7,1},{8,10},{10,12},{12... | collective-permute-start | bytes 1474568 | tf_op jit(solution)/shard_map/ppermute | solution.py:321
  62.8 23.9 %collective-permute-start.8 = (bf16[384,640]{1,0:T(8,128)(2,1)S(1)}, bf16[384,640]{1,0:T(8,128)(2,1)}, u32[]{:S(2)}, u32[]{:S(2)}) collective-permute-start(bf16[384,640]{1,0:T(8,128)(2,1)S(1)} %get-tuple-element.30), channel_id=1, source_target_pairs={{0,6},{2,0},{4,2},{6,4},{1,7},{3,1},{5,3},{7,5},{8,14},{10,8},{12,... | collective-permute-start | bytes 1474568 | tf_op jit(solution)/shard_map/ppermute | solution.py:321
  64.9 1.0 %copy-start.1 = (bf16[512,384]{1,0:T(8,128)(2,1)S(1)}, bf16[512,384]{1,0:T(8,128)(2,1)}, u32[]{:S(2)}) copy-start(bf16[512,384]{1,0:T(8,128)(2,1)} %get-tuple-element.16.q) | copy-start | bytes 1179652
  65.9 1.0 %copy-start.4 = (bf16[256,768]{1,0:T(8,128)(2,1)S(1)}, bf16[256,768]{1,0:T(8,128)(2,1)}, u32[]{:S(2)}) copy-start(bf16[256,768]{1,0:T(8,128)(2,1)} %get-tuple-element.23.head_rows) | copy-start | bytes 1179652
  67.8 1.0 %copy-start.2 = (bf16[512,384]{1,0:T(8,128)(2,1)S(1)}, bf16[512,384]{1,0:T(8,128)(2,1)}, u32[]{:S(2)}) copy-start(bf16[512,384]{1,0:T(8,128)(2,1)} %get-tuple-element.16.q) | copy-start | bytes 1179652
  70.0 23.5 %copy-start.3 = (bf16[512,384]{1,0:T(8,128)(2,1)}, bf16[512,384]{1,0:T(8,128)(2,1)S(1)}, u32[]{:S(2)}) copy-start(bf16[512,384]{1,0:T(8,128)(2,1)S(1)} %memory_attention.1.refs_0_) | copy-start | bytes 1179652
  70.0 16.6 %collective-permute-start.6 = (bf16[512,384]{1,0:T(8,128)(2,1)S(1)}, bf16[512,384]{1,0:T(8,128)(2,1)S(1)}, u32[]{:S(2)}, u32[]{:S(2)}) collective-permute-start(bf16[512,384]{1,0:T(8,128)(2,1)S(1)} %memory_attention.1.refs_0_), channel_id=1, source_target_pairs={{0,4},{2,6},{4,0},{6,2},{1,5},{3,7},{5,1},{7,3},{8,12},{10,14},{12... | collective-permute-start | bytes 1179656 | tf_op jit(solution)/shard_map/ppermute | solution.py:321
  71.5 22.0 %collective-permute-start.5 = (bf16[512,384]{1,0:T(8,128)(2,1)S(1)}, bf16[512,384]{1,0:T(8,128)(2,1)S(1)}, u32[]{:S(2)}, u32[]{:S(2)}) collective-permute-start(bf16[512,384]{1,0:T(8,128)(2,1)S(1)} %memory_attention.1.refs_0_), channel_id=1, source_target_pairs={{0,6},{2,0},{4,2},{6,4},{1,7},{3,1},{5,3},{7,5},{8,14},{10,8},{12,... | collective-permute-start | bytes 1179656 | tf_op jit(solution)/shard_map/ppermute | solution.py:321
  72.4 21.1 %collective-permute-start.4 = (bf16[512,384]{1,0:T(8,128)(2,1)S(1)}, bf16[512,384]{1,0:T(8,128)(2,1)S(1)}, u32[]{:S(2)}, u32[]{:S(2)}) collective-permute-start(bf16[512,384]{1,0:T(8,128)(2,1)S(1)} %memory_attention.1.refs_0_), channel_id=1, source_target_pairs={{0,2},{2,4},{4,6},{6,0},{1,3},{3,5},{5,7},{7,1},{8,10},{10,12},{12... | collective-permute-start | bytes 1179656 | tf_op jit(solution)/shard_map/ppermute | solution.py:321
  86.7 6.9 %copy-start.7 = (bf16[512,384]{1,0:T(8,128)(2,1)}, bf16[512,384]{1,0:T(8,128)(2,1)S(1)}, u32[]{:S(2)}) copy-start(bf16[512,384]{1,0:T(8,128)(2,1)S(1)} %collective-permute-done.6.refs_3_) | copy-start | bytes 1179652
  93.6 0.8 copy-start.8
  93.6 0.9 copy-start.9

commit v2 on v1

v2 whole, which is shorter than its diff:
```python
import functools

import jax
import jax.numpy as jnp
from jax import lax
from jax.experimental import pallas as pl
from jax.experimental.pallas import tpu as pltpu
from jax.sharding import Mesh
from jax.sharding import PartitionSpec as P

HD = 128
WIN = 64
HALF_WIN = 32
MEM = 256
ROWS = 512
EXT = ROWS + WIN
HEADS = 3
COLS = HEADS * HD
PARTS = 8
PART = MEM // PARTS
PAYLOAD = 2 * PART + 16
CHUNKS = 5
TAIL_LIMIT = 60 * 1024 * 1024
REST_LIMIT = 60 * 1024 * 1024
LIMIT = 32 * 1024 * 1024
BLOCK = 192
SPAN = ("z", "y", "core")
PLANE = ("y", "core", "phase")

outside_frame = 1048576
epsilon = 1e-06
F32 = jnp.float32
BF16 = jnp.bfloat16
SCALE2 = HD ** (-0.5) * 1.4426950408889634


def shape(dims, dtype):
    return jax.ShapeDtypeStruct(dims, dtype)


def normed(x):
    heads = []
    for h in range(HEADS):
        part = x[:, h * HD : (h + 1) * HD]
        square = jnp.mean(part * part, axis=-1, keepdims=True)
        heads.append(part * lax.rsqrt(square + epsilon))
    return jnp.concatenate(heads, axis=1).astype(BF16)


def pieces_of(row):
    full = jnp.broadcast_to(row, (16, COLS))
    high = full.astype(BF16).astype(F32)
    middle = (full - high).astype(BF16).astype(F32)
    low = full - high - middle
    at = lax.broadcasted_iota(jnp.int32, (16, COLS), 0)
    return jnp.where(at == 0, high, jnp.where(at == 1, middle, jnp.where(at == 2, low, 0.0))).astype(BF16)


def row_of(pieces):
    wide = pieces.astype(F32)
    return wide[0:1] + wide[1:2] + wide[2:3]


def tail_kernel(phase, decay, lat, w, out, tail, wkv, acc, sems):
    depth = lat.shape[1]
    step = depth // CHUNKS
    copies = []
    for k in range(CHUNKS):
        at = pl.ds(k * step, step)
        group = [
            pltpu.make_async_copy(lat.at[pl.ds(MEM, MEM), at], tail.at[:, at], sems.at[3 * k]),
            pltpu.make_async_copy(w.at[1, at], wkv.at[at, pl.ds(0, COLS)], sems.at[3 * k + 1]),
            pltpu.make_async_copy(w.at[2, at], wkv.at[at, pl.ds(COLS, COLS)], sems.at[3 * k + 2]),
        ]
        for copy in group:
            copy.start()
        copies.append(group)
    for k, group in enumerate(copies):
        for copy in group:
            copy.wait()
        at = slice(k * step, (k + 1) * step)
        part = jnp.dot(tail[:, at], wkv[at], preferred_element_type=F32)
        if k == 0:
            acc[...] = part
        else:
            acc[...] += part
    keys = normed(acc[:, :COLS])
    values = acc[:, COLS:].astype(BF16)
    first = phase[0] == 0
    rates = [jnp.where(first, decay[0, h], decay[1, h]) for h in range(HEADS)]
    lane = lax.broadcasted_iota(jnp.int32, (1, COLS), 1)
    row = jnp.where(lane < HD, rates[0], jnp.where(lane < 2 * HD, rates[1], rates[2]))
    tile = pieces_of(row)
    for d in range(PARTS):
        out[d, :PART] = keys[d * PART : (d + 1) * PART]
        out[d, PART : 2 * PART] = values[d * PART : (d + 1) * PART]
        out[d, 2 * PART :] = tile


def tails(phase, decay, latents, w3):
    depth = latents.shape[1]
    smem = pl.BlockSpec(memory_space=pltpu.SMEM)
    vmem = pl.BlockSpec(memory_space=pltpu.VMEM)
    hbm = pl.BlockSpec(memory_space=pl.ANY)
    return pl.pallas_call(
        tail_kernel,
        out_shape=shape((PARTS, PAYLOAD, COLS), BF16),
        in_specs=[smem, smem, hbm, hbm],
        out_specs=vmem,
        scratch_shapes=[
            pltpu.VMEM((MEM, depth), BF16),
            pltpu.VMEM((depth, 2 * COLS), BF16),
            pltpu.VMEM((MEM, 2 * COLS), F32),
            pltpu.SemaphoreType.DMA((3 * CHUNKS,)),
        ],
        cost_estimate=pl.CostEstimate(flops=2 * MEM * depth * 2 * COLS, bytes_accessed=5500000, transcendentals=0),
        compiler_params=pltpu.CompilerParams(vmem_limit_bytes=TAIL_LIMIT),
        name="tail_projection",
    )(phase, decay, latents, w3)


def rest_kernel(phase, lat, w, payload, q_out, kv_out, halo, rows, wkv, wq, sems):
    copies = [
        pltpu.make_async_copy(lat.at[pl.ds(0, MEM)], rows.at[pl.ds(0, MEM)], sems.at[0]),
        pltpu.make_async_copy(w.at[1], wkv.at[:, pl.ds(0, COLS)], sems.at[1]),
        pltpu.make_async_copy(w.at[2], wkv.at[:, pl.ds(COLS, COLS)], sems.at[2]),
        pltpu.make_async_copy(lat.at[pl.ds(MEM, MEM)], rows.at[pl.ds(MEM, MEM)], sems.at[3]),
        pltpu.make_async_copy(w.at[0], wq, sems.at[4]),
    ]
    for copy in copies:
        copy.start()
    copies[0].wait()
    copies[1].wait()
    keys = normed(jnp.dot(rows[:MEM], wkv[:, :COLS], preferred_element_type=F32))
    copies[2].wait()
    values = jnp.dot(rows[:MEM], wkv[:, COLS:], preferred_element_type=F32).astype(BF16)
    kv_out[:, :COLS] = keys
    kv_out[:, COLS:] = values
    first = phase[0] == 0
    halo[:PART] = jnp.where(first, payload[PARTS - 1, :PART], keys[:PART])
    halo[PART:] = jnp.where(first, payload[PARTS - 1, PART : 2 * PART], values[:PART])
    copies[3].wait()
    copies[4].wait()
    q_out[...] = normed(jnp.dot(rows[...], wq[...], preferred_element_type=F32))


def rest(phase, latents, w3, payload):
    depth = latents.shape[1]
    smem = pl.BlockSpec(memory_space=pltpu.SMEM)
    vmem = pl.BlockSpec(memory_space=pltpu.VMEM)
    hbm = pl.BlockSpec(memory_space=pl.ANY)
    return pl.pallas_call(
        rest_kernel,
        out_shape=(shape((ROWS, COLS), BF16), shape((MEM, 2 * COLS), BF16), shape((2 * PART, COLS), BF16)),
        in_specs=[smem, hbm, hbm, vmem],
        out_specs=(vmem, vmem, vmem),
        scratch_shapes=[
            pltpu.VMEM((ROWS, depth), BF16),
            pltpu.VMEM((depth, 2 * COLS), BF16),
            pltpu.VMEM((depth, COLS), BF16),
            pltpu.SemaphoreType.DMA((5,)),
        ],
        cost_estimate=pl.CostEstimate(flops=4 * ROWS * depth * COLS, bytes_accessed=9000000, transcendentals=0),
        compiler_params=pltpu.CompilerParams(vmem_limit_bytes=REST_LIMIT),
        name="rest_projection",
    )(phase, latents, w3, payload)


def vmem_call(kernel, outs, name, flops, args, smem=0, scratch=()):
    specs = [pl.BlockSpec(memory_space=pltpu.SMEM)] * smem
    specs += [pl.BlockSpec(memory_space=pltpu.VMEM)] * (len(args) - smem)
    single = not isinstance(outs, tuple)
    out_spec = pl.BlockSpec(memory_space=pltpu.VMEM)
    nbytes = sum(a.size * a.dtype.itemsize for a in args)
    return pl.pallas_call(
        kernel,
        out_shape=outs,
        in_specs=specs,
        out_specs=out_spec if single else tuple(out_spec for _ in outs),
        scratch_shapes=list(scratch),
        cost_estimate=pl.CostEstimate(flops=flops, bytes_accessed=nbytes, transcendentals=0),
        compiler_params=pltpu.CompilerParams(vmem_limit_bytes=LIMIT),
        name=name,
    )(*args)


def window_kernel(q, head_rows, tail_rows, halo, frame_row, frame_column, top, bottom, qx, kx, vx):
    edge = jnp.zeros((HALF_WIN, COLS), BF16)
    qx[:HALF_WIN] = edge
    qx[HALF_WIN + ROWS :] = edge
    qx[HALF_WIN : HALF_WIN + ROWS] = q[...]
    for ext, columns, rows in ((kx, slice(0, COLS), slice(0, PART)), (vx, slice(COLS, 2 * COLS), slice(PART, 2 * PART))):
        ext[:HALF_WIN] = halo[rows]
        ext[HALF_WIN + ROWS :] = halo[rows]
        ext[HALF_WIN : HALF_WIN + MEM] = head_rows[:, columns]
        for d in range(PARTS):
            at = HALF_WIN + MEM + d * PART
            ext[at : at + PART] = tail_rows[d, rows]
    ones = jnp.ones((BLOCK, HD), BF16)
    window_a = lax.broadcasted_iota(jnp.int32, (BLOCK, BLOCK), 0) // WIN
    window_b = lax.broadcasted_iota(jnp.int32, (BLOCK, BLOCK), 1) // WIN
    for b in range(EXT // BLOCK):
        rows = slice(b * BLOCK, (b + 1) * BLOCK)
        allowed = (window_a == window_b) & (frame_row[b] <= frame_column[rows, :1])
        low, high = max(b * BLOCK, HALF_WIN), min((b + 1) * BLOCK, HALF_WIN + ROWS)
        for h in range(HEADS):
            c = slice(h * HD, (h + 1) * HD)
            score = lax.dot_general(qx[rows, c], kx[rows, c], (((1,), (1,)), ((), ())), preferred_element_type=F32)
            weight = jnp.where(allowed, jnp.exp2(score * SCALE2), 0.0).astype(BF16)
            both = jnp.concatenate([vx[rows, c], ones], axis=1)
            result = jnp.dot(weight, both, preferred_element_type=F32)
            cut = result[low - b * BLOCK : high - b * BLOCK]
            top[low - HALF_WIN : high - HALF_WIN, c] = cut[:, :HD]
            bottom[low - HALF_WIN : high - HALF_WIN, c] = cut[:, HD:]


def coefficients(rate):
    return 1.0 - rate, jnp.sqrt(1.0 - rate * rate)


def pack(out, state, row):
    out[: 2 * PART] = state.astype(BF16)
    out[2 * PART :] = pieces_of(row)


def keep(out, state, row):
    out[: 2 * PART] = state
    out[2 * PART :] = jnp.broadcast_to(row, (8, COLS))


def plane_step(keys, values, rate, tail_keys, tail_values):
    for_keys, for_values = coefficients(rate)
    return (
        rate * keys + for_keys * tail_keys.astype(F32),
        rate * values + for_values * tail_values.astype(F32),
    )


def plane_kernel(arrived, state, payload):
    keys = values = jnp.zeros((PART, COLS), F32)
    total = jnp.ones((1, COLS), F32)
    for i in range(PARTS):
        rate = row_of(arrived[i, 2 * PART :])
        keys, values = plane_step(keys, values, rate, arrived[i, :PART], arrived[i, PART : 2 * PART])
        total = total * rate
    both = jnp.concatenate([keys, values], axis=0)
    keep(state, both, total)
    pack(payload, both, total)


def first_kernel(own, got, payload):
    entering, rate = got[: 2 * PART].astype(F32), row_of(got[2 * PART :])
    own_rate = own[2 * PART : 2 * PART + 1]
    pack(payload, own[: 2 * PART] + own_rate * entering, own_rate * rate)


def next_kernel(own, got_1, got_2, payload):
    rate = row_of(got_1[2 * PART :])
    entering = got_1[: 2 * PART].astype(F32) + rate * got_2[: 2 * PART].astype(F32)
    own_rate = own[2 * PART : 2 * PART + 1]
    payload[...] = (own[: 2 * PART] + own_rate * entering).astype(BF16)


def memory_kernel(got_1, got_2, got_4, arrived, out):
    near, middle = row_of(got_1[2 * PART :]), row_of(got_2[2 * PART :])
    far = got_2[: 2 * PART].astype(F32) + middle * got_4[...].astype(F32)
    entering = got_1[: 2 * PART].astype(F32) + near * far
    keys, values = entering[:PART], entering[PART:]
    for i in range(PARTS):
        out[i, :PART] = keys.astype(BF16)
        out[i, PART:] = values.astype(BF16)
        if i < PARTS - 1:
            rate = row_of(arrived[i, 2 * PART :])
            keys, values = plane_step(keys, values, rate, arrived[i, :PART], arrived[i, PART : 2 * PART])


def attend_kernel(base, phase, opened, q, memory, top, bottom, out):
    rows = out.shape[0]
    start = phase[0] * (ROWS // WIN)
    row = lax.broadcasted_iota(jnp.int32, (rows, HD), 0) + base
    window = (row + HALF_WIN) // WIN
    is_open = jnp.zeros((rows, HD), F32)
    for w in range((base + HALF_WIN) // WIN, (base + rows - 1 + HALF_WIN) // WIN + 1):
        flag = jnp.where(opened[0, start + w] == 1, 1.0, 0.0)
        is_open = jnp.where(window == w, flag, is_open)
    ones = jnp.ones((MEM, HD), BF16)
    at = slice(base, base + rows)
    for h in range(HEADS):
        c = slice(h * HD, (h + 1) * HD)
        keys = memory[:, :PART, c].reshape(MEM, HD)
        values = memory[:, PART:, c].reshape(MEM, HD)
        score = lax.dot_general(q[at, c], keys, (((1,), (1,)), ((), ())), preferred_element_type=F32)
        weight = jnp.exp2(score * SCALE2).astype(BF16)
        result = jnp.dot(weight, jnp.concatenate([values, ones], axis=1), preferred_element_type=F32)
        above = top[at, c] + is_open * result[:, :HD]
        below = bottom[at, c] + is_open * result[:, HD:]
        out[:, c] = (above / below).astype(BF16)


def final_kernel(column, lat, *refs):
    out = refs[-1]
    attended, weights = refs[:5], refs[5:9]
    total = lat[...].astype(F32)
    for a, w in zip(attended[:3], weights[:3]):
        total = total + jnp.dot(a[...], w[...], preferred_element_type=F32)
    far = jnp.concatenate([attended[3][...], attended[4][...]], axis=0)
    total = total + jnp.dot(far, weights[3][...], preferred_element_type=F32)
    out[...] = total.astype(BF16)


def final(r, column, latents, attended, weights, earlier=None):
    share = weights[0].shape[1]
    rows = attended[0].shape[0]
    vmem = pl.BlockSpec(memory_space=pltpu.VMEM)
    specs = [pl.BlockSpec((rows, share), lambda i, col: (r, col[0]))] + [vmem] * 9
    operands = [column, latents, *attended, *weights]
    aliases = {}
    if earlier is not None:
        specs.append(pl.BlockSpec(memory_space=pl.ANY))
        aliases = {len(operands): 0}
        operands.append(earlier)
    return pl.pallas_call(
        final_kernel,
        grid_spec=pltpu.PrefetchScalarGridSpec(
            num_scalar_prefetch=1,
            grid=(1,),
            in_specs=specs,
            out_specs=pl.BlockSpec((rows, share), lambda i, col: (r, 0)),
        ),
        out_shape=shape((ROWS, share), BF16),
        input_output_aliases=aliases,
        cost_estimate=pl.CostEstimate(flops=2 * rows * 4 * COLS * share, bytes_accessed=2000000, transcendentals=0),
        compiler_params=pltpu.CompilerParams(vmem_limit_bytes=LIMIT),
        name=f"output_projection_{r}",
    )(*operands)


def moved(x, axis, by, wrap=True):
    size = lax.axis_size(axis)
    pairs = [(i, (i + by) % size) for i in range(size) if wrap or 0 <= i + by < size]
    return lax.ppermute(x, axis, pairs)


def local(latents, w_qkv, w_out, decay, frame_ids, memory_mask):
    phase = lax.axis_index("phase")
    mp = lax.axis_index("mp")
    phase_ref = phase.reshape(1).astype(jnp.int32)
    w3 = jnp.transpose(w_qkv, (1, 0, 2))

    payload = tails(phase_ref, decay[0], latents, w3)
    arrived = lax.all_to_all(payload, PLANE, 0, 0, tiled=True)
    queries, head_rows, halo = rest(phase_ref, latents, w3, payload)
    arrived, queries = lax.optimization_barrier((arrived, queries))
    halo = lax.ppermute(halo, "phase", [(0, 1), (1, 0)])

    w_out, head_rows, frame_ids = lax.optimization_barrier((w_out, head_rows, frame_ids))
    share = w_out.shape[1] // 4
    offsets = (0, 1, -1, 2)
    weights = []
    for by in offsets:
        piece = lax.dynamic_slice_in_dim(w_out, ((mp + by) & 3) * share, share, 1)
        weights.append(moved(piece, "mp", by) if by else piece)

    frames_pad = jnp.pad(frame_ids[0], (HALF_WIN, HALF_WIN), constant_values=outside_frame)
    frames = lax.dynamic_slice_in_dim(frames_pad, phase * ROWS, EXT)
    frame_row = frames.reshape(EXT // BLOCK, 1, BLOCK)
    frame_column = jnp.broadcast_to(frames[:, None], (EXT, HD))
    top, bottom = vmem_call(
        window_kernel,
        (shape((ROWS, COLS), F32), shape((ROWS, COLS), F32)),
        "window_attention",
        4 * EXT * BLOCK * COLS * 2,
        (queries, head_rows, payload, halo, frame_row, frame_column),
        scratch=[pltpu.VMEM((EXT, COLS), BF16)] * 3,
    )

    wide = shape((2 * PART + 8, COLS), F32)
    packed = shape((PAYLOAD, COLS), BF16)
    plain = shape((2 * PART, COLS), BF16)
    plain_all = shape((PARTS, 2 * PART, COLS), BF16)
    own, sent = vmem_call(plane_kernel, (wide, packed), "plane_total", 1000000, (arrived,))
    got_1 = moved(sent, "z", 1, wrap=False)
    sent = vmem_call(first_kernel, packed, "through_1", 100000, (own, got_1))
    got_2 = moved(sent, "z", 2, wrap=False)
    sent = vmem_call(next_kernel, plain, "through_3", 100000, (own, got_1, got_2))
    got_4 = moved(sent, "z", 4, wrap=False)
    got_4, top, bottom, weights = lax.optimization_barrier((got_4, top, bottom, weights))
    memory = vmem_call(
        memory_kernel, plain_all, "section_memory", 1000000, (got_1, got_2, got_4, arrived)
    )
    memory = lax.all_to_all(memory, PLANE, 0, 0, tiled=True)

    pieces = []
    rows = ROWS // 2
    for r in range(2):
        pieces.append(
            vmem_call(
                functools.partial(attend_kernel, r * rows),
                shape((rows, COLS), BF16),
                f"memory_attention_{r}",
                4 * rows * MEM * COLS * 2,
                (phase_ref, memory_mask, queries, memory, top, bottom),
                smem=2,
            )
        )
    column = mp.reshape(1).astype(jnp.int32)
    near = [(moved(piece, "mp", 1), moved(piece, "mp", -1)) for piece in pieces]
    refined = None
    for r, (piece, (right, left)) in enumerate(zip(pieces, near)):
        far = (moved(right[: rows // 2], "mp", 1), moved(left[rows // 2 :], "mp", -1))
        refined = final(r, column, latents, (piece, right, left, *far), weights, refined)
    return refined


def solution(mesh):
    finer = Mesh(
        mesh.devices.reshape(8, 2, 2, mesh.shape["mp"], mesh.shape["phase"]),
        ("z", "y", "core", "mp", "phase"),
    )
    placed = (
        P((*SPAN, "phase"), None),
        P(None, None, "mp"),
        P("mp", None),
        P(SPAN, None, "mp"),
        P(SPAN, None),
        P(SPAN, None),
    )
    return jax.shard_map(
        local, mesh=finer, in_specs=placed, out_specs=P((*SPAN, "phase"), "mp"), check_vma=False
    )
```

time: 99.7 us -> 92.6 us (0.929)
  the two profiles are of different devices: /device:TPU:6 before, /device:TPU:32 now
where the time goes in v2:
time: 92.6 us; the launch traced here: 91.1 us
  starting transfers between devices  43.5 us (47%)
  Pallas kernels  22.3 us (24%)
  blocking collectives  12.6 us (14%)
  waiting for transfers between devices  8.31 us (9%)
  local copies, waits for them, and re-layouts  4.11 us (4%)
    ppermute x14, starting transfers between devices, moved(): return lax.ppermute(x, axis, pairs)  35.5 us
    all_to_all x1, blocking collectives, local(): memory = lax.all_to_all(memory, PLANE, 0, 0, tiled=True)  12.6 us
    ppermute x14, waiting for transfers between devices, moved(): return lax.ppermute(x, axis, pairs)  8.31 us
    pallas_call x1, Pallas kernels, rest(): pl.pallas_call(rest_kernel, out_shape=(shape((ROWS, COLS), BF16), shape((...  7.3 us
    pallas_call x7, Pallas kernels, vmem_call(): pl.pallas_call(kernel, out_shape=outs, in_specs=specs, out_specs=out_spec...  7.08 us
    pallas_call x1, Pallas kernels, tails(): pl.pallas_call(tail_kernel, out_shape=shape((PARTS, PAYLOAD, COLS), BF16)...  4.67 us
    all_to_all x1, starting transfers between devices, local(): arrived = lax.all_to_all(payload, PLANE, 0, 0, tiled=True)  4.48 us
    ppermute x1, starting transfers between devices, local(): halo = lax.ppermute(halo, 'phase', [(0, 1), (1, 0)])  3.52 us
  transfers between devices with their start and end apart: 16, of which 5 were waited for; matrix products, arithmetic and copies ran while one was open for 3% of the time, Pallas kernels for 15%

profile of v2, /device:TPU:32, one launch (start us, length us, event | category | flops | bytes accessed | tf_op | source)
XLA Modules:
  0.0 91.1 jit_solution(6133064354047673155)
XLA Ops:
  0.0 4.7 %tail_projection.1.payload.tail_rows = bf16[8,80,384]{2,1,0:T(8,128)(2,1)} custom-call(s32[1]{0:T(128)} %bitcast.1.phase, f32[2,3]{1,0:T(2,128)} %bitcast.8, bf16[512,2560]{1,0:T(8,128)(2,1)} %lat.7, bf16[3,2560,384]{2,1,0:T(8,128)(2,1)} %bitcast.5), custom_call_target="tpu_custom_call" | custom-call | flops 1006632960 | bytes 5500000 | tf_op jit(solution)/shard_map/tail_projection/pallas_call | solution.py:105
  4.7 4.5 %all-to-all-start = ((bf16[8,80,384]{2,1,0:T(8,128)(2,1)}), bf16[8,80,384]{2,1,0:T(8,128)(2,1)S(1)}, u32[]{:S(2)}, u32[]{:S(2)}) async-start(bf16[8,80,384]{2,1,0:T(8,128)(2,1)} %tail_projection.1.payload.tail_rows), calls=%async_computation | async-start | bytes 983040 | tf_op jit(solution)/shard_map/all_to_all | solution.py:351
  9.2 7.3 %rest_projection.1 = (bf16[512,384]{1,0:T(8,128)(2,1)}, bf16[256,768]{1,0:T(8,128)(2,1)}, bf16[64,384]{1,0:T(8,128)(2,1)}) custom-call(s32[1]{0:T(128)} %bitcast.1.phase, bf16[512,2560]{1,0:T(8,128)(2,1)} %lat.7, bf16[3,2560,384]{2,1,0:T(8,128)(2,1)} %bitcast.6, bf16[8,80,384]{2,1,0:T(8,128)(2,1)} %tail_projection.1.payload.tail_rows), custom_call_target="tpu_custom_call" | custom-call | flops 2013265920 | bytes 9000000 | tf_op jit(solution)/shard_map/rest_projection/pallas_call | solution.py:152
  16.5 0.0 copy-start.5
  16.5 0.0 copy-start.1
  16.5 0.0 copy-start.2
  16.5 2.8 %constant_dynamic-slice_fusion = (bf16[384,640]{1,0:T(8,128)(2,1)}, bf16[384,640]{1,0:T(8,128)(2,1)}, bf16[384,640]{1,0:T(8,128)(2,1)}, bf16[384,640]{1,0:T(8,128)(2,1)S(1)}) fusion(bf16[384,2560]{1,0:T(8,128)(2,1)} %param.8, s32[]{:T(128)S(6)} %select_n.19, s32[]{:T(128)S(6)} %select_n.18, s32[]{:T(128)S(6)} %select_n.17, s32[]{:T(128)S(6)} %select_n.16), kind=kLoop, calls=%fused_computation.1 | loop fusion | bytes 3932176 | tf_op jit(solution)/shard_map/dynamic_slice | solution.py:361
  19.3 0.0 copy-start.4
  19.3 3.0 %collective-permute-start.6 = (bf16[384,640]{1,0:T(8,128)(2,1)}, bf16[384,640]{1,0:T(8,128)(2,1)S(1)}, u32[]{:S(2)}, u32[]{:S(2)}) collective-permute-start(bf16[384,640]{1,0:T(8,128)(2,1)} %get-tuple-element.43), channel_id=1, source_target_pairs={{0,4},{2,6},{4,0},{6,2},{1,5},{3,7},{5,1},{7,3},{8,12},{10,14},{12... | collective-permute-start | bytes 1474568 | tf_op jit(solution)/shard_map/ppermute | solution.py:341
  22.3 1.1 %collective-permute-start.5 = (bf16[384,640]{1,0:T(8,128)(2,1)}, bf16[384,640]{1,0:T(8,128)(2,1)S(1)}, u32[]{:S(2)}, u32[]{:S(2)}) collective-permute-start(bf16[384,640]{1,0:T(8,128)(2,1)} %get-tuple-element.44), channel_id=1, source_target_pairs={{0,6},{2,0},{4,2},{6,4},{1,7},{3,1},{5,3},{7,5},{8,14},{10,8},{12,... | collective-permute-start | bytes 1474568 | tf_op jit(solution)/shard_map/ppermute | solution.py:341
  23.4 0.9 collective-permute-start.4
  24.3 0.0 all-to-all-done.arrived
  24.3 0.2 plane_total.1
  24.5 3.8 %collective-permute-start = (bf16[80,384]{1,0:T(8,128)(2,1)S(1)}, bf16[80,384]{1,0:T(8,128)(2,1)S(1)}, u32[]{:S(2)}, u32[]{:S(2)}) collective-permute-start(bf16[80,384]{1,0:T(8,128)(2,1)S(1)} %get-tuple-element.27), channel_id=1, source_target_pairs={{0,32},{32,64},{64,96},{96,128},{128,160},{160,192},{192,224},{1,3... | collective-permute-start | bytes 184328 | tf_op jit(solution)/shard_map/ppermute | solution.py:341
  28.3 2.3 %collective-permute-done.got.got_1 = bf16[80,384]{1,0:T(8,128)(2,1)S(1)} collective-permute-done((bf16[80,384]{1,0:T(8,128)(2,1)S(1)}, bf16[80,384]{1,0:T(8,128)(2,1)S(1)}, u32[]{:S(2)}, u32[]{:S(2)}) %collective-permute-start) | collective-permute-done | bytes 61472 | tf_op jit(solution)/shard_map/ppermute | solution.py:341
  30.6 0.7 through_1.1
  31.3 6.6 %collective-permute-start.1 = (bf16[80,384]{1,0:T(8,128)(2,1)}, bf16[80,384]{1,0:T(8,128)(2,1)}, u32[]{:S(2)}, u32[]{:S(2)}) collective-permute-start(bf16[80,384]{1,0:T(8,128)(2,1)} %through_1.1), channel_id=1, source_target_pairs={{0,64},{32,96},{64,128},{96,160},{128,192},{160,224},{1,65},{33,97... | collective-permute-start | bytes 184328 | tf_op jit(solution)/shard_map/ppermute | solution.py:341
  37.9 3.5 %collective-permute-start.3 = (bf16[64,384]{1,0:T(8,128)(2,1)}, bf16[64,384]{1,0:T(8,128)(2,1)}, u32[]{:S(2)}, u32[]{:S(2)}) collective-permute-start(bf16[64,384]{1,0:T(8,128)(2,1)} %get-tuple-element.31), channel_id=1, source_target_pairs={{0,1},{1,0},{2,3},{3,2},{4,5},{5,4},{6,7},{7,6},{8,9},{9,8},{10,11... | collective-permute-start | bytes 147464 | tf_op jit(solution)/shard_map/ppermute | solution.py:354
  41.4 0.0 collective-permute-done.1.got_2
  41.4 1.5 %through_3.1 = bf16[64,384]{1,0:T(8,128)(2,1)} custom-call(f32[72,384]{1,0:T(8,128)S(1)} %get-tuple-element.28.own, bf16[80,384]{1,0:T(8,128)(2,1)S(1)} %collective-permute-done.got.got_1, bf16[80,384]{1,0:T(8,128)(2,1)} %collective-permute-done.1.got_2), custom_call_target="tpu_custom_call" | custom-call | flops 100000 | bytes 233472 | tf_op jit(solution)/shard_map/through_3/pallas_call | solution.py:175
  42.9 7.1 %collective-permute-start.2 = (bf16[64,384]{1,0:T(8,128)(2,1)}, bf16[64,384]{1,0:T(8,128)(2,1)S(1)}, u32[]{:S(2)}, u32[]{:S(2)}) collective-permute-start(bf16[64,384]{1,0:T(8,128)(2,1)} %through_3.1), channel_id=1, source_target_pairs={{0,128},{32,160},{64,192},{96,224},{1,129},{33,161},{65,193},{97,2... | collective-permute-start | bytes 147464 | tf_op jit(solution)/shard_map/ppermute | solution.py:341
  50.0 0.0 copy-done.5
  50.0 0.1 pad_dynamic-slice_fusion
  50.1 0.1 reshape.12.frame_row
  50.2 0.0 collective-permute-done.3.halo
  50.2 0.1 broadcast_in_dim.2.frame_column
  50.3 0.0 copy-done.1
  50.3 0.0 copy-done.2
  50.3 0.0 copy-start.3
  50.3 1.0 %copy-done.3 = bf16[256,768]{1,0:T(8,128)(2,1)S(1)} copy-done((bf16[256,768]{1,0:T(8,128)(2,1)S(1)}, bf16[256,768]{1,0:T(8,128)(2,1)}, u32[]{:S(2)}) %copy-start.3) | copy-done | bytes 393240
  51.3 1.7 %window_attention.1 = (f32[512,384]{1,0:T(8,128)S(1)}, f32[512,384]{1,0:T(8,128)S(1)}) custom-call(bf16[512,384]{1,0:T(8,128)(2,1)S(1)} %copy-done.2, bf16[256,768]{1,0:T(8,128)(2,1)S(1)} %copy-done.3, bf16[8,80,384]{2,1,0:T(8,128)(2,1)S(1)} %copy-done.1, bf16[64,384]{1,0:T(8,128)(2,1)} %collective-permute-done.3.halo, s32[3,1,192]{2,1,0:T(1,128)S(1)} %reshape.12.frame_row, ...), custom_call_target="tpu_custom_call" | custom-call | flops 339738624 | bytes 1624320 | tf_op jit(solution)/shard_map/window_attention/pallas_call | solution.py:175
  53.0 0.0 collective-permute-done.6.refs_8_
  53.0 0.0 collective-permute-done.5.refs_7_
  53.0 0.0 collective-permute-done.4.refs_6_
  53.0 0.0 collective-permute-done.2.got_4
  53.1 1.0 %section_memory.1 = bf16[8,64,384]{2,1,0:T(8,128)(2,1)S(1)} custom-call(bf16[80,384]{1,0:T(8,128)(2,1)S(1)} %collective-permute-done.got.got_1, bf16[80,384]{1,0:T(8,128)(2,1)} %collective-permute-done.1.got_2, bf16[64,384]{1,0:T(8,128)(2,1)S(1)} %collective-permute-done.2.got_4, bf16[8,80,384]{2,1,0:T(8,128)(2,1)S(1)} %all-to-all-done.arrived), custom_call_target="tpu_custom_call" | custom-call | flops 1000000 | bytes 663552 | tf_op jit(solution)/shard_map/section_memory/pallas_call | solution.py:175
  54.1 12.6 %all_to_all.10.memory = bf16[8,64,384]{2,1,0:T(8,128)(2,1)S(1)} all-to-all(bf16[8,64,384]{2,1,0:T(8,128)(2,1)S(1)} %section_memory.1), channel_id=1, replica_groups=mesh['z'=8,'y'=2,'core'=2,'mp'=4,'phase'=2] {'y','core','phase'}, dimensions={0} | all-to-all | bytes 786432 | tf_op jit(solution)/shard_map/all_to_all | solution.py:391
  66.7 0.0 copy-done.4
  66.7 0.0 copy-start
  66.7 1.0 %memory_attention_0.1.refs_0_ = bf16[256,384]{1,0:T(8,128)(2,1)S(1)} custom-call(s32[1]{0:T(128)} %bitcast.1.phase, s32[1,17]{1,0:T(1,128)S(1)} %copy-done.4, bf16[512,384]{1,0:T(8,128)(2,1)S(1)} %copy-done.2, bf16[8,64,384]{2,1,0:T(8,128)(2,1)S(1)} %all_to_all.10.memory, f32[512,384]{1,0:T(8,128)S(1)} %get-tuple-element.37.top, ...), custom_call_target="tpu_custom_call" | custom-call | flops 201326592 | bytes 2359368 | tf_op jit(solution)/shard_map/memory_attention_0/pallas_call | solution.py:175
  67.7 2.4 %collective-permute-start.12 = (bf16[256,384]{1,0:T(8,128)(2,1)S(1)}, bf16[256,384]{1,0:T(8,128)(2,1)S(1)}, u32[]{:S(2)}, u32[]{:S(2)}) collective-permute-start(bf16[256,384]{1,0:T(8,128)(2,1)S(1)} %memory_attention_0.1.refs_0_), channel_id=1, source_target_pairs={{0,6},{2,0},{4,2},{6,4},{1,7},{3,1},{5,3},{7,5},{8,14},{10,8},{12,... | collective-permute-start | bytes 589832 | tf_op jit(solution)/shard_map/ppermute | solution.py:341
  70.2 0.0 collective-permute-start.11
  70.2 1.0 %memory_attention_1.1.refs_0_ = bf16[256,384]{1,0:T(8,128)(2,1)S(1)} custom-call(s32[1]{0:T(128)} %bitcast.1.phase, s32[1,17]{1,0:T(1,128)S(1)} %copy-done.4, bf16[512,384]{1,0:T(8,128)(2,1)S(1)} %copy-done.2, bf16[8,64,384]{2,1,0:T(8,128)(2,1)S(1)} %all_to_all.10.memory, f32[512,384]{1,0:T(8,128)S(1)} %get-tuple-element.37.top, ...), custom_call_target="tpu_custom_call" | custom-call | flops 201326592 | bytes 2359368 | tf_op jit(solution)/shard_map/memory_attention_1/pallas_call | solution.py:175
  71.2 3.3 %collective-permute-start.8 = (bf16[256,384]{1,0:T(8,128)(2,1)S(1)}, bf16[256,384]{1,0:T(8,128)(2,1)S(1)}, u32[]{:S(2)}, u32[]{:S(2)}) collective-permute-start(bf16[256,384]{1,0:T(8,128)(2,1)S(1)} %memory_attention_1.1.refs_0_), channel_id=1, source_target_pairs={{0,6},{2,0},{4,2},{6,4},{1,7},{3,1},{5,3},{7,5},{8,14},{10,8},{12,... | collective-permute-start | bytes 589832 | tf_op jit(solution)/shard_map/ppermute | solution.py:341
  74.5 0.0 collective-permute-start.7
  74.5 1.0 %collective-permute-done.12.refs_2_ = bf16[256,384]{1,0:T(8,128)(2,1)S(1)} collective-permute-done((bf16[256,384]{1,0:T(8,128)(2,1)S(1)}, bf16[256,384]{1,0:T(8,128)(2,1)S(1)}, u32[]{:S(2)}, u32[]{:S(2)}) %collective-permute-start.12) | collective-permute-done | bytes 196640 | tf_op jit(solution)/shard_map/ppermute | solution.py:341
  75.6 3.3 %collective-permute-start.14 = (bf16[128,384]{1,0:T(8,128)(2,1)S(1)}, bf16[128,384]{1,0:T(8,128)(2,1)S(1)}, u32[]{:S(2)}, u32[]{:S(2)}) collective-permute-start(bf16[128,384]{1,0:T(8,128)(2,1)S(1)} %slice.19), channel_id=1, source_target_pairs={{0,6},{2,0},{4,2},{6,4},{1,7},{3,1},{5,3},{7,5},{8,14},{10,8},{12,... | collective-permute-start | bytes 294920 | tf_op jit(solution)/shard_map/ppermute | solution.py:341
  78.8 0.0 collective-permute-done.11.refs_1_
  78.9 0.1 collective-permute-start.13
  79.0 0.8 collective-permute-done.8.refs_2_
  79.8 3.8 %collective-permute-start.10 = (bf16[128,384]{1,0:T(8,128)(2,1)S(1)}, bf16[128,384]{1,0:T(8,128)(2,1)S(1)}, u32[]{:S(2)}, u32[]{:S(2)}) collective-permute-start(bf16[128,384]{1,0:T(8,128)(2,1)S(1)} %slice.17), channel_id=1, source_target_pairs={{0,6},{2,0},{4,2},{6,4},{1,7},{3,1},{5,3},{7,5},{8,14},{10,8},{12,... | collective-permute-start | bytes 294920 | tf_op jit(solution)/shard_map/ppermute | solution.py:341
  83.5 0.0 collective-permute-done.7.refs_1_
  83.6 0.1 collective-permute-start.9
  83.7 0.0 collective-permute-done.14.refs_4_
  83.7 1.1 %collective-permute-done.13.refs_3_ = bf16[128,384]{1,0:T(8,128)(2,1)S(1)} collective-permute-done((bf16[128,384]{1,0:T(8,128)(2,1)S(1)}, bf16[128,384]{1,0:T(8,128)(2,1)S(1)}, u32[]{:S(2)}, u32[]{:S(2)}) %collective-permute-start.13) | collective-permute-done | bytes 98336 | tf_op jit(solution)/shard_map/ppermute | solution.py:341
  84.8 0.0 copy-done
  84.8 1.6 %output_projection_0.1.refs_9_ = bf16[512,640]{1,0:T(8,128)(2,1)} custom-call(s32[1]{0:T(128)} %bitcast.column, bf16[512,2560]{1,0:T(8,128)(2,1)S(1)} %copy-done, bf16[256,384]{1,0:T(8,128)(2,1)S(1)} %memory_attention_0.1.refs_0_, bf16[256,384]{1,0:T(8,128)(2,1)S(1)} %collective-permute-done.11.refs_1_, ...), custom_call_target="tpu_custom_call" | custom-call | flops 503316480 | bytes 2000000 | tf_op jit(solution)/shard_map/output_projection_0/pallas_call | solution.py:322
  86.4 0.0 collective-permute-done.10.refs_4_
  86.4 3.1 %collective-permute-done.9.refs_3_ = bf16[128,384]{1,0:T(8,128)(2,1)S(1)} collective-permute-done((bf16[128,384]{1,0:T(8,128)(2,1)S(1)}, bf16[128,384]{1,0:T(8,128)(2,1)S(1)}, u32[]{:S(2)}, u32[]{:S(2)}) %collective-permute-start.9) | collective-permute-done | bytes 98336 | tf_op jit(solution)/shard_map/ppermute | solution.py:341
  89.5 1.6 %output_projection_1.1 = bf16[512,640]{1,0:T(8,128)(2,1)} custom-call(s32[1]{0:T(128)} %bitcast.column, bf16[512,2560]{1,0:T(8,128)(2,1)S(1)} %copy-done, bf16[256,384]{1,0:T(8,128)(2,1)S(1)} %memory_attention_1.1.refs_0_, bf16[256,384]{1,0:T(8,128)(2,1)S(1)} %collective-permute-done.7.refs_1_, ...), custom_call_target="tpu_custom_call", output_to_operand_aliasing={{}: (11, {})} | custom-call | flops 503316480 | bytes 2000000 | tf_op jit(solution)/shard_map/output_projection_1/pallas_call | solution.py:322
  (4 shorter events, 0.0 us)
Async XLA Ops:
  4.7 19.7 %all-to-all-start = ((bf16[8,80,384]{2,1,0:T(8,128)(2,1)}), bf16[8,80,384]{2,1,0:T(8,128)(2,1)S(1)}, u32[]{:S(2)}, u32[]{:S(2)}) async-start(bf16[8,80,384]{2,1,0:T(8,128)(2,1)} %tail_projection.1.payload.tail_rows), calls=%async_computation | async-start | bytes 983040 | tf_op jit(solution)/shard_map/all_to_all | solution.py:351
  16.5 33.5 %copy-start.5 = (s32[1,1024]{1,0:T(1,128)S(1)}, s32[1,1024]{1,0:T(1,128)}, u32[]{:S(2)}) copy-start(s32[1,1024]{1,0:T(1,128)} %param.10) | copy-start | bytes 12292
  16.5 33.8 %copy-start.1 = (bf16[8,80,384]{2,1,0:T(8,128)(2,1)S(1)}, bf16[8,80,384]{2,1,0:T(8,128)(2,1)}, u32[]{:S(2)}) copy-start(bf16[8,80,384]{2,1,0:T(8,128)(2,1)} %tail_projection.1.payload.tail_rows) | copy-start | bytes 1474564
  16.5 33.8 %copy-start.2 = (bf16[512,384]{1,0:T(8,128)(2,1)S(1)}, bf16[512,384]{1,0:T(8,128)(2,1)}, u32[]{:S(2)}) copy-start(bf16[512,384]{1,0:T(8,128)(2,1)} %get-tuple-element.25.q) | copy-start | bytes 1179652
  19.3 47.4 %copy-start.4 = (s32[1,17]{1,0:T(1,128)S(1)}, s32[1,17]{1,0:T(1,128)}, u32[]{:S(2)}) copy-start(s32[1,17]{1,0:T(1,128)} %opened.3) | copy-start | bytes 208
  19.3 33.7 %collective-permute-start.6 = (bf16[384,640]{1,0:T(8,128)(2,1)}, bf16[384,640]{1,0:T(8,128)(2,1)S(1)}, u32[]{:S(2)}, u32[]{:S(2)}) collective-permute-start(bf16[384,640]{1,0:T(8,128)(2,1)} %get-tuple-element.43), channel_id=1, source_target_pairs={{0,4},{2,6},{4,0},{6,2},{1,5},{3,7},{5,1},{7,3},{8,12},{10,14},{12... | collective-permute-start | bytes 1474568 | tf_op jit(solution)/shard_map/ppermute | solution.py:341
  22.3 30.7 %collective-permute-start.5 = (bf16[384,640]{1,0:T(8,128)(2,1)}, bf16[384,640]{1,0:T(8,128)(2,1)S(1)}, u32[]{:S(2)}, u32[]{:S(2)}) collective-permute-start(bf16[384,640]{1,0:T(8,128)(2,1)} %get-tuple-element.44), channel_id=1, source_target_pairs={{0,6},{2,0},{4,2},{6,4},{1,7},{3,1},{5,3},{7,5},{8,14},{10,8},{12,... | collective-permute-start | bytes 1474568 | tf_op jit(solution)/shard_map/ppermute | solution.py:341
  23.4 29.6 %collective-permute-start.4 = (bf16[384,640]{1,0:T(8,128)(2,1)}, bf16[384,640]{1,0:T(8,128)(2,1)S(1)}, u32[]{:S(2)}, u32[]{:S(2)}) collective-permute-start(bf16[384,640]{1,0:T(8,128)(2,1)} %get-tuple-element.45), channel_id=1, source_target_pairs={{0,2},{2,4},{4,6},{6,0},{1,3},{3,5},{5,7},{7,1},{8,10},{10,12},{12... | collective-permute-start | bytes 1474568 | tf_op jit(solution)/shard_map/ppermute | solution.py:341
  24.5 6.1 %collective-permute-start = (bf16[80,384]{1,0:T(8,128)(2,1)S(1)}, bf16[80,384]{1,0:T(8,128)(2,1)S(1)}, u32[]{:S(2)}, u32[]{:S(2)}) collective-permute-start(bf16[80,384]{1,0:T(8,128)(2,1)S(1)} %get-tuple-element.27), channel_id=1, source_target_pairs={{0,32},{32,64},{64,96},{96,128},{128,160},{160,192},{192,224},{1,3... | collective-permute-start | bytes 184328 | tf_op jit(solution)/shard_map/ppermute | solution.py:341
  31.3 10.1 %collective-permute-start.1 = (bf16[80,384]{1,0:T(8,128)(2,1)}, bf16[80,384]{1,0:T(8,128)(2,1)}, u32[]{:S(2)}, u32[]{:S(2)}) collective-permute-start(bf16[80,384]{1,0:T(8,128)(2,1)} %through_1.1), channel_id=1, source_target_pairs={{0,64},{32,96},{64,128},{96,160},{128,192},{160,224},{1,65},{33,97... | collective-permute-start | bytes 184328 | tf_op jit(solution)/shard_map/ppermute | solution.py:341
  37.9 12.3 %collective-permute-start.3 = (bf16[64,384]{1,0:T(8,128)(2,1)}, bf16[64,384]{1,0:T(8,128)(2,1)}, u32[]{:S(2)}, u32[]{:S(2)}) collective-permute-start(bf16[64,384]{1,0:T(8,128)(2,1)} %get-tuple-element.31), channel_id=1, source_target_pairs={{0,1},{1,0},{2,3},{3,2},{4,5},{5,4},{6,7},{7,6},{8,9},{9,8},{10,11... | collective-permute-start | bytes 147464 | tf_op jit(solution)/shard_map/ppermute | solution.py:354
  42.9 10.2 %collective-permute-start.2 = (bf16[64,384]{1,0:T(8,128)(2,1)}, bf16[64,384]{1,0:T(8,128)(2,1)S(1)}, u32[]{:S(2)}, u32[]{:S(2)}) collective-permute-start(bf16[64,384]{1,0:T(8,128)(2,1)} %through_3.1), channel_id=1, source_target_pairs={{0,128},{32,160},{64,192},{96,224},{1,129},{33,161},{65,193},{97,2... | collective-permute-start | bytes 147464 | tf_op jit(solution)/shard_map/ppermute | solution.py:341
  50.3 1.0 %copy-start.3 = (bf16[256,768]{1,0:T(8,128)(2,1)S(1)}, bf16[256,768]{1,0:T(8,128)(2,1)}, u32[]{:S(2)}) copy-start(bf16[256,768]{1,0:T(8,128)(2,1)} %get-tuple-element.30.head_rows) | copy-start | bytes 1179652
  66.7 18.1 %copy-start = (bf16[512,2560]{1,0:T(8,128)(2,1)S(1)}, bf16[512,2560]{1,0:T(8,128)(2,1)}, u32[]{:S(2)}) copy-start(bf16[512,2560]{1,0:T(8,128)(2,1)} %lat.7) | copy-start | bytes 7864324
  67.7 7.8 %collective-permute-start.12 = (bf16[256,384]{1,0:T(8,128)(2,1)S(1)}, bf16[256,384]{1,0:T(8,128)(2,1)S(1)}, u32[]{:S(2)}, u32[]{:S(2)}) collective-permute-start(bf16[256,384]{1,0:T(8,128)(2,1)S(1)} %memory_attention_0.1.refs_0_), channel_id=1, source_target_pairs={{0,6},{2,0},{4,2},{6,4},{1,7},{3,1},{5,3},{7,5},{8,14},{10,8},{12,... | collective-permute-start | bytes 589832 | tf_op jit(solution)/shard_map/ppermute | solution.py:341
  70.2 8.7 %collective-permute-start.11 = (bf16[256,384]{1,0:T(8,128)(2,1)S(1)}, bf16[256,384]{1,0:T(8,128)(2,1)S(1)}, u32[]{:S(2)}, u32[]{:S(2)}) collective-permute-start(bf16[256,384]{1,0:T(8,128)(2,1)S(1)} %memory_attention_0.1.refs_0_), channel_id=1, source_target_pairs={{0,2},{2,4},{4,6},{6,0},{1,3},{3,5},{5,7},{7,1},{8,10},{10,12},{12... | collective-permute-start | bytes 589832 | tf_op jit(solution)/shard_map/ppermute | solution.py:341
  71.2 8.6 %collective-permute-start.8 = (bf16[256,384]{1,0:T(8,128)(2,1)S(1)}, bf16[256,384]{1,0:T(8,128)(2,1)S(1)}, u32[]{:S(2)}, u32[]{:S(2)}) collective-permute-start(bf16[256,384]{1,0:T(8,128)(2,1)S(1)} %memory_attention_1.1.refs_0_), channel_id=1, source_target_pairs={{0,6},{2,0},{4,2},{6,4},{1,7},{3,1},{5,3},{7,5},{8,14},{10,8},{12,... | collective-permute-start | bytes 589832 | tf_op jit(solution)/shard_map/ppermute | solution.py:341
  74.5 9.0 %collective-permute-start.7 = (bf16[256,384]{1,0:T(8,128)(2,1)S(1)}, bf16[256,384]{1,0:T(8,128)(2,1)S(1)}, u32[]{:S(2)}, u32[]{:S(2)}) collective-permute-start(bf16[256,384]{1,0:T(8,128)(2,1)S(1)} %memory_attention_1.1.refs_0_), channel_id=1, source_target_pairs={{0,2},{2,4},{4,6},{6,0},{1,3},{3,5},{5,7},{7,1},{8,10},{10,12},{12... | collective-permute-start | bytes 589832 | tf_op jit(solution)/shard_map/ppermute | solution.py:341
  75.6 8.1 %collective-permute-start.14 = (bf16[128,384]{1,0:T(8,128)(2,1)S(1)}, bf16[128,384]{1,0:T(8,128)(2,1)S(1)}, u32[]{:S(2)}, u32[]{:S(2)}) collective-permute-start(bf16[128,384]{1,0:T(8,128)(2,1)S(1)} %slice.19), channel_id=1, source_target_pairs={{0,6},{2,0},{4,2},{6,4},{1,7},{3,1},{5,3},{7,5},{8,14},{10,8},{12,... | collective-permute-start | bytes 294920 | tf_op jit(solution)/shard_map/ppermute | solution.py:341
  78.9 5.9 %collective-permute-start.13 = (bf16[128,384]{1,0:T(8,128)(2,1)S(1)}, bf16[128,384]{1,0:T(8,128)(2,1)S(1)}, u32[]{:S(2)}, u32[]{:S(2)}) collective-permute-start(bf16[128,384]{1,0:T(8,128)(2,1)S(1)} %slice.18), channel_id=1, source_target_pairs={{0,2},{2,4},{4,6},{6,0},{1,3},{3,5},{5,7},{7,1},{8,10},{10,12},{12... | collective-permute-start | bytes 294920 | tf_op jit(solution)/shard_map/ppermute | solution.py:341
  79.8 6.6 %collective-permute-start.10 = (bf16[128,384]{1,0:T(8,128)(2,1)S(1)}, bf16[128,384]{1,0:T(8,128)(2,1)S(1)}, u32[]{:S(2)}, u32[]{:S(2)}) collective-permute-start(bf16[128,384]{1,0:T(8,128)(2,1)S(1)} %slice.17), channel_id=1, source_target_pairs={{0,6},{2,0},{4,2},{6,4},{1,7},{3,1},{5,3},{7,5},{8,14},{10,8},{12,... | collective-permute-start | bytes 294920 | tf_op jit(solution)/shard_map/ppermute | solution.py:341
  83.6 5.9 %collective-permute-start.9 = (bf16[128,384]{1,0:T(8,128)(2,1)S(1)}, bf16[128,384]{1,0:T(8,128)(2,1)S(1)}, u32[]{:S(2)}, u32[]{:S(2)}) collective-permute-start(bf16[128,384]{1,0:T(8,128)(2,1)S(1)} %slice.16), channel_id=1, source_target_pairs={{0,2},{2,4},{4,6},{6,0},{1,3},{3,5},{5,7},{7,1},{8,10},{10,12},{12... | collective-permute-start | bytes 294920 | tf_op jit(solution)/shard_map/ppermute | solution.py:341

commit v3 on v2

--- a/solution.py
+++ b/solution.py
@@ -18,7 +18,7 @@
 COLS = HEADS * HD
 PARTS = 8
 PART = MEM // PARTS
-PAYLOAD = 2 * PART + 16
+PAYLOAD = 2 * PART + 8
 CHUNKS = 5
 TAIL_LIMIT = 60 * 1024 * 1024
 REST_LIMIT = 60 * 1024 * 1024
@@ -48,11 +48,11 @@
 
 
 def pieces_of(row):
-    full = jnp.broadcast_to(row, (16, COLS))
+    full = jnp.broadcast_to(row, (8, COLS))
     high = full.astype(BF16).astype(F32)
     middle = (full - high).astype(BF16).astype(F32)
     low = full - high - middle
-    at = lax.broadcasted_iota(jnp.int32, (16, COLS), 0)
+    at = lax.broadcasted_iota(jnp.int32, (8, COLS), 0)
     return jnp.where(at == 0, high, jnp.where(at == 1, middle, jnp.where(at == 2, low, 0.0))).astype(BF16)
 
 
@@ -119,51 +119,74 @@
     )(phase, decay, latents, w3)
 
 
-def rest_kernel(phase, lat, w, payload, q_out, kv_out, halo, rows, wkv, wq, sems):
+def call_on_hbm(kernel, outs, name, flops, nbytes, args, scratch):
+    vmem = pl.BlockSpec(memory_space=pltpu.VMEM)
+    hbm = pl.BlockSpec(memory_space=pl.ANY)
+    single = not isinstance(outs, tuple)
+    return pl.pallas_call(
+        kernel,
+        out_shape=outs,
+        in_specs=[pl.BlockSpec(memory_space=pltpu.SMEM), hbm, hbm] + [vmem] * (len(args) - 3),
+        out_specs=vmem if single else tuple(vmem for _ in outs),
+        scratch_shapes=scratch,
+        cost_estimate=pl.CostEstimate(flops=flops, bytes_accessed=nbytes, transcendentals=0),
+        compiler_params=pltpu.CompilerParams(vmem_limit_bytes=REST_LIMIT),
+        name=name,
+    )(*args)
+
+
+def head_kernel(which, after, lat, w, out, rows, part, sems):
     copies = [
-        pltpu.make_async_copy(lat.at[pl.ds(0, MEM)], rows.at[pl.ds(0, MEM)], sems.at[0]),
-        pltpu.make_async_copy(w.at[1], wkv.at[:, pl.ds(0, COLS)], sems.at[1]),
-        pltpu.make_async_copy(w.at[2], wkv.at[:, pl.ds(COLS, COLS)], sems.at[2]),
-        pltpu.make_async_copy(lat.at[pl.ds(MEM, MEM)], rows.at[pl.ds(MEM, MEM)], sems.at[3]),
-        pltpu.make_async_copy(w.at[0], wq, sems.at[4]),
+        pltpu.make_async_copy(w.at[which], part, sems.at[0]),
+        pltpu.make_async_copy(lat.at[pl.ds(0, MEM)], rows, sems.at[1]),
+    ]
+    for copy in copies:
+        copy.start()
+    for copy in copies:
+        copy.wait()
+    mixed = jnp.dot(rows[...], part[...], preferred_element_type=F32)
+    out[...] = normed(mixed) if which == 1 else mixed.astype(BF16)
+
+
+def heads(which, after, latents, w3):
+    depth = latents.shape[1]
+    return call_on_hbm(
+        functools.partial(head_kernel, which),
+        shape((MEM, COLS), BF16),
+        f"head_projection_{which}",
+        2 * MEM * depth * COLS,
+        3300000,
+        (after, latents, w3),
+        [pltpu.VMEM((MEM, depth), BF16), pltpu.VMEM((depth, COLS), BF16), pltpu.SemaphoreType.DMA((2,))],
+    )
+
+
+def query_kernel(after, lat, w, out, rows, part, sems):
+    copies = [
+        pltpu.make_async_copy(w.at[0], part, sems.at[0]),
+        pltpu.make_async_copy(lat.at[pl.ds(0, MEM)], rows.at[pl.ds(0, MEM)], sems.at[1]),
+        pltpu.make_async_copy(lat.at[pl.ds(MEM, MEM)], rows.at[pl.ds(MEM, MEM)], sems.at[2]),
     ]
     for copy in copies:
         copy.start()
     copies[0].wait()
-    copies[1].wait()
-    keys = normed(jnp.dot(rows[:MEM], wkv[:, :COLS], preferred_element_type=F32))
-    copies[2].wait()
-    values = jnp.dot(rows[:MEM], wkv[:, COLS:], preferred_element_type=F32).astype(BF16)
-    kv_out[:, :COLS] = keys
-    kv_out[:, COLS:] = values
-    first = phase[0] == 0
-    halo[:PART] = jnp.where(first, payload[PARTS - 1, :PART], keys[:PART])
-    halo[PART:] = jnp.where(first, payload[PARTS - 1, PART : 2 * PART], values[:PART])
-    copies[3].wait()
-    copies[4].wait()
-    q_out[...] = normed(jnp.dot(rows[...], wq[...], preferred_element_type=F32))
-
-
-def rest(phase, latents, w3, payload):
+    for r in range(2):
+        copies[1 + r].wait()
+        at = slice(r * MEM, (r + 1) * MEM)
+        out[at] = normed(jnp.dot(rows[at], part[...], preferred_element_type=F32))
+
+
+def query(after, latents, w3):
     depth = latents.shape[1]
-    smem = pl.BlockSpec(memory_space=pltpu.SMEM)
-    vmem = pl.BlockSpec(memory_space=pltpu.VMEM)
-    hbm = pl.BlockSpec(memory_space=pl.ANY)
-    return pl.pallas_call(
-        rest_kernel,
-        out_shape=(shape((ROWS, COLS), BF16), shape((MEM, 2 * COLS), BF16), shape((2 * PART, COLS), BF16)),
-        in_specs=[smem, hbm, hbm, vmem],
-        out_specs=(vmem, vmem, vmem),
-        scratch_shapes=[
-            pltpu.VMEM((ROWS, depth), BF16),
-            pltpu.VMEM((depth, 2 * COLS), BF16),
-            pltpu.VMEM((depth, COLS), BF16),
-            pltpu.SemaphoreType.DMA((5,)),
-        ],
-        cost_estimate=pl.CostEstimate(flops=4 * ROWS * depth * COLS, bytes_accessed=9000000, transcendentals=0),
-        compiler_params=pltpu.CompilerParams(vmem_limit_bytes=REST_LIMIT),
-        name="rest_projection",
-    )(phase, latents, w3, payload)
+    return call_on_hbm(
+        query_kernel,
+        shape((ROWS, COLS), BF16),
+        "query_projection",
+        2 * ROWS * depth * COLS,
+        4600000,
+        (after, latents, w3),
+        [pltpu.VMEM((ROWS, depth), BF16), pltpu.VMEM((depth, COLS), BF16), pltpu.SemaphoreType.DMA((3,))],
+    )
 
 
 def vmem_call(kernel, outs, name, flops, args, smem=0, scratch=()):
@@ -184,15 +207,15 @@
     )(*args)
 
 
-def window_kernel(q, head_rows, tail_rows, halo, frame_row, frame_column, top, bottom, qx, kx, vx):
+def window_kernel(q, head_keys, head_values, tail_rows, halo, frame_row, frame_column, top, bottom, qx, kx, vx):
     edge = jnp.zeros((HALF_WIN, COLS), BF16)
     qx[:HALF_WIN] = edge
     qx[HALF_WIN + ROWS :] = edge
     qx[HALF_WIN : HALF_WIN + ROWS] = q[...]
-    for ext, columns, rows in ((kx, slice(0, COLS), slice(0, PART)), (vx, slice(COLS, 2 * COLS), slice(PART, 2 * PART))):
+    for ext, head, rows in ((kx, head_keys, slice(0, PART)), (vx, head_values, slice(PART, 2 * PART))):
         ext[:HALF_WIN] = halo[rows]
         ext[HALF_WIN + ROWS :] = halo[rows]
-        ext[HALF_WIN : HALF_WIN + MEM] = head_rows[:, columns]
+        ext[HALF_WIN : HALF_WIN + MEM] = head[...]
         for d in range(PARTS):
             at = HALF_WIN + MEM + d * PART
             ext[at : at + PART] = tail_rows[d, rows]
@@ -248,23 +271,29 @@
     pack(payload, both, total)
 
 
-def first_kernel(own, got, payload):
-    entering, rate = got[: 2 * PART].astype(F32), row_of(got[2 * PART :])
-    own_rate = own[2 * PART : 2 * PART + 1]
-    pack(payload, own[: 2 * PART] + own_rate * entering, own_rate * rate)
-
-
-def next_kernel(own, got_1, got_2, payload):
-    rate = row_of(got_1[2 * PART :])
-    entering = got_1[: 2 * PART].astype(F32) + rate * got_2[: 2 * PART].astype(F32)
-    own_rate = own[2 * PART : 2 * PART + 1]
-    payload[...] = (own[: 2 * PART] + own_rate * entering).astype(BF16)
-
-
-def memory_kernel(got_1, got_2, got_4, arrived, out):
-    near, middle = row_of(got_1[2 * PART :]), row_of(got_2[2 * PART :])
-    far = got_2[: 2 * PART].astype(F32) + middle * got_4[...].astype(F32)
-    entering = got_1[: 2 * PART].astype(F32) + near * far
+def joined(upper, mine, rate, got):
+    other, other_rate = got[: 2 * PART].astype(F32), row_of(got[2 * PART :])
+    return jnp.where(upper, mine + rate * other, other + other_rate * mine), rate * other_rate
+
+
+def first_kernel(z, own, got_1, payload):
+    total, rate = joined((z[0] & 1) == 1, own[: 2 * PART], own[2 * PART : 2 * PART + 1], got_1)
+    pack(payload, total, rate)
+
+
+def next_kernel(z, own, got_1, got_2, payload):
+    total, rate = joined((z[0] & 1) == 1, own[: 2 * PART], own[2 * PART : 2 * PART + 1], got_1)
+    total, rate = joined((z[0] & 2) == 2, total, rate, got_2)
+    payload[...] = total.astype(BF16)
+
+
+def memory_kernel(z, got_1, got_2, got_4, arrived, out):
+    at_1, at_2, at_4 = (z[0] & 1) == 1, (z[0] & 2) == 2, (z[0] & 4) == 4
+    entering = jnp.where(at_1, got_1[: 2 * PART].astype(F32), 0.0)
+    rate = jnp.where(at_1, row_of(got_1[2 * PART :]), 1.0)
+    entering = jnp.where(at_2, entering + rate * got_2[: 2 * PART].astype(F32), entering)
+    rate = jnp.where(at_2, rate * row_of(got_2[2 * PART :]), rate)
+    entering = jnp.where(at_4, entering + rate * got_4[...].astype(F32), entering)
     keys, values = entering[:PART], entering[PART:]
     for i in range(PARTS):
         out[i, :PART] = keys.astype(BF16)
@@ -335,10 +364,13 @@
     )(*operands)
 
 
-def moved(x, axis, by, wrap=True):
+def moved(x, axis, by):
     size = lax.axis_size(axis)
-    pairs = [(i, (i + by) % size) for i in range(size) if wrap or 0 <= i + by < size]
-    return lax.ppermute(x, axis, pairs)
+    return lax.ppermute(x, axis, [(i, (i + by) % size) for i in range(size)])
+
+
+def swapped(x, axis, bit):
+    return lax.ppermute(x, axis, [(i, i ^ bit) for i in range(lax.axis_size(axis))])
 
 
 def local(latents, w_qkv, w_out, decay, frame_ids, memory_mask):
@@ -347,48 +379,63 @@
     phase_ref = phase.reshape(1).astype(jnp.int32)
     w3 = jnp.transpose(w_qkv, (1, 0, 2))
 
+    z_ref = lax.axis_index("z").reshape(1).astype(jnp.int32)
     payload = tails(phase_ref, decay[0], latents, w3)
     arrived = lax.all_to_all(payload, PLANE, 0, 0, tiled=True)
-    queries, head_rows, halo = rest(phase_ref, latents, w3, payload)
-    arrived, queries = lax.optimization_barrier((arrived, queries))
-    halo = lax.ppermute(halo, "phase", [(0, 1), (1, 0)])
-
-    w_out, head_rows, frame_ids = lax.optimization_barrier((w_out, head_rows, frame_ids))
+
+    w_out, payload = lax.optimization_barrier((w_out, payload))
     share = w_out.shape[1] // 4
     offsets = (0, 1, -1, 2)
-    weights = []
-    for by in offsets:
-        piece = lax.dynamic_slice_in_dim(w_out, ((mp + by) & 3) * share, share, 1)
-        weights.append(moved(piece, "mp", by) if by else piece)
-
+    sends = [lax.dynamic_slice_in_dim(w_out, ((mp + by) & 3) * share, share, 1) for by in offsets]
+    weights = [moved(piece, "mp", by) if by else piece for by, piece in zip(offsets, sends)]
+    arrived, _ = lax.optimization_barrier((arrived, sends))
+
+    wide = shape((2 * PART + 8, COLS), F32)
+    packed = shape((PAYLOAD, COLS), BF16)
+    plain = shape((2 * PART, COLS), BF16)
+    plain_all = shape((PARTS, 2 * PART, COLS), BF16)
+    own, sent = vmem_call(plane_kernel, (wide, packed), "plane_total", 1000000, (arrived,))
+    after, sent = lax.optimization_barrier((z_ref, sent))
+    got_1 = swapped(sent, "z", 1)
+    head_keys = heads(1, after, latents, w3)
+    got_1, head_keys = lax.optimization_barrier((got_1, head_keys))
+
+    sent = vmem_call(first_kernel, packed, "through_1", 100000, (z_ref, own, got_1), smem=1)
+    after, sent = lax.optimization_barrier((z_ref, sent))
+    got_2 = swapped(sent, "z", 2)
+    head_values = heads(2, after, latents, w3)
+    got_2, head_values = lax.optimization_barrier((got_2, head_values))
+
+    sent = vmem_call(next_kernel, plain, "through_3", 100000, (z_ref, own, got_1, got_2), smem=1)
+    got_4 = swapped(sent, "z", 4)
+    got_4, weights = lax.optimization_barrier((got_4, weights))
+    memory = vmem_call(
+        memory_kernel, plain_all, "section_memory", 1000000, (z_ref, got_1, got_2, got_4, arrived), smem=1
+    )
+    after, memory, head_keys, head_values, frame_ids = lax.optimization_barrier(
+        (z_ref, memory, head_keys, head_values, frame_ids)
+    )
+    memory = lax.all_to_all(memory, PLANE, 0, 0, tiled=True)
+    edge = jnp.where(
+        phase == 0,
+        payload[PARTS - 1, : 2 * PART],
+        jnp.concatenate([head_keys[:PART], head_values[:PART]], axis=0),
+    )
+    halo = swapped(edge, "phase", 1)
     frames_pad = jnp.pad(frame_ids[0], (HALF_WIN, HALF_WIN), constant_values=outside_frame)
     frames = lax.dynamic_slice_in_dim(frames_pad, phase * ROWS, EXT)
     frame_row = frames.reshape(EXT // BLOCK, 1, BLOCK)
     frame_column = jnp.broadcast_to(frames[:, None], (EXT, HD))
+    queries = query(after, latents, w3)
     top, bottom = vmem_call(
         window_kernel,
         (shape((ROWS, COLS), F32), shape((ROWS, COLS), F32)),
         "window_attention",
         4 * EXT * BLOCK * COLS * 2,
-        (queries, head_rows, payload, halo, frame_row, frame_column),
+        (queries, head_keys, head_values, payload, halo, frame_row, frame_column),
         scratch=[pltpu.VMEM((EXT, COLS), BF16)] * 3,
     )
-
-    wide = shape((2 * PART + 8, COLS), F32)
-    packed = shape((PAYLOAD, COLS), BF16)
-    plain = shape((2 * PART, COLS), BF16)
-    plain_all = shape((PARTS, 2 * PART, COLS), BF16)
-    own, sent = vmem_call(plane_kernel, (wide, packed), "plane_total", 1000000, (arrived,))
-    got_1 = moved(sent, "z", 1, wrap=False)
-    sent = vmem_call(first_kernel, packed, "through_1", 100000, (own, got_1))
-    got_2 = moved(sent, "z", 2, wrap=False)
-    sent = vmem_call(next_kernel, plain, "through_3", 100000, (own, got_1, got_2))
-    got_4 = moved(sent, "z", 4, wrap=False)
-    got_4, top, bottom, weights = lax.optimization_barrier((got_4, top, bottom, weights))
-    memory = vmem_call(
-        memory_kernel, plain_all, "section_memory", 1000000, (got_1, got_2, got_4, arrived)
-    )
-    memory = lax.all_to_all(memory, PLANE, 0, 0, tiled=True)
+    memory, top, bottom = lax.optimization_barrier((memory, top, bottom))
 
     pieces = []
     rows = ROWS // 2

time: 92.6 us -> 80.6 us (0.87)
  blocking collectives: 12.6 us -> 0 us
  starting transfers between devices: 43.5 us -> 39.6 us
  waiting for transfers between devices: 8.31 us -> 11.8 us
  Pallas kernels: 22.3 us -> 23.9 us
    all_to_all x1 -> x0, blocking collectives: 12.6 us -> none  [local(): memory = lax.all_to_all(memory, PLANE, 0, 0, tiled=True)]
    ppermute x15, starting transfers between devices: 39 us -> 31.7 us  [the longest x11 19.1 us: moved(): return lax.ppermute(x, axis, [(i, (i + by) % size) for i in range(size)])]
    pallas_call x1 -> x3, Pallas kernels: 7.3 us -> 11.6 us  [call_on_hbm(): pl.pallas_call(kernel, out_shape=outs, in_specs=[pl.BlockSpec(memory_spac...]
    all_to_all x0 -> x1, starting transfers between devices: none -> 3.45 us  [local(): memory = lax.all_to_all(memory, PLANE, 0, 0, tiled=True)]
    pallas_call x7, Pallas kernels: 7.08 us -> 4.18 us  [vmem_call(): pl.pallas_call(kernel, out_shape=outs, in_specs=specs, out_specs=out_spec...]
    all_to_all x1, waiting for transfers between devices: 0.01 us -> 2.62 us  [local(): arrived = lax.all_to_all(payload, PLANE, 0, 0, tiled=True)]
    dynamic_slice x1, local copies, waits for them, and re-layouts: 2.76 us -> 1.18 us  [local(): lax.dynamic_slice_in_dim(w_out, (mp + by & 3) * share, share, 1)]
    unnamed x12 -> x26, local copies, waits for them, and re-layouts: 1.01 us -> 2.02 us
  transfers between devices with their start and end apart: 16 -> 17, of which waited for: 5 -> 7; matrix products, arithmetic and copies ran while one was open for 3% -> 3% of each run, Pallas kernels for 15% -> 19%
where the time goes in v3:
time: 80.6 us; the launch traced here: 79.9 us
  starting transfers between devices  39.6 us (49%)
  Pallas kernels  23.9 us (30%)
  waiting for transfers between devices  11.8 us (15%)
  local copies, waits for them, and re-layouts  4.27 us (5%)
    ppermute x11, starting transfers between devices, moved(): return lax.ppermute(x, axis, [(i, (i + by) % size) for i in range(size)])  19.1 us
    ppermute x4, starting transfers between devices, swapped(): lax.ppermute(x, axis, [(i, i ^ bit) for i in range(lax.axis_size(axis))])  12.6 us
    pallas_call x3, Pallas kernels, call_on_hbm(): pl.pallas_call(kernel, out_shape=outs, in_specs=[pl.BlockSpec(memory_spac...  11.6 us
    ppermute x11, waiting for transfers between devices, moved(): return lax.ppermute(x, axis, [(i, (i + by) % size) for i in range(size)])  6.99 us
    pallas_call x1, Pallas kernels, tails(): pl.pallas_call(tail_kernel, out_shape=shape((PARTS, PAYLOAD, COLS), BF16)...  4.79 us
    all_to_all x1, starting transfers between devices, local(): arrived = lax.all_to_all(payload, PLANE, 0, 0, tiled=True)  4.48 us
    pallas_call x7, Pallas kernels, vmem_call(): pl.pallas_call(kernel, out_shape=outs, in_specs=specs, out_specs=out_spec...  4.18 us
    all_to_all x1, starting transfers between devices, local(): memory = lax.all_to_all(memory, PLANE, 0, 0, tiled=True)  3.45 us
  transfers between devices with their start and end apart: 17, of which 7 were waited for; matrix products, arithmetic and copies ran while one was open for 3% of the time, Pallas kernels for 19%

profile of v3, /device:TPU:32, one launch (start us, length us, event | category | flops | bytes accessed | tf_op | source)
XLA Modules:
  0.0 79.9 jit_solution(14202945594302414842)
XLA Ops:
  0.0 4.8 %tail_projection.1.tail_rows = bf16[8,72,384]{2,1,0:T(8,128)(2,1)} custom-call(s32[1]{0:T(128)} %bitcast.1.phase, f32[2,3]{1,0:T(2,128)} %bitcast.13, bf16[512,2560]{1,0:T(8,128)(2,1)} %lat.11, bf16[3,2560,384]{2,1,0:T(8,128)(2,1)} %bitcast.8), custom_call_target="tpu_custom_call" | custom-call | flops 1006632960 | bytes 5500000 | tf_op jit(solution)/shard_map/tail_projection/pallas_call | solution.py:105
  4.8 4.5 %all-to-all-start = ((bf16[8,72,384]{2,1,0:T(8,128)(2,1)}), bf16[8,72,384]{2,1,0:T(8,128)(2,1)S(1)}, u32[]{:S(2)}, u32[]{:S(2)}) async-start(bf16[8,72,384]{2,1,0:T(8,128)(2,1)} %tail_projection.1.tail_rows), calls=%async_computation | async-start | bytes 884736 | tf_op jit(solution)/shard_map/all_to_all | solution.py:384
  9.3 0.0 copy-done.11
  9.3 1.2 %constant_dynamic-slice_fusion = (bf16[384,640]{1,0:T(8,128)(2,1)}, bf16[384,640]{1,0:T(8,128)(2,1)}, bf16[384,640]{1,0:T(8,128)(2,1)}, bf16[384,640]{1,0:T(8,128)(2,1)S(1)}) fusion(bf16[384,2560]{1,0:T(8,128)(2,1)S(1)} %copy-done.11, s32[]{:T(128)S(6)} %select_n.26, s32[]{:T(128)S(6)} %select_n.25, s32[]{:T(128)S(6)} %select_n.24, s32[]{:T(128)S(6)} %select_n.23), kind=kLoop, calls=%fused_computation.2 | loop fusion | bytes 3932176 | tf_op jit(solution)/shard_map/dynamic_slice | solution.py:389
  10.5 3.0 %collective-permute-start.5 = (bf16[384,640]{1,0:T(8,128)(2,1)}, bf16[384,640]{1,0:T(8,128)(2,1)S(1)}, u32[]{:S(2)}, u32[]{:S(2)}) collective-permute-start(bf16[384,640]{1,0:T(8,128)(2,1)} %get-tuple-element.61), channel_id=1, source_target_pairs={{0,4},{2,6},{4,0},{6,2},{1,5},{3,7},{5,1},{7,3},{8,12},{10,14},{12... | collective-permute-start | bytes 1474568 | tf_op jit(solution)/shard_map/ppermute | solution.py:369
  13.5 1.1 %collective-permute-start.4 = (bf16[384,640]{1,0:T(8,128)(2,1)}, bf16[384,640]{1,0:T(8,128)(2,1)S(1)}, u32[]{:S(2)}, u32[]{:S(2)}) collective-permute-start(bf16[384,640]{1,0:T(8,128)(2,1)} %get-tuple-element.62), channel_id=1, source_target_pairs={{0,6},{2,0},{4,2},{6,4},{1,7},{3,1},{5,3},{7,5},{8,14},{10,8},{12,... | collective-permute-start | bytes 1474568 | tf_op jit(solution)/shard_map/ppermute | solution.py:369
  14.6 0.9 %collective-permute-start.3 = (bf16[384,640]{1,0:T(8,128)(2,1)}, bf16[384,640]{1,0:T(8,128)(2,1)S(1)}, u32[]{:S(2)}, u32[]{:S(2)}) collective-permute-start(bf16[384,640]{1,0:T(8,128)(2,1)} %get-tuple-element.63), channel_id=1, source_target_pairs={{0,2},{2,4},{4,6},{6,0},{1,3},{3,5},{5,7},{7,1},{8,10},{10,12},{12... | collective-permute-start | bytes 1474568 | tf_op jit(solution)/shard_map/ppermute | solution.py:369
  15.5 2.6 %all-to-all-done.arrived = bf16[8,72,384]{2,1,0:T(8,128)(2,1)S(1)} async-done(((bf16[8,72,384]{2,1,0:T(8,128)(2,1)}), bf16[8,72,384]{2,1,0:T(8,128)(2,1)S(1)}, u32[]{:S(2)}, u32[]{:S(2)}) %all-to-all-start) | async-done | bytes 442400 | tf_op jit(solution)/shard_map/all_to_all | solution.py:384
  18.1 0.2 plane_total.1
  18.3 0.9 %collective-permute-start = (bf16[72,384]{1,0:T(8,128)(2,1)S(1)}, bf16[72,384]{1,0:T(8,128)(2,1)S(1)}, u32[]{:S(2)}, u32[]{:S(2)}) collective-permute-start(bf16[72,384]{1,0:T(8,128)(2,1)S(1)} %get-tuple-element.36), channel_id=1, source_target_pairs={{0,32},{32,0},{64,96},{96,64},{128,160},{160,128},{192,224},{224,1... | collective-permute-start | bytes 165896 | tf_op jit(solution)/shard_map/ppermute | solution.py:373
  19.2 3.6 %head_projection_1.1.head_keys = bf16[256,384]{1,0:T(8,128)(2,1)} custom-call(s32[1]{0:T(128)} %bitcast.2.after.z, bf16[512,2560]{1,0:T(8,128)(2,1)} %lat.11, bf16[3,2560,384]{2,1,0:T(8,128)(2,1)} %bitcast.9), custom_call_target="tpu_custom_call" | custom-call | flops 503316480 | bytes 3300000 | tf_op jit(solution)/shard_map/head_projection_1/pallas_call | solution.py:126
  22.8 0.0 collective-permute-done.got_1
  22.8 0.0 copy-start.12
  22.8 0.0 copy-start.3
  22.9 0.0 slice-start
  22.9 3.2 %collective-permute-start.1 = (bf16[72,384]{1,0:T(8,128)(2,1)S(1)}, bf16[72,384]{1,0:T(8,128)(2,1)S(1)}, u32[]{:S(2)}, u32[]{:S(2)}) collective-permute-start(bf16[72,384]{1,0:T(8,128)(2,1)S(1)} %through_1.1), channel_id=1, source_target_pairs={{0,64},{32,96},{64,0},{96,32},{128,192},{160,224},{192,128},{224,1... | collective-permute-start | bytes 165896 | tf_op jit(solution)/shard_map/ppermute | solution.py:373
  26.1 3.5 %head_projection_2.1.head_values = bf16[256,384]{1,0:T(8,128)(2,1)} custom-call(s32[1]{0:T(128)} %bitcast.2.after.z, bf16[512,2560]{1,0:T(8,128)(2,1)} %lat.11, bf16[3,2560,384]{2,1,0:T(8,128)(2,1)} %bitcast.10), custom_call_target="tpu_custom_call" | custom-call | flops 503316480 | bytes 3300000 | tf_op jit(solution)/shard_map/head_projection_2/pallas_call | solution.py:126
  29.5 0.0 collective-permute-done.1.got_2
  29.5 0.1 through_3.1
  29.6 5.1 %collective-permute-start.2 = (bf16[64,384]{1,0:T(8,128)(2,1)S(1)}, bf16[64,384]{1,0:T(8,128)(2,1)S(1)}, u32[]{:S(2)}, u32[]{:S(2)}) collective-permute-start(bf16[64,384]{1,0:T(8,128)(2,1)S(1)} %through_3.1), channel_id=1, source_target_pairs={{0,128},{32,160},{64,192},{96,224},{128,0},{160,32},{192,64},{224,... | collective-permute-start | bytes 147464 | tf_op jit(solution)/shard_map/ppermute | solution.py:373
  34.6 0.0 collective-permute-done.5.refs_8_
  34.6 1.8 %collective-permute-done.4.refs_7_ = bf16[384,640]{1,0:T(8,128)(2,1)S(1)} collective-permute-done((bf16[384,640]{1,0:T(8,128)(2,1)}, bf16[384,640]{1,0:T(8,128)(2,1)S(1)}, u32[]{:S(2)}, u32[]{:S(2)}) %collective-permute-start.4) | collective-permute-done | bytes 491552 | tf_op jit(solution)/shard_map/ppermute | solution.py:369
  36.5 0.0 collective-permute-done.3.refs_6_
  36.5 1.2 %collective-permute-done.2.got_4 = bf16[64,384]{1,0:T(8,128)(2,1)S(1)} collective-permute-done((bf16[64,384]{1,0:T(8,128)(2,1)S(1)}, bf16[64,384]{1,0:T(8,128)(2,1)S(1)}, u32[]{:S(2)}, u32[]{:S(2)}) %collective-permute-start.2) | collective-permute-done | bytes 49184 | tf_op jit(solution)/shard_map/ppermute | solution.py:373
  37.7 1.0 %section_memory.1 = bf16[8,64,384]{2,1,0:T(8,128)(2,1)} custom-call(s32[1]{0:T(128)} %bitcast.2.after.z, bf16[72,384]{1,0:T(8,128)(2,1)S(1)} %collective-permute-done.got_1, bf16[72,384]{1,0:T(8,128)(2,1)S(1)} %collective-permute-done.1.got_2, bf16[64,384]{1,0:T(8,128)(2,1)S(1)} %collective-permute-done.2.got_4, bf16[8,72,384]{2,1,0:T(8,128)(2,1)S(1)} %all-to-all-done.arrived), custom_call_target="tpu_custom_call" | custom-call | flops 1000000 | bytes 602116 | tf_op jit(solution)/shard_map/section_memory/pallas_call | solution.py:198
  38.7 0.0 copy-done.12
  38.7 0.1 pad_dynamic-slice_fusion
  38.7 0.1 reshape.16.frame_row
  38.8 3.5 %all-to-all-start.1 = ((bf16[8,64,384]{2,1,0:T(8,128)(2,1)}), bf16[8,64,384]{2,1,0:T(8,128)(2,1)S(1)}, u32[]{:S(2)}, u32[]{:S(2)}) async-start(bf16[8,64,384]{2,1,0:T(8,128)(2,1)} %section_memory.1), calls=%async_computation.1 | async-start | bytes 786432 | tf_op jit(solution)/shard_map/all_to_all | solution.py:418
  42.3 0.7 slice.23
  43.0 0.0 copy-done.3
  43.0 0.0 slice-done
  43.0 0.0 copy-start.8
  43.1 0.0 copy-start.9
  43.1 0.0 copy-start.10
  43.1 3.5 %collective-permute-start.6 = (bf16[64,384]{1,0:T(8,128)(2,1)S(1)}, bf16[64,384]{1,0:T(8,128)(2,1)S(1)}, u32[]{:S(2)}, u32[]{:S(2)}) collective-permute-start(bf16[64,384]{1,0:T(8,128)(2,1)S(1)} %maximum_select_fusion), channel_id=1, source_target_pairs={{0,1},{1,0},{2,3},{3,2},{4,5},{5,4},{6,7},{7,6},{8,9},{9,8},{10,11... | collective-permute-start | bytes 147464 | tf_op jit(solution)/shard_map/ppermute | solution.py:373
  46.6 4.6 %query_projection.1.q = bf16[512,384]{1,0:T(8,128)(2,1)} custom-call(s32[1]{0:T(128)} %bitcast.2.after.z, bf16[512,2560]{1,0:T(8,128)(2,1)} %lat.11, bf16[3,2560,384]{2,1,0:T(8,128)(2,1)} %bitcast.11), custom_call_target="tpu_custom_call" | custom-call | flops 1006632960 | bytes 4600000 | tf_op jit(solution)/shard_map/query_projection/pallas_call | solution.py:126
  51.2 0.0 copy-done.4
  51.2 1.0 %collective-permute-done.6.halo = bf16[64,384]{1,0:T(8,128)(2,1)S(1)} collective-permute-done((bf16[64,384]{1,0:T(8,128)(2,1)S(1)}, bf16[64,384]{1,0:T(8,128)(2,1)S(1)}, u32[]{:S(2)}, u32[]{:S(2)}) %collective-permute-start.6) | collective-permute-done | bytes 49184 | tf_op jit(solution)/shard_map/ppermute | solution.py:373
  52.2 0.1 broadcast_in_dim.2.frame_column
  52.3 1.0 %copy-done.1 = bf16[512,384]{1,0:T(8,128)(2,1)S(1)} copy-done((bf16[512,384]{1,0:T(8,128)(2,1)S(1)}, bf16[512,384]{1,0:T(8,128)(2,1)}, u32[]{:S(2)}) %copy-start.1) | copy-done | bytes 393240
  53.3 0.9 %window_attention.1 = (f32[512,384]{1,0:T(8,128)S(1)}, f32[512,384]{1,0:T(8,128)S(1)}) custom-call(bf16[512,384]{1,0:T(8,128)(2,1)S(1)} %copy-done.1, bf16[256,384]{1,0:T(8,128)(2,1)S(1)} %copy-done.8, bf16[256,384]{1,0:T(8,128)(2,1)S(1)} %copy-done.9, bf16[8,72,384]{2,1,0:T(8,128)(2,1)S(1)} %copy-done.3, bf16[64,384]{1,0:T(8,128)(2,1)S(1)} %collective-permute-done.6.halo, ...), custom_call_target="tpu_custom_call" | custom-call | flops 339738624 | bytes 1575168 | tf_op jit(solution)/shard_map/window_attention/pallas_call | solution.py:198
  54.2 0.0 all-to-all-done.1.memory
  54.3 1.0 %copy-done.2 = bf16[512,384]{1,0:T(8,128)(2,1)S(1)} copy-done((bf16[512,384]{1,0:T(8,128)(2,1)S(1)}, bf16[512,384]{1,0:T(8,128)(2,1)}, u32[]{:S(2)}) %copy-start.2) | copy-done | bytes 393240
  55.3 1.0 %memory_attention_0.1.refs_0_ = bf16[256,384]{1,0:T(8,128)(2,1)S(1)} custom-call(s32[1]{0:T(128)} %bitcast.1.phase, s32[1,17]{1,0:T(1,128)S(1)} %copy-done.10, bf16[512,384]{1,0:T(8,128)(2,1)S(1)} %copy-done.2, bf16[8,64,384]{2,1,0:T(8,128)(2,1)S(1)} %all-to-all-done.1.memory, f32[512,384]{1,0:T(8,128)S(1)} %get-tuple-element.55.top, ...), custom_call_target="tpu_custom_call" | custom-call | flops 201326592 | bytes 2359368 | tf_op jit(solution)/shard_map/memory_attention_0/pallas_call | solution.py:198
  56.3 3.0 %collective-permute-start.12 = (bf16[256,384]{1,0:T(8,128)(2,1)S(1)}, bf16[256,384]{1,0:T(8,128)(2,1)S(1)}, u32[]{:S(2)}, u32[]{:S(2)}) collective-permute-start(bf16[256,384]{1,0:T(8,128)(2,1)S(1)} %memory_attention_0.1.refs_0_), channel_id=1, source_target_pairs={{0,6},{2,0},{4,2},{6,4},{1,7},{3,1},{5,3},{7,5},{8,14},{10,8},{12,... | collective-permute-start | bytes 589832 | tf_op jit(solution)/shard_map/ppermute | solution.py:369
  59.3 0.0 collective-permute-start.11
  59.3 1.0 %memory_attention_1.1.refs_0_ = bf16[256,384]{1,0:T(8,128)(2,1)S(1)} custom-call(s32[1]{0:T(128)} %bitcast.1.phase, s32[1,17]{1,0:T(1,128)S(1)} %copy-done.10, bf16[512,384]{1,0:T(8,128)(2,1)S(1)} %copy-done.2, bf16[8,64,384]{2,1,0:T(8,128)(2,1)S(1)} %all-to-all-done.1.memory, f32[512,384]{1,0:T(8,128)S(1)} %get-tuple-element.55.top, ...), custom_call_target="tpu_custom_call" | custom-call | flops 201326592 | bytes 2359368 | tf_op jit(solution)/shard_map/memory_attention_1/pallas_call | solution.py:198
  60.3 3.3 %collective-permute-start.8 = (bf16[256,384]{1,0:T(8,128)(2,1)S(1)}, bf16[256,384]{1,0:T(8,128)(2,1)S(1)}, u32[]{:S(2)}, u32[]{:S(2)}) collective-permute-start(bf16[256,384]{1,0:T(8,128)(2,1)S(1)} %memory_attention_1.1.refs_0_), channel_id=1, source_target_pairs={{0,6},{2,0},{4,2},{6,4},{1,7},{3,1},{5,3},{7,5},{8,14},{10,8},{12,... | collective-permute-start | bytes 589832 | tf_op jit(solution)/shard_map/ppermute | solution.py:369
  63.6 0.0 collective-permute-start.7
  63.6 0.0 collective-permute-done.12.refs_2_
  63.7 3.7 %collective-permute-start.14 = (bf16[128,384]{1,0:T(8,128)(2,1)S(1)}, bf16[128,384]{1,0:T(8,128)(2,1)S(1)}, u32[]{:S(2)}, u32[]{:S(2)}) collective-permute-start(bf16[128,384]{1,0:T(8,128)(2,1)S(1)} %slice.31), channel_id=1, source_target_pairs={{0,6},{2,0},{4,2},{6,4},{1,7},{3,1},{5,3},{7,5},{8,14},{10,8},{12,... | collective-permute-start | bytes 294920 | tf_op jit(solution)/shard_map/ppermute | solution.py:369
  67.4 0.0 collective-permute-done.11.refs_1_
  67.4 0.1 collective-permute-start.13
  67.5 1.0 %collective-permute-done.8.refs_2_ = bf16[256,384]{1,0:T(8,128)(2,1)S(1)} collective-permute-done((bf16[256,384]{1,0:T(8,128)(2,1)S(1)}, bf16[256,384]{1,0:T(8,128)(2,1)S(1)}, u32[]{:S(2)}, u32[]{:S(2)}) %collective-permute-start.8) | collective-permute-done | bytes 196640 | tf_op jit(solution)/shard_map/ppermute | solution.py:369
  68.5 3.8 %collective-permute-start.10 = (bf16[128,384]{1,0:T(8,128)(2,1)S(1)}, bf16[128,384]{1,0:T(8,128)(2,1)S(1)}, u32[]{:S(2)}, u32[]{:S(2)}) collective-permute-start(bf16[128,384]{1,0:T(8,128)(2,1)S(1)} %slice.29), channel_id=1, source_target_pairs={{0,6},{2,0},{4,2},{6,4},{1,7},{3,1},{5,3},{7,5},{8,14},{10,8},{12,... | collective-permute-start | bytes 294920 | tf_op jit(solution)/shard_map/ppermute | solution.py:369
  72.3 0.0 collective-permute-done.7.refs_1_
  72.3 0.1 collective-permute-start.9
  72.4 0.0 collective-permute-done.14.refs_4_
  72.4 0.9 %collective-permute-done.13.refs_3_ = bf16[128,384]{1,0:T(8,128)(2,1)S(1)} collective-permute-done((bf16[128,384]{1,0:T(8,128)(2,1)S(1)}, bf16[128,384]{1,0:T(8,128)(2,1)S(1)}, u32[]{:S(2)}, u32[]{:S(2)}) %collective-permute-start.13) | collective-permute-done | bytes 98336 | tf_op jit(solution)/shard_map/ppermute | solution.py:369
  73.3 1.6 %output_projection_0.1.refs_9_ = bf16[512,640]{1,0:T(8,128)(2,1)} custom-call(s32[1]{0:T(128)} %bitcast.column, bf16[512,2560]{1,0:T(8,128)(2,1)S(1)} %copy-done, bf16[256,384]{1,0:T(8,128)(2,1)S(1)} %memory_attention_0.1.refs_0_, bf16[256,384]{1,0:T(8,128)(2,1)S(1)} %collective-permute-done.11.refs_1_, ...), custom_call_target="tpu_custom_call" | custom-call | flops 503316480 | bytes 2000000 | tf_op jit(solution)/shard_map/output_projection_0/pallas_call | solution.py:351
  75.0 0.0 collective-permute-done.10.refs_4_
  75.0 3.2 %collective-permute-done.9.refs_3_ = bf16[128,384]{1,0:T(8,128)(2,1)S(1)} collective-permute-done((bf16[128,384]{1,0:T(8,128)(2,1)S(1)}, bf16[128,384]{1,0:T(8,128)(2,1)S(1)}, u32[]{:S(2)}, u32[]{:S(2)}) %collective-permute-start.9) | collective-permute-done | bytes 98336 | tf_op jit(solution)/shard_map/ppermute | solution.py:369
  78.2 1.6 %output_projection_1.1 = bf16[512,640]{1,0:T(8,128)(2,1)} custom-call(s32[1]{0:T(128)} %bitcast.column, bf16[512,2560]{1,0:T(8,128)(2,1)S(1)} %copy-done, bf16[256,384]{1,0:T(8,128)(2,1)S(1)} %memory_attention_1.1.refs_0_, bf16[256,384]{1,0:T(8,128)(2,1)S(1)} %collective-permute-done.7.refs_1_, ...), custom_call_target="tpu_custom_call", output_to_operand_aliasing={{}: (11, {})} | custom-call | flops 503316480 | bytes 2000000 | tf_op jit(solution)/shard_map/output_projection_1/pallas_call | solution.py:351
  (21 shorter events, 0.1 us)
Async XLA Ops:
  0.0 9.3 %copy-start.11 = (bf16[384,2560]{1,0:T(8,128)(2,1)S(1)}, bf16[384,2560]{1,0:T(8,128)(2,1)}, u32[]{:S(2)}) copy-start(bf16[384,2560]{1,0:T(8,128)(2,1)} %param.8) | copy-start | bytes 5898244
  4.8 13.3 %all-to-all-start = ((bf16[8,72,384]{2,1,0:T(8,128)(2,1)}), bf16[8,72,384]{2,1,0:T(8,128)(2,1)S(1)}, u32[]{:S(2)}, u32[]{:S(2)}) async-start(bf16[8,72,384]{2,1,0:T(8,128)(2,1)} %tail_projection.1.tail_rows), calls=%async_computation | async-start | bytes 884736 | tf_op jit(solution)/shard_map/all_to_all | solution.py:384
  10.5 24.2 %collective-permute-start.5 = (bf16[384,640]{1,0:T(8,128)(2,1)}, bf16[384,640]{1,0:T(8,128)(2,1)S(1)}, u32[]{:S(2)}, u32[]{:S(2)}) collective-permute-start(bf16[384,640]{1,0:T(8,128)(2,1)} %get-tuple-element.61), channel_id=1, source_target_pairs={{0,4},{2,6},{4,0},{6,2},{1,5},{3,7},{5,1},{7,3},{8,12},{10,14},{12... | collective-permute-start | bytes 1474568 | tf_op jit(solution)/shard_map/ppermute | solution.py:369
  13.5 23.0 %collective-permute-start.4 = (bf16[384,640]{1,0:T(8,128)(2,1)}, bf16[384,640]{1,0:T(8,128)(2,1)S(1)}, u32[]{:S(2)}, u32[]{:S(2)}) collective-permute-start(bf16[384,640]{1,0:T(8,128)(2,1)} %get-tuple-element.62), channel_id=1, source_target_pairs={{0,6},{2,0},{4,2},{6,4},{1,7},{3,1},{5,3},{7,5},{8,14},{10,8},{12,... | collective-permute-start | bytes 1474568 | tf_op jit(solution)/shard_map/ppermute | solution.py:369
  14.6 21.8 %collective-permute-start.3 = (bf16[384,640]{1,0:T(8,128)(2,1)}, bf16[384,640]{1,0:T(8,128)(2,1)S(1)}, u32[]{:S(2)}, u32[]{:S(2)}) collective-permute-start(bf16[384,640]{1,0:T(8,128)(2,1)} %get-tuple-element.63), channel_id=1, source_target_pairs={{0,2},{2,4},{4,6},{6,0},{1,3},{3,5},{5,7},{7,1},{8,10},{10,12},{12... | collective-permute-start | bytes 1474568 | tf_op jit(solution)/shard_map/ppermute | solution.py:369
  18.3 4.5 %collective-permute-start = (bf16[72,384]{1,0:T(8,128)(2,1)S(1)}, bf16[72,384]{1,0:T(8,128)(2,1)S(1)}, u32[]{:S(2)}, u32[]{:S(2)}) collective-permute-start(bf16[72,384]{1,0:T(8,128)(2,1)S(1)} %get-tuple-element.36), channel_id=1, source_target_pairs={{0,32},{32,0},{64,96},{96,64},{128,160},{160,128},{192,224},{224,1... | collective-permute-start | bytes 165896 | tf_op jit(solution)/shard_map/ppermute | solution.py:373
  22.8 15.8 %copy-start.12 = (s32[1,1024]{1,0:T(1,128)S(1)}, s32[1,1024]{1,0:T(1,128)}, u32[]{:S(2)}) copy-start(s32[1,1024]{1,0:T(1,128)} %param.10) | copy-start | bytes 12292
  22.8 20.2 %copy-start.3 = (bf16[8,72,384]{2,1,0:T(8,128)(2,1)S(1)}, bf16[8,72,384]{2,1,0:T(8,128)(2,1)}, u32[]{:S(2)}) copy-start(bf16[8,72,384]{2,1,0:T(8,128)(2,1)} %tail_projection.1.tail_rows) | copy-start | bytes 1327108
  22.9 20.2 %slice-start = ((bf16[256,384]{1,0:T(8,128)(2,1)}), bf16[32,384]{1,0:T(8,128)(2,1)S(1)}, s32[]{:S(2)}) async-start(bf16[256,384]{1,0:T(8,128)(2,1)} %head_projection_1.1.head_keys), calls=%async_computation.2 | async-start | bytes 49152 | tf_op jit(solution)/shard_map/slice | solution.py:422
  22.9 6.7 %collective-permute-start.1 = (bf16[72,384]{1,0:T(8,128)(2,1)S(1)}, bf16[72,384]{1,0:T(8,128)(2,1)S(1)}, u32[]{:S(2)}, u32[]{:S(2)}) collective-permute-start(bf16[72,384]{1,0:T(8,128)(2,1)S(1)} %through_1.1), channel_id=1, source_target_pairs={{0,64},{32,96},{64,0},{96,32},{128,192},{160,224},{192,128},{224,1... | collective-permute-start | bytes 165896 | tf_op jit(solution)/shard_map/ppermute | solution.py:373
  29.6 8.1 %collective-permute-start.2 = (bf16[64,384]{1,0:T(8,128)(2,1)S(1)}, bf16[64,384]{1,0:T(8,128)(2,1)S(1)}, u32[]{:S(2)}, u32[]{:S(2)}) collective-permute-start(bf16[64,384]{1,0:T(8,128)(2,1)S(1)} %through_3.1), channel_id=1, source_target_pairs={{0,128},{32,160},{64,192},{96,224},{128,0},{160,32},{192,64},{224,... | collective-permute-start | bytes 147464 | tf_op jit(solution)/shard_map/ppermute | solution.py:373
  36.5 14.7 %copy-start.4 = (bf16[384,640]{1,0:T(8,128)(2,1)}, bf16[384,640]{1,0:T(8,128)(2,1)S(1)}, u32[]{:S(2)}) copy-start(bf16[384,640]{1,0:T(8,128)(2,1)S(1)} %collective-permute-done.4.refs_7_) | copy-start | bytes 1474564
  36.5 14.7 %copy-start.6 = (bf16[384,640]{1,0:T(8,128)(2,1)}, bf16[384,640]{1,0:T(8,128)(2,1)S(1)}, u32[]{:S(2)}) copy-start(bf16[384,640]{1,0:T(8,128)(2,1)S(1)} %collective-permute-done.3.refs_6_) | copy-start | bytes 1474564
  38.8 15.4 %all-to-all-start.1 = ((bf16[8,64,384]{2,1,0:T(8,128)(2,1)}), bf16[8,64,384]{2,1,0:T(8,128)(2,1)S(1)}, u32[]{:S(2)}, u32[]{:S(2)}) async-start(bf16[8,64,384]{2,1,0:T(8,128)(2,1)} %section_memory.1), calls=%async_computation.1 | async-start | bytes 786432 | tf_op jit(solution)/shard_map/all_to_all | solution.py:418
  43.0 9.3 %copy-start.8 = (bf16[256,384]{1,0:T(8,128)(2,1)S(1)}, bf16[256,384]{1,0:T(8,128)(2,1)}, u32[]{:S(2)}) copy-start(bf16[256,384]{1,0:T(8,128)(2,1)} %head_projection_1.1.head_keys) | copy-start | bytes 589828
  43.1 9.3 %copy-start.9 = (bf16[256,384]{1,0:T(8,128)(2,1)S(1)}, bf16[256,384]{1,0:T(8,128)(2,1)}, u32[]{:S(2)}) copy-start(bf16[256,384]{1,0:T(8,128)(2,1)} %head_projection_2.1.head_values) | copy-start | bytes 589828
  43.1 11.2 %copy-start.10 = (s32[1,17]{1,0:T(1,128)S(1)}, s32[1,17]{1,0:T(1,128)}, u32[]{:S(2)}) copy-start(s32[1,17]{1,0:T(1,128)} %opened.3) | copy-start | bytes 208
  43.1 9.1 %collective-permute-start.6 = (bf16[64,384]{1,0:T(8,128)(2,1)S(1)}, bf16[64,384]{1,0:T(8,128)(2,1)S(1)}, u32[]{:S(2)}, u32[]{:S(2)}) collective-permute-start(bf16[64,384]{1,0:T(8,128)(2,1)S(1)} %maximum_select_fusion), channel_id=1, source_target_pairs={{0,1},{1,0},{2,3},{3,2},{4,5},{5,4},{6,7},{7,6},{8,9},{9,8},{10,11... | collective-permute-start | bytes 147464 | tf_op jit(solution)/shard_map/ppermute | solution.py:373
  52.3 1.0 %copy-start.1 = (bf16[512,384]{1,0:T(8,128)(2,1)S(1)}, bf16[512,384]{1,0:T(8,128)(2,1)}, u32[]{:S(2)}) copy-start(bf16[512,384]{1,0:T(8,128)(2,1)} %query_projection.1.q) | copy-start | bytes 1179652
  54.3 1.0 %copy-start.2 = (bf16[512,384]{1,0:T(8,128)(2,1)S(1)}, bf16[512,384]{1,0:T(8,128)(2,1)}, u32[]{:S(2)}) copy-start(bf16[512,384]{1,0:T(8,128)(2,1)} %query_projection.1.q) | copy-start | bytes 1179652
  55.2 18.1 %copy-start = (bf16[512,2560]{1,0:T(8,128)(2,1)S(1)}, bf16[512,2560]{1,0:T(8,128)(2,1)}, u32[]{:S(2)}) copy-start(bf16[512,2560]{1,0:T(8,128)(2,1)} %lat.11) | copy-start | bytes 7864324
  55.2 18.1 %copy-start.5 = (bf16[384,640]{1,0:T(8,128)(2,1)S(1)}, bf16[384,640]{1,0:T(8,128)(2,1)}, u32[]{:S(2)}) copy-start(bf16[384,640]{1,0:T(8,128)(2,1)} %copy-done.4) | copy-start | bytes 1474564
  55.3 18.1 %copy-start.7 = (bf16[384,640]{1,0:T(8,128)(2,1)S(1)}, bf16[384,640]{1,0:T(8,128)(2,1)}, u32[]{:S(2)}) copy-start(bf16[384,640]{1,0:T(8,128)(2,1)} %copy-done.6) | copy-start | bytes 1474564
  56.3 7.4 %collective-permute-start.12 = (bf16[256,384]{1,0:T(8,128)(2,1)S(1)}, bf16[256,384]{1,0:T(8,128)(2,1)S(1)}, u32[]{:S(2)}, u32[]{:S(2)}) collective-permute-start(bf16[256,384]{1,0:T(8,128)(2,1)S(1)} %memory_attention_0.1.refs_0_), channel_id=1, source_target_pairs={{0,6},{2,0},{4,2},{6,4},{1,7},{3,1},{5,3},{7,5},{8,14},{10,8},{12,... | collective-permute-start | bytes 589832 | tf_op jit(solution)/shard_map/ppermute | solution.py:369
  59.3 8.1 %collective-permute-start.11 = (bf16[256,384]{1,0:T(8,128)(2,1)S(1)}, bf16[256,384]{1,0:T(8,128)(2,1)S(1)}, u32[]{:S(2)}, u32[]{:S(2)}) collective-permute-start(bf16[256,384]{1,0:T(8,128)(2,1)S(1)} %memory_attention_0.1.refs_0_), channel_id=1, source_target_pairs={{0,2},{2,4},{4,6},{6,0},{1,3},{3,5},{5,7},{7,1},{8,10},{10,12},{12... | collective-permute-start | bytes 589832 | tf_op jit(solution)/shard_map/ppermute | solution.py:369
  60.3 8.2 %collective-permute-start.8 = (bf16[256,384]{1,0:T(8,128)(2,1)S(1)}, bf16[256,384]{1,0:T(8,128)(2,1)S(1)}, u32[]{:S(2)}, u32[]{:S(2)}) collective-permute-start(bf16[256,384]{1,0:T(8,128)(2,1)S(1)} %memory_attention_1.1.refs_0_), channel_id=1, source_target_pairs={{0,6},{2,0},{4,2},{6,4},{1,7},{3,1},{5,3},{7,5},{8,14},{10,8},{12,... | collective-permute-start | bytes 589832 | tf_op jit(solution)/shard_map/ppermute | solution.py:369
  63.6 8.7 %collective-permute-start.7 = (bf16[256,384]{1,0:T(8,128)(2,1)S(1)}, bf16[256,384]{1,0:T(8,128)(2,1)S(1)}, u32[]{:S(2)}, u32[]{:S(2)}) collective-permute-start(bf16[256,384]{1,0:T(8,128)(2,1)S(1)} %memory_attention_1.1.refs_0_), channel_id=1, source_target_pairs={{0,2},{2,4},{4,6},{6,0},{1,3},{3,5},{5,7},{7,1},{8,10},{10,12},{12... | collective-permute-start | bytes 589832 | tf_op jit(solution)/shard_map/ppermute | solution.py:369
  63.7 8.8 %collective-permute-start.14 = (bf16[128,384]{1,0:T(8,128)(2,1)S(1)}, bf16[128,384]{1,0:T(8,128)(2,1)S(1)}, u32[]{:S(2)}, u32[]{:S(2)}) collective-permute-start(bf16[128,384]{1,0:T(8,128)(2,1)S(1)} %slice.31), channel_id=1, source_target_pairs={{0,6},{2,0},{4,2},{6,4},{1,7},{3,1},{5,3},{7,5},{8,14},{10,8},{12,... | collective-permute-start | bytes 294920 | tf_op jit(solution)/shard_map/ppermute | solution.py:369
  67.4 5.9 %collective-permute-start.13 = (bf16[128,384]{1,0:T(8,128)(2,1)S(1)}, bf16[128,384]{1,0:T(8,128)(2,1)S(1)}, u32[]{:S(2)}, u32[]{:S(2)}) collective-permute-start(bf16[128,384]{1,0:T(8,128)(2,1)S(1)} %slice.30), channel_id=1, source_target_pairs={{0,2},{2,4},{4,6},{6,0},{1,3},{3,5},{5,7},{7,1},{8,10},{10,12},{12... | collective-permute-start | bytes 294920 | tf_op jit(solution)/shard_map/ppermute | solution.py:369
  68.5 6.4 %collective-permute-start.10 = (bf16[128,384]{1,0:T(8,128)(2,1)S(1)}, bf16[128,384]{1,0:T(8,128)(2,1)S(1)}, u32[]{:S(2)}, u32[]{:S(2)}) collective-permute-start(bf16[128,384]{1,0:T(8,128)(2,1)S(1)} %slice.29), channel_id=1, source_target_pairs={{0,6},{2,0},{4,2},{6,4},{1,7},{3,1},{5,3},{7,5},{8,14},{10,8},{12,... | collective-permute-start | bytes 294920 | tf_op jit(solution)/shard_map/ppermute | solution.py:369
  72.3 5.9 %collective-permute-start.9 = (bf16[128,384]{1,0:T(8,128)(2,1)S(1)}, bf16[128,384]{1,0:T(8,128)(2,1)S(1)}, u32[]{:S(2)}, u32[]{:S(2)}) collective-permute-start(bf16[128,384]{1,0:T(8,128)(2,1)S(1)} %slice.28), channel_id=1, source_target_pairs={{0,2},{2,4},{4,6},{6,0},{1,3},{3,5},{5,7},{7,1},{8,10},{10,12},{12... | collective-permute-start | bytes 294920 | tf_op jit(solution)/shard_map/ppermute | solution.py:369

commit v4 on v3

--- a/solution.py
+++ b/solution.py
@@ -22,6 +22,7 @@
 CHUNKS = 5
 TAIL_LIMIT = 60 * 1024 * 1024
 REST_LIMIT = 60 * 1024 * 1024
+ATTEND_LIMIT = 53 * 1024 * 1024
 LIMIT = 32 * 1024 * 1024
 BLOCK = 192
 SPAN = ("z", "y", "core")
@@ -135,7 +136,7 @@
     )(*args)
 
 
-def head_kernel(which, after, lat, w, out, rows, part, sems):
+def head_project(which, lat, w, rows, part, sems):
     copies = [
         pltpu.make_async_copy(w.at[which], part, sems.at[0]),
         pltpu.make_async_copy(lat.at[pl.ds(0, MEM)], rows, sems.at[1]),
@@ -144,19 +145,30 @@
         copy.start()
     for copy in copies:
         copy.wait()
-    mixed = jnp.dot(rows[...], part[...], preferred_element_type=F32)
-    out[...] = normed(mixed) if which == 1 else mixed.astype(BF16)
-
-
-def heads(which, after, latents, w3):
+    return jnp.dot(rows[...], part[...], preferred_element_type=F32)
+
+
+def head_values_kernel(after, lat, w, out, rows, part, sems):
+    out[...] = head_project(2, lat, w, rows, part, sems).astype(BF16)
+
+
+def head_keys_kernel(phase, lat, w, values, payload, out, edge, rows, part, sems):
+    keys = normed(head_project(1, lat, w, rows, part, sems))
+    out[...] = keys
+    first = phase[0] == 0
+    edge[:PART] = jnp.where(first, payload[PARTS - 1, :PART], keys[:PART])
+    edge[PART:] = jnp.where(first, payload[PARTS - 1, PART : 2 * PART], values[:PART])
+
+
+def heads(kernel, outs, name, after, latents, w3, *more):
     depth = latents.shape[1]
     return call_on_hbm(
-        functools.partial(head_kernel, which),
-        shape((MEM, COLS), BF16),
-        f"head_projection_{which}",
+        kernel,
+        outs,
+        name,
         2 * MEM * depth * COLS,
         3300000,
-        (after, latents, w3),
+        (after, latents, w3, *more),
         [pltpu.VMEM((MEM, depth), BF16), pltpu.VMEM((depth, COLS), BF16), pltpu.SemaphoreType.DMA((2,))],
     )
 
@@ -207,18 +219,7 @@
     )(*args)
 
 
-def window_kernel(q, head_keys, head_values, tail_rows, halo, frame_row, frame_column, top, bottom, qx, kx, vx):
-    edge = jnp.zeros((HALF_WIN, COLS), BF16)
-    qx[:HALF_WIN] = edge
-    qx[HALF_WIN + ROWS :] = edge
-    qx[HALF_WIN : HALF_WIN + ROWS] = q[...]
-    for ext, head, rows in ((kx, head_keys, slice(0, PART)), (vx, head_values, slice(PART, 2 * PART))):
-        ext[:HALF_WIN] = halo[rows]
-        ext[HALF_WIN + ROWS :] = halo[rows]
-        ext[HALF_WIN : HALF_WIN + MEM] = head[...]
-        for d in range(PARTS):
-            at = HALF_WIN + MEM + d * PART
-            ext[at : at + PART] = tail_rows[d, rows]
+def window_part(frame_row, frame_column, top, bottom, qx, kx, vx):
     ones = jnp.ones((BLOCK, HD), BF16)
     window_a = lax.broadcasted_iota(jnp.int32, (BLOCK, BLOCK), 0) // WIN
     window_b = lax.broadcasted_iota(jnp.int32, (BLOCK, BLOCK), 1) // WIN
@@ -303,65 +304,103 @@
             keys, values = plane_step(keys, values, rate, arrived[i, :PART], arrived[i, PART : 2 * PART])
 
 
-def attend_kernel(base, phase, opened, q, memory, top, bottom, out):
-    rows = out.shape[0]
+def attend_kernel(
+    phase, opened, q, head_keys, head_values, tail_rows, halo, rows_in, columns_in, memory_in,
+    out, top, bottom, qx, kx, vx, tail, frame_row, frame_column, memory, sems,
+):
+    own, upper = pl.ds(HALF_WIN, ROWS), pl.ds(HALF_WIN + ROWS, HALF_WIN)
+    lower, head = pl.ds(0, HALF_WIN), pl.ds(HALF_WIN, MEM)
+    first, second = pl.ds(0, PART), pl.ds(PART, PART)
+    pairs = [
+        (tail_rows, tail),
+        (q, qx.at[own]),
+        (head_keys, kx.at[head]),
+        (head_values, vx.at[head]),
+        (halo.at[first], kx.at[lower]),
+        (halo.at[first], kx.at[upper]),
+        (halo.at[second], vx.at[lower]),
+        (halo.at[second], vx.at[upper]),
+        (rows_in, frame_row),
+        (columns_in, frame_column),
+        (memory_in, memory),
+    ]
+    copies = [pltpu.make_async_copy(a, b, sems.at[i]) for i, (a, b) in enumerate(pairs)]
+    for copy in copies:
+        copy.start()
+    edge = jnp.zeros((HALF_WIN, COLS), BF16)
+    qx[:HALF_WIN] = edge
+    qx[HALF_WIN + ROWS :] = edge
+    copies[0].wait()
+    for d in range(PARTS):
+        at = HALF_WIN + MEM + d * PART
+        kx[at : at + PART] = tail[d, :PART]
+        vx[at : at + PART] = tail[d, PART : 2 * PART]
+    for copy in copies[1:-1]:
+        copy.wait()
+    window_part(frame_row, frame_column, top, bottom, qx, kx, vx)
     start = phase[0] * (ROWS // WIN)
-    row = lax.broadcasted_iota(jnp.int32, (rows, HD), 0) + base
-    window = (row + HALF_WIN) // WIN
-    is_open = jnp.zeros((rows, HD), F32)
-    for w in range((base + HALF_WIN) // WIN, (base + rows - 1 + HALF_WIN) // WIN + 1):
+    window = (lax.broadcasted_iota(jnp.int32, (ROWS, HD), 0) + HALF_WIN) // WIN
+    is_open = jnp.zeros((ROWS, HD), F32)
+    for w in range(ROWS // WIN + 1):
         flag = jnp.where(opened[0, start + w] == 1, 1.0, 0.0)
         is_open = jnp.where(window == w, flag, is_open)
     ones = jnp.ones((MEM, HD), BF16)
-    at = slice(base, base + rows)
+    copies[-1].wait()
     for h in range(HEADS):
         c = slice(h * HD, (h + 1) * HD)
         keys = memory[:, :PART, c].reshape(MEM, HD)
         values = memory[:, PART:, c].reshape(MEM, HD)
-        score = lax.dot_general(q[at, c], keys, (((1,), (1,)), ((), ())), preferred_element_type=F32)
+        score = lax.dot_general(
+            qx[HALF_WIN : HALF_WIN + ROWS, c], keys, (((1,), (1,)), ((), ())), preferred_element_type=F32
+        )
         weight = jnp.exp2(score * SCALE2).astype(BF16)
         result = jnp.dot(weight, jnp.concatenate([values, ones], axis=1), preferred_element_type=F32)
-        above = top[at, c] + is_open * result[:, :HD]
-        below = bottom[at, c] + is_open * result[:, HD:]
+        above = top[:, c] + is_open * result[:, :HD]
+        below = bottom[:, c] + is_open * result[:, HD:]
         out[:, c] = (above / below).astype(BF16)
 
 
-def final_kernel(column, lat, *refs):
-    out = refs[-1]
-    attended, weights = refs[:5], refs[5:9]
-    total = lat[...].astype(F32)
-    for a, w in zip(attended[:3], weights[:3]):
-        total = total + jnp.dot(a[...], w[...], preferred_element_type=F32)
-    far = jnp.concatenate([attended[3][...], attended[4][...]], axis=0)
-    total = total + jnp.dot(far, weights[3][...], preferred_element_type=F32)
-    out[...] = total.astype(BF16)
-
-
-def final(r, column, latents, attended, weights, earlier=None):
-    share = weights[0].shape[1]
-    rows = attended[0].shape[0]
-    vmem = pl.BlockSpec(memory_space=pltpu.VMEM)
-    specs = [pl.BlockSpec((rows, share), lambda i, col: (r, col[0]))] + [vmem] * 9
-    operands = [column, latents, *attended, *weights]
-    aliases = {}
-    if earlier is not None:
-        specs.append(pl.BlockSpec(memory_space=pl.ANY))
-        aliases = {len(operands): 0}
-        operands.append(earlier)
+def attention(phase, opened, *operands):
+    smem = pl.BlockSpec(memory_space=pltpu.SMEM)
+    hbm = pl.BlockSpec(memory_space=pl.ANY)
+    extended = pltpu.VMEM((EXT, COLS), BF16)
     return pl.pallas_call(
-        final_kernel,
-        grid_spec=pltpu.PrefetchScalarGridSpec(
-            num_scalar_prefetch=1,
-            grid=(1,),
-            in_specs=specs,
-            out_specs=pl.BlockSpec((rows, share), lambda i, col: (r, 0)),
+        attend_kernel,
+        out_shape=shape((ROWS, COLS), BF16),
+        in_specs=[smem, smem] + [hbm] * len(operands),
+        out_specs=pl.BlockSpec(memory_space=pltpu.VMEM),
+        scratch_shapes=[
+            pltpu.VMEM((ROWS, COLS), F32),
+            pltpu.VMEM((ROWS, COLS), F32),
+            extended,
+            extended,
+            extended,
+            pltpu.VMEM((PARTS, PAYLOAD, COLS), BF16),
+            pltpu.VMEM((EXT // BLOCK, 1, BLOCK), jnp.int32),
+            pltpu.VMEM((EXT, HD), jnp.int32),
+            pltpu.VMEM((PARTS, 2 * PART, COLS), BF16),
+            pltpu.SemaphoreType.DMA((11,)),
+        ],
+        cost_estimate=pl.CostEstimate(
+            flops=4 * ROWS * (MEM + BLOCK) * COLS * 2, bytes_accessed=3000000, transcendentals=0
         ),
-        out_shape=shape((ROWS, share), BF16),
-        input_output_aliases=aliases,
-        cost_estimate=pl.CostEstimate(flops=2 * rows * 4 * COLS * share, bytes_accessed=2000000, transcendentals=0),
-        compiler_params=pltpu.CompilerParams(vmem_limit_bytes=LIMIT),
-        name=f"output_projection_{r}",
-    )(*operands)
+        compiler_params=pltpu.CompilerParams(vmem_limit_bytes=ATTEND_LIMIT),
+        name="attention",
+    )(phase, opened, *operands)
+
+
+def near_kernel(lat, own, right, left, w_own, w_right, w_left, total):
+    sums = lat[...].astype(F32)
+    for a, w in ((own, w_own), (right, w_right), (left, w_left)):
+        sums = sums + jnp.dot(a[...], w[...], preferred_element_type=F32)
+    total[...] = sums
+
+
+def far_kernel(total, first, second, w, out):
+    half = ROWS // 2
+    for r, part in enumerate((first, second)):
+        at = slice(r * half, (r + 1) * half)
+        out[at] = (total[at] + jnp.dot(part[...], w[...], preferred_element_type=F32)).astype(BF16)
 
 
 def moved(x, axis, by):
@@ -388,75 +427,61 @@
     offsets = (0, 1, -1, 2)
     sends = [lax.dynamic_slice_in_dim(w_out, ((mp + by) & 3) * share, share, 1) for by in offsets]
     weights = [moved(piece, "mp", by) if by else piece for by, piece in zip(offsets, sends)]
-    arrived, _ = lax.optimization_barrier((arrived, sends))
+    half_keys = shape((MEM, COLS), BF16)
+    after, payload = lax.optimization_barrier((z_ref, payload))
+    head_values = heads(head_values_kernel, half_keys, "head_values", after, latents, w3)
+    arrived, _, head_values = lax.optimization_barrier((arrived, sends, head_values))
 
     wide = shape((2 * PART + 8, COLS), F32)
     packed = shape((PAYLOAD, COLS), BF16)
     plain = shape((2 * PART, COLS), BF16)
     plain_all = shape((PARTS, 2 * PART, COLS), BF16)
     own, sent = vmem_call(plane_kernel, (wide, packed), "plane_total", 1000000, (arrived,))
-    after, sent = lax.optimization_barrier((z_ref, sent))
     got_1 = swapped(sent, "z", 1)
-    head_keys = heads(1, after, latents, w3)
-    got_1, head_keys = lax.optimization_barrier((got_1, head_keys))
-
     sent = vmem_call(first_kernel, packed, "through_1", 100000, (z_ref, own, got_1), smem=1)
-    after, sent = lax.optimization_barrier((z_ref, sent))
+    latents, sent = lax.optimization_barrier((latents, sent))
     got_2 = swapped(sent, "z", 2)
-    head_values = heads(2, after, latents, w3)
-    got_2, head_values = lax.optimization_barrier((got_2, head_values))
+    own_columns = lax.dynamic_slice_in_dim(latents, mp * share, share, 1)
+    got_2, own_columns = lax.optimization_barrier((got_2, own_columns))
 
     sent = vmem_call(next_kernel, plain, "through_3", 100000, (z_ref, own, got_1, got_2), smem=1)
+    after, sent = lax.optimization_barrier((phase_ref, sent))
     got_4 = swapped(sent, "z", 4)
-    got_4, weights = lax.optimization_barrier((got_4, weights))
+    head_keys, edge = heads(
+        head_keys_kernel, (half_keys, plain), "head_keys", after, latents, w3, head_values, payload
+    )
+    got_4, head_keys = lax.optimization_barrier((got_4, head_keys))
     memory = vmem_call(
         memory_kernel, plain_all, "section_memory", 1000000, (z_ref, got_1, got_2, got_4, arrived), smem=1
     )
-    after, memory, head_keys, head_values, frame_ids = lax.optimization_barrier(
-        (z_ref, memory, head_keys, head_values, frame_ids)
-    )
+    after, memory, edge, frame_ids = lax.optimization_barrier((z_ref, memory, edge, frame_ids))
     memory = lax.all_to_all(memory, PLANE, 0, 0, tiled=True)
-    edge = jnp.where(
-        phase == 0,
-        payload[PARTS - 1, : 2 * PART],
-        jnp.concatenate([head_keys[:PART], head_values[:PART]], axis=0),
-    )
     halo = swapped(edge, "phase", 1)
     frames_pad = jnp.pad(frame_ids[0], (HALF_WIN, HALF_WIN), constant_values=outside_frame)
     frames = lax.dynamic_slice_in_dim(frames_pad, phase * ROWS, EXT)
     frame_row = frames.reshape(EXT // BLOCK, 1, BLOCK)
     frame_column = jnp.broadcast_to(frames[:, None], (EXT, HD))
     queries = query(after, latents, w3)
-    top, bottom = vmem_call(
-        window_kernel,
-        (shape((ROWS, COLS), F32), shape((ROWS, COLS), F32)),
-        "window_attention",
-        4 * EXT * BLOCK * COLS * 2,
-        (queries, head_keys, head_values, payload, halo, frame_row, frame_column),
-        scratch=[pltpu.VMEM((EXT, COLS), BF16)] * 3,
-    )
-    memory, top, bottom = lax.optimization_barrier((memory, top, bottom))
-
-    pieces = []
-    rows = ROWS // 2
-    for r in range(2):
-        pieces.append(
-            vmem_call(
-                functools.partial(attend_kernel, r * rows),
-                shape((rows, COLS), BF16),
-                f"memory_attention_{r}",
-                4 * rows * MEM * COLS * 2,
-                (phase_ref, memory_mask, queries, memory, top, bottom),
-                smem=2,
-            )
-        )
-    column = mp.reshape(1).astype(jnp.int32)
-    near = [(moved(piece, "mp", 1), moved(piece, "mp", -1)) for piece in pieces]
-    refined = None
-    for r, (piece, (right, left)) in enumerate(zip(pieces, near)):
-        far = (moved(right[: rows // 2], "mp", 1), moved(left[rows // 2 :], "mp", -1))
-        refined = final(r, column, latents, (piece, right, left, *far), weights, refined)
-    return refined
+    memory, weights = lax.optimization_barrier((memory, weights))
+    attended = attention(
+        phase_ref, memory_mask, queries, head_keys, head_values, payload, halo, frame_row, frame_column, memory
+    )
+    right, left = moved(attended, "mp", 1), moved(attended, "mp", -1)
+    far_1, far_2 = moved(right[: ROWS // 2], "mp", 1), moved(left[ROWS // 2 :], "mp", -1)
+    total = vmem_call(
+        near_kernel,
+        shape((ROWS, share), F32),
+        "near_projection",
+        6 * ROWS * COLS * share,
+        (own_columns, attended, right, left, *weights[:3]),
+    )
+    return vmem_call(
+        far_kernel,
+        shape((ROWS, share), BF16),
+        "far_projection",
+        2 * ROWS * COLS * share,
+        (total, far_1, far_2, weights[3]),
+    )
 
 
 def solution(mesh):

time: 80.6 us -> 82.9 us (1.029)
  waiting for transfers between devices: 11.8 us -> 20.1 us
  starting transfers between devices: 39.6 us -> 32.4 us
  Pallas kernels: 23.9 us -> 25.6 us
    ppermute x11 -> x7, starting transfers between devices: 19.1 us -> 9.15 us  [moved(): return lax.ppermute(x, axis, [(i, (i + by) % size) for i in range(size)])]
    ppermute x11 -> x7, waiting for transfers between devices: 6.99 us -> 13.4 us  [moved(): return lax.ppermute(x, axis, [(i, (i + by) % size) for i in range(size)])]
    ppermute x4, starting transfers between devices: 12.6 us -> 14.7 us  [swapped(): lax.ppermute(x, axis, [(i, i ^ bit) for i in range(lax.axis_size(axis))])]
    all_to_all x1, waiting for transfers between devices: 2.62 us -> 4.05 us  [local(): arrived = lax.all_to_all(payload, PLANE, 0, 0, tiled=True)]
    pallas_call x3, Pallas kernels: 11.6 us -> 12.9 us  [call_on_hbm(): pl.pallas_call(kernel, out_shape=outs, in_specs=[pl.BlockSpec(memory_spac...]
    dynamic_slice x0 -> x1, local copies, waits for them, and re-layouts: none -> 1.14 us  [local(): own_columns = lax.dynamic_slice_in_dim(latents, mp * share, share, 1)]
    unnamed x26 -> x12, local copies, waits for them, and re-layouts: 2.02 us -> 1.01 us
    pallas_call x2 -> x1, Pallas kernels: 3.28 us -> 4.1 us  [attention(): pl.pallas_call(attend_kernel, out_shape=shape((ROWS, COLS), BF16), in_spe...]
  transfers between devices with their start and end apart: 17 -> 13, of which waited for: 7 -> 7; matrix products, arithmetic and copies ran while one was open for 3% -> 3% of each run, Pallas kernels for 19% -> 19%
where the time goes in v4:
time: 82.9 us; the launch traced here: 81.9 us
  starting transfers between devices  32.4 us (39%)
  Pallas kernels  25.6 us (31%)
  waiting for transfers between devices  20.1 us (24%)
  local copies, waits for them, and re-layouts  3.65 us (4%)
    ppermute x4, starting transfers between devices, swapped(): lax.ppermute(x, axis, [(i, i ^ bit) for i in range(lax.axis_size(axis))])  14.7 us
    ppermute x7, waiting for transfers between devices, moved(): return lax.ppermute(x, axis, [(i, (i + by) % size) for i in range(size)])  13.4 us
    pallas_call x3, Pallas kernels, call_on_hbm(): pl.pallas_call(kernel, out_shape=outs, in_specs=[pl.BlockSpec(memory_spac...  12.9 us
    ppermute x7, starting transfers between devices, moved(): return lax.ppermute(x, axis, [(i, (i + by) % size) for i in range(size)])  9.15 us
    pallas_call x1, Pallas kernels, tails(): pl.pallas_call(tail_kernel, out_shape=shape((PARTS, PAYLOAD, COLS), BF16)...  4.7 us
    all_to_all x1, starting transfers between devices, local(): arrived = lax.all_to_all(payload, PLANE, 0, 0, tiled=True)  4.48 us
    pallas_call x1, Pallas kernels, attention(): pl.pallas_call(attend_kernel, out_shape=shape((ROWS, COLS), BF16), in_spe...  4.1 us
    all_to_all x1, starting transfers between devices, local(): memory = lax.all_to_all(memory, PLANE, 0, 0, tiled=True)  4.09 us
  transfers between devices with their start and end apart: 13, of which 7 were waited for; matrix products, arithmetic and copies ran while one was open for 3% of the time, Pallas kernels for 19%

profile of v4, /device:TPU:32, one launch (start us, length us, event | category | flops | bytes accessed | tf_op | source)
XLA Modules:
  0.0 81.9 jit_solution(5252698277562362463)
XLA Ops:
  0.0 4.7 %tail_projection.1.payload.tail_rows = bf16[8,72,384]{2,1,0:T(8,128)(2,1)} custom-call(s32[1]{0:T(128)} %bitcast.1.phase, f32[2,3]{1,0:T(2,128)} %bitcast.10, bf16[512,2560]{1,0:T(8,128)(2,1)} %lat.5, bf16[3,2560,384]{2,1,0:T(8,128)(2,1)} %bitcast.5), custom_call_target="tpu_custom_call" | custom-call | flops 1006632960 | bytes 5500000 | tf_op jit(solution)/shard_map/tail_projection/pallas_call | solution.py:106
  4.7 4.5 %all-to-all-start = ((bf16[8,72,384]{2,1,0:T(8,128)(2,1)}), bf16[8,72,384]{2,1,0:T(8,128)(2,1)S(1)}, u32[]{:S(2)}, u32[]{:S(2)}) async-start(bf16[8,72,384]{2,1,0:T(8,128)(2,1)} %tail_projection.1.payload.tail_rows), calls=%async_computation | async-start | bytes 884736 | tf_op jit(solution)/shard_map/all_to_all | solution.py:423
  9.2 0.0 copy-start.4
  9.2 3.6 %head_values.1.values = bf16[256,384]{1,0:T(8,128)(2,1)} custom-call(s32[1]{0:T(128)} %bitcast.after.z, bf16[512,2560]{1,0:T(8,128)(2,1)} %lat.5, bf16[3,2560,384]{2,1,0:T(8,128)(2,1)} %bitcast.6), custom_call_target="tpu_custom_call" | custom-call | flops 503316480 | bytes 3300000 | tf_op jit(solution)/shard_map/head_values/pallas_call | solution.py:127
  12.8 0.0 copy-done.4
  12.8 1.2 %constant_dynamic-slice_fusion.1 = (bf16[384,640]{1,0:T(8,128)(2,1)}, bf16[384,640]{1,0:T(8,128)(2,1)}, bf16[384,640]{1,0:T(8,128)(2,1)}, bf16[384,640]{1,0:T(8,128)(2,1)S(1)}) fusion(bf16[384,2560]{1,0:T(8,128)(2,1)S(1)} %copy-done.4, s32[]{:T(128)S(6)} %select_n.21, s32[]{:T(128)S(6)} %select_n.20, s32[]{:T(128)S(6)} %select_n.19, s32[]{:T(128)S(6)} %select_n.18), kind=kLoop, calls=%fused_computation.2 | loop fusion | bytes 3932176 | tf_op jit(solution)/shard_map/dynamic_slice | solution.py:428
  14.0 4.1 %all-to-all-done.arrived = bf16[8,72,384]{2,1,0:T(8,128)(2,1)S(1)} async-done(((bf16[8,72,384]{2,1,0:T(8,128)(2,1)}), bf16[8,72,384]{2,1,0:T(8,128)(2,1)S(1)}, u32[]{:S(2)}, u32[]{:S(2)}) %all-to-all-start) | async-done | bytes 442400 | tf_op jit(solution)/shard_map/all_to_all | solution.py:423
  18.0 0.2 plane_total.1
  18.2 0.9 %collective-permute-start = (bf16[72,384]{1,0:T(8,128)(2,1)S(1)}, bf16[72,384]{1,0:T(8,128)(2,1)S(1)}, u32[]{:S(2)}, u32[]{:S(2)}) collective-permute-start(bf16[72,384]{1,0:T(8,128)(2,1)S(1)} %get-tuple-element.37), channel_id=1, source_target_pairs={{0,32},{32,0},{64,96},{96,64},{128,160},{160,128},{192,224},{224,1... | collective-permute-start | bytes 165896 | tf_op jit(solution)/shard_map/ppermute | solution.py:412
  19.1 0.8 collective-permute-start.4
  19.9 2.4 %collective-permute-start.5 = (bf16[384,640]{1,0:T(8,128)(2,1)}, bf16[384,640]{1,0:T(8,128)(2,1)S(1)}, u32[]{:S(2)}, u32[]{:S(2)}) collective-permute-start(bf16[384,640]{1,0:T(8,128)(2,1)} %get-tuple-element.60), channel_id=1, source_target_pairs={{0,6},{2,0},{4,2},{6,4},{1,7},{3,1},{5,3},{7,5},{8,14},{10,8},{12,... | collective-permute-start | bytes 1474568 | tf_op jit(solution)/shard_map/ppermute | solution.py:408
  22.3 1.1 %collective-permute-start.6 = (bf16[384,640]{1,0:T(8,128)(2,1)}, bf16[384,640]{1,0:T(8,128)(2,1)S(1)}, u32[]{:S(2)}, u32[]{:S(2)}) collective-permute-start(bf16[384,640]{1,0:T(8,128)(2,1)} %get-tuple-element.59), channel_id=1, source_target_pairs={{0,4},{2,6},{4,0},{6,2},{1,5},{3,7},{5,1},{7,3},{8,12},{10,14},{12... | collective-permute-start | bytes 1474568 | tf_op jit(solution)/shard_map/ppermute | solution.py:408
  23.5 0.0 collective-permute-done.got_1
  23.5 3.4 %collective-permute-start.1 = (bf16[72,384]{1,0:T(8,128)(2,1)S(1)}, bf16[72,384]{1,0:T(8,128)(2,1)S(1)}, u32[]{:S(2)}, u32[]{:S(2)}) collective-permute-start(bf16[72,384]{1,0:T(8,128)(2,1)S(1)} %through_1.1), channel_id=1, source_target_pairs={{0,64},{32,96},{64,0},{96,32},{128,192},{160,224},{192,128},{224,1... | collective-permute-start | bytes 165896 | tf_op jit(solution)/shard_map/ppermute | solution.py:412
  26.9 1.1 %constant_dynamic-slice_fusion.lat = bf16[512,640]{1,0:T(8,128)(2,1)S(1)} fusion(bf16[512,2560]{1,0:T(8,128)(2,1)} %lat.5, s32[]{:T(128)S(6)} %select_n.22), kind=kLoop, calls=%fused_computation.1 | loop fusion | bytes 1310724 | tf_op jit(solution)/shard_map/dynamic_slice | solution.py:444
  28.0 1.0 %collective-permute-done.1.got_2 = bf16[72,384]{1,0:T(8,128)(2,1)S(1)} collective-permute-done((bf16[72,384]{1,0:T(8,128)(2,1)S(1)}, bf16[72,384]{1,0:T(8,128)(2,1)S(1)}, u32[]{:S(2)}, u32[]{:S(2)}) %collective-permute-start.1) | collective-permute-done | bytes 55328 | tf_op jit(solution)/shard_map/ppermute | solution.py:412
  29.0 0.1 through_3.1
  29.1 0.0 copy-start.5
  29.1 7.0 %collective-permute-start.2 = (bf16[64,384]{1,0:T(8,128)(2,1)S(1)}, bf16[64,384]{1,0:T(8,128)(2,1)S(1)}, u32[]{:S(2)}, u32[]{:S(2)}) collective-permute-start(bf16[64,384]{1,0:T(8,128)(2,1)S(1)} %through_3.1), channel_id=1, source_target_pairs={{0,128},{32,160},{64,192},{96,224},{128,0},{160,32},{192,64},{224,... | collective-permute-start | bytes 147464 | tf_op jit(solution)/shard_map/ppermute | solution.py:412
  36.1 4.7 %head_keys.1 = (bf16[256,384]{1,0:T(8,128)(2,1)}, bf16[64,384]{1,0:T(8,128)(2,1)}) custom-call(s32[1]{0:T(128)} %bitcast.1.phase, bf16[512,2560]{1,0:T(8,128)(2,1)} %lat.5, bf16[3,2560,384]{2,1,0:T(8,128)(2,1)} %bitcast.7, bf16[256,384]{1,0:T(8,128)(2,1)} %head_values.1.values, bf16[8,72,384]{2,1,0:T(8,128)(2,1)} %tail_projection.1.payload.tail_rows), custom_call_target="tpu_custom_call" | custom-call | flops 503316480 | bytes 3300000 | tf_op jit(solution)/shard_map/head_keys/pallas_call | solution.py:127
  40.8 0.0 collective-permute-done.2.got_4
  40.8 1.0 %section_memory.1 = bf16[8,64,384]{2,1,0:T(8,128)(2,1)} custom-call(s32[1]{0:T(128)} %bitcast.after.z, bf16[72,384]{1,0:T(8,128)(2,1)S(1)} %collective-permute-done.got_1, bf16[72,384]{1,0:T(8,128)(2,1)S(1)} %collective-permute-done.1.got_2, bf16[64,384]{1,0:T(8,128)(2,1)S(1)} %collective-permute-done.2.got_4, bf16[8,72,384]{2,1,0:T(8,128)(2,1)S(1)} %all-to-all-done.arrived), custom_call_target="tpu_custom_call" | custom-call | flops 1000000 | bytes 602116 | tf_op jit(solution)/shard_map/section_memory/pallas_call | solution.py:210
  41.7 4.1 %all-to-all-start.1 = ((bf16[8,64,384]{2,1,0:T(8,128)(2,1)}), bf16[8,64,384]{2,1,0:T(8,128)(2,1)}, u32[]{:S(2)}, u32[]{:S(2)}) async-start(bf16[8,64,384]{2,1,0:T(8,128)(2,1)} %section_memory.1), calls=%async_computation.1 | async-start | bytes 786432 | tf_op jit(solution)/shard_map/all_to_all | solution.py:458
  45.9 3.4 %collective-permute-start.3 = (bf16[64,384]{1,0:T(8,128)(2,1)}, bf16[64,384]{1,0:T(8,128)(2,1)S(1)}, u32[]{:S(2)}, u32[]{:S(2)}) collective-permute-start(bf16[64,384]{1,0:T(8,128)(2,1)} %get-tuple-element.51), channel_id=1, source_target_pairs={{0,1},{1,0},{2,3},{3,2},{4,5},{5,4},{6,7},{7,6},{8,9},{9,8},{10,11... | collective-permute-start | bytes 147464 | tf_op jit(solution)/shard_map/ppermute | solution.py:412
  49.2 0.0 copy-done.5
  49.2 0.1 pad_dynamic-slice_fusion
  49.3 0.1 reshape.12.rows_in
  49.4 0.0 copy-start
  49.4 0.0 copy-start.2
  49.4 0.0 copy-start.3
  49.4 4.6 %query_projection.1.q = bf16[512,384]{1,0:T(8,128)(2,1)} custom-call(s32[1]{0:T(128)} %bitcast.after.z, bf16[512,2560]{1,0:T(8,128)(2,1)} %lat.5, bf16[3,2560,384]{2,1,0:T(8,128)(2,1)} %bitcast.8), custom_call_target="tpu_custom_call" | custom-call | flops 1006632960 | bytes 4600000 | tf_op jit(solution)/shard_map/query_projection/pallas_call | solution.py:127
  54.1 0.0 collective-permute-done.4.w_right
  54.1 0.0 collective-permute-done.5.w_left
  54.1 0.0 collective-permute-done.6.w
  54.1 0.1 all-to-all-done.1.memory_in
  54.2 1.5 %collective-permute-done.3.halo = bf16[64,384]{1,0:T(8,128)(2,1)S(1)} collective-permute-done((bf16[64,384]{1,0:T(8,128)(2,1)}, bf16[64,384]{1,0:T(8,128)(2,1)S(1)}, u32[]{:S(2)}, u32[]{:S(2)}) %collective-permute-start.3) | collective-permute-done | bytes 49184 | tf_op jit(solution)/shard_map/ppermute | solution.py:412
  55.7 0.1 broadcast_in_dim.2.columns_in
  55.9 0.0 copy-done
  55.9 0.0 copy-done.2
  55.9 0.0 copy-done.3
  55.9 4.1 %attention.1.own = bf16[512,384]{1,0:T(8,128)(2,1)} custom-call(s32[1]{0:T(128)} %bitcast.1.phase, s32[1,17]{1,0:T(1,128)S(1)} %copy-done.3, bf16[512,384]{1,0:T(8,128)(2,1)} %query_projection.1.q, bf16[256,384]{1,0:T(8,128)(2,1)S(1)} %copy-done.2, bf16[256,384]{1,0:T(8,128)(2,1)S(1)} %copy-done, bf16[8,72,384]{2,1,0:T(8,128)(2,1)} %tail_projection.1.payload.tail_rows, ...), custom_call_target="tpu_custom_call" | custom-call | flops 704643072 | bytes 3000000 | tf_op jit(solution)/shard_map/attention/pallas_call | solution.py:367
  60.0 1.4 %collective-permute-start.8 = (bf16[512,384]{1,0:T(8,128)(2,1)}, bf16[512,384]{1,0:T(8,128)(2,1)S(1)}, u32[]{:S(2)}, u32[]{:S(2)}) collective-permute-start(bf16[512,384]{1,0:T(8,128)(2,1)} %attention.1.own), channel_id=1, source_target_pairs={{0,6},{2,0},{4,2},{6,4},{1,7},{3,1},{5,3},{7,5},{8,14},{10,8},{12,... | collective-permute-start | bytes 1179656 | tf_op jit(solution)/shard_map/ppermute | solution.py:408
  61.4 0.9 %collective-permute-start.7 = (bf16[512,384]{1,0:T(8,128)(2,1)}, bf16[512,384]{1,0:T(8,128)(2,1)S(1)}, u32[]{:S(2)}, u32[]{:S(2)}) collective-permute-start(bf16[512,384]{1,0:T(8,128)(2,1)} %attention.1.own), channel_id=1, source_target_pairs={{0,2},{2,4},{4,6},{6,0},{1,3},{3,5},{5,7},{7,1},{8,10},{10,12},{12... | collective-permute-start | bytes 1179656 | tf_op jit(solution)/shard_map/ppermute | solution.py:408
  62.3 8.8 %collective-permute-done.8.left = bf16[512,384]{1,0:T(8,128)(2,1)S(1)} collective-permute-done((bf16[512,384]{1,0:T(8,128)(2,1)}, bf16[512,384]{1,0:T(8,128)(2,1)S(1)}, u32[]{:S(2)}, u32[]{:S(2)}) %collective-permute-start.8) | collective-permute-done | bytes 393248 | tf_op jit(solution)/shard_map/ppermute | solution.py:408
  71.1 2.4 %collective-permute-start.10 = (bf16[256,384]{1,0:T(8,128)(2,1)S(1)}, bf16[256,384]{1,0:T(8,128)(2,1)S(1)}, u32[]{:S(2)}, u32[]{:S(2)}) collective-permute-start(bf16[256,384]{1,0:T(8,128)(2,1)S(1)} %slice.9), channel_id=1, source_target_pairs={{0,6},{2,0},{4,2},{6,4},{1,7},{3,1},{5,3},{7,5},{8,14},{10,8},{12,... | collective-permute-start | bytes 589832 | tf_op jit(solution)/shard_map/ppermute | solution.py:408
  73.6 0.0 collective-permute-done.7.right
  73.6 0.1 collective-permute-start.9
  73.7 0.0 copy-start.1
  73.7 1.0 %copy-done.1 = bf16[512,384]{1,0:T(8,128)(2,1)S(1)} copy-done((bf16[512,384]{1,0:T(8,128)(2,1)S(1)}, bf16[512,384]{1,0:T(8,128)(2,1)}, u32[]{:S(2)}) %copy-start.1) | copy-done | bytes 393240
  74.7 1.3 %near_projection.1.total = f32[512,640]{1,0:T(8,128)S(1)} custom-call(bf16[512,640]{1,0:T(8,128)(2,1)S(1)} %constant_dynamic-slice_fusion.lat, bf16[512,384]{1,0:T(8,128)(2,1)S(1)} %copy-done.1, bf16[512,384]{1,0:T(8,128)(2,1)S(1)} %collective-permute-done.7.right, bf16[512,384]{1,0:T(8,128)(2,1)S(1)} %collective-permute-done.8.left, ...), custom_call_target="tpu_custom_call" | custom-call | flops 754974720 | bytes 3309568 | tf_op jit(solution)/shard_map/near_projection/pallas_call | solution.py:210
  76.0 0.9 %collective-permute-done.10.second = bf16[256,384]{1,0:T(8,128)(2,1)S(1)} collective-permute-done((bf16[256,384]{1,0:T(8,128)(2,1)S(1)}, bf16[256,384]{1,0:T(8,128)(2,1)S(1)}, u32[]{:S(2)}, u32[]{:S(2)}) %collective-permute-start.10) | collective-permute-done | bytes 196640 | tf_op jit(solution)/shard_map/ppermute | solution.py:408
  76.9 3.7 %collective-permute-done.9.first = bf16[256,384]{1,0:T(8,128)(2,1)S(1)} collective-permute-done((bf16[256,384]{1,0:T(8,128)(2,1)S(1)}, bf16[256,384]{1,0:T(8,128)(2,1)S(1)}, u32[]{:S(2)}, u32[]{:S(2)}) %collective-permute-start.9) | collective-permute-done | bytes 196640 | tf_op jit(solution)/shard_map/ppermute | solution.py:408
  80.6 1.4 %far_projection.1 = bf16[512,640]{1,0:T(8,128)(2,1)} custom-call(f32[512,640]{1,0:T(8,128)S(1)} %near_projection.1.total, bf16[256,384]{1,0:T(8,128)(2,1)S(1)} %collective-permute-done.9.first, bf16[256,384]{1,0:T(8,128)(2,1)S(1)} %collective-permute-done.10.second, bf16[384,640]{1,0:T(8,128)(2,1)S(1)} %collective-permute-done.6.w), custom_call_target="tpu_custom_call" | custom-call | flops 251658240 | bytes 2195456 | tf_op jit(solution)/shard_map/far_projection/pallas_call | solution.py:210
  (3 shorter events, 0.1 us)
Async XLA Ops:
  4.7 13.3 %all-to-all-start = ((bf16[8,72,384]{2,1,0:T(8,128)(2,1)}), bf16[8,72,384]{2,1,0:T(8,128)(2,1)S(1)}, u32[]{:S(2)}, u32[]{:S(2)}) async-start(bf16[8,72,384]{2,1,0:T(8,128)(2,1)} %tail_projection.1.payload.tail_rows), calls=%async_computation | async-start | bytes 884736 | tf_op jit(solution)/shard_map/all_to_all | solution.py:423
  9.2 3.6 %copy-start.4 = (bf16[384,2560]{1,0:T(8,128)(2,1)S(1)}, bf16[384,2560]{1,0:T(8,128)(2,1)}, u32[]{:S(2)}) copy-start(bf16[384,2560]{1,0:T(8,128)(2,1)} %param.8) | copy-start | bytes 5898244
  18.2 5.2 %collective-permute-start = (bf16[72,384]{1,0:T(8,128)(2,1)S(1)}, bf16[72,384]{1,0:T(8,128)(2,1)S(1)}, u32[]{:S(2)}, u32[]{:S(2)}) collective-permute-start(bf16[72,384]{1,0:T(8,128)(2,1)S(1)} %get-tuple-element.37), channel_id=1, source_target_pairs={{0,32},{32,0},{64,96},{96,64},{128,160},{160,128},{192,224},{224,1... | collective-permute-start | bytes 165896 | tf_op jit(solution)/shard_map/ppermute | solution.py:412
  19.1 35.0 %collective-permute-start.4 = (bf16[384,640]{1,0:T(8,128)(2,1)}, bf16[384,640]{1,0:T(8,128)(2,1)S(1)}, u32[]{:S(2)}, u32[]{:S(2)}) collective-permute-start(bf16[384,640]{1,0:T(8,128)(2,1)} %get-tuple-element.61), channel_id=1, source_target_pairs={{0,2},{2,4},{4,6},{6,0},{1,3},{3,5},{5,7},{7,1},{8,10},{10,12},{12... | collective-permute-start | bytes 1474568 | tf_op jit(solution)/shard_map/ppermute | solution.py:408
  19.9 34.2 %collective-permute-start.5 = (bf16[384,640]{1,0:T(8,128)(2,1)}, bf16[384,640]{1,0:T(8,128)(2,1)S(1)}, u32[]{:S(2)}, u32[]{:S(2)}) collective-permute-start(bf16[384,640]{1,0:T(8,128)(2,1)} %get-tuple-element.60), channel_id=1, source_target_pairs={{0,6},{2,0},{4,2},{6,4},{1,7},{3,1},{5,3},{7,5},{8,14},{10,8},{12,... | collective-permute-start | bytes 1474568 | tf_op jit(solution)/shard_map/ppermute | solution.py:408
  22.3 31.8 %collective-permute-start.6 = (bf16[384,640]{1,0:T(8,128)(2,1)}, bf16[384,640]{1,0:T(8,128)(2,1)S(1)}, u32[]{:S(2)}, u32[]{:S(2)}) collective-permute-start(bf16[384,640]{1,0:T(8,128)(2,1)} %get-tuple-element.59), channel_id=1, source_target_pairs={{0,4},{2,6},{4,0},{6,2},{1,5},{3,7},{5,1},{7,3},{8,12},{10,14},{12... | collective-permute-start | bytes 1474568 | tf_op jit(solution)/shard_map/ppermute | solution.py:408
  23.5 5.5 %collective-permute-start.1 = (bf16[72,384]{1,0:T(8,128)(2,1)S(1)}, bf16[72,384]{1,0:T(8,128)(2,1)S(1)}, u32[]{:S(2)}, u32[]{:S(2)}) collective-permute-start(bf16[72,384]{1,0:T(8,128)(2,1)S(1)} %through_1.1), channel_id=1, source_target_pairs={{0,64},{32,96},{64,0},{96,32},{128,192},{160,224},{192,128},{224,1... | collective-permute-start | bytes 165896 | tf_op jit(solution)/shard_map/ppermute | solution.py:412
  29.1 20.2 %copy-start.5 = (s32[1,1024]{1,0:T(1,128)S(1)}, s32[1,1024]{1,0:T(1,128)}, u32[]{:S(2)}) copy-start(s32[1,1024]{1,0:T(1,128)} %param.10) | copy-start | bytes 12292
  29.1 11.7 %collective-permute-start.2 = (bf16[64,384]{1,0:T(8,128)(2,1)S(1)}, bf16[64,384]{1,0:T(8,128)(2,1)S(1)}, u32[]{:S(2)}, u32[]{:S(2)}) collective-permute-start(bf16[64,384]{1,0:T(8,128)(2,1)S(1)} %through_3.1), channel_id=1, source_target_pairs={{0,128},{32,160},{64,192},{96,224},{128,0},{160,32},{192,64},{224,... | collective-permute-start | bytes 147464 | tf_op jit(solution)/shard_map/ppermute | solution.py:412
  41.7 12.5 %all-to-all-start.1 = ((bf16[8,64,384]{2,1,0:T(8,128)(2,1)}), bf16[8,64,384]{2,1,0:T(8,128)(2,1)}, u32[]{:S(2)}, u32[]{:S(2)}) async-start(bf16[8,64,384]{2,1,0:T(8,128)(2,1)} %section_memory.1), calls=%async_computation.1 | async-start | bytes 786432 | tf_op jit(solution)/shard_map/all_to_all | solution.py:458
  45.9 9.9 %collective-permute-start.3 = (bf16[64,384]{1,0:T(8,128)(2,1)}, bf16[64,384]{1,0:T(8,128)(2,1)S(1)}, u32[]{:S(2)}, u32[]{:S(2)}) collective-permute-start(bf16[64,384]{1,0:T(8,128)(2,1)} %get-tuple-element.51), channel_id=1, source_target_pairs={{0,1},{1,0},{2,3},{3,2},{4,5},{5,4},{6,7},{7,6},{8,9},{9,8},{10,11... | collective-permute-start | bytes 147464 | tf_op jit(solution)/shard_map/ppermute | solution.py:412
  49.4 6.4 %copy-start = (bf16[256,384]{1,0:T(8,128)(2,1)S(1)}, bf16[256,384]{1,0:T(8,128)(2,1)}, u32[]{:S(2)}) copy-start(bf16[256,384]{1,0:T(8,128)(2,1)} %head_values.1.values) | copy-start | bytes 589828
  49.4 6.5 %copy-start.2 = (bf16[256,384]{1,0:T(8,128)(2,1)S(1)}, bf16[256,384]{1,0:T(8,128)(2,1)}, u32[]{:S(2)}) copy-start(bf16[256,384]{1,0:T(8,128)(2,1)} %get-tuple-element.50.head_keys) | copy-start | bytes 589828
  49.4 6.5 %copy-start.3 = (s32[1,17]{1,0:T(1,128)S(1)}, s32[1,17]{1,0:T(1,128)}, u32[]{:S(2)}) copy-start(s32[1,17]{1,0:T(1,128)} %opened.1) | copy-start | bytes 208
  60.0 11.1 %collective-permute-start.8 = (bf16[512,384]{1,0:T(8,128)(2,1)}, bf16[512,384]{1,0:T(8,128)(2,1)S(1)}, u32[]{:S(2)}, u32[]{:S(2)}) collective-permute-start(bf16[512,384]{1,0:T(8,128)(2,1)} %attention.1.own), channel_id=1, source_target_pairs={{0,6},{2,0},{4,2},{6,4},{1,7},{3,1},{5,3},{7,5},{8,14},{10,8},{12,... | collective-permute-start | bytes 1179656 | tf_op jit(solution)/shard_map/ppermute | solution.py:408
  61.4 12.2 %collective-permute-start.7 = (bf16[512,384]{1,0:T(8,128)(2,1)}, bf16[512,384]{1,0:T(8,128)(2,1)S(1)}, u32[]{:S(2)}, u32[]{:S(2)}) collective-permute-start(bf16[512,384]{1,0:T(8,128)(2,1)} %attention.1.own), channel_id=1, source_target_pairs={{0,2},{2,4},{4,6},{6,0},{1,3},{3,5},{5,7},{7,1},{8,10},{10,12},{12... | collective-permute-start | bytes 1179656 | tf_op jit(solution)/shard_map/ppermute | solution.py:408
  71.1 5.7 %collective-permute-start.10 = (bf16[256,384]{1,0:T(8,128)(2,1)S(1)}, bf16[256,384]{1,0:T(8,128)(2,1)S(1)}, u32[]{:S(2)}, u32[]{:S(2)}) collective-permute-start(bf16[256,384]{1,0:T(8,128)(2,1)S(1)} %slice.9), channel_id=1, source_target_pairs={{0,6},{2,0},{4,2},{6,4},{1,7},{3,1},{5,3},{7,5},{8,14},{10,8},{12,... | collective-permute-start | bytes 589832 | tf_op jit(solution)/shard_map/ppermute | solution.py:408
  73.6 7.0 %collective-permute-start.9 = (bf16[256,384]{1,0:T(8,128)(2,1)S(1)}, bf16[256,384]{1,0:T(8,128)(2,1)S(1)}, u32[]{:S(2)}, u32[]{:S(2)}) collective-permute-start(bf16[256,384]{1,0:T(8,128)(2,1)S(1)} %slice.8), channel_id=1, source_target_pairs={{0,2},{2,4},{4,6},{6,0},{1,3},{3,5},{5,7},{7,1},{8,10},{10,12},{12... | collective-permute-start | bytes 589832 | tf_op jit(solution)/shard_map/ppermute | solution.py:408
  73.7 1.0 %copy-start.1 = (bf16[512,384]{1,0:T(8,128)(2,1)S(1)}, bf16[512,384]{1,0:T(8,128)(2,1)}, u32[]{:S(2)}) copy-start(bf16[512,384]{1,0:T(8,128)(2,1)} %attention.1.own) | copy-start | bytes 1179652

commit v5 on v4

--- a/solution.py
+++ b/solution.py
@@ -24,7 +24,6 @@
 REST_LIMIT = 60 * 1024 * 1024
 ATTEND_LIMIT = 53 * 1024 * 1024
 LIMIT = 32 * 1024 * 1024
-BLOCK = 192
 SPAN = ("z", "y", "core")
 PLANE = ("y", "core", "phase")
 
@@ -127,7 +126,7 @@
     return pl.pallas_call(
         kernel,
         out_shape=outs,
-        in_specs=[pl.BlockSpec(memory_space=pltpu.SMEM), hbm, hbm] + [vmem] * (len(args) - 3),
+        in_specs=[pl.BlockSpec(memory_space=pltpu.SMEM)] + [hbm] * (len(args) - 1),
         out_specs=vmem if single else tuple(vmem for _ in outs),
         scratch_shapes=scratch,
         cost_estimate=pl.CostEstimate(flops=flops, bytes_accessed=nbytes, transcendentals=0),
@@ -152,16 +151,27 @@
     out[...] = head_project(2, lat, w, rows, part, sems).astype(BF16)
 
 
-def head_keys_kernel(phase, lat, w, values, payload, out, edge, rows, part, sems):
+def head_keys_kernel(phase, lat, w, values, payload, out, edge, rows, part, first_values, last, sems):
+    copies = [
+        pltpu.make_async_copy(values.at[pl.ds(0, PART)], first_values, sems.at[2]),
+        pltpu.make_async_copy(payload.at[PARTS - 1, pl.ds(0, 2 * PART)], last, sems.at[3]),
+    ]
+    for copy in copies:
+        copy.start()
     keys = normed(head_project(1, lat, w, rows, part, sems))
     out[...] = keys
+    for copy in copies:
+        copy.wait()
     first = phase[0] == 0
-    edge[:PART] = jnp.where(first, payload[PARTS - 1, :PART], keys[:PART])
-    edge[PART:] = jnp.where(first, payload[PARTS - 1, PART : 2 * PART], values[:PART])
+    edge[:PART] = jnp.where(first, last[:PART], keys[:PART])
+    edge[PART:] = jnp.where(first, last[PART:], first_values[...])
 
 
 def heads(kernel, outs, name, after, latents, w3, *more):
     depth = latents.shape[1]
+    scratch = [pltpu.VMEM((MEM, depth), BF16), pltpu.VMEM((depth, COLS), BF16)]
+    if more:
+        scratch += [pltpu.VMEM((PART, COLS), BF16), pltpu.VMEM((2 * PART, COLS), BF16)]
     return call_on_hbm(
         kernel,
         outs,
@@ -169,7 +179,7 @@
         2 * MEM * depth * COLS,
         3300000,
         (after, latents, w3, *more),
-        [pltpu.VMEM((MEM, depth), BF16), pltpu.VMEM((depth, COLS), BF16), pltpu.SemaphoreType.DMA((2,))],
+        scratch + [pltpu.SemaphoreType.DMA((4,))],
     )
 
 
@@ -219,25 +229,6 @@
     )(*args)
 
 
-def window_part(frame_row, frame_column, top, bottom, qx, kx, vx):
-    ones = jnp.ones((BLOCK, HD), BF16)
-    window_a = lax.broadcasted_iota(jnp.int32, (BLOCK, BLOCK), 0) // WIN
-    window_b = lax.broadcasted_iota(jnp.int32, (BLOCK, BLOCK), 1) // WIN
-    for b in range(EXT // BLOCK):
-        rows = slice(b * BLOCK, (b + 1) * BLOCK)
-        allowed = (window_a == window_b) & (frame_row[b] <= frame_column[rows, :1])
-        low, high = max(b * BLOCK, HALF_WIN), min((b + 1) * BLOCK, HALF_WIN + ROWS)
-        for h in range(HEADS):
-            c = slice(h * HD, (h + 1) * HD)
-            score = lax.dot_general(qx[rows, c], kx[rows, c], (((1,), (1,)), ((), ())), preferred_element_type=F32)
-            weight = jnp.where(allowed, jnp.exp2(score * SCALE2), 0.0).astype(BF16)
-            both = jnp.concatenate([vx[rows, c], ones], axis=1)
-            result = jnp.dot(weight, both, preferred_element_type=F32)
-            cut = result[low - b * BLOCK : high - b * BLOCK]
-            top[low - HALF_WIN : high - HALF_WIN, c] = cut[:, :HD]
-            bottom[low - HALF_WIN : high - HALF_WIN, c] = cut[:, HD:]
-
-
 def coefficients(rate):
     return 1.0 - rate, jnp.sqrt(1.0 - rate * rate)
 
@@ -305,95 +296,118 @@
 
 
 def attend_kernel(
-    phase, opened, q, head_keys, head_values, tail_rows, halo, rows_in, columns_in, memory_in,
+    r, phase, opened, q, head_keys, head_values, tail_rows, halo, rows_in, columns_in, memory_in,
     out, top, bottom, qx, kx, vx, tail, frame_row, frame_column, memory, sems,
 ):
-    own, upper = pl.ds(HALF_WIN, ROWS), pl.ds(HALF_WIN + ROWS, HALF_WIN)
-    lower, head = pl.ds(0, HALF_WIN), pl.ds(HALF_WIN, MEM)
+    half = ROWS // 2
+    base = r * half
+    low, high = base, base + half + WIN
     first, second = pl.ds(0, PART), pl.ds(PART, PART)
+    seen = pl.ds(low, high - low)
+    used = 1 if r == 0 else PARTS
     pairs = [
-        (tail_rows, tail),
-        (q, qx.at[own]),
-        (head_keys, kx.at[head]),
-        (head_values, vx.at[head]),
-        (halo.at[first], kx.at[lower]),
-        (halo.at[first], kx.at[upper]),
-        (halo.at[second], vx.at[lower]),
-        (halo.at[second], vx.at[upper]),
+        (q.at[pl.ds(base, half)], qx.at[pl.ds(HALF_WIN + base, half)]),
+        (memory_in, memory),
+        (tail_rows.at[pl.ds(0, used)], tail.at[pl.ds(0, used)]),
         (rows_in, frame_row),
-        (columns_in, frame_column),
-        (memory_in, memory),
+        (columns_in.at[seen], frame_column.at[seen]),
+    ]
+    if r == 0:
+        edge, head, source = pl.ds(0, HALF_WIN), pl.ds(HALF_WIN, MEM), pl.ds(0, MEM)
+    else:
+        edge, head, source = pl.ds(HALF_WIN + ROWS, HALF_WIN), pl.ds(low, HALF_WIN), pl.ds(MEM - HALF_WIN, HALF_WIN)
+    pairs += [
+        (head_keys.at[source], kx.at[head]),
+        (head_values.at[source], vx.at[head]),
+        (halo.at[first], kx.at[edge]),
+        (halo.at[second], vx.at[edge]),
     ]
     copies = [pltpu.make_async_copy(a, b, sems.at[i]) for i, (a, b) in enumerate(pairs)]
     for copy in copies:
         copy.start()
-    edge = jnp.zeros((HALF_WIN, COLS), BF16)
-    qx[:HALF_WIN] = edge
-    qx[HALF_WIN + ROWS :] = edge
-    copies[0].wait()
-    for d in range(PARTS):
-        at = HALF_WIN + MEM + d * PART
-        kx[at : at + PART] = tail[d, :PART]
-        vx[at : at + PART] = tail[d, PART : 2 * PART]
-    for copy in copies[1:-1]:
-        copy.wait()
-    window_part(frame_row, frame_column, top, bottom, qx, kx, vx)
+    blank = jnp.zeros((HALF_WIN, COLS), BF16)
+    qx[low : low + HALF_WIN] = blank
+    qx[high - HALF_WIN : high] = blank
     start = phase[0] * (ROWS // WIN)
-    window = (lax.broadcasted_iota(jnp.int32, (ROWS, HD), 0) + HALF_WIN) // WIN
-    is_open = jnp.zeros((ROWS, HD), F32)
-    for w in range(ROWS // WIN + 1):
+    window = (lax.broadcasted_iota(jnp.int32, (half, HD), 0) + base + HALF_WIN) // WIN
+    is_open = jnp.zeros((half, HD), F32)
+    for w in range(low // WIN, high // WIN):
         flag = jnp.where(opened[0, start + w] == 1, 1.0, 0.0)
         is_open = jnp.where(window == w, flag, is_open)
     ones = jnp.ones((MEM, HD), BF16)
-    copies[-1].wait()
+    copies[0].wait()
+    copies[1].wait()
     for h in range(HEADS):
         c = slice(h * HD, (h + 1) * HD)
         keys = memory[:, :PART, c].reshape(MEM, HD)
         values = memory[:, PART:, c].reshape(MEM, HD)
-        score = lax.dot_general(
-            qx[HALF_WIN : HALF_WIN + ROWS, c], keys, (((1,), (1,)), ((), ())), preferred_element_type=F32
-        )
+        own = qx[HALF_WIN + base : HALF_WIN + base + half, c]
+        score = lax.dot_general(own, keys, (((1,), (1,)), ((), ())), preferred_element_type=F32)
         weight = jnp.exp2(score * SCALE2).astype(BF16)
         result = jnp.dot(weight, jnp.concatenate([values, ones], axis=1), preferred_element_type=F32)
-        above = top[:, c] + is_open * result[:, :HD]
-        below = bottom[:, c] + is_open * result[:, HD:]
-        out[:, c] = (above / below).astype(BF16)
-
-
-def attention(phase, opened, *operands):
+        top[:, c] = is_open * result[:, :HD]
+        bottom[:, c] = is_open * result[:, HD:]
+    for copy in copies[2:]:
+        copy.wait()
+    for d in range(used):
+        at = HALF_WIN + MEM + d * PART
+        kx[at : at + PART] = tail[d, :PART]
+        vx[at : at + PART] = tail[d, PART : 2 * PART]
+    for begin, size in ((low, half), (low + half, WIN)):
+        rows = slice(begin, begin + size)
+        window_a = lax.broadcasted_iota(jnp.int32, (size, size), 0) // WIN
+        window_b = lax.broadcasted_iota(jnp.int32, (size, size), 1) // WIN
+        allowed = (window_a == window_b) & (frame_row[:, rows] <= frame_column[rows, :1])
+        begin_own, end_own = max(begin, low + HALF_WIN), min(begin + size, high - HALF_WIN)
+        to = slice(begin_own - HALF_WIN - base, end_own - HALF_WIN - base)
+        for h in range(HEADS):
+            c = slice(h * HD, (h + 1) * HD)
+            score = lax.dot_general(qx[rows, c], kx[rows, c], (((1,), (1,)), ((), ())), preferred_element_type=F32)
+            weight = jnp.where(allowed, jnp.exp2(score * SCALE2), 0.0).astype(BF16)
+            both = jnp.concatenate([vx[rows, c], jnp.ones((size, HD), BF16)], axis=1)
+            cut = jnp.dot(weight, both, preferred_element_type=F32)[begin_own - begin : end_own - begin]
+            above, below = top[to, c] + cut[:, :HD], bottom[to, c] + cut[:, HD:]
+            out[to, c] = (above / below).astype(BF16)
+
+
+def attention(r, phase, opened, *operands):
     smem = pl.BlockSpec(memory_space=pltpu.SMEM)
     hbm = pl.BlockSpec(memory_space=pl.ANY)
+    half = ROWS // 2
     extended = pltpu.VMEM((EXT, COLS), BF16)
     return pl.pallas_call(
-        attend_kernel,
-        out_shape=shape((ROWS, COLS), BF16),
+        functools.partial(attend_kernel, r),
+        out_shape=shape((half, COLS), BF16),
         in_specs=[smem, smem] + [hbm] * len(operands),
         out_specs=pl.BlockSpec(memory_space=pltpu.VMEM),
         scratch_shapes=[
-            pltpu.VMEM((ROWS, COLS), F32),
-            pltpu.VMEM((ROWS, COLS), F32),
+            pltpu.VMEM((half, COLS), F32),
+            pltpu.VMEM((half, COLS), F32),
             extended,
             extended,
             extended,
             pltpu.VMEM((PARTS, PAYLOAD, COLS), BF16),
-            pltpu.VMEM((EXT // BLOCK, 1, BLOCK), jnp.int32),
+            pltpu.VMEM((1, EXT), jnp.int32),
             pltpu.VMEM((EXT, HD), jnp.int32),
             pltpu.VMEM((PARTS, 2 * PART, COLS), BF16),
-            pltpu.SemaphoreType.DMA((11,)),
+            pltpu.SemaphoreType.DMA((9,)),
         ],
         cost_estimate=pl.CostEstimate(
-            flops=4 * ROWS * (MEM + BLOCK) * COLS * 2, bytes_accessed=3000000, transcendentals=0
+            flops=2 * ROWS * (MEM + half) * COLS * 2, bytes_accessed=1500000, transcendentals=0
         ),
         compiler_params=pltpu.CompilerParams(vmem_limit_bytes=ATTEND_LIMIT),
-        name="attention",
+        name=f"attention_{r}",
     )(phase, opened, *operands)
 
 
-def near_kernel(lat, own, right, left, w_own, w_right, w_left, total):
-    sums = lat[...].astype(F32)
-    for a, w in ((own, w_own), (right, w_right), (left, w_left)):
-        sums = sums + jnp.dot(a[...], w[...], preferred_element_type=F32)
-    total[...] = sums
+def near_kernel(lat, own_0, own_1, right_0, right_1, left_0, left_1, w_own, w_right, w_left, total):
+    half = ROWS // 2
+    for r, parts in enumerate(((own_0, right_0, left_0), (own_1, right_1, left_1))):
+        at = slice(r * half, (r + 1) * half)
+        sums = lat[at].astype(F32)
+        for a, w in zip(parts, (w_own, w_right, w_left)):
+            sums = sums + jnp.dot(a[...], w[...], preferred_element_type=F32)
+        total[at] = sums
 
 
 def far_kernel(total, first, second, w, out):
@@ -427,26 +441,27 @@
     offsets = (0, 1, -1, 2)
     sends = [lax.dynamic_slice_in_dim(w_out, ((mp + by) & 3) * share, share, 1) for by in offsets]
     weights = [moved(piece, "mp", by) if by else piece for by, piece in zip(offsets, sends)]
+    arrived, _ = lax.optimization_barrier((arrived, sends))
     half_keys = shape((MEM, COLS), BF16)
-    after, payload = lax.optimization_barrier((z_ref, payload))
-    head_values = heads(head_values_kernel, half_keys, "head_values", after, latents, w3)
-    arrived, _, head_values = lax.optimization_barrier((arrived, sends, head_values))
 
     wide = shape((2 * PART + 8, COLS), F32)
     packed = shape((PAYLOAD, COLS), BF16)
     plain = shape((2 * PART, COLS), BF16)
     plain_all = shape((PARTS, 2 * PART, COLS), BF16)
     own, sent = vmem_call(plane_kernel, (wide, packed), "plane_total", 1000000, (arrived,))
+    latents, sent = lax.optimization_barrier((latents, sent))
     got_1 = swapped(sent, "z", 1)
+    own_columns = lax.dynamic_slice_in_dim(latents, mp * share, share, 1)
+    got_1, own_columns = lax.optimization_barrier((got_1, own_columns))
     sent = vmem_call(first_kernel, packed, "through_1", 100000, (z_ref, own, got_1), smem=1)
-    latents, sent = lax.optimization_barrier((latents, sent))
+    after, sent = lax.optimization_barrier((z_ref, sent))
     got_2 = swapped(sent, "z", 2)
-    own_columns = lax.dynamic_slice_in_dim(latents, mp * share, share, 1)
-    got_2, own_columns = lax.optimization_barrier((got_2, own_columns))
+    head_values = heads(head_values_kernel, half_keys, "head_values", after, latents, w3)
+    got_2, head_values = lax.optimization_barrier((got_2, head_values))
 
     sent = vmem_call(next_kernel, plain, "through_3", 100000, (z_ref, own, got_1, got_2), smem=1)
     after, sent = lax.optimization_barrier((phase_ref, sent))
-    got_4 = swapped(sent, "z", 4)
+    got_4 = swapped(sent, "z", 7)
     head_keys, edge = heads(
         head_keys_kernel, (half_keys, plain), "head_keys", after, latents, w3, head_values, payload
     )
@@ -459,21 +474,26 @@
     halo = swapped(edge, "phase", 1)
     frames_pad = jnp.pad(frame_ids[0], (HALF_WIN, HALF_WIN), constant_values=outside_frame)
     frames = lax.dynamic_slice_in_dim(frames_pad, phase * ROWS, EXT)
-    frame_row = frames.reshape(EXT // BLOCK, 1, BLOCK)
+    frame_row = frames.reshape(1, EXT)
     frame_column = jnp.broadcast_to(frames[:, None], (EXT, HD))
     queries = query(after, latents, w3)
     memory, weights = lax.optimization_barrier((memory, weights))
-    attended = attention(
-        phase_ref, memory_mask, queries, head_keys, head_values, payload, halo, frame_row, frame_column, memory
-    )
-    right, left = moved(attended, "mp", 1), moved(attended, "mp", -1)
-    far_1, far_2 = moved(right[: ROWS // 2], "mp", 1), moved(left[ROWS // 2 :], "mp", -1)
+    halves = [
+        attention(
+            r, phase_ref, memory_mask, queries, head_keys, head_values, payload, halo, frame_row, frame_column, memory
+        )
+        for r in range(2)
+    ]
+    right = [moved(piece, "mp", 1) for piece in halves]
+    left = [moved(piece, "mp", -1) for piece in halves]
+    right[1], left[1] = lax.optimization_barrier((right[1], left[1]))
+    far_1, far_2 = moved(right[0], "mp", 1), moved(left[1], "mp", -1)
     total = vmem_call(
         near_kernel,
         shape((ROWS, share), F32),
         "near_projection",
         6 * ROWS * COLS * share,
-        (own_columns, attended, right, left, *weights[:3]),
+        (own_columns, *halves, *right, *left, *weights[:3]),
     )
     return vmem_call(
         far_kernel,

time: 82.9 us -> 78 us (0.941)
  waiting for transfers between devices: 20.1 us -> 11.3 us
  starting transfers between devices: 32.4 us -> 35.2 us
    ppermute x7 -> x9, waiting for transfers between devices: 13.4 us -> 6.22 us  [moved(): return lax.ppermute(x, axis, [(i, (i + by) % size) for i in range(size)])]
    ppermute x7 -> x9, starting transfers between devices: 9.15 us -> 15.1 us  [moved(): return lax.ppermute(x, axis, [(i, (i + by) % size) for i in range(size)])]
    all_to_all x1, waiting for transfers between devices: 4.05 us -> 1.17 us  [local(): arrived = lax.all_to_all(payload, PLANE, 0, 0, tiled=True)]
    ppermute x4, starting transfers between devices: 14.7 us -> 12.1 us  [swapped(): lax.ppermute(x, axis, [(i, i ^ bit) for i in range(lax.axis_size(axis))])]
    dynamic_slice x1, local copies, waits for them, and re-layouts: 1.17 us -> 2.63 us  [local(): lax.dynamic_slice_in_dim(w_out, (mp + by & 3) * share, share, 1)]
    ppermute x4, waiting for transfers between devices: 2.52 us -> 3.95 us  [swapped(): lax.ppermute(x, axis, [(i, i ^ bit) for i in range(lax.axis_size(axis))])]
    pallas_call x1 -> x2, Pallas kernels: 4.1 us -> 5.5 us  [attention(): pl.pallas_call(functools.partial(attend_kernel, r), out_shape=shape((half...]
    pallas_call x3, Pallas kernels: 12.9 us -> 11.7 us  [call_on_hbm(): pl.pallas_call(kernel, out_shape=outs, in_specs=[pl.BlockSpec(memory_spac...]
  transfers between devices with their start and end apart: 13 -> 15, of which waited for: 7 -> 5; matrix products, arithmetic and copies ran while one was open for 3% -> 5% of each run, Pallas kernels for 19% -> 22%
where the time goes in v5:
time: 78 us; the launch traced here: 76.6 us
  starting transfers between devices  35.2 us (45%)
  Pallas kernels  25.8 us (33%)
  waiting for transfers between devices  11.3 us (14%)
  local copies, waits for them, and re-layouts  4.01 us (5%)
    ppermute x9, starting transfers between devices, moved(): return lax.ppermute(x, axis, [(i, (i + by) % size) for i in range(size)])  15.1 us
    ppermute x4, starting transfers between devices, swapped(): lax.ppermute(x, axis, [(i, i ^ bit) for i in range(lax.axis_size(axis))])  12.1 us
    pallas_call x3, Pallas kernels, call_on_hbm(): pl.pallas_call(kernel, out_shape=outs, in_specs=[pl.BlockSpec(memory_spac...  11.7 us
    ppermute x9, waiting for transfers between devices, moved(): return lax.ppermute(x, axis, [(i, (i + by) % size) for i in range(size)])  6.22 us
    pallas_call x2, Pallas kernels, attention(): pl.pallas_call(functools.partial(attend_kernel, r), out_shape=shape((half...  5.5 us
    pallas_call x1, Pallas kernels, tails(): pl.pallas_call(tail_kernel, out_shape=shape((PARTS, PAYLOAD, COLS), BF16)...  4.68 us
    all_to_all x1, starting transfers between devices, local(): arrived = lax.all_to_all(payload, PLANE, 0, 0, tiled=True)  4.48 us
    ppermute x4, waiting for transfers between devices, swapped(): lax.ppermute(x, axis, [(i, i ^ bit) for i in range(lax.axis_size(axis))])  3.95 us
  transfers between devices with their start and end apart: 15, of which 5 were waited for; matrix products, arithmetic and copies ran while one was open for 5% of the time, Pallas kernels for 22%

profile of v5, /device:TPU:32, one launch (start us, length us, event | category | flops | bytes accessed | tf_op | source)
XLA Modules:
  0.0 76.6 jit_solution(2453759187050744268)
XLA Ops:
  0.0 4.7 %tail_projection.1.payload.tail_rows = bf16[8,72,384]{2,1,0:T(8,128)(2,1)} custom-call(s32[1]{0:T(128)} %bitcast.phase, f32[2,3]{1,0:T(2,128)} %bitcast.10, bf16[512,2560]{1,0:T(8,128)(2,1)} %lat.4, bf16[3,2560,384]{2,1,0:T(8,128)(2,1)} %bitcast.5), custom_call_target="tpu_custom_call" | custom-call | flops 1006632960 | bytes 5500000 | tf_op jit(solution)/shard_map/tail_projection/pallas_call | solution.py:105
  4.7 4.5 %all-to-all-start = ((bf16[8,72,384]{2,1,0:T(8,128)(2,1)}), bf16[8,72,384]{2,1,0:T(8,128)(2,1)S(1)}, u32[]{:S(2)}, u32[]{:S(2)}) async-start(bf16[8,72,384]{2,1,0:T(8,128)(2,1)} %tail_projection.1.payload.tail_rows), calls=%async_computation | async-start | bytes 884736 | tf_op jit(solution)/shard_map/all_to_all | solution.py:437
  9.2 2.6 %constant_dynamic-slice_fusion.1 = (bf16[384,640]{1,0:T(8,128)(2,1)}, bf16[384,640]{1,0:T(8,128)(2,1)}, bf16[384,640]{1,0:T(8,128)(2,1)}, bf16[384,640]{1,0:T(8,128)(2,1)S(1)}) fusion(bf16[384,2560]{1,0:T(8,128)(2,1)} %param.8, s32[]{:T(128)S(6)} %select_n.21, s32[]{:T(128)S(6)} %select_n.20, s32[]{:T(128)S(6)} %select_n.19, s32[]{:T(128)S(6)} %select_n.18), kind=kLoop, calls=%fused_computation.2 | loop fusion | bytes 3932176 | tf_op jit(solution)/shard_map/dynamic_slice | solution.py:442
  11.8 1.5 %collective-permute-start.4 = (bf16[384,640]{1,0:T(8,128)(2,1)}, bf16[384,640]{1,0:T(8,128)(2,1)S(1)}, u32[]{:S(2)}, u32[]{:S(2)}) collective-permute-start(bf16[384,640]{1,0:T(8,128)(2,1)} %get-tuple-element.67), channel_id=1, source_target_pairs={{0,2},{2,4},{4,6},{6,0},{1,3},{3,5},{5,7},{7,1},{8,10},{10,12},{12... | collective-permute-start | bytes 1474568 | tf_op jit(solution)/shard_map/ppermute | solution.py:422
  13.3 1.7 %collective-permute-start.5 = (bf16[384,640]{1,0:T(8,128)(2,1)}, bf16[384,640]{1,0:T(8,128)(2,1)S(1)}, u32[]{:S(2)}, u32[]{:S(2)}) collective-permute-start(bf16[384,640]{1,0:T(8,128)(2,1)} %get-tuple-element.66), channel_id=1, source_target_pairs={{0,6},{2,0},{4,2},{6,4},{1,7},{3,1},{5,3},{7,5},{8,14},{10,8},{12,... | collective-permute-start | bytes 1474568 | tf_op jit(solution)/shard_map/ppermute | solution.py:422
  15.0 1.8 %collective-permute-start.6 = (bf16[384,640]{1,0:T(8,128)(2,1)}, bf16[384,640]{1,0:T(8,128)(2,1)S(1)}, u32[]{:S(2)}, u32[]{:S(2)}) collective-permute-start(bf16[384,640]{1,0:T(8,128)(2,1)} %get-tuple-element.65), channel_id=1, source_target_pairs={{0,4},{2,6},{4,0},{6,2},{1,5},{3,7},{5,1},{7,3},{8,12},{10,14},{12... | collective-permute-start | bytes 1474568 | tf_op jit(solution)/shard_map/ppermute | solution.py:422
  16.8 1.2 %all-to-all-done.arrived = bf16[8,72,384]{2,1,0:T(8,128)(2,1)S(1)} async-done(((bf16[8,72,384]{2,1,0:T(8,128)(2,1)}), bf16[8,72,384]{2,1,0:T(8,128)(2,1)S(1)}, u32[]{:S(2)}, u32[]{:S(2)}) %all-to-all-start) | async-done | bytes 442400 | tf_op jit(solution)/shard_map/all_to_all | solution.py:437
  18.0 0.2 plane_total.1
  18.2 0.9 %collective-permute-start = (bf16[72,384]{1,0:T(8,128)(2,1)S(1)}, bf16[72,384]{1,0:T(8,128)(2,1)S(1)}, u32[]{:S(2)}, u32[]{:S(2)}) collective-permute-start(bf16[72,384]{1,0:T(8,128)(2,1)S(1)} %get-tuple-element.38), channel_id=1, source_target_pairs={{0,32},{32,0},{64,96},{96,64},{128,160},{160,128},{192,224},{224,1... | collective-permute-start | bytes 165896 | tf_op jit(solution)/shard_map/ppermute | solution.py:426
  19.1 1.1 %constant_dynamic-slice_fusion.lat = bf16[512,640]{1,0:T(8,128)(2,1)S(1)} fusion(bf16[512,2560]{1,0:T(8,128)(2,1)} %lat.4, s32[]{:T(128)S(6)} %select_n.22), kind=kLoop, calls=%fused_computation.1 | loop fusion | bytes 1310724 | tf_op jit(solution)/shard_map/dynamic_slice | solution.py:454
  20.2 2.3 %collective-permute-done.got_1 = bf16[72,384]{1,0:T(8,128)(2,1)S(1)} collective-permute-done((bf16[72,384]{1,0:T(8,128)(2,1)S(1)}, bf16[72,384]{1,0:T(8,128)(2,1)S(1)}, u32[]{:S(2)}, u32[]{:S(2)}) %collective-permute-start) | collective-permute-done | bytes 55328 | tf_op jit(solution)/shard_map/ppermute | solution.py:426
  22.5 3.4 %collective-permute-start.1 = (bf16[72,384]{1,0:T(8,128)(2,1)S(1)}, bf16[72,384]{1,0:T(8,128)(2,1)S(1)}, u32[]{:S(2)}, u32[]{:S(2)}) collective-permute-start(bf16[72,384]{1,0:T(8,128)(2,1)S(1)} %through_1.1), channel_id=1, source_target_pairs={{0,64},{32,96},{64,0},{96,32},{128,192},{160,224},{192,128},{224,1... | collective-permute-start | bytes 165896 | tf_op jit(solution)/shard_map/ppermute | solution.py:426
  25.9 3.5 %head_values.1.values = bf16[256,384]{1,0:T(8,128)(2,1)} custom-call(s32[1]{0:T(128)} %bitcast.3.z.after, bf16[512,2560]{1,0:T(8,128)(2,1)} %lat.4, bf16[3,2560,384]{2,1,0:T(8,128)(2,1)} %bitcast.6), custom_call_target="tpu_custom_call" | custom-call | flops 503316480 | bytes 3300000 | tf_op jit(solution)/shard_map/head_values/pallas_call | solution.py:126
  29.4 0.0 collective-permute-done.1.got_2
  29.4 0.1 through_3.1
  29.4 0.0 copy-start.4
  29.5 4.3 %collective-permute-start.2 = (bf16[64,384]{1,0:T(8,128)(2,1)S(1)}, bf16[64,384]{1,0:T(8,128)(2,1)S(1)}, u32[]{:S(2)}, u32[]{:S(2)}) collective-permute-start(bf16[64,384]{1,0:T(8,128)(2,1)S(1)} %through_3.1), channel_id=1, source_target_pairs={{0,224},{32,192},{64,160},{96,128},{128,96},{160,64},{192,32},{224... | collective-permute-start | bytes 147464 | tf_op jit(solution)/shard_map/ppermute | solution.py:426
  33.8 3.6 %head_keys.1 = (bf16[256,384]{1,0:T(8,128)(2,1)}, bf16[64,384]{1,0:T(8,128)(2,1)}) custom-call(s32[1]{0:T(128)} %bitcast.phase, bf16[512,2560]{1,0:T(8,128)(2,1)} %lat.4, bf16[3,2560,384]{2,1,0:T(8,128)(2,1)} %bitcast.7, bf16[256,384]{1,0:T(8,128)(2,1)} %head_values.1.values, bf16[8,72,384]{2,1,0:T(8,128)(2,1)} %tail_projection.1.payload.tail_rows), custom_call_target="tpu_custom_call" | custom-call | flops 503316480 | bytes 3300000 | tf_op jit(solution)/shard_map/head_keys/pallas_call | solution.py:126
  37.4 0.0 collective-permute-done.2.got_4
  37.5 0.9 %section_memory.1 = bf16[8,64,384]{2,1,0:T(8,128)(2,1)} custom-call(s32[1]{0:T(128)} %bitcast.3.z.after, bf16[72,384]{1,0:T(8,128)(2,1)S(1)} %collective-permute-done.got_1, bf16[72,384]{1,0:T(8,128)(2,1)S(1)} %collective-permute-done.1.got_2, bf16[64,384]{1,0:T(8,128)(2,1)S(1)} %collective-permute-done.2.got_4, bf16[8,72,384]{2,1,0:T(8,128)(2,1)S(1)} %all-to-all-done.arrived), custom_call_target="tpu_custom_call" | custom-call | flops 1000000 | bytes 602116 | tf_op jit(solution)/shard_map/section_memory/pallas_call | solution.py:220
  38.4 3.6 %all-to-all-start.1 = ((bf16[8,64,384]{2,1,0:T(8,128)(2,1)}), bf16[8,64,384]{2,1,0:T(8,128)(2,1)S(1)}, u32[]{:S(2)}, u32[]{:S(2)}) async-start(bf16[8,64,384]{2,1,0:T(8,128)(2,1)} %section_memory.1), calls=%async_computation.1 | async-start | bytes 786432 | tf_op jit(solution)/shard_map/all_to_all | solution.py:473
  42.0 3.5 %collective-permute-start.3 = (bf16[64,384]{1,0:T(8,128)(2,1)}, bf16[64,384]{1,0:T(8,128)(2,1)S(1)}, u32[]{:S(2)}, u32[]{:S(2)}) collective-permute-start(bf16[64,384]{1,0:T(8,128)(2,1)} %get-tuple-element.55), channel_id=1, source_target_pairs={{0,1},{1,0},{2,3},{3,2},{4,5},{5,4},{6,7},{7,6},{8,9},{9,8},{10,11... | collective-permute-start | bytes 147464 | tf_op jit(solution)/shard_map/ppermute | solution.py:426
  45.5 0.0 copy-done.4
  45.5 0.1 pad_dynamic-slice_fusion
  45.6 0.0 copy-start
  45.6 0.0 copy-start.1
  45.6 0.0 copy-start.2
  45.6 4.6 %query_projection.1.q = bf16[512,384]{1,0:T(8,128)(2,1)} custom-call(s32[1]{0:T(128)} %bitcast.3.z.after, bf16[512,2560]{1,0:T(8,128)(2,1)} %lat.4, bf16[3,2560,384]{2,1,0:T(8,128)(2,1)} %bitcast.8), custom_call_target="tpu_custom_call" | custom-call | flops 1006632960 | bytes 4600000 | tf_op jit(solution)/shard_map/query_projection/pallas_call | solution.py:126
  50.2 0.0 collective-permute-done.4.w_right
  50.3 0.0 collective-permute-done.5.w_left
  50.3 0.0 collective-permute-done.6.w
  50.3 0.0 all-to-all-done.1.memory_in
  50.3 0.0 copy-start.3
  50.3 1.7 %collective-permute-done.3.halo = bf16[64,384]{1,0:T(8,128)(2,1)S(1)} collective-permute-done((bf16[64,384]{1,0:T(8,128)(2,1)}, bf16[64,384]{1,0:T(8,128)(2,1)S(1)}, u32[]{:S(2)}, u32[]{:S(2)}) %collective-permute-start.3) | collective-permute-done | bytes 49184 | tf_op jit(solution)/shard_map/ppermute | solution.py:426
  52.0 0.0 copy-done.3
  52.0 0.1 broadcast_in_dim.2.columns_in
  52.1 0.0 copy-done
  52.1 0.0 copy-done.1
  52.1 0.0 copy-done.2
  52.1 2.8 %attention_1.1.own_1 = bf16[256,384]{1,0:T(8,128)(2,1)S(1)} custom-call(s32[1]{0:T(128)} %bitcast.phase, s32[1,17]{1,0:T(1,128)S(1)} %copy-done.2, bf16[512,384]{1,0:T(8,128)(2,1)} %query_projection.1.q, bf16[256,384]{1,0:T(8,128)(2,1)S(1)} %copy-done.1, bf16[256,384]{1,0:T(8,128)(2,1)S(1)} %copy-done, bf16[8,72,384]{2,1,0:T(8,128)(2,1)} %tail_projection.1.payload.tail_rows, ...), custom_call_target="tpu_custom_call" | custom-call | flops 402653184 | bytes 1500000 | tf_op jit(solution)/shard_map/attention_1/pallas_call | solution.py:378
  54.9 1.5 %collective-permute-start.8 = (bf16[256,384]{1,0:T(8,128)(2,1)S(1)}, bf16[256,384]{1,0:T(8,128)(2,1)S(1)}, u32[]{:S(2)}, u32[]{:S(2)}) collective-permute-start(bf16[256,384]{1,0:T(8,128)(2,1)S(1)} %attention_1.1.own_1), channel_id=1, source_target_pairs={{0,2},{2,4},{4,6},{6,0},{1,3},{3,5},{5,7},{7,1},{8,10},{10,12},{12... | collective-permute-start | bytes 589832 | tf_op jit(solution)/shard_map/ppermute | solution.py:422
  56.4 2.0 %collective-permute-start.9 = (bf16[256,384]{1,0:T(8,128)(2,1)S(1)}, bf16[256,384]{1,0:T(8,128)(2,1)S(1)}, u32[]{:S(2)}, u32[]{:S(2)}) collective-permute-start(bf16[256,384]{1,0:T(8,128)(2,1)S(1)} %attention_1.1.own_1), channel_id=1, source_target_pairs={{0,6},{2,0},{4,2},{6,4},{1,7},{3,1},{5,3},{7,5},{8,14},{10,8},{12,... | collective-permute-start | bytes 589832 | tf_op jit(solution)/shard_map/ppermute | solution.py:422
  58.4 2.7 %attention_0.1.own_0 = bf16[256,384]{1,0:T(8,128)(2,1)S(1)} custom-call(s32[1]{0:T(128)} %bitcast.phase, s32[1,17]{1,0:T(1,128)S(1)} %copy-done.2, bf16[512,384]{1,0:T(8,128)(2,1)} %query_projection.1.q, bf16[256,384]{1,0:T(8,128)(2,1)S(1)} %copy-done.1, bf16[256,384]{1,0:T(8,128)(2,1)S(1)} %copy-done, bf16[8,72,384]{2,1,0:T(8,128)(2,1)} %tail_projection.1.payload.tail_rows, ...), custom_call_target="tpu_custom_call" | custom-call | flops 402653184 | bytes 1500000 | tf_op jit(solution)/shard_map/attention_0/pallas_call | solution.py:378
  61.2 0.1 collective-permute-start.7
  61.2 3.2 %collective-permute-start.10 = (bf16[256,384]{1,0:T(8,128)(2,1)S(1)}, bf16[256,384]{1,0:T(8,128)(2,1)S(1)}, u32[]{:S(2)}, u32[]{:S(2)}) collective-permute-start(bf16[256,384]{1,0:T(8,128)(2,1)S(1)} %attention_0.1.own_0), channel_id=1, source_target_pairs={{0,6},{2,0},{4,2},{6,4},{1,7},{3,1},{5,3},{7,5},{8,14},{10,8},{12,... | collective-permute-start | bytes 589832 | tf_op jit(solution)/shard_map/ppermute | solution.py:422
  64.5 0.0 collective-permute-done.8.right_1
  64.5 0.0 collective-permute-done.9.left_1
  64.5 3.9 %collective-permute-done.7.right_0 = bf16[256,384]{1,0:T(8,128)(2,1)S(1)} collective-permute-done((bf16[256,384]{1,0:T(8,128)(2,1)S(1)}, bf16[256,384]{1,0:T(8,128)(2,1)S(1)}, u32[]{:S(2)}, u32[]{:S(2)}) %collective-permute-start.7) | collective-permute-done | bytes 196640 | tf_op jit(solution)/shard_map/ppermute | solution.py:422
  68.3 0.0 collective-permute-start.11
  68.3 3.2 %collective-permute-start.12 = (bf16[256,384]{1,0:T(8,128)(2,1)S(1)}, bf16[256,384]{1,0:T(8,128)(2,1)S(1)}, u32[]{:S(2)}, u32[]{:S(2)}) collective-permute-start(bf16[256,384]{1,0:T(8,128)(2,1)S(1)} %collective-permute-done.9.left_1), channel_id=1, source_target_pairs={{0,6},{2,0},{4,2},{6,4},{1,7},{3,1},{5,3},{7,5},{8,14},{10,8},{12,... | collective-permute-start | bytes 589832 | tf_op jit(solution)/shard_map/ppermute | solution.py:422
  71.6 0.0 collective-permute-done.10.left_0
  71.6 1.3 %near_projection.1.total = f32[512,640]{1,0:T(8,128)S(1)} custom-call(bf16[512,640]{1,0:T(8,128)(2,1)S(1)} %constant_dynamic-slice_fusion.lat, bf16[256,384]{1,0:T(8,128)(2,1)S(1)} %attention_0.1.own_0, bf16[256,384]{1,0:T(8,128)(2,1)S(1)} %attention_1.1.own_1, bf16[256,384]{1,0:T(8,128)(2,1)S(1)} %collective-permute-done.7.right_0, ...), custom_call_target="tpu_custom_call" | custom-call | flops 754974720 | bytes 3309568 | tf_op jit(solution)/shard_map/near_projection/pallas_call | solution.py:220
  72.9 2.3 %collective-permute-done.11.first = bf16[256,384]{1,0:T(8,128)(2,1)S(1)} collective-permute-done((bf16[256,384]{1,0:T(8,128)(2,1)S(1)}, bf16[256,384]{1,0:T(8,128)(2,1)S(1)}, u32[]{:S(2)}, u32[]{:S(2)}) %collective-permute-start.11) | collective-permute-done | bytes 196640 | tf_op jit(solution)/shard_map/ppermute | solution.py:422
  75.2 0.0 collective-permute-done.12.second
  75.2 1.4 %far_projection.1 = bf16[512,640]{1,0:T(8,128)(2,1)} custom-call(f32[512,640]{1,0:T(8,128)S(1)} %near_projection.1.total, bf16[256,384]{1,0:T(8,128)(2,1)S(1)} %collective-permute-done.11.first, bf16[256,384]{1,0:T(8,128)(2,1)S(1)} %collective-permute-done.12.second, bf16[384,640]{1,0:T(8,128)(2,1)S(1)} %collective-permute-done.6.w), custom_call_target="tpu_custom_call" | custom-call | flops 251658240 | bytes 2195456 | tf_op jit(solution)/shard_map/far_projection/pallas_call | solution.py:220
  (2 shorter events, 0.0 us)
Async XLA Ops:
  4.7 13.3 %all-to-all-start = ((bf16[8,72,384]{2,1,0:T(8,128)(2,1)}), bf16[8,72,384]{2,1,0:T(8,128)(2,1)S(1)}, u32[]{:S(2)}, u32[]{:S(2)}) async-start(bf16[8,72,384]{2,1,0:T(8,128)(2,1)} %tail_projection.1.payload.tail_rows), calls=%async_computation | async-start | bytes 884736 | tf_op jit(solution)/shard_map/all_to_all | solution.py:437
  11.8 38.4 %collective-permute-start.4 = (bf16[384,640]{1,0:T(8,128)(2,1)}, bf16[384,640]{1,0:T(8,128)(2,1)S(1)}, u32[]{:S(2)}, u32[]{:S(2)}) collective-permute-start(bf16[384,640]{1,0:T(8,128)(2,1)} %get-tuple-element.67), channel_id=1, source_target_pairs={{0,2},{2,4},{4,6},{6,0},{1,3},{3,5},{5,7},{7,1},{8,10},{10,12},{12... | collective-permute-start | bytes 1474568 | tf_op jit(solution)/shard_map/ppermute | solution.py:422
  13.3 37.0 %collective-permute-start.5 = (bf16[384,640]{1,0:T(8,128)(2,1)}, bf16[384,640]{1,0:T(8,128)(2,1)S(1)}, u32[]{:S(2)}, u32[]{:S(2)}) collective-permute-start(bf16[384,640]{1,0:T(8,128)(2,1)} %get-tuple-element.66), channel_id=1, source_target_pairs={{0,6},{2,0},{4,2},{6,4},{1,7},{3,1},{5,3},{7,5},{8,14},{10,8},{12,... | collective-permute-start | bytes 1474568 | tf_op jit(solution)/shard_map/ppermute | solution.py:422
  15.0 35.2 %collective-permute-start.6 = (bf16[384,640]{1,0:T(8,128)(2,1)}, bf16[384,640]{1,0:T(8,128)(2,1)S(1)}, u32[]{:S(2)}, u32[]{:S(2)}) collective-permute-start(bf16[384,640]{1,0:T(8,128)(2,1)} %get-tuple-element.65), channel_id=1, source_target_pairs={{0,4},{2,6},{4,0},{6,2},{1,5},{3,7},{5,1},{7,3},{8,12},{10,14},{12... | collective-permute-start | bytes 1474568 | tf_op jit(solution)/shard_map/ppermute | solution.py:422
  18.2 4.3 %collective-permute-start = (bf16[72,384]{1,0:T(8,128)(2,1)S(1)}, bf16[72,384]{1,0:T(8,128)(2,1)S(1)}, u32[]{:S(2)}, u32[]{:S(2)}) collective-permute-start(bf16[72,384]{1,0:T(8,128)(2,1)S(1)} %get-tuple-element.38), channel_id=1, source_target_pairs={{0,32},{32,0},{64,96},{96,64},{128,160},{160,128},{192,224},{224,1... | collective-permute-start | bytes 165896 | tf_op jit(solution)/shard_map/ppermute | solution.py:426
  22.5 6.8 %collective-permute-start.1 = (bf16[72,384]{1,0:T(8,128)(2,1)S(1)}, bf16[72,384]{1,0:T(8,128)(2,1)S(1)}, u32[]{:S(2)}, u32[]{:S(2)}) collective-permute-start(bf16[72,384]{1,0:T(8,128)(2,1)S(1)} %through_1.1), channel_id=1, source_target_pairs={{0,64},{32,96},{64,0},{96,32},{128,192},{160,224},{192,128},{224,1... | collective-permute-start | bytes 165896 | tf_op jit(solution)/shard_map/ppermute | solution.py:426
  29.4 16.1 %copy-start.4 = (s32[1,1024]{1,0:T(1,128)S(1)}, s32[1,1024]{1,0:T(1,128)}, u32[]{:S(2)}) copy-start(s32[1,1024]{1,0:T(1,128)} %param.10) | copy-start | bytes 12292
  29.5 8.0 %collective-permute-start.2 = (bf16[64,384]{1,0:T(8,128)(2,1)S(1)}, bf16[64,384]{1,0:T(8,128)(2,1)S(1)}, u32[]{:S(2)}, u32[]{:S(2)}) collective-permute-start(bf16[64,384]{1,0:T(8,128)(2,1)S(1)} %through_3.1), channel_id=1, source_target_pairs={{0,224},{32,192},{64,160},{96,128},{128,96},{160,64},{192,32},{224... | collective-permute-start | bytes 147464 | tf_op jit(solution)/shard_map/ppermute | solution.py:426
  38.4 11.9 %all-to-all-start.1 = ((bf16[8,64,384]{2,1,0:T(8,128)(2,1)}), bf16[8,64,384]{2,1,0:T(8,128)(2,1)S(1)}, u32[]{:S(2)}, u32[]{:S(2)}) async-start(bf16[8,64,384]{2,1,0:T(8,128)(2,1)} %section_memory.1), calls=%async_computation.1 | async-start | bytes 786432 | tf_op jit(solution)/shard_map/all_to_all | solution.py:473
  42.0 10.0 %collective-permute-start.3 = (bf16[64,384]{1,0:T(8,128)(2,1)}, bf16[64,384]{1,0:T(8,128)(2,1)S(1)}, u32[]{:S(2)}, u32[]{:S(2)}) collective-permute-start(bf16[64,384]{1,0:T(8,128)(2,1)} %get-tuple-element.55), channel_id=1, source_target_pairs={{0,1},{1,0},{2,3},{3,2},{4,5},{5,4},{6,7},{7,6},{8,9},{9,8},{10,11... | collective-permute-start | bytes 147464 | tf_op jit(solution)/shard_map/ppermute | solution.py:426
  45.6 6.5 %copy-start = (bf16[256,384]{1,0:T(8,128)(2,1)S(1)}, bf16[256,384]{1,0:T(8,128)(2,1)}, u32[]{:S(2)}) copy-start(bf16[256,384]{1,0:T(8,128)(2,1)} %head_values.1.values) | copy-start | bytes 589828
  45.6 6.5 %copy-start.1 = (bf16[256,384]{1,0:T(8,128)(2,1)S(1)}, bf16[256,384]{1,0:T(8,128)(2,1)}, u32[]{:S(2)}) copy-start(bf16[256,384]{1,0:T(8,128)(2,1)} %get-tuple-element.54.head_keys) | copy-start | bytes 589828
  45.6 6.5 %copy-start.2 = (s32[1,17]{1,0:T(1,128)S(1)}, s32[1,17]{1,0:T(1,128)}, u32[]{:S(2)}) copy-start(s32[1,17]{1,0:T(1,128)} %opened.3) | copy-start | bytes 208
  50.3 1.7 %copy-start.3 = (bf16[8,64,384]{2,1,0:T(8,128)(2,1)}, bf16[8,64,384]{2,1,0:T(8,128)(2,1)S(1)}, u32[]{:S(2)}) copy-start(bf16[8,64,384]{2,1,0:T(8,128)(2,1)S(1)} %all-to-all-done.1.memory_in) | copy-start | bytes 1179652
  54.9 9.6 %collective-permute-start.8 = (bf16[256,384]{1,0:T(8,128)(2,1)S(1)}, bf16[256,384]{1,0:T(8,128)(2,1)S(1)}, u32[]{:S(2)}, u32[]{:S(2)}) collective-permute-start(bf16[256,384]{1,0:T(8,128)(2,1)S(1)} %attention_1.1.own_1), channel_id=1, source_target_pairs={{0,2},{2,4},{4,6},{6,0},{1,3},{3,5},{5,7},{7,1},{8,10},{10,12},{12... | collective-permute-start | bytes 589832 | tf_op jit(solution)/shard_map/ppermute | solution.py:422
  56.4 8.1 %collective-permute-start.9 = (bf16[256,384]{1,0:T(8,128)(2,1)S(1)}, bf16[256,384]{1,0:T(8,128)(2,1)S(1)}, u32[]{:S(2)}, u32[]{:S(2)}) collective-permute-start(bf16[256,384]{1,0:T(8,128)(2,1)S(1)} %attention_1.1.own_1), channel_id=1, source_target_pairs={{0,6},{2,0},{4,2},{6,4},{1,7},{3,1},{5,3},{7,5},{8,14},{10,8},{12,... | collective-permute-start | bytes 589832 | tf_op jit(solution)/shard_map/ppermute | solution.py:422
  61.2 7.2 %collective-permute-start.7 = (bf16[256,384]{1,0:T(8,128)(2,1)S(1)}, bf16[256,384]{1,0:T(8,128)(2,1)S(1)}, u32[]{:S(2)}, u32[]{:S(2)}) collective-permute-start(bf16[256,384]{1,0:T(8,128)(2,1)S(1)} %attention_0.1.own_0), channel_id=1, source_target_pairs={{0,2},{2,4},{4,6},{6,0},{1,3},{3,5},{5,7},{7,1},{8,10},{10,12},{12... | collective-permute-start | bytes 589832 | tf_op jit(solution)/shard_map/ppermute | solution.py:422
  61.2 10.3 %collective-permute-start.10 = (bf16[256,384]{1,0:T(8,128)(2,1)S(1)}, bf16[256,384]{1,0:T(8,128)(2,1)S(1)}, u32[]{:S(2)}, u32[]{:S(2)}) collective-permute-start(bf16[256,384]{1,0:T(8,128)(2,1)S(1)} %attention_0.1.own_0), channel_id=1, source_target_pairs={{0,6},{2,0},{4,2},{6,4},{1,7},{3,1},{5,3},{7,5},{8,14},{10,8},{12,... | collective-permute-start | bytes 589832 | tf_op jit(solution)/shard_map/ppermute | solution.py:422
  68.3 6.9 %collective-permute-start.11 = (bf16[256,384]{1,0:T(8,128)(2,1)S(1)}, bf16[256,384]{1,0:T(8,128)(2,1)S(1)}, u32[]{:S(2)}, u32[]{:S(2)}) collective-permute-start(bf16[256,384]{1,0:T(8,128)(2,1)S(1)} %collective-permute-done.7.right_0), channel_id=1, source_target_pairs={{0,2},{2,4},{4,6},{6,0},{1,3},{3,5},{5,7},{7,1},{8,10},{10,12},{12... | collective-permute-start | bytes 589832 | tf_op jit(solution)/shard_map/ppermute | solution.py:422
  68.3 6.9 %collective-permute-start.12 = (bf16[256,384]{1,0:T(8,128)(2,1)S(1)}, bf16[256,384]{1,0:T(8,128)(2,1)S(1)}, u32[]{:S(2)}, u32[]{:S(2)}) collective-permute-start(bf16[256,384]{1,0:T(8,128)(2,1)S(1)} %collective-permute-done.9.left_1), channel_id=1, source_target_pairs={{0,6},{2,0},{4,2},{6,4},{1,7},{3,1},{5,3},{7,5},{8,14},{10,8},{12,... | collective-permute-start | bytes 589832 | tf_op jit(solution)/shard_map/ppermute | solution.py:422

commit v6 on v5

--- a/solution.py
+++ b/solution.py
@@ -23,6 +23,7 @@
 TAIL_LIMIT = 60 * 1024 * 1024
 REST_LIMIT = 60 * 1024 * 1024
 ATTEND_LIMIT = 53 * 1024 * 1024
+QUERY_LIMIT = 60 * 1024 * 1024
 LIMIT = 32 * 1024 * 1024
 SPAN = ("z", "y", "core")
 PLANE = ("y", "core", "phase")
@@ -119,7 +120,7 @@
     )(phase, decay, latents, w3)
 
 
-def call_on_hbm(kernel, outs, name, flops, nbytes, args, scratch):
+def call_on_hbm(kernel, outs, name, flops, nbytes, args, scratch, limit=REST_LIMIT):
     vmem = pl.BlockSpec(memory_space=pltpu.VMEM)
     hbm = pl.BlockSpec(memory_space=pl.ANY)
     single = not isinstance(outs, tuple)
@@ -130,7 +131,7 @@
         out_specs=vmem if single else tuple(vmem for _ in outs),
         scratch_shapes=scratch,
         cost_estimate=pl.CostEstimate(flops=flops, bytes_accessed=nbytes, transcendentals=0),
-        compiler_params=pltpu.CompilerParams(vmem_limit_bytes=REST_LIMIT),
+        compiler_params=pltpu.CompilerParams(vmem_limit_bytes=limit),
         name=name,
     )(*args)
 
@@ -208,6 +209,7 @@
         4600000,
         (after, latents, w3),
         [pltpu.VMEM((ROWS, depth), BF16), pltpu.VMEM((depth, COLS), BF16), pltpu.SemaphoreType.DMA((3,))],
+        QUERY_LIMIT,
     )
 
 
@@ -400,21 +402,50 @@
     )(phase, opened, *operands)
 
 
-def near_kernel(lat, own_0, own_1, right_0, right_1, left_0, left_1, w_own, w_right, w_left, total):
-    half = ROWS // 2
-    for r, parts in enumerate(((own_0, right_0, left_0), (own_1, right_1, left_1))):
-        at = slice(r * half, (r + 1) * half)
-        sums = lat[at].astype(F32)
-        for a, w in zip(parts, (w_own, w_right, w_left)):
-            sums = sums + jnp.dot(a[...], w[...], preferred_element_type=F32)
-        total[at] = sums
-
-
-def far_kernel(total, first, second, w, out):
-    half = ROWS // 2
-    for r, part in enumerate((first, second)):
-        at = slice(r * half, (r + 1) * half)
-        out[at] = (total[at] + jnp.dot(part[...], w[...], preferred_element_type=F32)).astype(BF16)
+def joined_rows(core, pair, whole):
+    half = pair[0].shape[0]
+    for which, part in ((core[0], pair[0]), (1 - core[0], pair[1])):
+        whole[pl.ds(pl.multiple_of(which * half, half), half)] = part[...]
+
+
+def near_kernel(r, core, lat, own, right, left, w_own, w_right, w_right_2, w_left, w_left_2, total, whole, whole_2):
+    rows = total.shape[0]
+    sums = lat[r * rows : (r + 1) * rows].astype(F32)
+    sums = sums + jnp.dot(own[...], w_own[...], preferred_element_type=F32)
+    joined_rows(core, (w_right, w_right_2), whole)
+    joined_rows(core, (w_left, w_left_2), whole_2)
+    for a, w in ((right, whole), (left, whole_2)):
+        sums = sums + jnp.dot(a[...], w[...], preferred_element_type=F32)
+    total[...] = sums
+
+
+def far_kernel(core, total, part, w, w_2, *refs):
+    out, whole = refs[-2:]
+    joined_rows(core, (w, w_2), whole)
+    out[...] = (total[...] + jnp.dot(part[...], whole[...], preferred_element_type=F32)).astype(BF16)
+
+
+def far(r, core, total, part, pair, earlier=None):
+    rows, share = total.shape
+    vmem = pl.BlockSpec(memory_space=pltpu.VMEM)
+    operands = [core, total, part, *pair]
+    specs, aliases = [pl.BlockSpec(memory_space=pltpu.SMEM)] + [vmem] * 4, {}
+    if earlier is not None:
+        operands.append(earlier)
+        specs.append(pl.BlockSpec(memory_space=pl.ANY))
+        aliases = {5: 0}
+    return pl.pallas_call(
+        far_kernel,
+        grid=(1,),
+        in_specs=specs,
+        out_specs=pl.BlockSpec((rows, share), lambda i: (r, 0)),
+        out_shape=shape((ROWS, share), BF16),
+        scratch_shapes=[pltpu.VMEM((COLS, share), BF16)],
+        input_output_aliases=aliases,
+        cost_estimate=pl.CostEstimate(flops=2 * rows * COLS * share, bytes_accessed=1500000, transcendentals=0),
+        compiler_params=pltpu.CompilerParams(vmem_limit_bytes=LIMIT),
+        name=f"far_projection_{r}",
+    )(*operands)
 
 
 def moved(x, axis, by):
@@ -439,8 +470,13 @@
     w_out, payload = lax.optimization_barrier((w_out, payload))
     share = w_out.shape[1] // 4
     offsets = (0, 1, -1, 2)
-    sends = [lax.dynamic_slice_in_dim(w_out, ((mp + by) & 3) * share, share, 1) for by in offsets]
-    weights = [moved(piece, "mp", by) if by else piece for by, piece in zip(offsets, sends)]
+    core = lax.axis_index("core")
+    deep = COLS // 2
+    own_weight = lax.dynamic_slice_in_dim(w_out, mp * share, share, 1)
+    sends = [
+        lax.dynamic_slice(w_out, (core * deep, ((mp + by) & 3) * share), (deep, share)) for by in offsets[1:]
+    ]
+    weights = [moved(piece, "mp", by) for by, piece in zip(offsets[1:], sends)]
     arrived, _ = lax.optimization_barrier((arrived, sends))
     half_keys = shape((MEM, COLS), BF16)
 
@@ -449,35 +485,38 @@
     plain = shape((2 * PART, COLS), BF16)
     plain_all = shape((PARTS, 2 * PART, COLS), BF16)
     own, sent = vmem_call(plane_kernel, (wide, packed), "plane_total", 1000000, (arrived,))
-    latents, sent = lax.optimization_barrier((latents, sent))
+    after, sent = lax.optimization_barrier((z_ref, sent))
     got_1 = swapped(sent, "z", 1)
-    own_columns = lax.dynamic_slice_in_dim(latents, mp * share, share, 1)
-    got_1, own_columns = lax.optimization_barrier((got_1, own_columns))
+    head_values = heads(head_values_kernel, half_keys, "head_values", after, latents, w3)
+    got_1, head_values = lax.optimization_barrier((got_1, head_values))
+
     sent = vmem_call(first_kernel, packed, "through_1", 100000, (z_ref, own, got_1), smem=1)
-    after, sent = lax.optimization_barrier((z_ref, sent))
+    after, sent = lax.optimization_barrier((phase_ref, sent))
     got_2 = swapped(sent, "z", 2)
-    head_values = heads(head_values_kernel, half_keys, "head_values", after, latents, w3)
-    got_2, head_values = lax.optimization_barrier((got_2, head_values))
-
-    sent = vmem_call(next_kernel, plain, "through_3", 100000, (z_ref, own, got_1, got_2), smem=1)
-    after, sent = lax.optimization_barrier((phase_ref, sent))
-    got_4 = swapped(sent, "z", 7)
     head_keys, edge = heads(
         head_keys_kernel, (half_keys, plain), "head_keys", after, latents, w3, head_values, payload
     )
-    got_4, head_keys = lax.optimization_barrier((got_4, head_keys))
+    got_2, head_keys, edge = lax.optimization_barrier((got_2, head_keys, edge))
+
+    sent = vmem_call(next_kernel, plain, "through_3", 100000, (z_ref, own, got_1, got_2), smem=1)
+    latents, sent, edge = lax.optimization_barrier((latents, sent, edge))
+    got_4 = swapped(sent, "z", 7)
+    halo = swapped(edge, "phase", 1)
+    own_columns = lax.dynamic_slice_in_dim(latents, mp * share, share, 1)
+    got_4, own_columns, halo, weights = lax.optimization_barrier((got_4, own_columns, halo, weights))
     memory = vmem_call(
         memory_kernel, plain_all, "section_memory", 1000000, (z_ref, got_1, got_2, got_4, arrived), smem=1
     )
-    after, memory, edge, frame_ids = lax.optimization_barrier((z_ref, memory, edge, frame_ids))
+    after, memory, frame_ids = lax.optimization_barrier((z_ref, memory, frame_ids))
     memory = lax.all_to_all(memory, PLANE, 0, 0, tiled=True)
-    halo = swapped(edge, "phase", 1)
     frames_pad = jnp.pad(frame_ids[0], (HALF_WIN, HALF_WIN), constant_values=outside_frame)
     frames = lax.dynamic_slice_in_dim(frames_pad, phase * ROWS, EXT)
     frame_row = frames.reshape(1, EXT)
     frame_column = jnp.broadcast_to(frames[:, None], (EXT, HD))
     queries = query(after, latents, w3)
+    weights = [(half, swapped(half, "core", 1)) for half in weights]
     memory, weights = lax.optimization_barrier((memory, weights))
+    core_ref = core.reshape(1).astype(jnp.int32)
     halves = [
         attention(
             r, phase_ref, memory_mask, queries, head_keys, head_values, payload, halo, frame_row, frame_column, memory
@@ -487,21 +526,20 @@
     right = [moved(piece, "mp", 1) for piece in halves]
     left = [moved(piece, "mp", -1) for piece in halves]
     right[1], left[1] = lax.optimization_barrier((right[1], left[1]))
-    far_1, far_2 = moved(right[0], "mp", 1), moved(left[1], "mp", -1)
-    total = vmem_call(
-        near_kernel,
-        shape((ROWS, share), F32),
-        "near_projection",
-        6 * ROWS * COLS * share,
-        (own_columns, *halves, *right, *left, *weights[:3]),
-    )
-    return vmem_call(
-        far_kernel,
-        shape((ROWS, share), BF16),
-        "far_projection",
-        2 * ROWS * COLS * share,
-        (total, far_1, far_2, weights[3]),
-    )
+    far_parts = moved(right[0], "mp", 1), moved(left[1], "mp", -1)
+    refined = None
+    for r in (1, 0):
+        total = vmem_call(
+            functools.partial(near_kernel, r),
+            shape((ROWS // 2, share), F32),
+            f"near_projection_{r}",
+            3 * ROWS * COLS * share,
+            (core_ref, own_columns, halves[r], right[r], left[r], own_weight, *weights[0], *weights[1]),
+            smem=1,
+            scratch=[pltpu.VMEM((COLS, share), BF16)] * 2,
+        )
+        refined = far(r, core_ref, total, far_parts[r], weights[2], refined)
+    return refined
 
 
 def solution(mesh):

time: 78 us -> 79.8 us (1.023)
  waiting for transfers between devices: 11.3 us -> 17.1 us
  starting transfers between devices: 35.2 us -> 30.6 us
  Pallas kernels: 25.8 us -> 26.8 us
    ppermute x9, starting transfers between devices: 15.1 us -> 11.4 us  [moved(): return lax.ppermute(x, axis, [(i, (i + by) % size) for i in range(size)])]
    ppermute x9, waiting for transfers between devices: 6.22 us -> 9.23 us  [moved(): return lax.ppermute(x, axis, [(i, (i + by) % size) for i in range(size)])]
    all_to_all x1, waiting for transfers between devices: 0.01 us -> 2.57 us  [local(): memory = lax.all_to_all(memory, PLANE, 0, 0, tiled=True)]
    pallas_call x0 -> x2, Pallas kernels: none -> 2.24 us  [far(): pl.pallas_call(far_kernel, grid=(1,), in_specs=specs, out_specs=pl.BlockS...]
    all_to_all x1, waiting for transfers between devices: 1.17 us -> 2.46 us  [local(): arrived = lax.all_to_all(payload, PLANE, 0, 0, tiled=True)]
    pallas_call x6, Pallas kernels: 3.89 us -> 2.67 us  [vmem_call(): pl.pallas_call(kernel, out_shape=outs, in_specs=specs, out_specs=out_spec...]
    ppermute x4 -> x7, waiting for transfers between devices: 3.95 us -> 2.83 us  [swapped(): lax.ppermute(x, axis, [(i, i ^ bit) for i in range(lax.axis_size(axis))])]
    ppermute x4 -> x7, starting transfers between devices: 12.1 us -> 11.3 us  [swapped(): lax.ppermute(x, axis, [(i, i ^ bit) for i in range(lax.axis_size(axis))])]
  transfers between devices with their start and end apart: 15 -> 18, of which waited for: 5 -> 6; matrix products, arithmetic and copies ran while one was open for 5% -> 4% of each run, Pallas kernels for 22% -> 22%
where the time goes in v6:
time: 79.8 us; the launch traced here: 79 us
  starting transfers between devices  30.6 us (38%)
  Pallas kernels  26.8 us (34%)
  waiting for transfers between devices  17.1 us (21%)
  local copies, waits for them, and re-layouts  4.3 us (5%)
    pallas_call x3, Pallas kernels, call_on_hbm(): pl.pallas_call(kernel, out_shape=outs, in_specs=[pl.BlockSpec(memory_spac...  11.8 us
    ppermute x9, starting transfers between devices, moved(): return lax.ppermute(x, axis, [(i, (i + by) % size) for i in range(size)])  11.4 us
    ppermute x7, starting transfers between devices, swapped(): lax.ppermute(x, axis, [(i, i ^ bit) for i in range(lax.axis_size(axis))])  11.3 us
    ppermute x9, waiting for transfers between devices, moved(): return lax.ppermute(x, axis, [(i, (i + by) % size) for i in range(size)])  9.23 us
    pallas_call x2, Pallas kernels, attention(): pl.pallas_call(functools.partial(attend_kernel, r), out_shape=shape((half...  5.5 us
    pallas_call x1, Pallas kernels, tails(): pl.pallas_call(tail_kernel, out_shape=shape((PARTS, PAYLOAD, COLS), BF16)...  4.65 us
    all_to_all x1, starting transfers between devices, local(): arrived = lax.all_to_all(payload, PLANE, 0, 0, tiled=True)  4.48 us
    all_to_all x1, starting transfers between devices, local(): memory = lax.all_to_all(memory, PLANE, 0, 0, tiled=True)  3.45 us
  transfers between devices with their start and end apart: 18, of which 6 were waited for; matrix products, arithmetic and copies ran while one was open for 4% of the time, Pallas kernels for 22%

profile of v6, /device:TPU:32, one launch (start us, length us, event | category | flops | bytes accessed | tf_op | source)
XLA Modules:
  0.0 79.0 jit_solution(14634104576722534857)
XLA Ops:
  0.0 4.7 %tail_projection.1.payload.tail_rows = bf16[8,72,384]{2,1,0:T(8,128)(2,1)} custom-call(s32[1]{0:T(128)} %bitcast.2.phase, f32[2,3]{1,0:T(2,128)} %bitcast.11, bf16[512,2560]{1,0:T(8,128)(2,1)} %lat.6, bf16[3,2560,384]{2,1,0:T(8,128)(2,1)} %bitcast.6), custom_call_target="tpu_custom_call" | custom-call | flops 1006632960 | bytes 5500000 | tf_op jit(solution)/shard_map/tail_projection/pallas_call | solution.py:106
  4.7 4.5 %all-to-all-start = ((bf16[8,72,384]{2,1,0:T(8,128)(2,1)}), bf16[8,72,384]{2,1,0:T(8,128)(2,1)S(1)}, u32[]{:S(2)}, u32[]{:S(2)}) async-start(bf16[8,72,384]{2,1,0:T(8,128)(2,1)} %tail_projection.1.payload.tail_rows), calls=%async_computation | async-start | bytes 884736 | tf_op jit(solution)/shard_map/all_to_all | solution.py:468
  9.1 1.2 %fusion = (bf16[192,640]{1,0:T(8,128)(2,1)S(1)}, bf16[192,640]{1,0:T(8,128)(2,1)S(1)}, bf16[192,640]{1,0:T(8,128)(2,1)S(1)}) fusion(bf16[384,2560]{1,0:T(8,128)(2,1)} %param.8, s32[]{:T(128)S(6)} %select_n.21, s32[]{:T(128)S(6)} %select_n.24, s32[]{:T(128)S(6)} %select_n.23, s32[]{:T(128)S(6)} %select_n.22), kind=kLoop, calls=%fused_computation.3 | loop fusion | bytes 1474576 | tf_op jit(solution)/shard_map/dynamic_slice | solution.py:477
  10.4 3.1 %collective-permute-start.6 = (bf16[192,640]{1,0:T(8,128)(2,1)S(1)}, bf16[192,640]{1,0:T(8,128)(2,1)S(1)}, u32[]{:S(2)}, u32[]{:S(2)}) collective-permute-start(bf16[192,640]{1,0:T(8,128)(2,1)S(1)} %get-tuple-element.79), channel_id=1, source_target_pairs={{0,4},{2,6},{4,0},{6,2},{1,5},{3,7},{5,1},{7,3},{8,12},{10,14},{12... | collective-permute-start | bytes 737288 | tf_op jit(solution)/shard_map/ppermute | solution.py:453
  13.5 1.1 %collective-permute-start.5 = (bf16[192,640]{1,0:T(8,128)(2,1)S(1)}, bf16[192,640]{1,0:T(8,128)(2,1)S(1)}, u32[]{:S(2)}, u32[]{:S(2)}) collective-permute-start(bf16[192,640]{1,0:T(8,128)(2,1)S(1)} %get-tuple-element.80), channel_id=1, source_target_pairs={{0,6},{2,0},{4,2},{6,4},{1,7},{3,1},{5,3},{7,5},{8,14},{10,8},{12,... | collective-permute-start | bytes 737288 | tf_op jit(solution)/shard_map/ppermute | solution.py:453
  14.6 0.9 %collective-permute-start.4 = (bf16[192,640]{1,0:T(8,128)(2,1)S(1)}, bf16[192,640]{1,0:T(8,128)(2,1)S(1)}, u32[]{:S(2)}, u32[]{:S(2)}) collective-permute-start(bf16[192,640]{1,0:T(8,128)(2,1)S(1)} %get-tuple-element.81), channel_id=1, source_target_pairs={{0,2},{2,4},{4,6},{6,0},{1,3},{3,5},{5,7},{7,1},{8,10},{10,12},{12... | collective-permute-start | bytes 737288 | tf_op jit(solution)/shard_map/ppermute | solution.py:453
  15.5 2.5 %all-to-all-done.arrived = bf16[8,72,384]{2,1,0:T(8,128)(2,1)S(1)} async-done(((bf16[8,72,384]{2,1,0:T(8,128)(2,1)}), bf16[8,72,384]{2,1,0:T(8,128)(2,1)S(1)}, u32[]{:S(2)}, u32[]{:S(2)}) %all-to-all-start) | async-done | bytes 442400 | tf_op jit(solution)/shard_map/all_to_all | solution.py:468
  18.0 0.2 plane_total.1
  18.2 0.9 %collective-permute-start = (bf16[72,384]{1,0:T(8,128)(2,1)S(1)}, bf16[72,384]{1,0:T(8,128)(2,1)S(1)}, u32[]{:S(2)}, u32[]{:S(2)}) collective-permute-start(bf16[72,384]{1,0:T(8,128)(2,1)S(1)} %get-tuple-element.46), channel_id=1, source_target_pairs={{0,32},{32,0},{64,96},{96,64},{128,160},{160,128},{192,224},{224,1... | collective-permute-start | bytes 165896 | tf_op jit(solution)/shard_map/ppermute | solution.py:457
  19.1 3.5 %head_values.1.values = bf16[256,384]{1,0:T(8,128)(2,1)} custom-call(s32[1]{0:T(128)} %bitcast.1.after.z, bf16[512,2560]{1,0:T(8,128)(2,1)} %lat.6, bf16[3,2560,384]{2,1,0:T(8,128)(2,1)} %bitcast.7), custom_call_target="tpu_custom_call" | custom-call | flops 503316480 | bytes 3300000 | tf_op jit(solution)/shard_map/head_values/pallas_call | solution.py:127
  22.5 0.0 collective-permute-done.got_1
  22.6 3.3 %collective-permute-start.1 = (bf16[72,384]{1,0:T(8,128)(2,1)S(1)}, bf16[72,384]{1,0:T(8,128)(2,1)S(1)}, u32[]{:S(2)}, u32[]{:S(2)}) collective-permute-start(bf16[72,384]{1,0:T(8,128)(2,1)S(1)} %through_1.1), channel_id=1, source_target_pairs={{0,64},{32,96},{64,0},{96,32},{128,192},{160,224},{192,128},{224,1... | collective-permute-start | bytes 165896 | tf_op jit(solution)/shard_map/ppermute | solution.py:457
  25.9 3.7 %head_keys.1 = (bf16[256,384]{1,0:T(8,128)(2,1)}, bf16[64,384]{1,0:T(8,128)(2,1)}) custom-call(s32[1]{0:T(128)} %bitcast.2.phase, bf16[512,2560]{1,0:T(8,128)(2,1)} %lat.6, bf16[3,2560,384]{2,1,0:T(8,128)(2,1)} %bitcast.8, bf16[256,384]{1,0:T(8,128)(2,1)} %head_values.1.values, bf16[8,72,384]{2,1,0:T(8,128)(2,1)} %tail_projection.1.payload.tail_rows), custom_call_target="tpu_custom_call" | custom-call | flops 503316480 | bytes 3300000 | tf_op jit(solution)/shard_map/head_keys/pallas_call | solution.py:127
  29.5 0.0 copy-start.4
  29.6 0.0 collective-permute-done.1.got_2
  29.6 0.1 through_3.1
  29.6 4.4 %collective-permute-start.2 = (bf16[64,384]{1,0:T(8,128)(2,1)S(1)}, bf16[64,384]{1,0:T(8,128)(2,1)S(1)}, u32[]{:S(2)}, u32[]{:S(2)}) collective-permute-start(bf16[64,384]{1,0:T(8,128)(2,1)S(1)} %through_3.1), channel_id=1, source_target_pairs={{0,224},{32,192},{64,160},{96,128},{128,96},{160,64},{192,32},{224... | collective-permute-start | bytes 147464 | tf_op jit(solution)/shard_map/ppermute | solution.py:457
  34.0 1.8 %collective-permute-start.3 = (bf16[64,384]{1,0:T(8,128)(2,1)}, bf16[64,384]{1,0:T(8,128)(2,1)S(1)}, u32[]{:S(2)}, u32[]{:S(2)}) collective-permute-start(bf16[64,384]{1,0:T(8,128)(2,1)} %get-tuple-element.59), channel_id=1, source_target_pairs={{0,1},{1,0},{2,3},{3,2},{4,5},{5,4},{6,7},{7,6},{8,9},{9,8},{10,11... | collective-permute-start | bytes 147464 | tf_op jit(solution)/shard_map/ppermute | solution.py:457
  35.8 1.1 %constant_dynamic-slice_fusion.1.lat = bf16[512,640]{1,0:T(8,128)(2,1)S(1)} fusion(bf16[512,2560]{1,0:T(8,128)(2,1)} %lat.6, s32[]{:T(128)S(6)} %select_n.25), kind=kLoop, calls=%fused_computation.2 | loop fusion | bytes 1310724 | tf_op jit(solution)/shard_map/dynamic_slice | solution.py:505
  37.0 0.0 collective-permute-done.6.w
  37.0 0.0 collective-permute-done.5.w_left
  37.0 0.0 collective-permute-done.4.w_right
  37.0 0.0 collective-permute-done.2.got_4
  37.0 2.8 %collective-permute-done.3.halo = bf16[64,384]{1,0:T(8,128)(2,1)S(1)} collective-permute-done((bf16[64,384]{1,0:T(8,128)(2,1)}, bf16[64,384]{1,0:T(8,128)(2,1)S(1)}, u32[]{:S(2)}, u32[]{:S(2)}) %collective-permute-start.3) | collective-permute-done | bytes 49184 | tf_op jit(solution)/shard_map/ppermute | solution.py:457
  39.8 0.9 %section_memory.1 = bf16[8,64,384]{2,1,0:T(8,128)(2,1)} custom-call(s32[1]{0:T(128)} %bitcast.1.after.z, bf16[72,384]{1,0:T(8,128)(2,1)S(1)} %collective-permute-done.got_1, bf16[72,384]{1,0:T(8,128)(2,1)S(1)} %collective-permute-done.1.got_2, bf16[64,384]{1,0:T(8,128)(2,1)S(1)} %collective-permute-done.2.got_4, bf16[8,72,384]{2,1,0:T(8,128)(2,1)S(1)} %all-to-all-done.arrived), custom_call_target="tpu_custom_call" | custom-call | flops 1000000 | bytes 602116 | tf_op jit(solution)/shard_map/section_memory/pallas_call | solution.py:222
  40.8 3.5 %all-to-all-start.1 = ((bf16[8,64,384]{2,1,0:T(8,128)(2,1)}), bf16[8,64,384]{2,1,0:T(8,128)(2,1)S(1)}, u32[]{:S(2)}, u32[]{:S(2)}) async-start(bf16[8,64,384]{2,1,0:T(8,128)(2,1)} %section_memory.1), calls=%async_computation.1 | async-start | bytes 786432 | tf_op jit(solution)/shard_map/all_to_all | solution.py:511
  44.2 0.4 collective-permute-start.7
  44.6 0.2 collective-permute-start.8
  44.8 0.3 collective-permute-start.9
  45.1 0.0 copy-done.4
  45.2 0.1 pad_dynamic-slice_fusion
  45.2 0.0 copy-start
  45.2 0.0 copy-start.1
  45.2 0.0 copy-start.2
  45.2 4.6 %query_projection.1.q = bf16[512,384]{1,0:T(8,128)(2,1)} custom-call(s32[1]{0:T(128)} %bitcast.1.after.z, bf16[512,2560]{1,0:T(8,128)(2,1)} %lat.6, bf16[3,2560,384]{2,1,0:T(8,128)(2,1)} %bitcast.9), custom_call_target="tpu_custom_call" | custom-call | flops 1006632960 | bytes 4600000 | tf_op jit(solution)/shard_map/query_projection/pallas_call | solution.py:127
  49.9 0.0 collective-permute-done.7.w_right_2
  49.9 0.0 collective-permute-done.8.w_left_2
  49.9 0.0 collective-permute-done.9.w_2
  49.9 2.6 %all-to-all-done.1.memory_in = bf16[8,64,384]{2,1,0:T(8,128)(2,1)S(1)} async-done(((bf16[8,64,384]{2,1,0:T(8,128)(2,1)}), bf16[8,64,384]{2,1,0:T(8,128)(2,1)S(1)}, u32[]{:S(2)}, u32[]{:S(2)}) %all-to-all-start.1) | async-done | bytes 393248 | tf_op jit(solution)/shard_map/all_to_all | solution.py:511
  52.5 0.0 copy-start.3
  52.5 0.1 broadcast_in_dim.2.columns_in
  52.6 0.6 copy-done.3
  53.2 0.0 copy-done
  53.2 0.0 copy-done.1
  53.2 0.0 copy-done.2
  53.3 2.8 %attention_1.1.own = bf16[256,384]{1,0:T(8,128)(2,1)S(1)} custom-call(s32[1]{0:T(128)} %bitcast.2.phase, s32[1,17]{1,0:T(1,128)S(1)} %copy-done.2, bf16[512,384]{1,0:T(8,128)(2,1)} %query_projection.1.q, bf16[256,384]{1,0:T(8,128)(2,1)S(1)} %copy-done.1, bf16[256,384]{1,0:T(8,128)(2,1)S(1)} %copy-done, bf16[8,72,384]{2,1,0:T(8,128)(2,1)} %tail_projection.1.payload.tail_rows, ...), custom_call_target="tpu_custom_call" | custom-call | flops 402653184 | bytes 1500000 | tf_op jit(solution)/shard_map/attention_1/pallas_call | solution.py:380
  56.0 2.8 %collective-permute-start.14 = (bf16[256,384]{1,0:T(8,128)(2,1)S(1)}, bf16[256,384]{1,0:T(8,128)(2,1)S(1)}, u32[]{:S(2)}, u32[]{:S(2)}) collective-permute-start(bf16[256,384]{1,0:T(8,128)(2,1)S(1)} %attention_1.1.own), channel_id=1, source_target_pairs={{0,6},{2,0},{4,2},{6,4},{1,7},{3,1},{5,3},{7,5},{8,14},{10,8},{12,... | collective-permute-start | bytes 589832 | tf_op jit(solution)/shard_map/ppermute | solution.py:453
  58.9 0.0 collective-permute-start.13
  58.9 2.7 %attention_0.1.own = bf16[256,384]{1,0:T(8,128)(2,1)S(1)} custom-call(s32[1]{0:T(128)} %bitcast.2.phase, s32[1,17]{1,0:T(1,128)S(1)} %copy-done.2, bf16[512,384]{1,0:T(8,128)(2,1)} %query_projection.1.q, bf16[256,384]{1,0:T(8,128)(2,1)S(1)} %copy-done.1, bf16[256,384]{1,0:T(8,128)(2,1)S(1)} %copy-done, bf16[8,72,384]{2,1,0:T(8,128)(2,1)} %tail_projection.1.payload.tail_rows, ...), custom_call_target="tpu_custom_call" | custom-call | flops 402653184 | bytes 1500000 | tf_op jit(solution)/shard_map/attention_0/pallas_call | solution.py:380
  61.6 0.8 %collective-permute-start.10 = (bf16[256,384]{1,0:T(8,128)(2,1)S(1)}, bf16[256,384]{1,0:T(8,128)(2,1)S(1)}, u32[]{:S(2)}, u32[]{:S(2)}) collective-permute-start(bf16[256,384]{1,0:T(8,128)(2,1)S(1)} %attention_0.1.own), channel_id=1, source_target_pairs={{0,2},{2,4},{4,6},{6,0},{1,3},{3,5},{5,7},{7,1},{8,10},{10,12},{12... | collective-permute-start | bytes 589832 | tf_op jit(solution)/shard_map/ppermute | solution.py:453
  62.4 2.6 %collective-permute-start.11 = (bf16[256,384]{1,0:T(8,128)(2,1)S(1)}, bf16[256,384]{1,0:T(8,128)(2,1)S(1)}, u32[]{:S(2)}, u32[]{:S(2)}) collective-permute-start(bf16[256,384]{1,0:T(8,128)(2,1)S(1)} %attention_0.1.own), channel_id=1, source_target_pairs={{0,6},{2,0},{4,2},{6,4},{1,7},{3,1},{5,3},{7,5},{8,14},{10,8},{12,... | collective-permute-start | bytes 589832 | tf_op jit(solution)/shard_map/ppermute | solution.py:453
  65.0 0.0 collective-permute-done.14.left
  65.0 2.8 %collective-permute-done.13.right = bf16[256,384]{1,0:T(8,128)(2,1)S(1)} collective-permute-done((bf16[256,384]{1,0:T(8,128)(2,1)S(1)}, bf16[256,384]{1,0:T(8,128)(2,1)S(1)}, u32[]{:S(2)}, u32[]{:S(2)}) %collective-permute-start.13) | collective-permute-done | bytes 196640 | tf_op jit(solution)/shard_map/ppermute | solution.py:453
  67.9 0.0 collective-permute-start.15
  67.9 3.1 %collective-permute-done.10.right = bf16[256,384]{1,0:T(8,128)(2,1)S(1)} collective-permute-done((bf16[256,384]{1,0:T(8,128)(2,1)S(1)}, bf16[256,384]{1,0:T(8,128)(2,1)S(1)}, u32[]{:S(2)}, u32[]{:S(2)}) %collective-permute-start.10) | collective-permute-done | bytes 196640 | tf_op jit(solution)/shard_map/ppermute | solution.py:453
  70.9 0.0 collective-permute-start.12
  70.9 1.1 %constant_dynamic-slice_fusion.w_own = bf16[384,640]{1,0:T(8,128)(2,1)S(1)} fusion(bf16[384,2560]{1,0:T(8,128)(2,1)} %param.8, s32[]{:T(128)S(6)} %select_n.25), kind=kLoop, calls=%fused_computation.1 | loop fusion | bytes 983044 | tf_op jit(solution)/shard_map/dynamic_slice | solution.py:475
  72.0 0.7 near_projection_1.1.total
  72.7 0.0 collective-permute-done.11.left
  72.8 0.7 near_projection_0.1.total
  73.5 0.0 collective-permute-done.15.part
  73.5 1.1 %far_projection_1.1.refs_0_ = bf16[512,640]{1,0:T(8,128)(2,1)} custom-call(s32[1]{0:T(128)} %bitcast.core, f32[256,640]{1,0:T(8,128)S(1)} %near_projection_1.1.total, bf16[256,384]{1,0:T(8,128)(2,1)S(1)} %collective-permute-done.15.part, bf16[192,640]{1,0:T(8,128)(2,1)S(1)} %collective-permute-done.6.w, bf16[192,640]{1,0:T(8,128)(2,1)S(1)} %collective-permute-done.9.w_2), custom_call_target="tpu_custom_call" | custom-call | flops 125829120 | bytes 1500000 | tf_op jit(solution)/shard_map/far_projection_1/pallas_call | solution.py:437
  74.6 3.3 %collective-permute-done.12.part = bf16[256,384]{1,0:T(8,128)(2,1)S(1)} collective-permute-done((bf16[256,384]{1,0:T(8,128)(2,1)S(1)}, bf16[256,384]{1,0:T(8,128)(2,1)S(1)}, u32[]{:S(2)}, u32[]{:S(2)}) %collective-permute-start.12) | collective-permute-done | bytes 196640 | tf_op jit(solution)/shard_map/ppermute | solution.py:453
  77.9 1.1 %far_projection_0.1 = bf16[512,640]{1,0:T(8,128)(2,1)} custom-call(s32[1]{0:T(128)} %bitcast.core, f32[256,640]{1,0:T(8,128)S(1)} %near_projection_0.1.total, bf16[256,384]{1,0:T(8,128)(2,1)S(1)} %collective-permute-done.12.part, bf16[192,640]{1,0:T(8,128)(2,1)S(1)} %collective-permute-done.6.w, ...), custom_call_target="tpu_custom_call", output_to_operand_aliasing={{}: (5, {})} | custom-call | flops 125829120 | bytes 1500000 | tf_op jit(solution)/shard_map/far_projection_0/pallas_call | solution.py:437
  (2 shorter events, 0.1 us)
Async XLA Ops:
  4.7 13.3 %all-to-all-start = ((bf16[8,72,384]{2,1,0:T(8,128)(2,1)}), bf16[8,72,384]{2,1,0:T(8,128)(2,1)S(1)}, u32[]{:S(2)}, u32[]{:S(2)}) async-start(bf16[8,72,384]{2,1,0:T(8,128)(2,1)} %tail_projection.1.payload.tail_rows), calls=%async_computation | async-start | bytes 884736 | tf_op jit(solution)/shard_map/all_to_all | solution.py:468
  10.4 26.6 %collective-permute-start.6 = (bf16[192,640]{1,0:T(8,128)(2,1)S(1)}, bf16[192,640]{1,0:T(8,128)(2,1)S(1)}, u32[]{:S(2)}, u32[]{:S(2)}) collective-permute-start(bf16[192,640]{1,0:T(8,128)(2,1)S(1)} %get-tuple-element.79), channel_id=1, source_target_pairs={{0,4},{2,6},{4,0},{6,2},{1,5},{3,7},{5,1},{7,3},{8,12},{10,14},{12... | collective-permute-start | bytes 737288 | tf_op jit(solution)/shard_map/ppermute | solution.py:453
  13.5 23.5 %collective-permute-start.5 = (bf16[192,640]{1,0:T(8,128)(2,1)S(1)}, bf16[192,640]{1,0:T(8,128)(2,1)S(1)}, u32[]{:S(2)}, u32[]{:S(2)}) collective-permute-start(bf16[192,640]{1,0:T(8,128)(2,1)S(1)} %get-tuple-element.80), channel_id=1, source_target_pairs={{0,6},{2,0},{4,2},{6,4},{1,7},{3,1},{5,3},{7,5},{8,14},{10,8},{12,... | collective-permute-start | bytes 737288 | tf_op jit(solution)/shard_map/ppermute | solution.py:453
  14.6 22.3 %collective-permute-start.4 = (bf16[192,640]{1,0:T(8,128)(2,1)S(1)}, bf16[192,640]{1,0:T(8,128)(2,1)S(1)}, u32[]{:S(2)}, u32[]{:S(2)}) collective-permute-start(bf16[192,640]{1,0:T(8,128)(2,1)S(1)} %get-tuple-element.81), channel_id=1, source_target_pairs={{0,2},{2,4},{4,6},{6,0},{1,3},{3,5},{5,7},{7,1},{8,10},{10,12},{12... | collective-permute-start | bytes 737288 | tf_op jit(solution)/shard_map/ppermute | solution.py:453
  18.2 4.4 %collective-permute-start = (bf16[72,384]{1,0:T(8,128)(2,1)S(1)}, bf16[72,384]{1,0:T(8,128)(2,1)S(1)}, u32[]{:S(2)}, u32[]{:S(2)}) collective-permute-start(bf16[72,384]{1,0:T(8,128)(2,1)S(1)} %get-tuple-element.46), channel_id=1, source_target_pairs={{0,32},{32,0},{64,96},{96,64},{128,160},{160,128},{192,224},{224,1... | collective-permute-start | bytes 165896 | tf_op jit(solution)/shard_map/ppermute | solution.py:457
  22.6 7.0 %collective-permute-start.1 = (bf16[72,384]{1,0:T(8,128)(2,1)S(1)}, bf16[72,384]{1,0:T(8,128)(2,1)S(1)}, u32[]{:S(2)}, u32[]{:S(2)}) collective-permute-start(bf16[72,384]{1,0:T(8,128)(2,1)S(1)} %through_1.1), channel_id=1, source_target_pairs={{0,64},{32,96},{64,0},{96,32},{128,192},{160,224},{192,128},{224,1... | collective-permute-start | bytes 165896 | tf_op jit(solution)/shard_map/ppermute | solution.py:457
  29.5 15.6 %copy-start.4 = (s32[1,1024]{1,0:T(1,128)S(1)}, s32[1,1024]{1,0:T(1,128)}, u32[]{:S(2)}) copy-start(s32[1,1024]{1,0:T(1,128)} %param.10) | copy-start | bytes 12292
  29.6 7.4 %collective-permute-start.2 = (bf16[64,384]{1,0:T(8,128)(2,1)S(1)}, bf16[64,384]{1,0:T(8,128)(2,1)S(1)}, u32[]{:S(2)}, u32[]{:S(2)}) collective-permute-start(bf16[64,384]{1,0:T(8,128)(2,1)S(1)} %through_3.1), channel_id=1, source_target_pairs={{0,224},{32,192},{64,160},{96,128},{128,96},{160,64},{192,32},{224... | collective-permute-start | bytes 147464 | tf_op jit(solution)/shard_map/ppermute | solution.py:457
  34.0 5.8 %collective-permute-start.3 = (bf16[64,384]{1,0:T(8,128)(2,1)}, bf16[64,384]{1,0:T(8,128)(2,1)S(1)}, u32[]{:S(2)}, u32[]{:S(2)}) collective-permute-start(bf16[64,384]{1,0:T(8,128)(2,1)} %get-tuple-element.59), channel_id=1, source_target_pairs={{0,1},{1,0},{2,3},{3,2},{4,5},{5,4},{6,7},{7,6},{8,9},{9,8},{10,11... | collective-permute-start | bytes 147464 | tf_op jit(solution)/shard_map/ppermute | solution.py:457
  40.8 11.7 %all-to-all-start.1 = ((bf16[8,64,384]{2,1,0:T(8,128)(2,1)}), bf16[8,64,384]{2,1,0:T(8,128)(2,1)S(1)}, u32[]{:S(2)}, u32[]{:S(2)}) async-start(bf16[8,64,384]{2,1,0:T(8,128)(2,1)} %section_memory.1), calls=%async_computation.1 | async-start | bytes 786432 | tf_op jit(solution)/shard_map/all_to_all | solution.py:511
  44.2 5.7 %collective-permute-start.7 = (bf16[192,640]{1,0:T(8,128)(2,1)S(1)}, bf16[192,640]{1,0:T(8,128)(2,1)S(1)}, u32[]{:S(2)}, u32[]{:S(2)}) collective-permute-start(bf16[192,640]{1,0:T(8,128)(2,1)S(1)} %collective-permute-done.4.w_right), channel_id=1, source_target_pairs={{0,8},{8,0},{1,9},{9,1},{2,10},{10,2},{3,11},{11,3},{4,12},{12,4},... | collective-permute-start | bytes 737288 | tf_op jit(solution)/shard_map/ppermute | solution.py:457
  44.6 5.3 %collective-permute-start.8 = (bf16[192,640]{1,0:T(8,128)(2,1)S(1)}, bf16[192,640]{1,0:T(8,128)(2,1)S(1)}, u32[]{:S(2)}, u32[]{:S(2)}) collective-permute-start(bf16[192,640]{1,0:T(8,128)(2,1)S(1)} %collective-permute-done.5.w_left), channel_id=1, source_target_pairs={{0,8},{8,0},{1,9},{9,1},{2,10},{10,2},{3,11},{11,3},{4,12},{12,4},... | collective-permute-start | bytes 737288 | tf_op jit(solution)/shard_map/ppermute | solution.py:457
  44.8 5.1 %collective-permute-start.9 = (bf16[192,640]{1,0:T(8,128)(2,1)S(1)}, bf16[192,640]{1,0:T(8,128)(2,1)S(1)}, u32[]{:S(2)}, u32[]{:S(2)}) collective-permute-start(bf16[192,640]{1,0:T(8,128)(2,1)S(1)} %collective-permute-done.6.w), channel_id=1, source_target_pairs={{0,8},{8,0},{1,9},{9,1},{2,10},{10,2},{3,11},{11,3},{4,12},{12,4},... | collective-permute-start | bytes 737288 | tf_op jit(solution)/shard_map/ppermute | solution.py:457
  45.2 8.0 %copy-start = (bf16[256,384]{1,0:T(8,128)(2,1)S(1)}, bf16[256,384]{1,0:T(8,128)(2,1)}, u32[]{:S(2)}) copy-start(bf16[256,384]{1,0:T(8,128)(2,1)} %head_values.1.values) | copy-start | bytes 589828
  45.2 8.0 %copy-start.1 = (bf16[256,384]{1,0:T(8,128)(2,1)S(1)}, bf16[256,384]{1,0:T(8,128)(2,1)}, u32[]{:S(2)}) copy-start(bf16[256,384]{1,0:T(8,128)(2,1)} %get-tuple-element.63.head_keys) | copy-start | bytes 589828
  45.2 8.0 %copy-start.2 = (s32[1,17]{1,0:T(1,128)S(1)}, s32[1,17]{1,0:T(1,128)}, u32[]{:S(2)}) copy-start(s32[1,17]{1,0:T(1,128)} %opened.3) | copy-start | bytes 208
  52.5 0.7 copy-start.3
  56.0 9.0 %collective-permute-start.14 = (bf16[256,384]{1,0:T(8,128)(2,1)S(1)}, bf16[256,384]{1,0:T(8,128)(2,1)S(1)}, u32[]{:S(2)}, u32[]{:S(2)}) collective-permute-start(bf16[256,384]{1,0:T(8,128)(2,1)S(1)} %attention_1.1.own), channel_id=1, source_target_pairs={{0,6},{2,0},{4,2},{6,4},{1,7},{3,1},{5,3},{7,5},{8,14},{10,8},{12,... | collective-permute-start | bytes 589832 | tf_op jit(solution)/shard_map/ppermute | solution.py:453
  58.9 9.0 %collective-permute-start.13 = (bf16[256,384]{1,0:T(8,128)(2,1)S(1)}, bf16[256,384]{1,0:T(8,128)(2,1)S(1)}, u32[]{:S(2)}, u32[]{:S(2)}) collective-permute-start(bf16[256,384]{1,0:T(8,128)(2,1)S(1)} %attention_1.1.own), channel_id=1, source_target_pairs={{0,2},{2,4},{4,6},{6,0},{1,3},{3,5},{5,7},{7,1},{8,10},{10,12},{12... | collective-permute-start | bytes 589832 | tf_op jit(solution)/shard_map/ppermute | solution.py:453
  61.6 9.3 %collective-permute-start.10 = (bf16[256,384]{1,0:T(8,128)(2,1)S(1)}, bf16[256,384]{1,0:T(8,128)(2,1)S(1)}, u32[]{:S(2)}, u32[]{:S(2)}) collective-permute-start(bf16[256,384]{1,0:T(8,128)(2,1)S(1)} %attention_0.1.own), channel_id=1, source_target_pairs={{0,2},{2,4},{4,6},{6,0},{1,3},{3,5},{5,7},{7,1},{8,10},{10,12},{12... | collective-permute-start | bytes 589832 | tf_op jit(solution)/shard_map/ppermute | solution.py:453
  62.4 10.3 %collective-permute-start.11 = (bf16[256,384]{1,0:T(8,128)(2,1)S(1)}, bf16[256,384]{1,0:T(8,128)(2,1)S(1)}, u32[]{:S(2)}, u32[]{:S(2)}) collective-permute-start(bf16[256,384]{1,0:T(8,128)(2,1)S(1)} %attention_0.1.own), channel_id=1, source_target_pairs={{0,6},{2,0},{4,2},{6,4},{1,7},{3,1},{5,3},{7,5},{8,14},{10,8},{12,... | collective-permute-start | bytes 589832 | tf_op jit(solution)/shard_map/ppermute | solution.py:453
  67.9 5.7 %collective-permute-start.15 = (bf16[256,384]{1,0:T(8,128)(2,1)S(1)}, bf16[256,384]{1,0:T(8,128)(2,1)S(1)}, u32[]{:S(2)}, u32[]{:S(2)}) collective-permute-start(bf16[256,384]{1,0:T(8,128)(2,1)S(1)} %collective-permute-done.14.left), channel_id=1, source_target_pairs={{0,6},{2,0},{4,2},{6,4},{1,7},{3,1},{5,3},{7,5},{8,14},{10,8},{12,... | collective-permute-start | bytes 589832 | tf_op jit(solution)/shard_map/ppermute | solution.py:453
  70.9 7.0 %collective-permute-start.12 = (bf16[256,384]{1,0:T(8,128)(2,1)S(1)}, bf16[256,384]{1,0:T(8,128)(2,1)S(1)}, u32[]{:S(2)}, u32[]{:S(2)}) collective-permute-start(bf16[256,384]{1,0:T(8,128)(2,1)S(1)} %collective-permute-done.10.right), channel_id=1, source_target_pairs={{0,2},{2,4},{4,6},{6,0},{1,3},{3,5},{5,7},{7,1},{8,10},{10,12},{12... | collective-permute-start | bytes 589832 | tf_op jit(solution)/shard_map/ppermute | solution.py:453

commit v7 on v6

--- a/solution.py
+++ b/solution.py
@@ -62,14 +62,14 @@
     return wide[0:1] + wide[1:2] + wide[2:3]
 
 
-def tail_kernel(phase, decay, lat, w, out, tail, wkv, acc, sems):
+def project_kernel(phase, decay, lat, w, out, head_keys, head_values, edge, rows, wkv, acc, sems):
     depth = lat.shape[1]
     step = depth // CHUNKS
     copies = []
     for k in range(CHUNKS):
         at = pl.ds(k * step, step)
         group = [
-            pltpu.make_async_copy(lat.at[pl.ds(MEM, MEM), at], tail.at[:, at], sems.at[3 * k]),
+            pltpu.make_async_copy(lat.at[:, at], rows.at[:, at], sems.at[3 * k]),
             pltpu.make_async_copy(w.at[1, at], wkv.at[at, pl.ds(0, COLS)], sems.at[3 * k + 1]),
             pltpu.make_async_copy(w.at[2, at], wkv.at[at, pl.ds(COLS, COLS)], sems.at[3 * k + 2]),
         ]
@@ -80,43 +80,53 @@
         for copy in group:
             copy.wait()
         at = slice(k * step, (k + 1) * step)
-        part = jnp.dot(tail[:, at], wkv[at], preferred_element_type=F32)
+        part = jnp.dot(rows[:, at], wkv[at], preferred_element_type=F32)
         if k == 0:
             acc[...] = part
         else:
             acc[...] += part
     keys = normed(acc[:, :COLS])
     values = acc[:, COLS:].astype(BF16)
+    head_keys[...] = keys[:MEM]
+    head_values[...] = values[:MEM]
     first = phase[0] == 0
+    edge[:PART] = jnp.where(first, keys[ROWS - PART :], keys[:PART])
+    edge[PART:] = jnp.where(first, values[ROWS - PART :], values[:PART])
     rates = [jnp.where(first, decay[0, h], decay[1, h]) for h in range(HEADS)]
     lane = lax.broadcasted_iota(jnp.int32, (1, COLS), 1)
     row = jnp.where(lane < HD, rates[0], jnp.where(lane < 2 * HD, rates[1], rates[2]))
     tile = pieces_of(row)
     for d in range(PARTS):
-        out[d, :PART] = keys[d * PART : (d + 1) * PART]
-        out[d, PART : 2 * PART] = values[d * PART : (d + 1) * PART]
+        at = ROWS - MEM + d * PART
+        out[d, :PART] = keys[at : at + PART]
+        out[d, PART : 2 * PART] = values[at : at + PART]
         out[d, 2 * PART :] = tile
 
 
-def tails(phase, decay, latents, w3):
+def project(phase, decay, latents, w3):
     depth = latents.shape[1]
     smem = pl.BlockSpec(memory_space=pltpu.SMEM)
     vmem = pl.BlockSpec(memory_space=pltpu.VMEM)
     hbm = pl.BlockSpec(memory_space=pl.ANY)
     return pl.pallas_call(
-        tail_kernel,
-        out_shape=shape((PARTS, PAYLOAD, COLS), BF16),
+        project_kernel,
+        out_shape=(
+            shape((PARTS, PAYLOAD, COLS), BF16),
+            shape((MEM, COLS), BF16),
+            shape((MEM, COLS), BF16),
+            shape((2 * PART, COLS), BF16),
+        ),
         in_specs=[smem, smem, hbm, hbm],
-        out_specs=vmem,
+        out_specs=(vmem,) * 4,
         scratch_shapes=[
-            pltpu.VMEM((MEM, depth), BF16),
+            pltpu.VMEM((ROWS, depth), BF16),
             pltpu.VMEM((depth, 2 * COLS), BF16),
-            pltpu.VMEM((MEM, 2 * COLS), F32),
+            pltpu.VMEM((ROWS, 2 * COLS), F32),
             pltpu.SemaphoreType.DMA((3 * CHUNKS,)),
         ],
-        cost_estimate=pl.CostEstimate(flops=2 * MEM * depth * 2 * COLS, bytes_accessed=5500000, transcendentals=0),
+        cost_estimate=pl.CostEstimate(flops=2 * ROWS * depth * 2 * COLS, bytes_accessed=7000000, transcendentals=0),
         compiler_params=pltpu.CompilerParams(vmem_limit_bytes=TAIL_LIMIT),
-        name="tail_projection",
+        name="key_value_projection",
     )(phase, decay, latents, w3)
 
 
@@ -134,54 +144,6 @@
         compiler_params=pltpu.CompilerParams(vmem_limit_bytes=limit),
         name=name,
     )(*args)
-
-
-def head_project(which, lat, w, rows, part, sems):
-    copies = [
-        pltpu.make_async_copy(w.at[which], part, sems.at[0]),
-        pltpu.make_async_copy(lat.at[pl.ds(0, MEM)], rows, sems.at[1]),
-    ]
-    for copy in copies:
-        copy.start()
-    for copy in copies:
-        copy.wait()
-    return jnp.dot(rows[...], part[...], preferred_element_type=F32)
-
-
-def head_values_kernel(after, lat, w, out, rows, part, sems):
-    out[...] = head_project(2, lat, w, rows, part, sems).astype(BF16)
-
-
-def head_keys_kernel(phase, lat, w, values, payload, out, edge, rows, part, first_values, last, sems):
-    copies = [
-        pltpu.make_async_copy(values.at[pl.ds(0, PART)], first_values, sems.at[2]),
-        pltpu.make_async_copy(payload.at[PARTS - 1, pl.ds(0, 2 * PART)], last, sems.at[3]),
-    ]
-    for copy in copies:
-        copy.start()
-    keys = normed(head_project(1, lat, w, rows, part, sems))
-    out[...] = keys
-    for copy in copies:
-        copy.wait()
-    first = phase[0] == 0
-    edge[:PART] = jnp.where(first, last[:PART], keys[:PART])
-    edge[PART:] = jnp.where(first, last[PART:], first_values[...])
-
-
-def heads(kernel, outs, name, after, latents, w3, *more):
-    depth = latents.shape[1]
-    scratch = [pltpu.VMEM((MEM, depth), BF16), pltpu.VMEM((depth, COLS), BF16)]
-    if more:
-        scratch += [pltpu.VMEM((PART, COLS), BF16), pltpu.VMEM((2 * PART, COLS), BF16)]
-    return call_on_hbm(
-        kernel,
-        outs,
-        name,
-        2 * MEM * depth * COLS,
-        3300000,
-        (after, latents, w3, *more),
-        scratch + [pltpu.SemaphoreType.DMA((4,))],
-    )
 
 
 def query_kernel(after, lat, w, out, rows, part, sems):
@@ -464,7 +426,7 @@
     w3 = jnp.transpose(w_qkv, (1, 0, 2))
 
     z_ref = lax.axis_index("z").reshape(1).astype(jnp.int32)
-    payload = tails(phase_ref, decay[0], latents, w3)
+    payload, head_keys, head_values, edge = project(phase_ref, decay[0], latents, w3)
     arrived = lax.all_to_all(payload, PLANE, 0, 0, tiled=True)
 
     w_out, payload = lax.optimization_barrier((w_out, payload))
@@ -472,38 +434,32 @@
     offsets = (0, 1, -1, 2)
     core = lax.axis_index("core")
     deep = COLS // 2
-    own_weight = lax.dynamic_slice_in_dim(w_out, mp * share, share, 1)
     sends = [
         lax.dynamic_slice(w_out, (core * deep, ((mp + by) & 3) * share), (deep, share)) for by in offsets[1:]
     ]
     weights = [moved(piece, "mp", by) for by, piece in zip(offsets[1:], sends)]
-    arrived, _ = lax.optimization_barrier((arrived, sends))
-    half_keys = shape((MEM, COLS), BF16)
+    halo = swapped(edge, "phase", 1)
+    arrived, _, halo = lax.optimization_barrier((arrived, sends, halo))
 
     wide = shape((2 * PART + 8, COLS), F32)
     packed = shape((PAYLOAD, COLS), BF16)
     plain = shape((2 * PART, COLS), BF16)
     plain_all = shape((PARTS, 2 * PART, COLS), BF16)
     own, sent = vmem_call(plane_kernel, (wide, packed), "plane_total", 1000000, (arrived,))
-    after, sent = lax.optimization_barrier((z_ref, sent))
+    latents, sent = lax.optimization_barrier((latents, sent))
     got_1 = swapped(sent, "z", 1)
-    head_values = heads(head_values_kernel, half_keys, "head_values", after, latents, w3)
-    got_1, head_values = lax.optimization_barrier((got_1, head_values))
+    own_columns = lax.dynamic_slice_in_dim(latents, mp * share, share, 1)
+    got_1, own_columns = lax.optimization_barrier((got_1, own_columns))
 
     sent = vmem_call(first_kernel, packed, "through_1", 100000, (z_ref, own, got_1), smem=1)
-    after, sent = lax.optimization_barrier((phase_ref, sent))
+    w_out, sent = lax.optimization_barrier((w_out, sent))
     got_2 = swapped(sent, "z", 2)
-    head_keys, edge = heads(
-        head_keys_kernel, (half_keys, plain), "head_keys", after, latents, w3, head_values, payload
-    )
-    got_2, head_keys, edge = lax.optimization_barrier((got_2, head_keys, edge))
+    own_weight = lax.dynamic_slice_in_dim(w_out, mp * share, share, 1)
+    got_2, own_weight = lax.optimization_barrier((got_2, own_weight))
 
     sent = vmem_call(next_kernel, plain, "through_3", 100000, (z_ref, own, got_1, got_2), smem=1)
-    latents, sent, edge = lax.optimization_barrier((latents, sent, edge))
     got_4 = swapped(sent, "z", 7)
-    halo = swapped(edge, "phase", 1)
-    own_columns = lax.dynamic_slice_in_dim(latents, mp * share, share, 1)
-    got_4, own_columns, halo, weights = lax.optimization_barrier((got_4, own_columns, halo, weights))
+    got_4, weights = lax.optimization_barrier((got_4, weights))
     memory = vmem_call(
         memory_kernel, plain_all, "section_memory", 1000000, (z_ref, got_1, got_2, got_4, arrived), smem=1
     )

time: 79.8 us -> 79.1 us (level)
  Pallas kernels: 26.8 us -> 21.2 us
  starting transfers between devices: 30.6 us -> 34.2 us
  waiting for transfers between devices: 17.1 us -> 19 us
    pallas_call x3 -> x1, Pallas kernels: 11.8 us -> 4.64 us  [call_on_hbm(): pl.pallas_call(kernel, out_shape=outs, in_specs=[pl.BlockSpec(memory_spac...]
    ppermute x7, waiting for transfers between devices: 2.83 us -> 6.03 us  [swapped(): lax.ppermute(x, axis, [(i, i ^ bit) for i in range(lax.axis_size(axis))])]
    ppermute x7, starting transfers between devices: 11.3 us -> 14.3 us  [swapped(): lax.ppermute(x, axis, [(i, i ^ bit) for i in range(lax.axis_size(axis))])]
    all_to_all x1, waiting for transfers between devices: 2.46 us -> 0.01 us  [local(): arrived = lax.all_to_all(payload, PLANE, 0, 0, tiled=True)]
    pallas_call x1, Pallas kernels: 4.65 us -> 6.16 us  [project(): pl.pallas_call(project_kernel, out_shape=(shape((PARTS, PAYLOAD, COLS), B...]
    ppermute x9, waiting for transfers between devices: 9.23 us -> 10.3 us  [moved(): return lax.ppermute(x, axis, [(i, (i + by) % size) for i in range(size)])]
  transfers between devices with their start and end apart: 18 -> 18, of which waited for: 6 -> 9; matrix products, arithmetic and copies ran while one was open for 4% -> 5% of each run, Pallas kernels for 22% -> 13%
where the time goes in v7:
time: 79.1 us; the launch traced here: 78.4 us
  starting transfers between devices  34.2 us (43%)
  Pallas kernels  21.2 us (27%)
  waiting for transfers between devices  19 us (24%)
  local copies, waits for them, and re-layouts  3.69 us (5%)
    ppermute x7, starting transfers between devices, swapped(): lax.ppermute(x, axis, [(i, i ^ bit) for i in range(lax.axis_size(axis))])  14.3 us
    ppermute x9, starting transfers between devices, moved(): return lax.ppermute(x, axis, [(i, (i + by) % size) for i in range(size)])  11.4 us
    ppermute x9, waiting for transfers between devices, moved(): return lax.ppermute(x, axis, [(i, (i + by) % size) for i in range(size)])  10.3 us
    pallas_call x1, Pallas kernels, project(): pl.pallas_call(project_kernel, out_shape=(shape((PARTS, PAYLOAD, COLS), B...  6.16 us
    ppermute x7, waiting for transfers between devices, swapped(): lax.ppermute(x, axis, [(i, i ^ bit) for i in range(lax.axis_size(axis))])  6.03 us
    pallas_call x2, Pallas kernels, attention(): pl.pallas_call(functools.partial(attend_kernel, r), out_shape=shape((half...  5.5 us
    pallas_call x1, Pallas kernels, call_on_hbm(): pl.pallas_call(kernel, out_shape=outs, in_specs=[pl.BlockSpec(memory_spac...  4.64 us
    all_to_all x1, starting transfers between devices, local(): arrived = lax.all_to_all(payload, PLANE, 0, 0, tiled=True)  4.48 us
  transfers between devices with their start and end apart: 18, of which 9 were waited for; matrix products, arithmetic and copies ran while one was open for 5% of the time, Pallas kernels for 13%

profile of v7, /device:TPU:32, one launch (start us, length us, event | category | flops | bytes accessed | tf_op | source)
XLA Modules:
  0.0 78.4 jit_solution(14208642510832791605)
XLA Ops:
  0.0 6.2 %key_value_projection.1 = (bf16[8,72,384]{2,1,0:T(8,128)(2,1)}, bf16[256,384]{1,0:T(8,128)(2,1)}, bf16[256,384]{1,0:T(8,128)(2,1)}, bf16[64,384]{1,0:T(8,128)(2,1)}) custom-call(s32[1]{0:T(128)} %bitcast.1.phase, f32[2,3]{1,0:T(2,128)} %bitcast.9, bf16[512,2560]{1,0:T(8,128)(2,1)} %lat.2, bf16[3,2560,384]{2,1,0:T(8,128)(2,1)} %bitcast.6), custom_call_target="tpu_custom_call" | custom-call | flops 2013265920 | bytes 7000000 | tf_op jit(solution)/shard_map/key_value_projection/pallas_call | solution.py:111
  6.2 4.5 %all-to-all-start = ((bf16[8,72,384]{2,1,0:T(8,128)(2,1)}), bf16[8,72,384]{2,1,0:T(8,128)(2,1)S(1)}, u32[]{:S(2)}, u32[]{:S(2)}) async-start(bf16[8,72,384]{2,1,0:T(8,128)(2,1)} %get-tuple-element.56.tail_rows), calls=%async_computation | async-start | bytes 884736 | tf_op jit(solution)/shard_map/all_to_all | solution.py:430
  10.7 3.5 %collective-permute-start = (bf16[64,384]{1,0:T(8,128)(2,1)}, bf16[64,384]{1,0:T(8,128)(2,1)S(1)}, u32[]{:S(2)}, u32[]{:S(2)}) collective-permute-start(bf16[64,384]{1,0:T(8,128)(2,1)} %get-tuple-element.41), channel_id=1, source_target_pairs={{0,1},{1,0},{2,3},{3,2},{4,5},{5,4},{6,7},{7,6},{8,9},{9,8},{10,11... | collective-permute-start | bytes 147464 | tf_op jit(solution)/shard_map/ppermute | solution.py:419
  14.2 1.2 %fusion = (bf16[192,640]{1,0:T(8,128)(2,1)S(1)}, bf16[192,640]{1,0:T(8,128)(2,1)S(1)}, bf16[192,640]{1,0:T(8,128)(2,1)S(1)}) fusion(bf16[384,2560]{1,0:T(8,128)(2,1)} %param.8, s32[]{:T(128)S(6)} %select_n.21, s32[]{:T(128)S(6)} %select_n.24, s32[]{:T(128)S(6)} %select_n.23, s32[]{:T(128)S(6)} %select_n.22), kind=kLoop, calls=%fused_computation.3 | loop fusion | bytes 1474576 | tf_op jit(solution)/shard_map/dynamic_slice | solution.py:438
  15.4 0.0 copy-start.3
  15.4 3.1 %collective-permute-start.6 = (bf16[192,640]{1,0:T(8,128)(2,1)S(1)}, bf16[192,640]{1,0:T(8,128)(2,1)S(1)}, u32[]{:S(2)}, u32[]{:S(2)}) collective-permute-start(bf16[192,640]{1,0:T(8,128)(2,1)S(1)} %get-tuple-element.73), channel_id=1, source_target_pairs={{0,4},{2,6},{4,0},{6,2},{1,5},{3,7},{5,1},{7,3},{8,12},{10,14},{12... | collective-permute-start | bytes 737288 | tf_op jit(solution)/shard_map/ppermute | solution.py:415
  18.6 1.1 %collective-permute-start.5 = (bf16[192,640]{1,0:T(8,128)(2,1)S(1)}, bf16[192,640]{1,0:T(8,128)(2,1)S(1)}, u32[]{:S(2)}, u32[]{:S(2)}) collective-permute-start(bf16[192,640]{1,0:T(8,128)(2,1)S(1)} %get-tuple-element.74), channel_id=1, source_target_pairs={{0,6},{2,0},{4,2},{6,4},{1,7},{3,1},{5,3},{7,5},{8,14},{10,8},{12,... | collective-permute-start | bytes 737288 | tf_op jit(solution)/shard_map/ppermute | solution.py:415
  19.7 0.9 %collective-permute-start.4 = (bf16[192,640]{1,0:T(8,128)(2,1)S(1)}, bf16[192,640]{1,0:T(8,128)(2,1)S(1)}, u32[]{:S(2)}, u32[]{:S(2)}) collective-permute-start(bf16[192,640]{1,0:T(8,128)(2,1)S(1)} %get-tuple-element.75), channel_id=1, source_target_pairs={{0,2},{2,4},{4,6},{6,0},{1,3},{3,5},{5,7},{7,1},{8,10},{10,12},{12... | collective-permute-start | bytes 737288 | tf_op jit(solution)/shard_map/ppermute | solution.py:415
  20.6 0.6 collective-permute-done.halo
  21.2 0.0 all-to-all-done.arrived
  21.2 0.2 plane_total.1
  21.4 0.8 %collective-permute-start.1 = (bf16[72,384]{1,0:T(8,128)(2,1)S(1)}, bf16[72,384]{1,0:T(8,128)(2,1)S(1)}, u32[]{:S(2)}, u32[]{:S(2)}) collective-permute-start(bf16[72,384]{1,0:T(8,128)(2,1)S(1)} %get-tuple-element.44), channel_id=1, source_target_pairs={{0,32},{32,0},{64,96},{96,64},{128,160},{160,128},{192,224},{224,1... | collective-permute-start | bytes 165896 | tf_op jit(solution)/shard_map/ppermute | solution.py:419
  22.2 1.1 %constant_dynamic-slice_fusion.1.lat = bf16[512,640]{1,0:T(8,128)(2,1)S(1)} fusion(bf16[512,2560]{1,0:T(8,128)(2,1)} %lat.2, s32[]{:T(128)S(6)} %select_n.25), kind=kLoop, calls=%fused_computation.2 | loop fusion | bytes 1310724 | tf_op jit(solution)/shard_map/dynamic_slice | solution.py:451
  23.3 2.3 %collective-permute-done.1.got_1 = bf16[72,384]{1,0:T(8,128)(2,1)S(1)} collective-permute-done((bf16[72,384]{1,0:T(8,128)(2,1)S(1)}, bf16[72,384]{1,0:T(8,128)(2,1)S(1)}, u32[]{:S(2)}, u32[]{:S(2)}) %collective-permute-start.1) | collective-permute-done | bytes 55328 | tf_op jit(solution)/shard_map/ppermute | solution.py:419
  25.6 3.4 %collective-permute-start.2 = (bf16[72,384]{1,0:T(8,128)(2,1)S(1)}, bf16[72,384]{1,0:T(8,128)(2,1)S(1)}, u32[]{:S(2)}, u32[]{:S(2)}) collective-permute-start(bf16[72,384]{1,0:T(8,128)(2,1)S(1)} %through_1.1), channel_id=1, source_target_pairs={{0,64},{32,96},{64,0},{96,32},{128,192},{160,224},{192,128},{224,1... | collective-permute-start | bytes 165896 | tf_op jit(solution)/shard_map/ppermute | solution.py:419
  29.0 1.1 %constant_dynamic-slice_fusion.w_own = bf16[384,640]{1,0:T(8,128)(2,1)S(1)} fusion(bf16[384,2560]{1,0:T(8,128)(2,1)} %param.8, s32[]{:T(128)S(6)} %select_n.25), kind=kLoop, calls=%fused_computation.1 | loop fusion | bytes 983044 | tf_op jit(solution)/shard_map/dynamic_slice | solution.py:457
  30.1 1.1 %collective-permute-done.2.got_2 = bf16[72,384]{1,0:T(8,128)(2,1)S(1)} collective-permute-done((bf16[72,384]{1,0:T(8,128)(2,1)S(1)}, bf16[72,384]{1,0:T(8,128)(2,1)S(1)}, u32[]{:S(2)}, u32[]{:S(2)}) %collective-permute-start.2) | collective-permute-done | bytes 55328 | tf_op jit(solution)/shard_map/ppermute | solution.py:419
  31.1 0.1 through_3.1
  31.2 5.7 %collective-permute-start.3 = (bf16[64,384]{1,0:T(8,128)(2,1)S(1)}, bf16[64,384]{1,0:T(8,128)(2,1)S(1)}, u32[]{:S(2)}, u32[]{:S(2)}) collective-permute-start(bf16[64,384]{1,0:T(8,128)(2,1)S(1)} %through_3.1), channel_id=1, source_target_pairs={{0,224},{32,192},{64,160},{96,128},{128,96},{160,64},{192,32},{224... | collective-permute-start | bytes 147464 | tf_op jit(solution)/shard_map/ppermute | solution.py:419
  36.9 0.0 collective-permute-done.6.w
  36.9 0.0 collective-permute-done.5.w_left
  36.9 0.0 collective-permute-done.4.w_right
  36.9 2.1 %collective-permute-done.3.got_4 = bf16[64,384]{1,0:T(8,128)(2,1)S(1)} collective-permute-done((bf16[64,384]{1,0:T(8,128)(2,1)S(1)}, bf16[64,384]{1,0:T(8,128)(2,1)S(1)}, u32[]{:S(2)}, u32[]{:S(2)}) %collective-permute-start.3) | collective-permute-done | bytes 49184 | tf_op jit(solution)/shard_map/ppermute | solution.py:419
  39.0 1.0 %section_memory.1 = bf16[8,64,384]{2,1,0:T(8,128)(2,1)} custom-call(s32[1]{0:T(128)} %bitcast.4.z.after, bf16[72,384]{1,0:T(8,128)(2,1)S(1)} %collective-permute-done.1.got_1, bf16[72,384]{1,0:T(8,128)(2,1)S(1)} %collective-permute-done.2.got_2, bf16[64,384]{1,0:T(8,128)(2,1)S(1)} %collective-permute-done.3.got_4, bf16[8,72,384]{2,1,0:T(8,128)(2,1)S(1)} %all-to-all-done.arrived), custom_call_target="tpu_custom_call" | custom-call | flops 1000000 | bytes 602116 | tf_op jit(solution)/shard_map/section_memory/pallas_call | solution.py:184
  40.0 4.1 %all-to-all-start.1 = ((bf16[8,64,384]{2,1,0:T(8,128)(2,1)}), bf16[8,64,384]{2,1,0:T(8,128)(2,1)}, u32[]{:S(2)}, u32[]{:S(2)}) async-start(bf16[8,64,384]{2,1,0:T(8,128)(2,1)} %section_memory.1), calls=%async_computation.1 | async-start | bytes 786432 | tf_op jit(solution)/shard_map/all_to_all | solution.py:467
  44.1 0.4 collective-permute-start.7
  44.4 0.2 collective-permute-start.8
  44.7 0.3 collective-permute-start.9
  45.0 0.0 copy-done.3
  45.0 0.1 pad_dynamic-slice_fusion
  45.0 0.0 copy-start
  45.0 0.0 copy-start.1
  45.1 0.0 copy-start.2
  45.1 4.6 %query_projection.1.q = bf16[512,384]{1,0:T(8,128)(2,1)} custom-call(s32[1]{0:T(128)} %bitcast.4.z.after, bf16[512,2560]{1,0:T(8,128)(2,1)} %lat.2, bf16[3,2560,384]{2,1,0:T(8,128)(2,1)} %bitcast.7), custom_call_target="tpu_custom_call" | custom-call | flops 1006632960 | bytes 4600000 | tf_op jit(solution)/shard_map/query_projection/pallas_call | solution.py:137
  49.7 0.0 collective-permute-done.7.w_right_2
  49.7 0.0 collective-permute-done.8.w_left_2
  49.7 0.0 collective-permute-done.9.w_2
  49.7 2.7 %all-to-all-done.1.memory_in = bf16[8,64,384]{2,1,0:T(8,128)(2,1)} async-done(((bf16[8,64,384]{2,1,0:T(8,128)(2,1)}), bf16[8,64,384]{2,1,0:T(8,128)(2,1)}, u32[]{:S(2)}, u32[]{:S(2)}) %all-to-all-start.1) | async-done | bytes 393248 | tf_op jit(solution)/shard_map/all_to_all | solution.py:467
  52.4 0.1 broadcast_in_dim.2.columns_in
  52.6 0.0 copy-done
  52.6 0.0 copy-done.1
  52.6 0.0 copy-done.2
  52.6 2.8 %attention_1.1.own = bf16[256,384]{1,0:T(8,128)(2,1)S(1)} custom-call(s32[1]{0:T(128)} %bitcast.1.phase, s32[1,17]{1,0:T(1,128)S(1)} %copy-done.2, bf16[512,384]{1,0:T(8,128)(2,1)} %query_projection.1.q, bf16[256,384]{1,0:T(8,128)(2,1)S(1)} %copy-done, bf16[256,384]{1,0:T(8,128)(2,1)S(1)} %copy-done.1, bf16[8,72,384]{2,1,0:T(8,128)(2,1)} %get-tuple-element.56.tail_rows, ...), custom_call_target="tpu_custom_call" | custom-call | flops 402653184 | bytes 1500000 | tf_op jit(solution)/shard_map/attention_1/pallas_call | solution.py:342
  55.4 2.8 %collective-permute-start.14 = (bf16[256,384]{1,0:T(8,128)(2,1)S(1)}, bf16[256,384]{1,0:T(8,128)(2,1)S(1)}, u32[]{:S(2)}, u32[]{:S(2)}) collective-permute-start(bf16[256,384]{1,0:T(8,128)(2,1)S(1)} %attention_1.1.own), channel_id=1, source_target_pairs={{0,6},{2,0},{4,2},{6,4},{1,7},{3,1},{5,3},{7,5},{8,14},{10,8},{12,... | collective-permute-start | bytes 589832 | tf_op jit(solution)/shard_map/ppermute | solution.py:415
  58.2 0.0 collective-permute-start.13
  58.2 2.7 %attention_0.1.own = bf16[256,384]{1,0:T(8,128)(2,1)S(1)} custom-call(s32[1]{0:T(128)} %bitcast.1.phase, s32[1,17]{1,0:T(1,128)S(1)} %copy-done.2, bf16[512,384]{1,0:T(8,128)(2,1)} %query_projection.1.q, bf16[256,384]{1,0:T(8,128)(2,1)S(1)} %copy-done, bf16[256,384]{1,0:T(8,128)(2,1)S(1)} %copy-done.1, bf16[8,72,384]{2,1,0:T(8,128)(2,1)} %get-tuple-element.56.tail_rows, ...), custom_call_target="tpu_custom_call" | custom-call | flops 402653184 | bytes 1500000 | tf_op jit(solution)/shard_map/attention_0/pallas_call | solution.py:342
  60.9 0.8 %collective-permute-start.10 = (bf16[256,384]{1,0:T(8,128)(2,1)S(1)}, bf16[256,384]{1,0:T(8,128)(2,1)S(1)}, u32[]{:S(2)}, u32[]{:S(2)}) collective-permute-start(bf16[256,384]{1,0:T(8,128)(2,1)S(1)} %attention_0.1.own), channel_id=1, source_target_pairs={{0,2},{2,4},{4,6},{6,0},{1,3},{3,5},{5,7},{7,1},{8,10},{10,12},{12... | collective-permute-start | bytes 589832 | tf_op jit(solution)/shard_map/ppermute | solution.py:415
  61.8 2.6 %collective-permute-start.11 = (bf16[256,384]{1,0:T(8,128)(2,1)S(1)}, bf16[256,384]{1,0:T(8,128)(2,1)S(1)}, u32[]{:S(2)}, u32[]{:S(2)}) collective-permute-start(bf16[256,384]{1,0:T(8,128)(2,1)S(1)} %attention_0.1.own), channel_id=1, source_target_pairs={{0,6},{2,0},{4,2},{6,4},{1,7},{3,1},{5,3},{7,5},{8,14},{10,8},{12,... | collective-permute-start | bytes 589832 | tf_op jit(solution)/shard_map/ppermute | solution.py:415
  64.3 0.0 collective-permute-done.14.left
  64.3 2.8 %collective-permute-done.13.right = bf16[256,384]{1,0:T(8,128)(2,1)S(1)} collective-permute-done((bf16[256,384]{1,0:T(8,128)(2,1)S(1)}, bf16[256,384]{1,0:T(8,128)(2,1)S(1)}, u32[]{:S(2)}, u32[]{:S(2)}) %collective-permute-start.13) | collective-permute-done | bytes 196640 | tf_op jit(solution)/shard_map/ppermute | solution.py:415
  67.2 0.0 collective-permute-start.15
  67.2 3.1 %collective-permute-done.10.right = bf16[256,384]{1,0:T(8,128)(2,1)S(1)} collective-permute-done((bf16[256,384]{1,0:T(8,128)(2,1)S(1)}, bf16[256,384]{1,0:T(8,128)(2,1)S(1)}, u32[]{:S(2)}, u32[]{:S(2)}) %collective-permute-start.10) | collective-permute-done | bytes 196640 | tf_op jit(solution)/shard_map/ppermute | solution.py:415
  70.3 0.0 collective-permute-start.12
  70.3 0.7 near_projection_1.1.total
  71.0 0.0 collective-permute-done.11.left
  71.0 0.7 near_projection_0.1.total
  71.7 1.1 %collective-permute-done.15.part = bf16[256,384]{1,0:T(8,128)(2,1)S(1)} collective-permute-done((bf16[256,384]{1,0:T(8,128)(2,1)S(1)}, bf16[256,384]{1,0:T(8,128)(2,1)S(1)}, u32[]{:S(2)}, u32[]{:S(2)}) %collective-permute-start.15) | collective-permute-done | bytes 196640 | tf_op jit(solution)/shard_map/ppermute | solution.py:415
  72.9 1.1 %far_projection_1.1.refs_0_ = bf16[512,640]{1,0:T(8,128)(2,1)} custom-call(s32[1]{0:T(128)} %bitcast.core, f32[256,640]{1,0:T(8,128)S(1)} %near_projection_1.1.total, bf16[256,384]{1,0:T(8,128)(2,1)S(1)} %collective-permute-done.15.part, bf16[192,640]{1,0:T(8,128)(2,1)S(1)} %collective-permute-done.6.w, bf16[192,640]{1,0:T(8,128)(2,1)S(1)} %collective-permute-done.9.w_2), custom_call_target="tpu_custom_call" | custom-call | flops 125829120 | bytes 1500000 | tf_op jit(solution)/shard_map/far_projection_1/pallas_call | solution.py:399
  74.0 3.3 %collective-permute-done.12.part = bf16[256,384]{1,0:T(8,128)(2,1)S(1)} collective-permute-done((bf16[256,384]{1,0:T(8,128)(2,1)S(1)}, bf16[256,384]{1,0:T(8,128)(2,1)S(1)}, u32[]{:S(2)}, u32[]{:S(2)}) %collective-permute-start.12) | collective-permute-done | bytes 196640 | tf_op jit(solution)/shard_map/ppermute | solution.py:415
  77.2 1.1 %far_projection_0.1 = bf16[512,640]{1,0:T(8,128)(2,1)} custom-call(s32[1]{0:T(128)} %bitcast.core, f32[256,640]{1,0:T(8,128)S(1)} %near_projection_0.1.total, bf16[256,384]{1,0:T(8,128)(2,1)S(1)} %collective-permute-done.12.part, bf16[192,640]{1,0:T(8,128)(2,1)S(1)} %collective-permute-done.6.w, ...), custom_call_target="tpu_custom_call", output_to_operand_aliasing={{}: (5, {})} | custom-call | flops 125829120 | bytes 1500000 | tf_op jit(solution)/shard_map/far_projection_0/pallas_call | solution.py:399
  (2 shorter events, 0.0 us)
Async XLA Ops:
  6.2 15.0 %all-to-all-start = ((bf16[8,72,384]{2,1,0:T(8,128)(2,1)}), bf16[8,72,384]{2,1,0:T(8,128)(2,1)S(1)}, u32[]{:S(2)}, u32[]{:S(2)}) async-start(bf16[8,72,384]{2,1,0:T(8,128)(2,1)} %get-tuple-element.56.tail_rows), calls=%async_computation | async-start | bytes 884736 | tf_op jit(solution)/shard_map/all_to_all | solution.py:430
  10.7 10.5 %collective-permute-start = (bf16[64,384]{1,0:T(8,128)(2,1)}, bf16[64,384]{1,0:T(8,128)(2,1)S(1)}, u32[]{:S(2)}, u32[]{:S(2)}) collective-permute-start(bf16[64,384]{1,0:T(8,128)(2,1)} %get-tuple-element.41), channel_id=1, source_target_pairs={{0,1},{1,0},{2,3},{3,2},{4,5},{5,4},{6,7},{7,6},{8,9},{9,8},{10,11... | collective-permute-start | bytes 147464 | tf_op jit(solution)/shard_map/ppermute | solution.py:419
  15.4 29.5 %copy-start.3 = (s32[1,1024]{1,0:T(1,128)S(1)}, s32[1,1024]{1,0:T(1,128)}, u32[]{:S(2)}) copy-start(s32[1,1024]{1,0:T(1,128)} %param.10) | copy-start | bytes 12292
  15.4 21.4 %collective-permute-start.6 = (bf16[192,640]{1,0:T(8,128)(2,1)S(1)}, bf16[192,640]{1,0:T(8,128)(2,1)S(1)}, u32[]{:S(2)}, u32[]{:S(2)}) collective-permute-start(bf16[192,640]{1,0:T(8,128)(2,1)S(1)} %get-tuple-element.73), channel_id=1, source_target_pairs={{0,4},{2,6},{4,0},{6,2},{1,5},{3,7},{5,1},{7,3},{8,12},{10,14},{12... | collective-permute-start | bytes 737288 | tf_op jit(solution)/shard_map/ppermute | solution.py:415
  18.6 18.3 %collective-permute-start.5 = (bf16[192,640]{1,0:T(8,128)(2,1)S(1)}, bf16[192,640]{1,0:T(8,128)(2,1)S(1)}, u32[]{:S(2)}, u32[]{:S(2)}) collective-permute-start(bf16[192,640]{1,0:T(8,128)(2,1)S(1)} %get-tuple-element.74), channel_id=1, source_target_pairs={{0,6},{2,0},{4,2},{6,4},{1,7},{3,1},{5,3},{7,5},{8,14},{10,8},{12,... | collective-permute-start | bytes 737288 | tf_op jit(solution)/shard_map/ppermute | solution.py:415
  19.7 17.2 %collective-permute-start.4 = (bf16[192,640]{1,0:T(8,128)(2,1)S(1)}, bf16[192,640]{1,0:T(8,128)(2,1)S(1)}, u32[]{:S(2)}, u32[]{:S(2)}) collective-permute-start(bf16[192,640]{1,0:T(8,128)(2,1)S(1)} %get-tuple-element.75), channel_id=1, source_target_pairs={{0,2},{2,4},{4,6},{6,0},{1,3},{3,5},{5,7},{7,1},{8,10},{10,12},{12... | collective-permute-start | bytes 737288 | tf_op jit(solution)/shard_map/ppermute | solution.py:415
  21.4 4.2 %collective-permute-start.1 = (bf16[72,384]{1,0:T(8,128)(2,1)S(1)}, bf16[72,384]{1,0:T(8,128)(2,1)S(1)}, u32[]{:S(2)}, u32[]{:S(2)}) collective-permute-start(bf16[72,384]{1,0:T(8,128)(2,1)S(1)} %get-tuple-element.44), channel_id=1, source_target_pairs={{0,32},{32,0},{64,96},{96,64},{128,160},{160,128},{192,224},{224,1... | collective-permute-start | bytes 165896 | tf_op jit(solution)/shard_map/ppermute | solution.py:419
  25.6 5.5 %collective-permute-start.2 = (bf16[72,384]{1,0:T(8,128)(2,1)S(1)}, bf16[72,384]{1,0:T(8,128)(2,1)S(1)}, u32[]{:S(2)}, u32[]{:S(2)}) collective-permute-start(bf16[72,384]{1,0:T(8,128)(2,1)S(1)} %through_1.1), channel_id=1, source_target_pairs={{0,64},{32,96},{64,0},{96,32},{128,192},{160,224},{192,128},{224,1... | collective-permute-start | bytes 165896 | tf_op jit(solution)/shard_map/ppermute | solution.py:419
  31.2 7.8 %collective-permute-start.3 = (bf16[64,384]{1,0:T(8,128)(2,1)S(1)}, bf16[64,384]{1,0:T(8,128)(2,1)S(1)}, u32[]{:S(2)}, u32[]{:S(2)}) collective-permute-start(bf16[64,384]{1,0:T(8,128)(2,1)S(1)} %through_3.1), channel_id=1, source_target_pairs={{0,224},{32,192},{64,160},{96,128},{128,96},{160,64},{192,32},{224... | collective-permute-start | bytes 147464 | tf_op jit(solution)/shard_map/ppermute | solution.py:419
  40.0 12.5 %all-to-all-start.1 = ((bf16[8,64,384]{2,1,0:T(8,128)(2,1)}), bf16[8,64,384]{2,1,0:T(8,128)(2,1)}, u32[]{:S(2)}, u32[]{:S(2)}) async-start(bf16[8,64,384]{2,1,0:T(8,128)(2,1)} %section_memory.1), calls=%async_computation.1 | async-start | bytes 786432 | tf_op jit(solution)/shard_map/all_to_all | solution.py:467
  44.1 5.6 %collective-permute-start.7 = (bf16[192,640]{1,0:T(8,128)(2,1)S(1)}, bf16[192,640]{1,0:T(8,128)(2,1)S(1)}, u32[]{:S(2)}, u32[]{:S(2)}) collective-permute-start(bf16[192,640]{1,0:T(8,128)(2,1)S(1)} %collective-permute-done.4.w_right), channel_id=1, source_target_pairs={{0,8},{8,0},{1,9},{9,1},{2,10},{10,2},{3,11},{11,3},{4,12},{12,4},... | collective-permute-start | bytes 737288 | tf_op jit(solution)/shard_map/ppermute | solution.py:419
  44.4 5.3 %collective-permute-start.8 = (bf16[192,640]{1,0:T(8,128)(2,1)S(1)}, bf16[192,640]{1,0:T(8,128)(2,1)S(1)}, u32[]{:S(2)}, u32[]{:S(2)}) collective-permute-start(bf16[192,640]{1,0:T(8,128)(2,1)S(1)} %collective-permute-done.5.w_left), channel_id=1, source_target_pairs={{0,8},{8,0},{1,9},{9,1},{2,10},{10,2},{3,11},{11,3},{4,12},{12,4},... | collective-permute-start | bytes 737288 | tf_op jit(solution)/shard_map/ppermute | solution.py:419
  44.7 5.1 %collective-permute-start.9 = (bf16[192,640]{1,0:T(8,128)(2,1)S(1)}, bf16[192,640]{1,0:T(8,128)(2,1)S(1)}, u32[]{:S(2)}, u32[]{:S(2)}) collective-permute-start(bf16[192,640]{1,0:T(8,128)(2,1)S(1)} %collective-permute-done.6.w), channel_id=1, source_target_pairs={{0,8},{8,0},{1,9},{9,1},{2,10},{10,2},{3,11},{11,3},{4,12},{12,4},... | collective-permute-start | bytes 737288 | tf_op jit(solution)/shard_map/ppermute | solution.py:419
  45.0 7.5 %copy-start = (bf16[256,384]{1,0:T(8,128)(2,1)S(1)}, bf16[256,384]{1,0:T(8,128)(2,1)}, u32[]{:S(2)}) copy-start(bf16[256,384]{1,0:T(8,128)(2,1)} %get-tuple-element.54.head_keys) | copy-start | bytes 589828
  45.0 7.5 %copy-start.1 = (bf16[256,384]{1,0:T(8,128)(2,1)S(1)}, bf16[256,384]{1,0:T(8,128)(2,1)}, u32[]{:S(2)}) copy-start(bf16[256,384]{1,0:T(8,128)(2,1)} %get-tuple-element.55.head_values) | copy-start | bytes 589828
  45.1 7.5 %copy-start.2 = (s32[1,17]{1,0:T(1,128)S(1)}, s32[1,17]{1,0:T(1,128)}, u32[]{:S(2)}) copy-start(s32[1,17]{1,0:T(1,128)} %opened.3) | copy-start | bytes 208
  55.4 9.0 %collective-permute-start.14 = (bf16[256,384]{1,0:T(8,128)(2,1)S(1)}, bf16[256,384]{1,0:T(8,128)(2,1)S(1)}, u32[]{:S(2)}, u32[]{:S(2)}) collective-permute-start(bf16[256,384]{1,0:T(8,128)(2,1)S(1)} %attention_1.1.own), channel_id=1, source_target_pairs={{0,6},{2,0},{4,2},{6,4},{1,7},{3,1},{5,3},{7,5},{8,14},{10,8},{12,... | collective-permute-start | bytes 589832 | tf_op jit(solution)/shard_map/ppermute | solution.py:415
  58.2 9.0 %collective-permute-start.13 = (bf16[256,384]{1,0:T(8,128)(2,1)S(1)}, bf16[256,384]{1,0:T(8,128)(2,1)S(1)}, u32[]{:S(2)}, u32[]{:S(2)}) collective-permute-start(bf16[256,384]{1,0:T(8,128)(2,1)S(1)} %attention_1.1.own), channel_id=1, source_target_pairs={{0,2},{2,4},{4,6},{6,0},{1,3},{3,5},{5,7},{7,1},{8,10},{10,12},{12... | collective-permute-start | bytes 589832 | tf_op jit(solution)/shard_map/ppermute | solution.py:415
  60.9 9.3 %collective-permute-start.10 = (bf16[256,384]{1,0:T(8,128)(2,1)S(1)}, bf16[256,384]{1,0:T(8,128)(2,1)S(1)}, u32[]{:S(2)}, u32[]{:S(2)}) collective-permute-start(bf16[256,384]{1,0:T(8,128)(2,1)S(1)} %attention_0.1.own), channel_id=1, source_target_pairs={{0,2},{2,4},{4,6},{6,0},{1,3},{3,5},{5,7},{7,1},{8,10},{10,12},{12... | collective-permute-start | bytes 589832 | tf_op jit(solution)/shard_map/ppermute | solution.py:415
  61.8 9.2 %collective-permute-start.11 = (bf16[256,384]{1,0:T(8,128)(2,1)S(1)}, bf16[256,384]{1,0:T(8,128)(2,1)S(1)}, u32[]{:S(2)}, u32[]{:S(2)}) collective-permute-start(bf16[256,384]{1,0:T(8,128)(2,1)S(1)} %attention_0.1.own), channel_id=1, source_target_pairs={{0,6},{2,0},{4,2},{6,4},{1,7},{3,1},{5,3},{7,5},{8,14},{10,8},{12,... | collective-permute-start | bytes 589832 | tf_op jit(solution)/shard_map/ppermute | solution.py:415
  67.2 5.7 %collective-permute-start.15 = (bf16[256,384]{1,0:T(8,128)(2,1)S(1)}, bf16[256,384]{1,0:T(8,128)(2,1)S(1)}, u32[]{:S(2)}, u32[]{:S(2)}) collective-permute-start(bf16[256,384]{1,0:T(8,128)(2,1)S(1)} %collective-permute-done.14.left), channel_id=1, source_target_pairs={{0,6},{2,0},{4,2},{6,4},{1,7},{3,1},{5,3},{7,5},{8,14},{10,8},{12,... | collective-permute-start | bytes 589832 | tf_op jit(solution)/shard_map/ppermute | solution.py:415
  70.3 7.0 %collective-permute-start.12 = (bf16[256,384]{1,0:T(8,128)(2,1)S(1)}, bf16[256,384]{1,0:T(8,128)(2,1)S(1)}, u32[]{:S(2)}, u32[]{:S(2)}) collective-permute-start(bf16[256,384]{1,0:T(8,128)(2,1)S(1)} %collective-permute-done.10.right), channel_id=1, source_target_pairs={{0,2},{2,4},{4,6},{6,0},{1,3},{3,5},{5,7},{7,1},{8,10},{10,12},{12... | collective-permute-start | bytes 589832 | tf_op jit(solution)/shard_map/ppermute | solution.py:415

commit v8 on v7

--- a/solution.py
+++ b/solution.py
@@ -439,7 +439,7 @@
     ]
     weights = [moved(piece, "mp", by) for by, piece in zip(offsets[1:], sends)]
     halo = swapped(edge, "phase", 1)
-    arrived, _, halo = lax.optimization_barrier((arrived, sends, halo))
+    arrived, _ = lax.optimization_barrier((arrived, sends))
 
     wide = shape((2 * PART + 8, COLS), F32)
     packed = shape((PAYLOAD, COLS), BF16)
@@ -455,10 +455,10 @@
     w_out, sent = lax.optimization_barrier((w_out, sent))
     got_2 = swapped(sent, "z", 2)
     own_weight = lax.dynamic_slice_in_dim(w_out, mp * share, share, 1)
-    got_2, own_weight = lax.optimization_barrier((got_2, own_weight))
+    got_2, own_weight, halo = lax.optimization_barrier((got_2, own_weight, halo))
 
     sent = vmem_call(next_kernel, plain, "through_3", 100000, (z_ref, own, got_1, got_2), smem=1)
-    got_4 = swapped(sent, "z", 7)
+    got_4 = lax.ppermute(sent, "z", [(i, 7 - i) for i in range(4)])
     got_4, weights = lax.optimization_barrier((got_4, weights))
     memory = vmem_call(
         memory_kernel, plain_all, "section_memory", 1000000, (z_ref, got_1, got_2, got_4, arrived), smem=1

time: 79.1 us -> 79.4 us (level)
  starting transfers between devices: 34.2 us -> 35.2 us
    ppermute x0 -> x1, starting transfers between devices: none -> 7.51 us  [local(): got_4 = lax.ppermute(sent, 'z', [(i, 7 - i) for i in range(4)])]
    ppermute x7 -> x6, starting transfers between devices: 14.3 us -> 7.97 us  [swapped(): lax.ppermute(x, axis, [(i, i ^ bit) for i in range(lax.axis_size(axis))])]
    ppermute x7 -> x6, waiting for transfers between devices: 6.03 us -> 3.96 us  [swapped(): lax.ppermute(x, axis, [(i, i ^ bit) for i in range(lax.axis_size(axis))])]
    ppermute x0 -> x1, waiting for transfers between devices: none -> 1.7 us  [local(): got_4 = lax.ppermute(sent, 'z', [(i, 7 - i) for i in range(4)])]
  transfers between devices with their start and end apart: 18 -> 18, of which waited for: 9 -> 8; matrix products, arithmetic and copies ran while one was open for 5% -> 4% of each run, Pallas kernels for 13% -> 13%
where the time goes in v8:
time: 79.4 us; the launch traced here: 79 us
  starting transfers between devices  35.2 us (44%)
  Pallas kernels  21.2 us (27%)
  waiting for transfers between devices  18.7 us (24%)
  local copies, waits for them, and re-layouts  3.69 us (5%)
    ppermute x9, starting transfers between devices, moved(): return lax.ppermute(x, axis, [(i, (i + by) % size) for i in range(size)])  11.2 us
    ppermute x9, waiting for transfers between devices, moved(): return lax.ppermute(x, axis, [(i, (i + by) % size) for i in range(size)])  10.3 us
    ppermute x6, starting transfers between devices, swapped(): lax.ppermute(x, axis, [(i, i ^ bit) for i in range(lax.axis_size(axis))])  7.97 us
    ppermute x1, starting transfers between devices, local(): got_4 = lax.ppermute(sent, 'z', [(i, 7 - i) for i in range(4)])  7.51 us
    pallas_call x1, Pallas kernels, project(): pl.pallas_call(project_kernel, out_shape=(shape((PARTS, PAYLOAD, COLS), B...  6.16 us
    pallas_call x2, Pallas kernels, attention(): pl.pallas_call(functools.partial(attend_kernel, r), out_shape=shape((half...  5.5 us
    pallas_call x1, Pallas kernels, call_on_hbm(): pl.pallas_call(kernel, out_shape=outs, in_specs=[pl.BlockSpec(memory_spac...  4.64 us
    all_to_all x1, starting transfers between devices, local(): arrived = lax.all_to_all(payload, PLANE, 0, 0, tiled=True)  4.48 us
  transfers between devices with their start and end apart: 18, of which 8 were waited for; matrix products, arithmetic and copies ran while one was open for 4% of the time, Pallas kernels for 13%

profile of v8, /device:TPU:32, one launch (start us, length us, event | category | flops | bytes accessed | tf_op | source)
XLA Modules:
  0.0 79.0 jit_solution(697055897896960387)
XLA Ops:
  0.0 6.2 %key_value_projection.1 = (bf16[8,72,384]{2,1,0:T(8,128)(2,1)}, bf16[256,384]{1,0:T(8,128)(2,1)}, bf16[256,384]{1,0:T(8,128)(2,1)}, bf16[64,384]{1,0:T(8,128)(2,1)}) custom-call(s32[1]{0:T(128)} %bitcast.1.phase, f32[2,3]{1,0:T(2,128)} %bitcast.9, bf16[512,2560]{1,0:T(8,128)(2,1)} %lat.2, bf16[3,2560,384]{2,1,0:T(8,128)(2,1)} %bitcast.6), custom_call_target="tpu_custom_call" | custom-call | flops 2013265920 | bytes 7000000 | tf_op jit(solution)/shard_map/key_value_projection/pallas_call | solution.py:111
  6.2 4.5 %all-to-all-start = ((bf16[8,72,384]{2,1,0:T(8,128)(2,1)}), bf16[8,72,384]{2,1,0:T(8,128)(2,1)S(1)}, u32[]{:S(2)}, u32[]{:S(2)}) async-start(bf16[8,72,384]{2,1,0:T(8,128)(2,1)} %get-tuple-element.56.tail_rows), calls=%async_computation | async-start | bytes 884736 | tf_op jit(solution)/shard_map/all_to_all | solution.py:430
  10.7 3.5 %collective-permute-start.2 = (bf16[64,384]{1,0:T(8,128)(2,1)}, bf16[64,384]{1,0:T(8,128)(2,1)S(1)}, u32[]{:S(2)}, u32[]{:S(2)}) collective-permute-start(bf16[64,384]{1,0:T(8,128)(2,1)} %get-tuple-element.50), channel_id=1, source_target_pairs={{0,1},{1,0},{2,3},{3,2},{4,5},{5,4},{6,7},{7,6},{8,9},{9,8},{10,11... | collective-permute-start | bytes 147464 | tf_op jit(solution)/shard_map/ppermute | solution.py:419
  14.2 1.2 %fusion = (bf16[192,640]{1,0:T(8,128)(2,1)S(1)}, bf16[192,640]{1,0:T(8,128)(2,1)S(1)}, bf16[192,640]{1,0:T(8,128)(2,1)S(1)}) fusion(bf16[384,2560]{1,0:T(8,128)(2,1)} %param.8, s32[]{:T(128)S(6)} %select_n.21, s32[]{:T(128)S(6)} %select_n.24, s32[]{:T(128)S(6)} %select_n.23, s32[]{:T(128)S(6)} %select_n.22), kind=kLoop, calls=%fused_computation.3 | loop fusion | bytes 1474576 | tf_op jit(solution)/shard_map/dynamic_slice | solution.py:438
  15.4 0.0 copy-start.3
  15.4 3.1 %collective-permute-start.6 = (bf16[192,640]{1,0:T(8,128)(2,1)S(1)}, bf16[192,640]{1,0:T(8,128)(2,1)S(1)}, u32[]{:S(2)}, u32[]{:S(2)}) collective-permute-start(bf16[192,640]{1,0:T(8,128)(2,1)S(1)} %get-tuple-element.73), channel_id=1, source_target_pairs={{0,4},{2,6},{4,0},{6,2},{1,5},{3,7},{5,1},{7,3},{8,12},{10,14},{12... | collective-permute-start | bytes 737288 | tf_op jit(solution)/shard_map/ppermute | solution.py:415
  18.6 1.1 %collective-permute-start.5 = (bf16[192,640]{1,0:T(8,128)(2,1)S(1)}, bf16[192,640]{1,0:T(8,128)(2,1)S(1)}, u32[]{:S(2)}, u32[]{:S(2)}) collective-permute-start(bf16[192,640]{1,0:T(8,128)(2,1)S(1)} %get-tuple-element.74), channel_id=1, source_target_pairs={{0,6},{2,0},{4,2},{6,4},{1,7},{3,1},{5,3},{7,5},{8,14},{10,8},{12,... | collective-permute-start | bytes 737288 | tf_op jit(solution)/shard_map/ppermute | solution.py:415
  19.7 0.9 %collective-permute-start.4 = (bf16[192,640]{1,0:T(8,128)(2,1)S(1)}, bf16[192,640]{1,0:T(8,128)(2,1)S(1)}, u32[]{:S(2)}, u32[]{:S(2)}) collective-permute-start(bf16[192,640]{1,0:T(8,128)(2,1)S(1)} %get-tuple-element.75), channel_id=1, source_target_pairs={{0,2},{2,4},{4,6},{6,0},{1,3},{3,5},{5,7},{7,1},{8,10},{10,12},{12... | collective-permute-start | bytes 737288 | tf_op jit(solution)/shard_map/ppermute | solution.py:415
  20.6 0.0 all-to-all-done.arrived
  20.6 0.2 plane_total.1
  20.8 0.2 collective-permute-start
  21.0 1.1 %constant_dynamic-slice_fusion.1.lat = bf16[512,640]{1,0:T(8,128)(2,1)S(1)} fusion(bf16[512,2560]{1,0:T(8,128)(2,1)} %lat.2, s32[]{:T(128)S(6)} %select_n.25), kind=kLoop, calls=%fused_computation.2 | loop fusion | bytes 1310724 | tf_op jit(solution)/shard_map/dynamic_slice | solution.py:451
  22.1 2.9 %collective-permute-done.got_1 = bf16[72,384]{1,0:T(8,128)(2,1)S(1)} collective-permute-done((bf16[72,384]{1,0:T(8,128)(2,1)S(1)}, bf16[72,384]{1,0:T(8,128)(2,1)S(1)}, u32[]{:S(2)}, u32[]{:S(2)}) %collective-permute-start) | collective-permute-done | bytes 55328 | tf_op jit(solution)/shard_map/ppermute | solution.py:419
  25.1 3.4 %collective-permute-start.1 = (bf16[72,384]{1,0:T(8,128)(2,1)S(1)}, bf16[72,384]{1,0:T(8,128)(2,1)S(1)}, u32[]{:S(2)}, u32[]{:S(2)}) collective-permute-start(bf16[72,384]{1,0:T(8,128)(2,1)S(1)} %through_1.1), channel_id=1, source_target_pairs={{0,64},{32,96},{64,0},{96,32},{128,192},{160,224},{192,128},{224,1... | collective-permute-start | bytes 165896 | tf_op jit(solution)/shard_map/ppermute | solution.py:419
  28.4 1.1 %constant_dynamic-slice_fusion.w_own = bf16[384,640]{1,0:T(8,128)(2,1)S(1)} fusion(bf16[384,2560]{1,0:T(8,128)(2,1)} %param.8, s32[]{:T(128)S(6)} %select_n.25), kind=kLoop, calls=%fused_computation.1 | loop fusion | bytes 983044 | tf_op jit(solution)/shard_map/dynamic_slice | solution.py:457
  29.5 0.0 collective-permute-done.2.halo
  29.5 1.0 %collective-permute-done.1.got_2 = bf16[72,384]{1,0:T(8,128)(2,1)S(1)} collective-permute-done((bf16[72,384]{1,0:T(8,128)(2,1)S(1)}, bf16[72,384]{1,0:T(8,128)(2,1)S(1)}, u32[]{:S(2)}, u32[]{:S(2)}) %collective-permute-start.1) | collective-permute-done | bytes 55328 | tf_op jit(solution)/shard_map/ppermute | solution.py:419
  30.5 0.1 through_3.1
  30.6 7.5 %collective-permute-start.3 = (bf16[64,384]{1,0:T(8,128)(2,1)S(1)}, bf16[64,384]{1,0:T(8,128)(2,1)S(1)}, u32[]{:S(2)}, u32[]{:S(2)}) collective-permute-start(bf16[64,384]{1,0:T(8,128)(2,1)S(1)} %through_3.1), channel_id=1, source_target_pairs={{0,224},{32,192},{64,160},{96,128},{1,225},{33,193},{65,161},{97,1... | collective-permute-start | bytes 147464 | tf_op jit(solution)/shard_map/ppermute | solution.py:461
  38.1 0.0 collective-permute-done.6.w
  38.1 0.0 collective-permute-done.5.w_left
  38.1 0.0 collective-permute-done.4.w_right
  38.1 1.7 %collective-permute-done.3.got_4 = bf16[64,384]{1,0:T(8,128)(2,1)S(1)} collective-permute-done((bf16[64,384]{1,0:T(8,128)(2,1)S(1)}, bf16[64,384]{1,0:T(8,128)(2,1)S(1)}, u32[]{:S(2)}, u32[]{:S(2)}) %collective-permute-start.3) | collective-permute-done | bytes 49184 | tf_op jit(solution)/shard_map/ppermute | solution.py:461
  39.8 1.0 %section_memory.1 = bf16[8,64,384]{2,1,0:T(8,128)(2,1)} custom-call(s32[1]{0:T(128)} %bitcast.4.z.after, bf16[72,384]{1,0:T(8,128)(2,1)S(1)} %collective-permute-done.got_1, bf16[72,384]{1,0:T(8,128)(2,1)S(1)} %collective-permute-done.1.got_2, bf16[64,384]{1,0:T(8,128)(2,1)S(1)} %collective-permute-done.3.got_4, bf16[8,72,384]{2,1,0:T(8,128)(2,1)S(1)} %all-to-all-done.arrived), custom_call_target="tpu_custom_call" | custom-call | flops 1000000 | bytes 602116 | tf_op jit(solution)/shard_map/section_memory/pallas_call | solution.py:184
  40.8 4.1 %all-to-all-start.1 = ((bf16[8,64,384]{2,1,0:T(8,128)(2,1)}), bf16[8,64,384]{2,1,0:T(8,128)(2,1)}, u32[]{:S(2)}, u32[]{:S(2)}) async-start(bf16[8,64,384]{2,1,0:T(8,128)(2,1)} %section_memory.1), calls=%async_computation.1 | async-start | bytes 786432 | tf_op jit(solution)/shard_map/all_to_all | solution.py:467
  44.9 0.4 collective-permute-start.7
  45.3 0.2 collective-permute-start.8
  45.5 0.3 collective-permute-start.9
  45.8 0.0 copy-done.3
  45.8 0.1 pad_dynamic-slice_fusion
  45.9 0.0 copy-start
  45.9 0.0 copy-start.1
  45.9 0.0 copy-start.2
  45.9 4.6 %query_projection.1.q = bf16[512,384]{1,0:T(8,128)(2,1)} custom-call(s32[1]{0:T(128)} %bitcast.4.z.after, bf16[512,2560]{1,0:T(8,128)(2,1)} %lat.2, bf16[3,2560,384]{2,1,0:T(8,128)(2,1)} %bitcast.7), custom_call_target="tpu_custom_call" | custom-call | flops 1006632960 | bytes 4600000 | tf_op jit(solution)/shard_map/query_projection/pallas_call | solution.py:137
  50.5 0.0 collective-permute-done.7.w_right_2
  50.6 0.0 collective-permute-done.8.w_left_2
  50.6 0.0 collective-permute-done.9.w_2
  50.6 2.7 %all-to-all-done.1.memory_in = bf16[8,64,384]{2,1,0:T(8,128)(2,1)} async-done(((bf16[8,64,384]{2,1,0:T(8,128)(2,1)}), bf16[8,64,384]{2,1,0:T(8,128)(2,1)}, u32[]{:S(2)}, u32[]{:S(2)}) %all-to-all-start.1) | async-done | bytes 393248 | tf_op jit(solution)/shard_map/all_to_all | solution.py:467
  53.3 0.1 broadcast_in_dim.2.columns_in
  53.4 0.0 copy-done
  53.4 0.0 copy-done.1
  53.4 0.0 copy-done.2
  53.4 2.8 %attention_1.1.own = bf16[256,384]{1,0:T(8,128)(2,1)S(1)} custom-call(s32[1]{0:T(128)} %bitcast.1.phase, s32[1,17]{1,0:T(1,128)S(1)} %copy-done.2, bf16[512,384]{1,0:T(8,128)(2,1)} %query_projection.1.q, bf16[256,384]{1,0:T(8,128)(2,1)S(1)} %copy-done, bf16[256,384]{1,0:T(8,128)(2,1)S(1)} %copy-done.1, bf16[8,72,384]{2,1,0:T(8,128)(2,1)} %get-tuple-element.56.tail_rows, ...), custom_call_target="tpu_custom_call" | custom-call | flops 402653184 | bytes 1500000 | tf_op jit(solution)/shard_map/attention_1/pallas_call | solution.py:342
  56.2 2.6 %collective-permute-start.14 = (bf16[256,384]{1,0:T(8,128)(2,1)S(1)}, bf16[256,384]{1,0:T(8,128)(2,1)S(1)}, u32[]{:S(2)}, u32[]{:S(2)}) collective-permute-start(bf16[256,384]{1,0:T(8,128)(2,1)S(1)} %attention_1.1.own), channel_id=1, source_target_pairs={{0,6},{2,0},{4,2},{6,4},{1,7},{3,1},{5,3},{7,5},{8,14},{10,8},{12,... | collective-permute-start | bytes 589832 | tf_op jit(solution)/shard_map/ppermute | solution.py:415
  58.8 0.0 collective-permute-start.13
  58.8 2.7 %attention_0.1.own = bf16[256,384]{1,0:T(8,128)(2,1)S(1)} custom-call(s32[1]{0:T(128)} %bitcast.1.phase, s32[1,17]{1,0:T(1,128)S(1)} %copy-done.2, bf16[512,384]{1,0:T(8,128)(2,1)} %query_projection.1.q, bf16[256,384]{1,0:T(8,128)(2,1)S(1)} %copy-done, bf16[256,384]{1,0:T(8,128)(2,1)S(1)} %copy-done.1, bf16[8,72,384]{2,1,0:T(8,128)(2,1)} %get-tuple-element.56.tail_rows, ...), custom_call_target="tpu_custom_call" | custom-call | flops 402653184 | bytes 1500000 | tf_op jit(solution)/shard_map/attention_0/pallas_call | solution.py:342
  61.6 0.3 collective-permute-start.10
  61.9 3.1 %collective-permute-start.11 = (bf16[256,384]{1,0:T(8,128)(2,1)S(1)}, bf16[256,384]{1,0:T(8,128)(2,1)S(1)}, u32[]{:S(2)}, u32[]{:S(2)}) collective-permute-start(bf16[256,384]{1,0:T(8,128)(2,1)S(1)} %attention_0.1.own), channel_id=1, source_target_pairs={{0,6},{2,0},{4,2},{6,4},{1,7},{3,1},{5,3},{7,5},{8,14},{10,8},{12,... | collective-permute-start | bytes 589832 | tf_op jit(solution)/shard_map/ppermute | solution.py:415
  65.0 0.0 collective-permute-done.14.left
  65.0 2.8 %collective-permute-done.13.right = bf16[256,384]{1,0:T(8,128)(2,1)S(1)} collective-permute-done((bf16[256,384]{1,0:T(8,128)(2,1)S(1)}, bf16[256,384]{1,0:T(8,128)(2,1)S(1)}, u32[]{:S(2)}, u32[]{:S(2)}) %collective-permute-start.13) | collective-permute-done | bytes 196640 | tf_op jit(solution)/shard_map/ppermute | solution.py:415
  67.8 0.0 collective-permute-start.15
  67.8 3.1 %collective-permute-done.10.right = bf16[256,384]{1,0:T(8,128)(2,1)S(1)} collective-permute-done((bf16[256,384]{1,0:T(8,128)(2,1)S(1)}, bf16[256,384]{1,0:T(8,128)(2,1)S(1)}, u32[]{:S(2)}, u32[]{:S(2)}) %collective-permute-start.10) | collective-permute-done | bytes 196640 | tf_op jit(solution)/shard_map/ppermute | solution.py:415
  70.9 0.0 collective-permute-start.12
  70.9 0.7 near_projection_1.1.total
  71.6 0.0 collective-permute-done.11.left
  71.6 0.7 near_projection_0.1.total
  72.4 1.1 %collective-permute-done.15.part = bf16[256,384]{1,0:T(8,128)(2,1)S(1)} collective-permute-done((bf16[256,384]{1,0:T(8,128)(2,1)S(1)}, bf16[256,384]{1,0:T(8,128)(2,1)S(1)}, u32[]{:S(2)}, u32[]{:S(2)}) %collective-permute-start.15) | collective-permute-done | bytes 196640 | tf_op jit(solution)/shard_map/ppermute | solution.py:415
  73.5 1.1 %far_projection_1.1.refs_0_ = bf16[512,640]{1,0:T(8,128)(2,1)} custom-call(s32[1]{0:T(128)} %bitcast.core, f32[256,640]{1,0:T(8,128)S(1)} %near_projection_1.1.total, bf16[256,384]{1,0:T(8,128)(2,1)S(1)} %collective-permute-done.15.part, bf16[192,640]{1,0:T(8,128)(2,1)S(1)} %collective-permute-done.6.w, bf16[192,640]{1,0:T(8,128)(2,1)S(1)} %collective-permute-done.9.w_2), custom_call_target="tpu_custom_call" | custom-call | flops 125829120 | bytes 1500000 | tf_op jit(solution)/shard_map/far_projection_1/pallas_call | solution.py:399
  74.6 3.3 %collective-permute-done.12.part = bf16[256,384]{1,0:T(8,128)(2,1)S(1)} collective-permute-done((bf16[256,384]{1,0:T(8,128)(2,1)S(1)}, bf16[256,384]{1,0:T(8,128)(2,1)S(1)}, u32[]{:S(2)}, u32[]{:S(2)}) %collective-permute-start.12) | collective-permute-done | bytes 196640 | tf_op jit(solution)/shard_map/ppermute | solution.py:415
  77.9 1.1 %far_projection_0.1 = bf16[512,640]{1,0:T(8,128)(2,1)} custom-call(s32[1]{0:T(128)} %bitcast.core, f32[256,640]{1,0:T(8,128)S(1)} %near_projection_0.1.total, bf16[256,384]{1,0:T(8,128)(2,1)S(1)} %collective-permute-done.12.part, bf16[192,640]{1,0:T(8,128)(2,1)S(1)} %collective-permute-done.6.w, ...), custom_call_target="tpu_custom_call", output_to_operand_aliasing={{}: (5, {})} | custom-call | flops 125829120 | bytes 1500000 | tf_op jit(solution)/shard_map/far_projection_0/pallas_call | solution.py:399
  (2 shorter events, 0.0 us)
Async XLA Ops:
  6.2 14.4 %all-to-all-start = ((bf16[8,72,384]{2,1,0:T(8,128)(2,1)}), bf16[8,72,384]{2,1,0:T(8,128)(2,1)S(1)}, u32[]{:S(2)}, u32[]{:S(2)}) async-start(bf16[8,72,384]{2,1,0:T(8,128)(2,1)} %get-tuple-element.56.tail_rows), calls=%async_computation | async-start | bytes 884736 | tf_op jit(solution)/shard_map/all_to_all | solution.py:430
  10.7 18.8 %collective-permute-start.2 = (bf16[64,384]{1,0:T(8,128)(2,1)}, bf16[64,384]{1,0:T(8,128)(2,1)S(1)}, u32[]{:S(2)}, u32[]{:S(2)}) collective-permute-start(bf16[64,384]{1,0:T(8,128)(2,1)} %get-tuple-element.50), channel_id=1, source_target_pairs={{0,1},{1,0},{2,3},{3,2},{4,5},{5,4},{6,7},{7,6},{8,9},{9,8},{10,11... | collective-permute-start | bytes 147464 | tf_op jit(solution)/shard_map/ppermute | solution.py:419
  15.4 30.4 %copy-start.3 = (s32[1,1024]{1,0:T(1,128)S(1)}, s32[1,1024]{1,0:T(1,128)}, u32[]{:S(2)}) copy-start(s32[1,1024]{1,0:T(1,128)} %param.10) | copy-start | bytes 12292
  15.4 22.7 %collective-permute-start.6 = (bf16[192,640]{1,0:T(8,128)(2,1)S(1)}, bf16[192,640]{1,0:T(8,128)(2,1)S(1)}, u32[]{:S(2)}, u32[]{:S(2)}) collective-permute-start(bf16[192,640]{1,0:T(8,128)(2,1)S(1)} %get-tuple-element.73), channel_id=1, source_target_pairs={{0,4},{2,6},{4,0},{6,2},{1,5},{3,7},{5,1},{7,3},{8,12},{10,14},{12... | collective-permute-start | bytes 737288 | tf_op jit(solution)/shard_map/ppermute | solution.py:415
  18.6 19.6 %collective-permute-start.5 = (bf16[192,640]{1,0:T(8,128)(2,1)S(1)}, bf16[192,640]{1,0:T(8,128)(2,1)S(1)}, u32[]{:S(2)}, u32[]{:S(2)}) collective-permute-start(bf16[192,640]{1,0:T(8,128)(2,1)S(1)} %get-tuple-element.74), channel_id=1, source_target_pairs={{0,6},{2,0},{4,2},{6,4},{1,7},{3,1},{5,3},{7,5},{8,14},{10,8},{12,... | collective-permute-start | bytes 737288 | tf_op jit(solution)/shard_map/ppermute | solution.py:415
  19.7 18.4 %collective-permute-start.4 = (bf16[192,640]{1,0:T(8,128)(2,1)S(1)}, bf16[192,640]{1,0:T(8,128)(2,1)S(1)}, u32[]{:S(2)}, u32[]{:S(2)}) collective-permute-start(bf16[192,640]{1,0:T(8,128)(2,1)S(1)} %get-tuple-element.75), channel_id=1, source_target_pairs={{0,2},{2,4},{4,6},{6,0},{1,3},{3,5},{5,7},{7,1},{8,10},{10,12},{12... | collective-permute-start | bytes 737288 | tf_op jit(solution)/shard_map/ppermute | solution.py:415
  20.8 4.2 %collective-permute-start = (bf16[72,384]{1,0:T(8,128)(2,1)S(1)}, bf16[72,384]{1,0:T(8,128)(2,1)S(1)}, u32[]{:S(2)}, u32[]{:S(2)}) collective-permute-start(bf16[72,384]{1,0:T(8,128)(2,1)S(1)} %get-tuple-element.43), channel_id=1, source_target_pairs={{0,32},{32,0},{64,96},{96,64},{128,160},{160,128},{192,224},{224,1... | collective-permute-start | bytes 165896 | tf_op jit(solution)/shard_map/ppermute | solution.py:419
  25.1 5.5 %collective-permute-start.1 = (bf16[72,384]{1,0:T(8,128)(2,1)S(1)}, bf16[72,384]{1,0:T(8,128)(2,1)S(1)}, u32[]{:S(2)}, u32[]{:S(2)}) collective-permute-start(bf16[72,384]{1,0:T(8,128)(2,1)S(1)} %through_1.1), channel_id=1, source_target_pairs={{0,64},{32,96},{64,0},{96,32},{128,192},{160,224},{192,128},{224,1... | collective-permute-start | bytes 165896 | tf_op jit(solution)/shard_map/ppermute | solution.py:419
  30.6 9.2 %collective-permute-start.3 = (bf16[64,384]{1,0:T(8,128)(2,1)S(1)}, bf16[64,384]{1,0:T(8,128)(2,1)S(1)}, u32[]{:S(2)}, u32[]{:S(2)}) collective-permute-start(bf16[64,384]{1,0:T(8,128)(2,1)S(1)} %through_3.1), channel_id=1, source_target_pairs={{0,224},{32,192},{64,160},{96,128},{1,225},{33,193},{65,161},{97,1... | collective-permute-start | bytes 147464 | tf_op jit(solution)/shard_map/ppermute | solution.py:461
  40.8 12.5 %all-to-all-start.1 = ((bf16[8,64,384]{2,1,0:T(8,128)(2,1)}), bf16[8,64,384]{2,1,0:T(8,128)(2,1)}, u32[]{:S(2)}, u32[]{:S(2)}) async-start(bf16[8,64,384]{2,1,0:T(8,128)(2,1)} %section_memory.1), calls=%async_computation.1 | async-start | bytes 786432 | tf_op jit(solution)/shard_map/all_to_all | solution.py:467
  44.9 5.6 %collective-permute-start.7 = (bf16[192,640]{1,0:T(8,128)(2,1)S(1)}, bf16[192,640]{1,0:T(8,128)(2,1)S(1)}, u32[]{:S(2)}, u32[]{:S(2)}) collective-permute-start(bf16[192,640]{1,0:T(8,128)(2,1)S(1)} %collective-permute-done.4.w_right), channel_id=1, source_target_pairs={{0,8},{8,0},{1,9},{9,1},{2,10},{10,2},{3,11},{11,3},{4,12},{12,4},... | collective-permute-start | bytes 737288 | tf_op jit(solution)/shard_map/ppermute | solution.py:419
  45.3 5.3 %collective-permute-start.8 = (bf16[192,640]{1,0:T(8,128)(2,1)S(1)}, bf16[192,640]{1,0:T(8,128)(2,1)S(1)}, u32[]{:S(2)}, u32[]{:S(2)}) collective-permute-start(bf16[192,640]{1,0:T(8,128)(2,1)S(1)} %collective-permute-done.5.w_left), channel_id=1, source_target_pairs={{0,8},{8,0},{1,9},{9,1},{2,10},{10,2},{3,11},{11,3},{4,12},{12,4},... | collective-permute-start | bytes 737288 | tf_op jit(solution)/shard_map/ppermute | solution.py:419
  45.5 5.1 %collective-permute-start.9 = (bf16[192,640]{1,0:T(8,128)(2,1)S(1)}, bf16[192,640]{1,0:T(8,128)(2,1)S(1)}, u32[]{:S(2)}, u32[]{:S(2)}) collective-permute-start(bf16[192,640]{1,0:T(8,128)(2,1)S(1)} %collective-permute-done.6.w), channel_id=1, source_target_pairs={{0,8},{8,0},{1,9},{9,1},{2,10},{10,2},{3,11},{11,3},{4,12},{12,4},... | collective-permute-start | bytes 737288 | tf_op jit(solution)/shard_map/ppermute | solution.py:419
  45.9 7.5 %copy-start = (bf16[256,384]{1,0:T(8,128)(2,1)S(1)}, bf16[256,384]{1,0:T(8,128)(2,1)}, u32[]{:S(2)}) copy-start(bf16[256,384]{1,0:T(8,128)(2,1)} %get-tuple-element.54.head_keys) | copy-start | bytes 589828
  45.9 7.5 %copy-start.1 = (bf16[256,384]{1,0:T(8,128)(2,1)S(1)}, bf16[256,384]{1,0:T(8,128)(2,1)}, u32[]{:S(2)}) copy-start(bf16[256,384]{1,0:T(8,128)(2,1)} %get-tuple-element.55.head_values) | copy-start | bytes 589828
  45.9 7.5 %copy-start.2 = (s32[1,17]{1,0:T(1,128)S(1)}, s32[1,17]{1,0:T(1,128)}, u32[]{:S(2)}) copy-start(s32[1,17]{1,0:T(1,128)} %opened.3) | copy-start | bytes 208
  56.2 8.8 %collective-permute-start.14 = (bf16[256,384]{1,0:T(8,128)(2,1)S(1)}, bf16[256,384]{1,0:T(8,128)(2,1)S(1)}, u32[]{:S(2)}, u32[]{:S(2)}) collective-permute-start(bf16[256,384]{1,0:T(8,128)(2,1)S(1)} %attention_1.1.own), channel_id=1, source_target_pairs={{0,6},{2,0},{4,2},{6,4},{1,7},{3,1},{5,3},{7,5},{8,14},{10,8},{12,... | collective-permute-start | bytes 589832 | tf_op jit(solution)/shard_map/ppermute | solution.py:415
  58.8 9.0 %collective-permute-start.13 = (bf16[256,384]{1,0:T(8,128)(2,1)S(1)}, bf16[256,384]{1,0:T(8,128)(2,1)S(1)}, u32[]{:S(2)}, u32[]{:S(2)}) collective-permute-start(bf16[256,384]{1,0:T(8,128)(2,1)S(1)} %attention_1.1.own), channel_id=1, source_target_pairs={{0,2},{2,4},{4,6},{6,0},{1,3},{3,5},{5,7},{7,1},{8,10},{10,12},{12... | collective-permute-start | bytes 589832 | tf_op jit(solution)/shard_map/ppermute | solution.py:415
  61.6 9.3 %collective-permute-start.10 = (bf16[256,384]{1,0:T(8,128)(2,1)S(1)}, bf16[256,384]{1,0:T(8,128)(2,1)S(1)}, u32[]{:S(2)}, u32[]{:S(2)}) collective-permute-start(bf16[256,384]{1,0:T(8,128)(2,1)S(1)} %attention_0.1.own), channel_id=1, source_target_pairs={{0,2},{2,4},{4,6},{6,0},{1,3},{3,5},{5,7},{7,1},{8,10},{10,12},{12... | collective-permute-start | bytes 589832 | tf_op jit(solution)/shard_map/ppermute | solution.py:415
  61.9 9.7 %collective-permute-start.11 = (bf16[256,384]{1,0:T(8,128)(2,1)S(1)}, bf16[256,384]{1,0:T(8,128)(2,1)S(1)}, u32[]{:S(2)}, u32[]{:S(2)}) collective-permute-start(bf16[256,384]{1,0:T(8,128)(2,1)S(1)} %attention_0.1.own), channel_id=1, source_target_pairs={{0,6},{2,0},{4,2},{6,4},{1,7},{3,1},{5,3},{7,5},{8,14},{10,8},{12,... | collective-permute-start | bytes 589832 | tf_op jit(solution)/shard_map/ppermute | solution.py:415
  67.8 5.7 %collective-permute-start.15 = (bf16[256,384]{1,0:T(8,128)(2,1)S(1)}, bf16[256,384]{1,0:T(8,128)(2,1)S(1)}, u32[]{:S(2)}, u32[]{:S(2)}) collective-permute-start(bf16[256,384]{1,0:T(8,128)(2,1)S(1)} %collective-permute-done.14.left), channel_id=1, source_target_pairs={{0,6},{2,0},{4,2},{6,4},{1,7},{3,1},{5,3},{7,5},{8,14},{10,8},{12,... | collective-permute-start | bytes 589832 | tf_op jit(solution)/shard_map/ppermute | solution.py:415
  70.9 7.0 %collective-permute-start.12 = (bf16[256,384]{1,0:T(8,128)(2,1)S(1)}, bf16[256,384]{1,0:T(8,128)(2,1)S(1)}, u32[]{:S(2)}, u32[]{:S(2)}) collective-permute-start(bf16[256,384]{1,0:T(8,128)(2,1)S(1)} %collective-permute-done.10.right), channel_id=1, source_target_pairs={{0,2},{2,4},{4,6},{6,0},{1,3},{3,5},{5,7},{7,1},{8,10},{10,12},{12... | collective-permute-start | bytes 589832 | tf_op jit(solution)/shard_map/ppermute | solution.py:415

commit v9 on v5

--- a/solution.py
+++ b/solution.py
@@ -61,16 +61,17 @@
     return wide[0:1] + wide[1:2] + wide[2:3]
 
 
-def tail_kernel(phase, decay, lat, w, out, tail, wkv, acc, sems):
+def tail_kernel(phase, decay, lat, w, out, edge, tail, wkv, acc, sems):
     depth = lat.shape[1]
     step = depth // CHUNKS
     copies = []
     for k in range(CHUNKS):
         at = pl.ds(k * step, step)
         group = [
-            pltpu.make_async_copy(lat.at[pl.ds(MEM, MEM), at], tail.at[:, at], sems.at[3 * k]),
-            pltpu.make_async_copy(w.at[1, at], wkv.at[at, pl.ds(0, COLS)], sems.at[3 * k + 1]),
-            pltpu.make_async_copy(w.at[2, at], wkv.at[at, pl.ds(COLS, COLS)], sems.at[3 * k + 2]),
+            pltpu.make_async_copy(lat.at[pl.ds(MEM, MEM), at], tail.at[pl.ds(0, MEM), at], sems.at[4 * k]),
+            pltpu.make_async_copy(lat.at[pl.ds(0, PART), at], tail.at[pl.ds(MEM, PART), at], sems.at[4 * k + 1]),
+            pltpu.make_async_copy(w.at[1, at], wkv.at[at, pl.ds(0, COLS)], sems.at[4 * k + 2]),
+            pltpu.make_async_copy(w.at[2, at], wkv.at[at, pl.ds(COLS, COLS)], sems.at[4 * k + 3]),
         ]
         for copy in group:
             copy.start()
@@ -87,6 +88,9 @@
     keys = normed(acc[:, :COLS])
     values = acc[:, COLS:].astype(BF16)
     first = phase[0] == 0
+    last, lead = slice(MEM - PART, MEM), slice(MEM, MEM + PART)
+    edge[:PART] = jnp.where(first, keys[last], keys[lead])
+    edge[PART:] = jnp.where(first, values[last], values[lead])
     rates = [jnp.where(first, decay[0, h], decay[1, h]) for h in range(HEADS)]
     lane = lax.broadcasted_iota(jnp.int32, (1, COLS), 1)
     row = jnp.where(lane < HD, rates[0], jnp.where(lane < 2 * HD, rates[1], rates[2]))
@@ -104,14 +108,14 @@
     hbm = pl.BlockSpec(memory_space=pl.ANY)
     return pl.pallas_call(
         tail_kernel,
-        out_shape=shape((PARTS, PAYLOAD, COLS), BF16),
+        out_shape=(shape((PARTS, PAYLOAD, COLS), BF16), shape((2 * PART, COLS), BF16)),
         in_specs=[smem, smem, hbm, hbm],
-        out_specs=vmem,
+        out_specs=(vmem, vmem),
         scratch_shapes=[
-            pltpu.VMEM((MEM, depth), BF16),
+            pltpu.VMEM((MEM + PART, depth), BF16),
             pltpu.VMEM((depth, 2 * COLS), BF16),
-            pltpu.VMEM((MEM, 2 * COLS), F32),
-            pltpu.SemaphoreType.DMA((3 * CHUNKS,)),
+            pltpu.VMEM((MEM + PART, 2 * COLS), F32),
+            pltpu.SemaphoreType.DMA((4 * CHUNKS,)),
         ],
         cost_estimate=pl.CostEstimate(flops=2 * MEM * depth * 2 * COLS, bytes_accessed=5500000, transcendentals=0),
         compiler_params=pltpu.CompilerParams(vmem_limit_bytes=TAIL_LIMIT),
@@ -151,35 +155,20 @@
     out[...] = head_project(2, lat, w, rows, part, sems).astype(BF16)
 
 
-def head_keys_kernel(phase, lat, w, values, payload, out, edge, rows, part, first_values, last, sems):
-    copies = [
-        pltpu.make_async_copy(values.at[pl.ds(0, PART)], first_values, sems.at[2]),
-        pltpu.make_async_copy(payload.at[PARTS - 1, pl.ds(0, 2 * PART)], last, sems.at[3]),
-    ]
-    for copy in copies:
-        copy.start()
-    keys = normed(head_project(1, lat, w, rows, part, sems))
-    out[...] = keys
-    for copy in copies:
-        copy.wait()
-    first = phase[0] == 0
-    edge[:PART] = jnp.where(first, last[:PART], keys[:PART])
-    edge[PART:] = jnp.where(first, last[PART:], first_values[...])
-
-
-def heads(kernel, outs, name, after, latents, w3, *more):
+def head_keys_kernel(after, lat, w, out, rows, part, sems):
+    out[...] = normed(head_project(1, lat, w, rows, part, sems))
+
+
+def heads(kernel, name, after, latents, w3):
     depth = latents.shape[1]
-    scratch = [pltpu.VMEM((MEM, depth), BF16), pltpu.VMEM((depth, COLS), BF16)]
-    if more:
-        scratch += [pltpu.VMEM((PART, COLS), BF16), pltpu.VMEM((2 * PART, COLS), BF16)]
     return call_on_hbm(
         kernel,
-        outs,
+        shape((MEM, COLS), BF16),
         name,
         2 * MEM * depth * COLS,
         3300000,
-        (after, latents, w3, *more),
-        scratch + [pltpu.SemaphoreType.DMA((4,))],
+        (after, latents, w3),
+        [pltpu.VMEM((MEM, depth), BF16), pltpu.VMEM((depth, COLS), BF16), pltpu.SemaphoreType.DMA((2,))],
     )
 
 
@@ -433,7 +422,7 @@
     w3 = jnp.transpose(w_qkv, (1, 0, 2))
 
     z_ref = lax.axis_index("z").reshape(1).astype(jnp.int32)
-    payload = tails(phase_ref, decay[0], latents, w3)
+    payload, edge = tails(phase_ref, decay[0], latents, w3)
     arrived = lax.all_to_all(payload, PLANE, 0, 0, tiled=True)
 
     w_out, payload = lax.optimization_barrier((w_out, payload))
@@ -442,7 +431,6 @@
     sends = [lax.dynamic_slice_in_dim(w_out, ((mp + by) & 3) * share, share, 1) for by in offsets]
     weights = [moved(piece, "mp", by) if by else piece for by, piece in zip(offsets, sends)]
     arrived, _ = lax.optimization_barrier((arrived, sends))
-    half_keys = shape((MEM, COLS), BF16)
 
     wide = shape((2 * PART + 8, COLS), F32)
     packed = shape((PAYLOAD, COLS), BF16)
@@ -451,27 +439,26 @@
     own, sent = vmem_call(plane_kernel, (wide, packed), "plane_total", 1000000, (arrived,))
     latents, sent = lax.optimization_barrier((latents, sent))
     got_1 = swapped(sent, "z", 1)
+    halo = swapped(edge, "phase", 1)
     own_columns = lax.dynamic_slice_in_dim(latents, mp * share, share, 1)
-    got_1, own_columns = lax.optimization_barrier((got_1, own_columns))
+    got_1, own_columns, halo = lax.optimization_barrier((got_1, own_columns, halo))
+
     sent = vmem_call(first_kernel, packed, "through_1", 100000, (z_ref, own, got_1), smem=1)
     after, sent = lax.optimization_barrier((z_ref, sent))
     got_2 = swapped(sent, "z", 2)
-    head_values = heads(head_values_kernel, half_keys, "head_values", after, latents, w3)
+    head_values = heads(head_values_kernel, "head_values", after, latents, w3)
     got_2, head_values = lax.optimization_barrier((got_2, head_values))
 
     sent = vmem_call(next_kernel, plain, "through_3", 100000, (z_ref, own, got_1, got_2), smem=1)
-    after, sent = lax.optimization_barrier((phase_ref, sent))
+    after, sent = lax.optimization_barrier((z_ref, sent))
     got_4 = swapped(sent, "z", 7)
-    head_keys, edge = heads(
-        head_keys_kernel, (half_keys, plain), "head_keys", after, latents, w3, head_values, payload
-    )
+    head_keys = heads(head_keys_kernel, "head_keys", after, latents, w3)
     got_4, head_keys = lax.optimization_barrier((got_4, head_keys))
     memory = vmem_call(
         memory_kernel, plain_all, "section_memory", 1000000, (z_ref, got_1, got_2, got_4, arrived), smem=1
     )
-    after, memory, edge, frame_ids = lax.optimization_barrier((z_ref, memory, edge, frame_ids))
+    after, memory, frame_ids = lax.optimization_barrier((z_ref, memory, frame_ids))
     memory = lax.all_to_all(memory, PLANE, 0, 0, tiled=True)
-    halo = swapped(edge, "phase", 1)
     frames_pad = jnp.pad(frame_ids[0], (HALF_WIN, HALF_WIN), constant_values=outside_frame)
     frames = lax.dynamic_slice_in_dim(frames_pad, phase * ROWS, EXT)
     frame_row = frames.reshape(1, EXT)

time: 78 us -> 78.5 us (level)
  waiting for transfers between devices: 11.3 us -> 13.1 us
  starting transfers between devices: 35.2 us -> 34.4 us
    all_to_all x1, waiting for transfers between devices: 0.01 us -> 3.47 us  [local(): memory = lax.all_to_all(memory, PLANE, 0, 0, tiled=True)]
    dynamic_slice x1, local copies, waits for them, and re-layouts: 2.63 us -> 1.14 us  [local(): lax.dynamic_slice_in_dim(w_out, (mp + by & 3) * share, share, 1)]
    all_to_all x1, waiting for transfers between devices: 1.17 us -> 0.01 us  [local(): arrived = lax.all_to_all(payload, PLANE, 0, 0, tiled=True)]
    ppermute x4, waiting for transfers between devices: 3.95 us -> 2.9 us  [swapped(): lax.ppermute(x, axis, [(i, i ^ bit) for i in range(lax.axis_size(axis))])]
  transfers between devices with their start and end apart: 15 -> 15, of which waited for: 5 -> 4; matrix products, arithmetic and copies ran while one was open for 5% -> 3% of each run, Pallas kernels for 22% -> 22%
where the time goes in v9:
time: 78.5 us; the launch traced here: 77.1 us
  starting transfers between devices  34.4 us (44%)
  Pallas kernels  26.1 us (33%)
  waiting for transfers between devices  13.1 us (17%)
  local copies, waits for them, and re-layouts  3.27 us (4%)
    ppermute x9, starting transfers between devices, moved(): return lax.ppermute(x, axis, [(i, (i + by) % size) for i in range(size)])  15.1 us
    pallas_call x3, Pallas kernels, call_on_hbm(): pl.pallas_call(kernel, out_shape=outs, in_specs=[pl.BlockSpec(memory_spac...  11.7 us
    ppermute x4, starting transfers between devices, swapped(): lax.ppermute(x, axis, [(i, i ^ bit) for i in range(lax.axis_size(axis))])  11.4 us
    ppermute x9, waiting for transfers between devices, moved(): return lax.ppermute(x, axis, [(i, (i + by) % size) for i in range(size)])  6.7 us
    pallas_call x2, Pallas kernels, attention(): pl.pallas_call(functools.partial(attend_kernel, r), out_shape=shape((half...  5.5 us
    pallas_call x1, Pallas kernels, tails(): pl.pallas_call(tail_kernel, out_shape=(shape((PARTS, PAYLOAD, COLS), BF16...  5.06 us
    all_to_all x1, starting transfers between devices, local(): arrived = lax.all_to_all(payload, PLANE, 0, 0, tiled=True)  4.48 us
    pallas_call x6, Pallas kernels, vmem_call(): pl.pallas_call(kernel, out_shape=outs, in_specs=specs, out_specs=out_spec...  3.9 us
  transfers between devices with their start and end apart: 15, of which 4 were waited for; matrix products, arithmetic and copies ran while one was open for 3% of the time, Pallas kernels for 22%

profile of v9, /device:TPU:32, one launch (start us, length us, event | category | flops | bytes accessed | tf_op | source)
XLA Modules:
  0.0 77.1 jit_solution(15585007075225556558)
XLA Ops:
  0.0 0.0 copy-start.4
  0.0 5.1 %tail_projection.1 = (bf16[8,72,384]{2,1,0:T(8,128)(2,1)}, bf16[64,384]{1,0:T(8,128)(2,1)}) custom-call(s32[1]{0:T(128)} %bitcast.phase, f32[2,3]{1,0:T(2,128)} %bitcast.10, bf16[512,2560]{1,0:T(8,128)(2,1)} %lat.4, bf16[3,2560,384]{2,1,0:T(8,128)(2,1)} %bitcast.5), custom_call_target="tpu_custom_call" | custom-call | flops 1006632960 | bytes 5500000 | tf_op jit(solution)/shard_map/tail_projection/pallas_call | solution.py:109
  5.1 4.5 %all-to-all-start = ((bf16[8,72,384]{2,1,0:T(8,128)(2,1)}), bf16[8,72,384]{2,1,0:T(8,128)(2,1)S(1)}, u32[]{:S(2)}, u32[]{:S(2)}) async-start(bf16[8,72,384]{2,1,0:T(8,128)(2,1)} %get-tuple-element.54.tail_rows), calls=%async_computation | async-start | bytes 884736 | tf_op jit(solution)/shard_map/all_to_all | solution.py:426
  9.6 3.5 %collective-permute-start.1 = (bf16[64,384]{1,0:T(8,128)(2,1)}, bf16[64,384]{1,0:T(8,128)(2,1)S(1)}, u32[]{:S(2)}, u32[]{:S(2)}) collective-permute-start(bf16[64,384]{1,0:T(8,128)(2,1)} %get-tuple-element.41), channel_id=1, source_target_pairs={{0,1},{1,0},{2,3},{3,2},{4,5},{5,4},{6,7},{7,6},{8,9},{9,8},{10,11... | collective-permute-start | bytes 147464 | tf_op jit(solution)/shard_map/ppermute | solution.py:415
  13.1 0.0 copy-done.4
  13.1 1.1 %constant_dynamic-slice_fusion.1 = (bf16[384,640]{1,0:T(8,128)(2,1)}, bf16[384,640]{1,0:T(8,128)(2,1)}, bf16[384,640]{1,0:T(8,128)(2,1)}, bf16[384,640]{1,0:T(8,128)(2,1)S(1)}) fusion(bf16[384,2560]{1,0:T(8,128)(2,1)S(1)} %copy-done.4, s32[]{:T(128)S(6)} %select_n.21, s32[]{:T(128)S(6)} %select_n.20, s32[]{:T(128)S(6)} %select_n.19, s32[]{:T(128)S(6)} %select_n.18), kind=kLoop, calls=%fused_computation.2 | loop fusion | bytes 3932176 | tf_op jit(solution)/shard_map/dynamic_slice | solution.py:431
  14.2 1.5 %collective-permute-start.4 = (bf16[384,640]{1,0:T(8,128)(2,1)}, bf16[384,640]{1,0:T(8,128)(2,1)S(1)}, u32[]{:S(2)}, u32[]{:S(2)}) collective-permute-start(bf16[384,640]{1,0:T(8,128)(2,1)} %get-tuple-element.67), channel_id=1, source_target_pairs={{0,2},{2,4},{4,6},{6,0},{1,3},{3,5},{5,7},{7,1},{8,10},{10,12},{12... | collective-permute-start | bytes 1474568 | tf_op jit(solution)/shard_map/ppermute | solution.py:411
  15.7 1.7 %collective-permute-start.5 = (bf16[384,640]{1,0:T(8,128)(2,1)}, bf16[384,640]{1,0:T(8,128)(2,1)S(1)}, u32[]{:S(2)}, u32[]{:S(2)}) collective-permute-start(bf16[384,640]{1,0:T(8,128)(2,1)} %get-tuple-element.66), channel_id=1, source_target_pairs={{0,6},{2,0},{4,2},{6,4},{1,7},{3,1},{5,3},{7,5},{8,14},{10,8},{12,... | collective-permute-start | bytes 1474568 | tf_op jit(solution)/shard_map/ppermute | solution.py:411
  17.5 1.8 %collective-permute-start.6 = (bf16[384,640]{1,0:T(8,128)(2,1)}, bf16[384,640]{1,0:T(8,128)(2,1)S(1)}, u32[]{:S(2)}, u32[]{:S(2)}) collective-permute-start(bf16[384,640]{1,0:T(8,128)(2,1)} %get-tuple-element.65), channel_id=1, source_target_pairs={{0,4},{2,6},{4,0},{6,2},{1,5},{3,7},{5,1},{7,3},{8,12},{10,14},{12... | collective-permute-start | bytes 1474568 | tf_op jit(solution)/shard_map/ppermute | solution.py:411
  19.3 0.0 all-to-all-done.arrived
  19.3 0.2 plane_total.1
  19.5 0.2 collective-permute-start
  19.7 1.1 %constant_dynamic-slice_fusion.lat = bf16[512,640]{1,0:T(8,128)(2,1)S(1)} fusion(bf16[512,2560]{1,0:T(8,128)(2,1)} %lat.4, s32[]{:T(128)S(6)} %select_n.22), kind=kLoop, calls=%fused_computation.1 | loop fusion | bytes 1310724 | tf_op jit(solution)/shard_map/dynamic_slice | solution.py:443
  20.8 0.0 collective-permute-done.1.halo
  20.8 2.9 %collective-permute-done.got_1 = bf16[72,384]{1,0:T(8,128)(2,1)S(1)} collective-permute-done((bf16[72,384]{1,0:T(8,128)(2,1)S(1)}, bf16[72,384]{1,0:T(8,128)(2,1)S(1)}, u32[]{:S(2)}, u32[]{:S(2)}) %collective-permute-start) | collective-permute-done | bytes 55328 | tf_op jit(solution)/shard_map/ppermute | solution.py:415
  23.7 3.4 %collective-permute-start.2 = (bf16[72,384]{1,0:T(8,128)(2,1)S(1)}, bf16[72,384]{1,0:T(8,128)(2,1)S(1)}, u32[]{:S(2)}, u32[]{:S(2)}) collective-permute-start(bf16[72,384]{1,0:T(8,128)(2,1)S(1)} %through_1.1), channel_id=1, source_target_pairs={{0,64},{32,96},{64,0},{96,32},{128,192},{160,224},{192,128},{224,1... | collective-permute-start | bytes 165896 | tf_op jit(solution)/shard_map/ppermute | solution.py:415
  27.1 3.5 %head_values.1 = bf16[256,384]{1,0:T(8,128)(2,1)} custom-call(s32[1]{0:T(128)} %bitcast.3.z.after, bf16[512,2560]{1,0:T(8,128)(2,1)} %lat.4, bf16[3,2560,384]{2,1,0:T(8,128)(2,1)} %bitcast.6), custom_call_target="tpu_custom_call" | custom-call | flops 503316480 | bytes 3300000 | tf_op jit(solution)/shard_map/head_values/pallas_call | solution.py:130
  30.6 0.0 collective-permute-done.2.got_2
  30.6 0.1 through_3.1
  30.6 0.0 copy-start.5
  30.6 4.3 %collective-permute-start.3 = (bf16[64,384]{1,0:T(8,128)(2,1)S(1)}, bf16[64,384]{1,0:T(8,128)(2,1)S(1)}, u32[]{:S(2)}, u32[]{:S(2)}) collective-permute-start(bf16[64,384]{1,0:T(8,128)(2,1)S(1)} %through_3.1), channel_id=1, source_target_pairs={{0,224},{32,192},{64,160},{96,128},{128,96},{160,64},{192,32},{224... | collective-permute-start | bytes 147464 | tf_op jit(solution)/shard_map/ppermute | solution.py:415
  35.0 3.6 %head_keys.1 = bf16[256,384]{1,0:T(8,128)(2,1)} custom-call(s32[1]{0:T(128)} %bitcast.3.z.after, bf16[512,2560]{1,0:T(8,128)(2,1)} %lat.4, bf16[3,2560,384]{2,1,0:T(8,128)(2,1)} %bitcast.7), custom_call_target="tpu_custom_call" | custom-call | flops 503316480 | bytes 3300000 | tf_op jit(solution)/shard_map/head_keys/pallas_call | solution.py:130
  38.6 0.0 collective-permute-done.3.got_4
  38.6 1.0 %section_memory.1 = bf16[8,64,384]{2,1,0:T(8,128)(2,1)} custom-call(s32[1]{0:T(128)} %bitcast.3.z.after, bf16[72,384]{1,0:T(8,128)(2,1)S(1)} %collective-permute-done.got_1, bf16[72,384]{1,0:T(8,128)(2,1)S(1)} %collective-permute-done.2.got_2, bf16[64,384]{1,0:T(8,128)(2,1)S(1)} %collective-permute-done.3.got_4, bf16[8,72,384]{2,1,0:T(8,128)(2,1)S(1)} %all-to-all-done.arrived), custom_call_target="tpu_custom_call" | custom-call | flops 1000000 | bytes 602116 | tf_op jit(solution)/shard_map/section_memory/pallas_call | solution.py:209
  39.5 3.5 %all-to-all-start.1 = ((bf16[8,64,384]{2,1,0:T(8,128)(2,1)}), bf16[8,64,384]{2,1,0:T(8,128)(2,1)S(1)}, u32[]{:S(2)}, u32[]{:S(2)}) async-start(bf16[8,64,384]{2,1,0:T(8,128)(2,1)} %section_memory.1), calls=%async_computation.1 | async-start | bytes 786432 | tf_op jit(solution)/shard_map/all_to_all | solution.py:461
  43.0 0.0 copy-done.5
  43.0 0.1 pad_dynamic-slice_fusion
  43.1 0.0 copy-start
  43.1 0.0 copy-start.1
  43.1 0.0 copy-start.2
  43.1 4.7 %query_projection.1.q = bf16[512,384]{1,0:T(8,128)(2,1)} custom-call(s32[1]{0:T(128)} %bitcast.3.z.after, bf16[512,2560]{1,0:T(8,128)(2,1)} %lat.4, bf16[3,2560,384]{2,1,0:T(8,128)(2,1)} %bitcast.8), custom_call_target="tpu_custom_call" | custom-call | flops 1006632960 | bytes 4600000 | tf_op jit(solution)/shard_map/query_projection/pallas_call | solution.py:130
  47.8 0.0 collective-permute-done.4.w_right
  47.8 0.0 collective-permute-done.5.w_left
  47.8 0.0 collective-permute-done.6.w
  47.8 3.5 %all-to-all-done.1.memory_in = bf16[8,64,384]{2,1,0:T(8,128)(2,1)S(1)} async-done(((bf16[8,64,384]{2,1,0:T(8,128)(2,1)}), bf16[8,64,384]{2,1,0:T(8,128)(2,1)S(1)}, u32[]{:S(2)}, u32[]{:S(2)}) %all-to-all-start.1) | async-done | bytes 393248 | tf_op jit(solution)/shard_map/all_to_all | solution.py:461
  51.3 0.0 copy-start.3
  51.3 0.7 copy-done.3
  52.0 0.1 broadcast_in_dim.2.columns_in
  52.1 0.0 copy-done
  52.2 0.0 copy-done.1
  52.2 0.0 copy-done.2
  52.2 2.8 %attention_1.1.own_1 = bf16[256,384]{1,0:T(8,128)(2,1)S(1)} custom-call(s32[1]{0:T(128)} %bitcast.phase, s32[1,17]{1,0:T(1,128)S(1)} %copy-done.2, bf16[512,384]{1,0:T(8,128)(2,1)} %query_projection.1.q, bf16[256,384]{1,0:T(8,128)(2,1)S(1)} %copy-done.1, bf16[256,384]{1,0:T(8,128)(2,1)S(1)} %copy-done, bf16[8,72,384]{2,1,0:T(8,128)(2,1)} %get-tuple-element.54.tail_rows, ...), custom_call_target="tpu_custom_call" | custom-call | flops 402653184 | bytes 1500000 | tf_op jit(solution)/shard_map/attention_1/pallas_call | solution.py:367
  54.9 1.0 %collective-permute-start.8 = (bf16[256,384]{1,0:T(8,128)(2,1)S(1)}, bf16[256,384]{1,0:T(8,128)(2,1)S(1)}, u32[]{:S(2)}, u32[]{:S(2)}) collective-permute-start(bf16[256,384]{1,0:T(8,128)(2,1)S(1)} %attention_1.1.own_1), channel_id=1, source_target_pairs={{0,2},{2,4},{4,6},{6,0},{1,3},{3,5},{5,7},{7,1},{8,10},{10,12},{12... | collective-permute-start | bytes 589832 | tf_op jit(solution)/shard_map/ppermute | solution.py:411
  55.9 2.5 %collective-permute-start.9 = (bf16[256,384]{1,0:T(8,128)(2,1)S(1)}, bf16[256,384]{1,0:T(8,128)(2,1)S(1)}, u32[]{:S(2)}, u32[]{:S(2)}) collective-permute-start(bf16[256,384]{1,0:T(8,128)(2,1)S(1)} %attention_1.1.own_1), channel_id=1, source_target_pairs={{0,6},{2,0},{4,2},{6,4},{1,7},{3,1},{5,3},{7,5},{8,14},{10,8},{12,... | collective-permute-start | bytes 589832 | tf_op jit(solution)/shard_map/ppermute | solution.py:411
  58.4 2.7 %attention_0.1.own_0 = bf16[256,384]{1,0:T(8,128)(2,1)S(1)} custom-call(s32[1]{0:T(128)} %bitcast.phase, s32[1,17]{1,0:T(1,128)S(1)} %copy-done.2, bf16[512,384]{1,0:T(8,128)(2,1)} %query_projection.1.q, bf16[256,384]{1,0:T(8,128)(2,1)S(1)} %copy-done.1, bf16[256,384]{1,0:T(8,128)(2,1)S(1)} %copy-done, bf16[8,72,384]{2,1,0:T(8,128)(2,1)} %get-tuple-element.54.tail_rows, ...), custom_call_target="tpu_custom_call" | custom-call | flops 402653184 | bytes 1500000 | tf_op jit(solution)/shard_map/attention_0/pallas_call | solution.py:367
  61.2 0.1 collective-permute-start.7
  61.3 3.2 %collective-permute-start.10 = (bf16[256,384]{1,0:T(8,128)(2,1)S(1)}, bf16[256,384]{1,0:T(8,128)(2,1)S(1)}, u32[]{:S(2)}, u32[]{:S(2)}) collective-permute-start(bf16[256,384]{1,0:T(8,128)(2,1)S(1)} %attention_0.1.own_0), channel_id=1, source_target_pairs={{0,6},{2,0},{4,2},{6,4},{1,7},{3,1},{5,3},{7,5},{8,14},{10,8},{12,... | collective-permute-start | bytes 589832 | tf_op jit(solution)/shard_map/ppermute | solution.py:411
  64.5 0.0 collective-permute-done.8.right_1
  64.5 0.0 collective-permute-done.9.left_1
  64.5 4.3 %collective-permute-done.7.right_0 = bf16[256,384]{1,0:T(8,128)(2,1)S(1)} collective-permute-done((bf16[256,384]{1,0:T(8,128)(2,1)S(1)}, bf16[256,384]{1,0:T(8,128)(2,1)S(1)}, u32[]{:S(2)}, u32[]{:S(2)}) %collective-permute-start.7) | collective-permute-done | bytes 196640 | tf_op jit(solution)/shard_map/ppermute | solution.py:411
  68.8 0.0 collective-permute-start.11
  68.8 3.2 %collective-permute-start.12 = (bf16[256,384]{1,0:T(8,128)(2,1)S(1)}, bf16[256,384]{1,0:T(8,128)(2,1)S(1)}, u32[]{:S(2)}, u32[]{:S(2)}) collective-permute-start(bf16[256,384]{1,0:T(8,128)(2,1)S(1)} %collective-permute-done.9.left_1), channel_id=1, source_target_pairs={{0,6},{2,0},{4,2},{6,4},{1,7},{3,1},{5,3},{7,5},{8,14},{10,8},{12,... | collective-permute-start | bytes 589832 | tf_op jit(solution)/shard_map/ppermute | solution.py:411
  72.1 0.0 collective-permute-done.10.left_0
  72.1 1.3 %near_projection.1.total = f32[512,640]{1,0:T(8,128)S(1)} custom-call(bf16[512,640]{1,0:T(8,128)(2,1)S(1)} %constant_dynamic-slice_fusion.lat, bf16[256,384]{1,0:T(8,128)(2,1)S(1)} %attention_0.1.own_0, bf16[256,384]{1,0:T(8,128)(2,1)S(1)} %attention_1.1.own_1, bf16[256,384]{1,0:T(8,128)(2,1)S(1)} %collective-permute-done.7.right_0, ...), custom_call_target="tpu_custom_call" | custom-call | flops 754974720 | bytes 3309568 | tf_op jit(solution)/shard_map/near_projection/pallas_call | solution.py:209
  73.4 2.3 %collective-permute-done.11.first = bf16[256,384]{1,0:T(8,128)(2,1)S(1)} collective-permute-done((bf16[256,384]{1,0:T(8,128)(2,1)S(1)}, bf16[256,384]{1,0:T(8,128)(2,1)S(1)}, u32[]{:S(2)}, u32[]{:S(2)}) %collective-permute-start.11) | collective-permute-done | bytes 196640 | tf_op jit(solution)/shard_map/ppermute | solution.py:411
  75.7 0.0 collective-permute-done.12.second
  75.7 1.4 %far_projection.1 = bf16[512,640]{1,0:T(8,128)(2,1)} custom-call(f32[512,640]{1,0:T(8,128)S(1)} %near_projection.1.total, bf16[256,384]{1,0:T(8,128)(2,1)S(1)} %collective-permute-done.11.first, bf16[256,384]{1,0:T(8,128)(2,1)S(1)} %collective-permute-done.12.second, bf16[384,640]{1,0:T(8,128)(2,1)S(1)} %collective-permute-done.6.w), custom_call_target="tpu_custom_call" | custom-call | flops 251658240 | bytes 2195456 | tf_op jit(solution)/shard_map/far_projection/pallas_call | solution.py:209
  (2 shorter events, 0.0 us)
Async XLA Ops:
  0.0 13.1 %copy-start.4 = (bf16[384,2560]{1,0:T(8,128)(2,1)S(1)}, bf16[384,2560]{1,0:T(8,128)(2,1)}, u32[]{:S(2)}) copy-start(bf16[384,2560]{1,0:T(8,128)(2,1)} %param.8) | copy-start | bytes 5898244
  5.1 14.2 %all-to-all-start = ((bf16[8,72,384]{2,1,0:T(8,128)(2,1)}), bf16[8,72,384]{2,1,0:T(8,128)(2,1)S(1)}, u32[]{:S(2)}, u32[]{:S(2)}) async-start(bf16[8,72,384]{2,1,0:T(8,128)(2,1)} %get-tuple-element.54.tail_rows), calls=%async_computation | async-start | bytes 884736 | tf_op jit(solution)/shard_map/all_to_all | solution.py:426
  9.6 11.3 %collective-permute-start.1 = (bf16[64,384]{1,0:T(8,128)(2,1)}, bf16[64,384]{1,0:T(8,128)(2,1)S(1)}, u32[]{:S(2)}, u32[]{:S(2)}) collective-permute-start(bf16[64,384]{1,0:T(8,128)(2,1)} %get-tuple-element.41), channel_id=1, source_target_pairs={{0,1},{1,0},{2,3},{3,2},{4,5},{5,4},{6,7},{7,6},{8,9},{9,8},{10,11... | collective-permute-start | bytes 147464 | tf_op jit(solution)/shard_map/ppermute | solution.py:415
  14.2 33.5 %collective-permute-start.4 = (bf16[384,640]{1,0:T(8,128)(2,1)}, bf16[384,640]{1,0:T(8,128)(2,1)S(1)}, u32[]{:S(2)}, u32[]{:S(2)}) collective-permute-start(bf16[384,640]{1,0:T(8,128)(2,1)} %get-tuple-element.67), channel_id=1, source_target_pairs={{0,2},{2,4},{4,6},{6,0},{1,3},{3,5},{5,7},{7,1},{8,10},{10,12},{12... | collective-permute-start | bytes 1474568 | tf_op jit(solution)/shard_map/ppermute | solution.py:411
  15.7 32.1 %collective-permute-start.5 = (bf16[384,640]{1,0:T(8,128)(2,1)}, bf16[384,640]{1,0:T(8,128)(2,1)S(1)}, u32[]{:S(2)}, u32[]{:S(2)}) collective-permute-start(bf16[384,640]{1,0:T(8,128)(2,1)} %get-tuple-element.66), channel_id=1, source_target_pairs={{0,6},{2,0},{4,2},{6,4},{1,7},{3,1},{5,3},{7,5},{8,14},{10,8},{12,... | collective-permute-start | bytes 1474568 | tf_op jit(solution)/shard_map/ppermute | solution.py:411
  17.5 30.3 %collective-permute-start.6 = (bf16[384,640]{1,0:T(8,128)(2,1)}, bf16[384,640]{1,0:T(8,128)(2,1)S(1)}, u32[]{:S(2)}, u32[]{:S(2)}) collective-permute-start(bf16[384,640]{1,0:T(8,128)(2,1)} %get-tuple-element.65), channel_id=1, source_target_pairs={{0,4},{2,6},{4,0},{6,2},{1,5},{3,7},{5,1},{7,3},{8,12},{10,14},{12... | collective-permute-start | bytes 1474568 | tf_op jit(solution)/shard_map/ppermute | solution.py:411
  19.5 4.2 %collective-permute-start = (bf16[72,384]{1,0:T(8,128)(2,1)S(1)}, bf16[72,384]{1,0:T(8,128)(2,1)S(1)}, u32[]{:S(2)}, u32[]{:S(2)}) collective-permute-start(bf16[72,384]{1,0:T(8,128)(2,1)S(1)} %get-tuple-element.39), channel_id=1, source_target_pairs={{0,32},{32,0},{64,96},{96,64},{128,160},{160,128},{192,224},{224,1... | collective-permute-start | bytes 165896 | tf_op jit(solution)/shard_map/ppermute | solution.py:415
  23.7 6.8 %collective-permute-start.2 = (bf16[72,384]{1,0:T(8,128)(2,1)S(1)}, bf16[72,384]{1,0:T(8,128)(2,1)S(1)}, u32[]{:S(2)}, u32[]{:S(2)}) collective-permute-start(bf16[72,384]{1,0:T(8,128)(2,1)S(1)} %through_1.1), channel_id=1, source_target_pairs={{0,64},{32,96},{64,0},{96,32},{128,192},{160,224},{192,128},{224,1... | collective-permute-start | bytes 165896 | tf_op jit(solution)/shard_map/ppermute | solution.py:415
  30.6 12.4 %copy-start.5 = (s32[1,1024]{1,0:T(1,128)S(1)}, s32[1,1024]{1,0:T(1,128)}, u32[]{:S(2)}) copy-start(s32[1,1024]{1,0:T(1,128)} %param.10) | copy-start | bytes 12292
  30.6 7.9 %collective-permute-start.3 = (bf16[64,384]{1,0:T(8,128)(2,1)S(1)}, bf16[64,384]{1,0:T(8,128)(2,1)S(1)}, u32[]{:S(2)}, u32[]{:S(2)}) collective-permute-start(bf16[64,384]{1,0:T(8,128)(2,1)S(1)} %through_3.1), channel_id=1, source_target_pairs={{0,224},{32,192},{64,160},{96,128},{128,96},{160,64},{192,32},{224... | collective-permute-start | bytes 147464 | tf_op jit(solution)/shard_map/ppermute | solution.py:415
  39.5 11.7 %all-to-all-start.1 = ((bf16[8,64,384]{2,1,0:T(8,128)(2,1)}), bf16[8,64,384]{2,1,0:T(8,128)(2,1)S(1)}, u32[]{:S(2)}, u32[]{:S(2)}) async-start(bf16[8,64,384]{2,1,0:T(8,128)(2,1)} %section_memory.1), calls=%async_computation.1 | async-start | bytes 786432 | tf_op jit(solution)/shard_map/all_to_all | solution.py:461
  43.1 9.1 %copy-start = (bf16[256,384]{1,0:T(8,128)(2,1)S(1)}, bf16[256,384]{1,0:T(8,128)(2,1)}, u32[]{:S(2)}) copy-start(bf16[256,384]{1,0:T(8,128)(2,1)} %head_values.1) | copy-start | bytes 589828
  43.1 9.1 %copy-start.1 = (bf16[256,384]{1,0:T(8,128)(2,1)S(1)}, bf16[256,384]{1,0:T(8,128)(2,1)}, u32[]{:S(2)}) copy-start(bf16[256,384]{1,0:T(8,128)(2,1)} %head_keys.1) | copy-start | bytes 589828
  43.1 9.1 %copy-start.2 = (s32[1,17]{1,0:T(1,128)S(1)}, s32[1,17]{1,0:T(1,128)}, u32[]{:S(2)}) copy-start(s32[1,17]{1,0:T(1,128)} %opened.3) | copy-start | bytes 208
  51.3 0.7 copy-start.3
  54.9 9.6 %collective-permute-start.8 = (bf16[256,384]{1,0:T(8,128)(2,1)S(1)}, bf16[256,384]{1,0:T(8,128)(2,1)S(1)}, u32[]{:S(2)}, u32[]{:S(2)}) collective-permute-start(bf16[256,384]{1,0:T(8,128)(2,1)S(1)} %attention_1.1.own_1), channel_id=1, source_target_pairs={{0,2},{2,4},{4,6},{6,0},{1,3},{3,5},{5,7},{7,1},{8,10},{10,12},{12... | collective-permute-start | bytes 589832 | tf_op jit(solution)/shard_map/ppermute | solution.py:411
  55.9 8.6 %collective-permute-start.9 = (bf16[256,384]{1,0:T(8,128)(2,1)S(1)}, bf16[256,384]{1,0:T(8,128)(2,1)S(1)}, u32[]{:S(2)}, u32[]{:S(2)}) collective-permute-start(bf16[256,384]{1,0:T(8,128)(2,1)S(1)} %attention_1.1.own_1), channel_id=1, source_target_pairs={{0,6},{2,0},{4,2},{6,4},{1,7},{3,1},{5,3},{7,5},{8,14},{10,8},{12,... | collective-permute-start | bytes 589832 | tf_op jit(solution)/shard_map/ppermute | solution.py:411
  61.2 7.7 %collective-permute-start.7 = (bf16[256,384]{1,0:T(8,128)(2,1)S(1)}, bf16[256,384]{1,0:T(8,128)(2,1)S(1)}, u32[]{:S(2)}, u32[]{:S(2)}) collective-permute-start(bf16[256,384]{1,0:T(8,128)(2,1)S(1)} %attention_0.1.own_0), channel_id=1, source_target_pairs={{0,2},{2,4},{4,6},{6,0},{1,3},{3,5},{5,7},{7,1},{8,10},{10,12},{12... | collective-permute-start | bytes 589832 | tf_op jit(solution)/shard_map/ppermute | solution.py:411
  61.3 10.8 %collective-permute-start.10 = (bf16[256,384]{1,0:T(8,128)(2,1)S(1)}, bf16[256,384]{1,0:T(8,128)(2,1)S(1)}, u32[]{:S(2)}, u32[]{:S(2)}) collective-permute-start(bf16[256,384]{1,0:T(8,128)(2,1)S(1)} %attention_0.1.own_0), channel_id=1, source_target_pairs={{0,6},{2,0},{4,2},{6,4},{1,7},{3,1},{5,3},{7,5},{8,14},{10,8},{12,... | collective-permute-start | bytes 589832 | tf_op jit(solution)/shard_map/ppermute | solution.py:411
  68.8 6.9 %collective-permute-start.11 = (bf16[256,384]{1,0:T(8,128)(2,1)S(1)}, bf16[256,384]{1,0:T(8,128)(2,1)S(1)}, u32[]{:S(2)}, u32[]{:S(2)}) collective-permute-start(bf16[256,384]{1,0:T(8,128)(2,1)S(1)} %collective-permute-done.7.right_0), channel_id=1, source_target_pairs={{0,2},{2,4},{4,6},{6,0},{1,3},{3,5},{5,7},{7,1},{8,10},{10,12},{12... | collective-permute-start | bytes 589832 | tf_op jit(solution)/shard_map/ppermute | solution.py:411
  68.8 6.9 %collective-permute-start.12 = (bf16[256,384]{1,0:T(8,128)(2,1)S(1)}, bf16[256,384]{1,0:T(8,128)(2,1)S(1)}, u32[]{:S(2)}, u32[]{:S(2)}) collective-permute-start(bf16[256,384]{1,0:T(8,128)(2,1)S(1)} %collective-permute-done.9.left_1), channel_id=1, source_target_pairs={{0,6},{2,0},{4,2},{6,4},{1,7},{3,1},{5,3},{7,5},{8,14},{10,8},{12,... | collective-permute-start | bytes 589832 | tf_op jit(solution)/shard_map/ppermute | solution.py:411

commit v10 on v9

--- a/solution.py
+++ b/solution.py
@@ -389,21 +389,19 @@
     )(phase, opened, *operands)
 
 
-def near_kernel(lat, own_0, own_1, right_0, right_1, left_0, left_1, w_own, w_right, w_left, total):
+def near_kernel(r, lat, own, right, left, w_own, w_right, w_left, total):
+    rows = total.shape[0]
+    sums = lat[r * rows : (r + 1) * rows].astype(F32)
+    for a, w in ((own, w_own), (right, w_right), (left, w_left)):
+        sums = sums + jnp.dot(a[...], w[...], preferred_element_type=F32)
+    total[...] = sums
+
+
+def far_kernel(total_0, total_1, first, second, w, out):
     half = ROWS // 2
-    for r, parts in enumerate(((own_0, right_0, left_0), (own_1, right_1, left_1))):
+    for r, (total, part) in enumerate(((total_0, first), (total_1, second))):
         at = slice(r * half, (r + 1) * half)
-        sums = lat[at].astype(F32)
-        for a, w in zip(parts, (w_own, w_right, w_left)):
-            sums = sums + jnp.dot(a[...], w[...], preferred_element_type=F32)
-        total[at] = sums
-
-
-def far_kernel(total, first, second, w, out):
-    half = ROWS // 2
-    for r, part in enumerate((first, second)):
-        at = slice(r * half, (r + 1) * half)
-        out[at] = (total[at] + jnp.dot(part[...], w[...], preferred_element_type=F32)).astype(BF16)
+        out[at] = (total[...] + jnp.dot(part[...], w[...], preferred_element_type=F32)).astype(BF16)
 
 
 def moved(x, axis, by):
@@ -474,20 +472,25 @@
     right = [moved(piece, "mp", 1) for piece in halves]
     left = [moved(piece, "mp", -1) for piece in halves]
     right[1], left[1] = lax.optimization_barrier((right[1], left[1]))
-    far_1, far_2 = moved(right[0], "mp", 1), moved(left[1], "mp", -1)
-    total = vmem_call(
-        near_kernel,
-        shape((ROWS, share), F32),
-        "near_projection",
-        6 * ROWS * COLS * share,
-        (own_columns, *halves, *right, *left, *weights[:3]),
-    )
+    far_2 = moved(left[1], "mp", -1)
+    totals = [None, None]
+    for r in (1, 0):
+        totals[r] = vmem_call(
+            functools.partial(near_kernel, r),
+            shape((ROWS // 2, share), F32),
+            f"near_projection_{r}",
+            3 * ROWS * COLS * share,
+            (own_columns, halves[r], right[r], left[r], *weights[:3]),
+        )
+        if r == 1:
+            right[0], totals[1] = lax.optimization_barrier((right[0], totals[1]))
+            far_1 = moved(right[0], "mp", 1)
     return vmem_call(
         far_kernel,
         shape((ROWS, share), BF16),
         "far_projection",
         2 * ROWS * COLS * share,
-        (total, far_1, far_2, weights[3]),
+        (*totals, far_1, far_2, weights[3]),
     )
 
 

time: 78.5 us -> 78.2 us (level); the launches traced: 77.1 us -> 77.8 us
  waiting for transfers between devices: 13.1 us -> 17.8 us
  starting transfers between devices: 34.4 us -> 30.4 us
    ppermute x9, waiting for transfers between devices: 6.7 us -> 11.4 us  [moved(): return lax.ppermute(x, axis, [(i, (i + by) % size) for i in range(size)])]
    ppermute x9, starting transfers between devices: 15.1 us -> 11.1 us  [moved(): return lax.ppermute(x, axis, [(i, (i + by) % size) for i in range(size)])]
    pallas_call x6 -> x7, Pallas kernels: 3.9 us -> 4.07 us  [vmem_call(): pl.pallas_call(kernel, out_shape=outs, in_specs=specs, out_specs=out_spec...]
  transfers between devices with their start and end apart: 15 -> 15, of which waited for: 4 -> 6; matrix products, arithmetic and copies ran while one was open for 3% -> 3% of each run, Pallas kernels for 22% -> 22%
where the time goes in v10:
time: 78.2 us; the launch traced here: 77.8 us
  starting transfers between devices  30.4 us (39%)
  Pallas kernels  26.3 us (34%)
  waiting for transfers between devices  17.8 us (23%)
  local copies, waits for them, and re-layouts  3.13 us (4%)
    pallas_call x3, Pallas kernels, call_on_hbm(): pl.pallas_call(kernel, out_shape=outs, in_specs=[pl.BlockSpec(memory_spac...  11.7 us
    ppermute x9, waiting for transfers between devices, moved(): return lax.ppermute(x, axis, [(i, (i + by) % size) for i in range(size)])  11.4 us
    ppermute x4, starting transfers between devices, swapped(): lax.ppermute(x, axis, [(i, i ^ bit) for i in range(lax.axis_size(axis))])  11.4 us
    ppermute x9, starting transfers between devices, moved(): return lax.ppermute(x, axis, [(i, (i + by) % size) for i in range(size)])  11.1 us
    pallas_call x2, Pallas kernels, attention(): pl.pallas_call(functools.partial(attend_kernel, r), out_shape=shape((half...  5.5 us
    pallas_call x1, Pallas kernels, tails(): pl.pallas_call(tail_kernel, out_shape=(shape((PARTS, PAYLOAD, COLS), BF16...  5.06 us
    all_to_all x1, starting transfers between devices, local(): arrived = lax.all_to_all(payload, PLANE, 0, 0, tiled=True)  4.48 us
    pallas_call x7, Pallas kernels, vmem_call(): pl.pallas_call(kernel, out_shape=outs, in_specs=specs, out_specs=out_spec...  4.07 us
  transfers between devices with their start and end apart: 15, of which 6 were waited for; matrix products, arithmetic and copies ran while one was open for 3% of the time, Pallas kernels for 22%

profile of v10, /device:TPU:32, one launch (start us, length us, event | category | flops | bytes accessed | tf_op | source)
XLA Modules:
  0.0 77.8 jit_solution(8100743182587762942)
XLA Ops:
  0.0 0.0 copy-start.4
  0.0 5.1 %tail_projection.1 = (bf16[8,72,384]{2,1,0:T(8,128)(2,1)}, bf16[64,384]{1,0:T(8,128)(2,1)}) custom-call(s32[1]{0:T(128)} %bitcast.phase, f32[2,3]{1,0:T(2,128)} %bitcast.10, bf16[512,2560]{1,0:T(8,128)(2,1)} %lat.4, bf16[3,2560,384]{2,1,0:T(8,128)(2,1)} %bitcast.5), custom_call_target="tpu_custom_call" | custom-call | flops 1006632960 | bytes 5500000 | tf_op jit(solution)/shard_map/tail_projection/pallas_call | solution.py:109
  5.1 4.5 %all-to-all-start = ((bf16[8,72,384]{2,1,0:T(8,128)(2,1)}), bf16[8,72,384]{2,1,0:T(8,128)(2,1)S(1)}, u32[]{:S(2)}, u32[]{:S(2)}) async-start(bf16[8,72,384]{2,1,0:T(8,128)(2,1)} %get-tuple-element.56.tail_rows), calls=%async_computation | async-start | bytes 884736 | tf_op jit(solution)/shard_map/all_to_all | solution.py:424
  9.6 3.5 %collective-permute-start.1 = (bf16[64,384]{1,0:T(8,128)(2,1)}, bf16[64,384]{1,0:T(8,128)(2,1)S(1)}, u32[]{:S(2)}, u32[]{:S(2)}) collective-permute-start(bf16[64,384]{1,0:T(8,128)(2,1)} %get-tuple-element.43), channel_id=1, source_target_pairs={{0,1},{1,0},{2,3},{3,2},{4,5},{5,4},{6,7},{7,6},{8,9},{9,8},{10,11... | collective-permute-start | bytes 147464 | tf_op jit(solution)/shard_map/ppermute | solution.py:413
  13.1 0.0 copy-done.4
  13.1 1.1 %constant_dynamic-slice_fusion.1 = (bf16[384,640]{1,0:T(8,128)(2,1)}, bf16[384,640]{1,0:T(8,128)(2,1)}, bf16[384,640]{1,0:T(8,128)(2,1)}, bf16[384,640]{1,0:T(8,128)(2,1)S(1)}) fusion(bf16[384,2560]{1,0:T(8,128)(2,1)S(1)} %copy-done.4, s32[]{:T(128)S(6)} %select_n.21, s32[]{:T(128)S(6)} %select_n.20, s32[]{:T(128)S(6)} %select_n.19, s32[]{:T(128)S(6)} %select_n.18), kind=kLoop, calls=%fused_computation.2 | loop fusion | bytes 3932176 | tf_op jit(solution)/shard_map/dynamic_slice | solution.py:429
  14.2 3.0 %collective-permute-start.6 = (bf16[384,640]{1,0:T(8,128)(2,1)}, bf16[384,640]{1,0:T(8,128)(2,1)S(1)}, u32[]{:S(2)}, u32[]{:S(2)}) collective-permute-start(bf16[384,640]{1,0:T(8,128)(2,1)} %get-tuple-element.69), channel_id=1, source_target_pairs={{0,4},{2,6},{4,0},{6,2},{1,5},{3,7},{5,1},{7,3},{8,12},{10,14},{12... | collective-permute-start | bytes 1474568 | tf_op jit(solution)/shard_map/ppermute | solution.py:409
  17.3 1.1 %collective-permute-start.5 = (bf16[384,640]{1,0:T(8,128)(2,1)}, bf16[384,640]{1,0:T(8,128)(2,1)S(1)}, u32[]{:S(2)}, u32[]{:S(2)}) collective-permute-start(bf16[384,640]{1,0:T(8,128)(2,1)} %get-tuple-element.70), channel_id=1, source_target_pairs={{0,6},{2,0},{4,2},{6,4},{1,7},{3,1},{5,3},{7,5},{8,14},{10,8},{12,... | collective-permute-start | bytes 1474568 | tf_op jit(solution)/shard_map/ppermute | solution.py:409
  18.4 0.9 %collective-permute-start.4 = (bf16[384,640]{1,0:T(8,128)(2,1)}, bf16[384,640]{1,0:T(8,128)(2,1)S(1)}, u32[]{:S(2)}, u32[]{:S(2)}) collective-permute-start(bf16[384,640]{1,0:T(8,128)(2,1)} %get-tuple-element.71), channel_id=1, source_target_pairs={{0,2},{2,4},{4,6},{6,0},{1,3},{3,5},{5,7},{7,1},{8,10},{10,12},{12... | collective-permute-start | bytes 1474568 | tf_op jit(solution)/shard_map/ppermute | solution.py:409
  19.3 0.0 all-to-all-done.arrived
  19.3 0.2 plane_total.1
  19.5 0.2 collective-permute-start
  19.7 1.1 %constant_dynamic-slice_fusion.lat = bf16[512,640]{1,0:T(8,128)(2,1)S(1)} fusion(bf16[512,2560]{1,0:T(8,128)(2,1)} %lat.4, s32[]{:T(128)S(6)} %select_n.22), kind=kLoop, calls=%fused_computation.1 | loop fusion | bytes 1310724 | tf_op jit(solution)/shard_map/dynamic_slice | solution.py:441
  20.8 0.0 collective-permute-done.1.halo
  20.8 2.9 %collective-permute-done.got_1 = bf16[72,384]{1,0:T(8,128)(2,1)S(1)} collective-permute-done((bf16[72,384]{1,0:T(8,128)(2,1)S(1)}, bf16[72,384]{1,0:T(8,128)(2,1)S(1)}, u32[]{:S(2)}, u32[]{:S(2)}) %collective-permute-start) | collective-permute-done | bytes 55328 | tf_op jit(solution)/shard_map/ppermute | solution.py:413
  23.7 3.4 %collective-permute-start.2 = (bf16[72,384]{1,0:T(8,128)(2,1)S(1)}, bf16[72,384]{1,0:T(8,128)(2,1)S(1)}, u32[]{:S(2)}, u32[]{:S(2)}) collective-permute-start(bf16[72,384]{1,0:T(8,128)(2,1)S(1)} %through_1.1), channel_id=1, source_target_pairs={{0,64},{32,96},{64,0},{96,32},{128,192},{160,224},{192,128},{224,1... | collective-permute-start | bytes 165896 | tf_op jit(solution)/shard_map/ppermute | solution.py:413
  27.1 3.5 %head_values.1 = bf16[256,384]{1,0:T(8,128)(2,1)} custom-call(s32[1]{0:T(128)} %bitcast.3.z.after, bf16[512,2560]{1,0:T(8,128)(2,1)} %lat.4, bf16[3,2560,384]{2,1,0:T(8,128)(2,1)} %bitcast.6), custom_call_target="tpu_custom_call" | custom-call | flops 503316480 | bytes 3300000 | tf_op jit(solution)/shard_map/head_values/pallas_call | solution.py:130
  30.6 0.0 collective-permute-done.2.got_2
  30.6 0.1 through_3.1
  30.6 0.0 copy-start.5
  30.6 4.3 %collective-permute-start.3 = (bf16[64,384]{1,0:T(8,128)(2,1)S(1)}, bf16[64,384]{1,0:T(8,128)(2,1)S(1)}, u32[]{:S(2)}, u32[]{:S(2)}) collective-permute-start(bf16[64,384]{1,0:T(8,128)(2,1)S(1)} %through_3.1), channel_id=1, source_target_pairs={{0,224},{32,192},{64,160},{96,128},{128,96},{160,64},{192,32},{224... | collective-permute-start | bytes 147464 | tf_op jit(solution)/shard_map/ppermute | solution.py:413
  35.0 3.6 %head_keys.1 = bf16[256,384]{1,0:T(8,128)(2,1)} custom-call(s32[1]{0:T(128)} %bitcast.3.z.after, bf16[512,2560]{1,0:T(8,128)(2,1)} %lat.4, bf16[3,2560,384]{2,1,0:T(8,128)(2,1)} %bitcast.7), custom_call_target="tpu_custom_call" | custom-call | flops 503316480 | bytes 3300000 | tf_op jit(solution)/shard_map/head_keys/pallas_call | solution.py:130
  38.6 0.0 collective-permute-done.3.got_4
  38.6 1.0 %section_memory.1 = bf16[8,64,384]{2,1,0:T(8,128)(2,1)} custom-call(s32[1]{0:T(128)} %bitcast.3.z.after, bf16[72,384]{1,0:T(8,128)(2,1)S(1)} %collective-permute-done.got_1, bf16[72,384]{1,0:T(8,128)(2,1)S(1)} %collective-permute-done.2.got_2, bf16[64,384]{1,0:T(8,128)(2,1)S(1)} %collective-permute-done.3.got_4, bf16[8,72,384]{2,1,0:T(8,128)(2,1)S(1)} %all-to-all-done.arrived), custom_call_target="tpu_custom_call" | custom-call | flops 1000000 | bytes 602116 | tf_op jit(solution)/shard_map/section_memory/pallas_call | solution.py:209
  39.5 3.5 %all-to-all-start.1 = ((bf16[8,64,384]{2,1,0:T(8,128)(2,1)}), bf16[8,64,384]{2,1,0:T(8,128)(2,1)S(1)}, u32[]{:S(2)}, u32[]{:S(2)}) async-start(bf16[8,64,384]{2,1,0:T(8,128)(2,1)} %section_memory.1), calls=%async_computation.1 | async-start | bytes 786432 | tf_op jit(solution)/shard_map/all_to_all | solution.py:459
  43.0 0.0 copy-done.5
  43.0 0.1 pad_dynamic-slice_fusion
  43.1 0.0 copy-start
  43.1 0.0 copy-start.1
  43.1 0.0 copy-start.2
  43.1 4.7 %query_projection.1.q = bf16[512,384]{1,0:T(8,128)(2,1)} custom-call(s32[1]{0:T(128)} %bitcast.3.z.after, bf16[512,2560]{1,0:T(8,128)(2,1)} %lat.4, bf16[3,2560,384]{2,1,0:T(8,128)(2,1)} %bitcast.8), custom_call_target="tpu_custom_call" | custom-call | flops 1006632960 | bytes 4600000 | tf_op jit(solution)/shard_map/query_projection/pallas_call | solution.py:130
  47.8 0.0 collective-permute-done.6.w
  47.8 0.0 collective-permute-done.5.w_left
  47.8 0.0 collective-permute-done.4.w_right
  47.8 3.5 %all-to-all-done.1.memory_in = bf16[8,64,384]{2,1,0:T(8,128)(2,1)S(1)} async-done(((bf16[8,64,384]{2,1,0:T(8,128)(2,1)}), bf16[8,64,384]{2,1,0:T(8,128)(2,1)S(1)}, u32[]{:S(2)}, u32[]{:S(2)}) %all-to-all-start.1) | async-done | bytes 393248 | tf_op jit(solution)/shard_map/all_to_all | solution.py:459
  51.3 0.0 copy-start.3
  51.3 0.1 broadcast_in_dim.2.columns_in
  51.4 0.6 copy-done.3
  52.0 0.0 copy-done
  52.0 0.0 copy-done.1
  52.0 0.0 copy-done.2
  52.0 2.8 %attention_1.1.own = bf16[256,384]{1,0:T(8,128)(2,1)S(1)} custom-call(s32[1]{0:T(128)} %bitcast.phase, s32[1,17]{1,0:T(1,128)S(1)} %copy-done.2, bf16[512,384]{1,0:T(8,128)(2,1)} %query_projection.1.q, bf16[256,384]{1,0:T(8,128)(2,1)S(1)} %copy-done.1, bf16[256,384]{1,0:T(8,128)(2,1)S(1)} %copy-done, bf16[8,72,384]{2,1,0:T(8,128)(2,1)} %get-tuple-element.56.tail_rows, ...), custom_call_target="tpu_custom_call" | custom-call | flops 402653184 | bytes 1500000 | tf_op jit(solution)/shard_map/attention_1/pallas_call | solution.py:367
  54.8 2.6 %collective-permute-start.9 = (bf16[256,384]{1,0:T(8,128)(2,1)S(1)}, bf16[256,384]{1,0:T(8,128)(2,1)S(1)}, u32[]{:S(2)}, u32[]{:S(2)}) collective-permute-start(bf16[256,384]{1,0:T(8,128)(2,1)S(1)} %attention_1.1.own), channel_id=1, source_target_pairs={{0,6},{2,0},{4,2},{6,4},{1,7},{3,1},{5,3},{7,5},{8,14},{10,8},{12,... | collective-permute-start | bytes 589832 | tf_op jit(solution)/shard_map/ppermute | solution.py:409
  57.4 0.0 collective-permute-start.8
  57.4 2.7 %attention_0.1.own = bf16[256,384]{1,0:T(8,128)(2,1)S(1)} custom-call(s32[1]{0:T(128)} %bitcast.phase, s32[1,17]{1,0:T(1,128)S(1)} %copy-done.2, bf16[512,384]{1,0:T(8,128)(2,1)} %query_projection.1.q, bf16[256,384]{1,0:T(8,128)(2,1)S(1)} %copy-done.1, bf16[256,384]{1,0:T(8,128)(2,1)S(1)} %copy-done, bf16[8,72,384]{2,1,0:T(8,128)(2,1)} %get-tuple-element.56.tail_rows, ...), custom_call_target="tpu_custom_call" | custom-call | flops 402653184 | bytes 1500000 | tf_op jit(solution)/shard_map/attention_0/pallas_call | solution.py:367
  60.1 0.4 collective-permute-start.7
  60.6 3.0 %collective-permute-start.10 = (bf16[256,384]{1,0:T(8,128)(2,1)S(1)}, bf16[256,384]{1,0:T(8,128)(2,1)S(1)}, u32[]{:S(2)}, u32[]{:S(2)}) collective-permute-start(bf16[256,384]{1,0:T(8,128)(2,1)S(1)} %attention_0.1.own), channel_id=1, source_target_pairs={{0,6},{2,0},{4,2},{6,4},{1,7},{3,1},{5,3},{7,5},{8,14},{10,8},{12,... | collective-permute-start | bytes 589832 | tf_op jit(solution)/shard_map/ppermute | solution.py:409
  63.5 0.0 collective-permute-done.9.left
  63.5 2.8 %collective-permute-done.8.right = bf16[256,384]{1,0:T(8,128)(2,1)S(1)} collective-permute-done((bf16[256,384]{1,0:T(8,128)(2,1)S(1)}, bf16[256,384]{1,0:T(8,128)(2,1)S(1)}, u32[]{:S(2)}, u32[]{:S(2)}) %collective-permute-start.8) | collective-permute-done | bytes 196640 | tf_op jit(solution)/shard_map/ppermute | solution.py:409
  66.4 0.0 collective-permute-start.12
  66.4 0.7 near_projection_1.1.total_1
  67.1 2.3 %collective-permute-done.7.right = bf16[256,384]{1,0:T(8,128)(2,1)S(1)} collective-permute-done((bf16[256,384]{1,0:T(8,128)(2,1)S(1)}, bf16[256,384]{1,0:T(8,128)(2,1)S(1)}, u32[]{:S(2)}, u32[]{:S(2)}) %collective-permute-start.7) | collective-permute-done | bytes 196640 | tf_op jit(solution)/shard_map/ppermute | solution.py:409
  69.5 0.0 collective-permute-start.11
  69.5 0.0 collective-permute-done.10.left
  69.5 0.7 near_projection_0.1.total_0
  70.2 1.9 %collective-permute-done.12.second = bf16[256,384]{1,0:T(8,128)(2,1)S(1)} collective-permute-done((bf16[256,384]{1,0:T(8,128)(2,1)S(1)}, bf16[256,384]{1,0:T(8,128)(2,1)S(1)}, u32[]{:S(2)}, u32[]{:S(2)}) %collective-permute-start.12) | collective-permute-done | bytes 196640 | tf_op jit(solution)/shard_map/ppermute | solution.py:409
  72.1 4.4 %collective-permute-done.11.first = bf16[256,384]{1,0:T(8,128)(2,1)S(1)} collective-permute-done((bf16[256,384]{1,0:T(8,128)(2,1)S(1)}, bf16[256,384]{1,0:T(8,128)(2,1)S(1)}, u32[]{:S(2)}, u32[]{:S(2)}) %collective-permute-start.11) | collective-permute-done | bytes 196640 | tf_op jit(solution)/shard_map/ppermute | solution.py:409
  76.5 1.4 %far_projection.1 = bf16[512,640]{1,0:T(8,128)(2,1)} custom-call(f32[256,640]{1,0:T(8,128)S(1)} %near_projection_0.1.total_0, f32[256,640]{1,0:T(8,128)S(1)} %near_projection_1.1.total_1, bf16[256,384]{1,0:T(8,128)(2,1)S(1)} %collective-permute-done.11.first, bf16[256,384]{1,0:T(8,128)(2,1)S(1)} %collective-permute-done.12.second, ...), custom_call_target="tpu_custom_call" | custom-call | flops 251658240 | bytes 2195456 | tf_op jit(solution)/shard_map/far_projection/pallas_call | solution.py:209
  (2 shorter events, 0.0 us)
Async XLA Ops:
  0.0 13.1 %copy-start.4 = (bf16[384,2560]{1,0:T(8,128)(2,1)S(1)}, bf16[384,2560]{1,0:T(8,128)(2,1)}, u32[]{:S(2)}) copy-start(bf16[384,2560]{1,0:T(8,128)(2,1)} %param.8) | copy-start | bytes 5898244
  5.1 14.2 %all-to-all-start = ((bf16[8,72,384]{2,1,0:T(8,128)(2,1)}), bf16[8,72,384]{2,1,0:T(8,128)(2,1)S(1)}, u32[]{:S(2)}, u32[]{:S(2)}) async-start(bf16[8,72,384]{2,1,0:T(8,128)(2,1)} %get-tuple-element.56.tail_rows), calls=%async_computation | async-start | bytes 884736 | tf_op jit(solution)/shard_map/all_to_all | solution.py:424
  9.6 11.3 %collective-permute-start.1 = (bf16[64,384]{1,0:T(8,128)(2,1)}, bf16[64,384]{1,0:T(8,128)(2,1)S(1)}, u32[]{:S(2)}, u32[]{:S(2)}) collective-permute-start(bf16[64,384]{1,0:T(8,128)(2,1)} %get-tuple-element.43), channel_id=1, source_target_pairs={{0,1},{1,0},{2,3},{3,2},{4,5},{5,4},{6,7},{7,6},{8,9},{9,8},{10,11... | collective-permute-start | bytes 147464 | tf_op jit(solution)/shard_map/ppermute | solution.py:413
  14.2 33.5 %collective-permute-start.6 = (bf16[384,640]{1,0:T(8,128)(2,1)}, bf16[384,640]{1,0:T(8,128)(2,1)S(1)}, u32[]{:S(2)}, u32[]{:S(2)}) collective-permute-start(bf16[384,640]{1,0:T(8,128)(2,1)} %get-tuple-element.69), channel_id=1, source_target_pairs={{0,4},{2,6},{4,0},{6,2},{1,5},{3,7},{5,1},{7,3},{8,12},{10,14},{12... | collective-permute-start | bytes 1474568 | tf_op jit(solution)/shard_map/ppermute | solution.py:409
  17.3 30.5 %collective-permute-start.5 = (bf16[384,640]{1,0:T(8,128)(2,1)}, bf16[384,640]{1,0:T(8,128)(2,1)S(1)}, u32[]{:S(2)}, u32[]{:S(2)}) collective-permute-start(bf16[384,640]{1,0:T(8,128)(2,1)} %get-tuple-element.70), channel_id=1, source_target_pairs={{0,6},{2,0},{4,2},{6,4},{1,7},{3,1},{5,3},{7,5},{8,14},{10,8},{12,... | collective-permute-start | bytes 1474568 | tf_op jit(solution)/shard_map/ppermute | solution.py:409
  18.4 29.4 %collective-permute-start.4 = (bf16[384,640]{1,0:T(8,128)(2,1)}, bf16[384,640]{1,0:T(8,128)(2,1)S(1)}, u32[]{:S(2)}, u32[]{:S(2)}) collective-permute-start(bf16[384,640]{1,0:T(8,128)(2,1)} %get-tuple-element.71), channel_id=1, source_target_pairs={{0,2},{2,4},{4,6},{6,0},{1,3},{3,5},{5,7},{7,1},{8,10},{10,12},{12... | collective-permute-start | bytes 1474568 | tf_op jit(solution)/shard_map/ppermute | solution.py:409
  19.5 4.2 %collective-permute-start = (bf16[72,384]{1,0:T(8,128)(2,1)S(1)}, bf16[72,384]{1,0:T(8,128)(2,1)S(1)}, u32[]{:S(2)}, u32[]{:S(2)}) collective-permute-start(bf16[72,384]{1,0:T(8,128)(2,1)S(1)} %get-tuple-element.41), channel_id=1, source_target_pairs={{0,32},{32,0},{64,96},{96,64},{128,160},{160,128},{192,224},{224,1... | collective-permute-start | bytes 165896 | tf_op jit(solution)/shard_map/ppermute | solution.py:413
  23.7 6.8 %collective-permute-start.2 = (bf16[72,384]{1,0:T(8,128)(2,1)S(1)}, bf16[72,384]{1,0:T(8,128)(2,1)S(1)}, u32[]{:S(2)}, u32[]{:S(2)}) collective-permute-start(bf16[72,384]{1,0:T(8,128)(2,1)S(1)} %through_1.1), channel_id=1, source_target_pairs={{0,64},{32,96},{64,0},{96,32},{128,192},{160,224},{192,128},{224,1... | collective-permute-start | bytes 165896 | tf_op jit(solution)/shard_map/ppermute | solution.py:413
  30.6 12.4 %copy-start.5 = (s32[1,1024]{1,0:T(1,128)S(1)}, s32[1,1024]{1,0:T(1,128)}, u32[]{:S(2)}) copy-start(s32[1,1024]{1,0:T(1,128)} %param.10) | copy-start | bytes 12292
  30.6 7.9 %collective-permute-start.3 = (bf16[64,384]{1,0:T(8,128)(2,1)S(1)}, bf16[64,384]{1,0:T(8,128)(2,1)S(1)}, u32[]{:S(2)}, u32[]{:S(2)}) collective-permute-start(bf16[64,384]{1,0:T(8,128)(2,1)S(1)} %through_3.1), channel_id=1, source_target_pairs={{0,224},{32,192},{64,160},{96,128},{128,96},{160,64},{192,32},{224... | collective-permute-start | bytes 147464 | tf_op jit(solution)/shard_map/ppermute | solution.py:413
  39.5 11.7 %all-to-all-start.1 = ((bf16[8,64,384]{2,1,0:T(8,128)(2,1)}), bf16[8,64,384]{2,1,0:T(8,128)(2,1)S(1)}, u32[]{:S(2)}, u32[]{:S(2)}) async-start(bf16[8,64,384]{2,1,0:T(8,128)(2,1)} %section_memory.1), calls=%async_computation.1 | async-start | bytes 786432 | tf_op jit(solution)/shard_map/all_to_all | solution.py:459
  43.1 8.9 %copy-start = (bf16[256,384]{1,0:T(8,128)(2,1)S(1)}, bf16[256,384]{1,0:T(8,128)(2,1)}, u32[]{:S(2)}) copy-start(bf16[256,384]{1,0:T(8,128)(2,1)} %head_values.1) | copy-start | bytes 589828
  43.1 8.9 %copy-start.1 = (bf16[256,384]{1,0:T(8,128)(2,1)S(1)}, bf16[256,384]{1,0:T(8,128)(2,1)}, u32[]{:S(2)}) copy-start(bf16[256,384]{1,0:T(8,128)(2,1)} %head_keys.1) | copy-start | bytes 589828
  43.1 8.9 %copy-start.2 = (s32[1,17]{1,0:T(1,128)S(1)}, s32[1,17]{1,0:T(1,128)}, u32[]{:S(2)}) copy-start(s32[1,17]{1,0:T(1,128)} %opened.3) | copy-start | bytes 208
  51.3 0.7 copy-start.3
  54.8 8.8 %collective-permute-start.9 = (bf16[256,384]{1,0:T(8,128)(2,1)S(1)}, bf16[256,384]{1,0:T(8,128)(2,1)S(1)}, u32[]{:S(2)}, u32[]{:S(2)}) collective-permute-start(bf16[256,384]{1,0:T(8,128)(2,1)S(1)} %attention_1.1.own), channel_id=1, source_target_pairs={{0,6},{2,0},{4,2},{6,4},{1,7},{3,1},{5,3},{7,5},{8,14},{10,8},{12,... | collective-permute-start | bytes 589832 | tf_op jit(solution)/shard_map/ppermute | solution.py:409
  57.4 9.0 %collective-permute-start.8 = (bf16[256,384]{1,0:T(8,128)(2,1)S(1)}, bf16[256,384]{1,0:T(8,128)(2,1)S(1)}, u32[]{:S(2)}, u32[]{:S(2)}) collective-permute-start(bf16[256,384]{1,0:T(8,128)(2,1)S(1)} %attention_1.1.own), channel_id=1, source_target_pairs={{0,2},{2,4},{4,6},{6,0},{1,3},{3,5},{5,7},{7,1},{8,10},{10,12},{12... | collective-permute-start | bytes 589832 | tf_op jit(solution)/shard_map/ppermute | solution.py:409
  60.1 9.3 %collective-permute-start.7 = (bf16[256,384]{1,0:T(8,128)(2,1)S(1)}, bf16[256,384]{1,0:T(8,128)(2,1)S(1)}, u32[]{:S(2)}, u32[]{:S(2)}) collective-permute-start(bf16[256,384]{1,0:T(8,128)(2,1)S(1)} %attention_0.1.own), channel_id=1, source_target_pairs={{0,2},{2,4},{4,6},{6,0},{1,3},{3,5},{5,7},{7,1},{8,10},{10,12},{12... | collective-permute-start | bytes 589832 | tf_op jit(solution)/shard_map/ppermute | solution.py:409
  60.6 8.9 %collective-permute-start.10 = (bf16[256,384]{1,0:T(8,128)(2,1)S(1)}, bf16[256,384]{1,0:T(8,128)(2,1)S(1)}, u32[]{:S(2)}, u32[]{:S(2)}) collective-permute-start(bf16[256,384]{1,0:T(8,128)(2,1)S(1)} %attention_0.1.own), channel_id=1, source_target_pairs={{0,6},{2,0},{4,2},{6,4},{1,7},{3,1},{5,3},{7,5},{8,14},{10,8},{12,... | collective-permute-start | bytes 589832 | tf_op jit(solution)/shard_map/ppermute | solution.py:409
  66.4 5.7 %collective-permute-start.12 = (bf16[256,384]{1,0:T(8,128)(2,1)S(1)}, bf16[256,384]{1,0:T(8,128)(2,1)S(1)}, u32[]{:S(2)}, u32[]{:S(2)}) collective-permute-start(bf16[256,384]{1,0:T(8,128)(2,1)S(1)} %collective-permute-done.9.left), channel_id=1, source_target_pairs={{0,6},{2,0},{4,2},{6,4},{1,7},{3,1},{5,3},{7,5},{8,14},{10,8},{12,... | collective-permute-start | bytes 589832 | tf_op jit(solution)/shard_map/ppermute | solution.py:409
  69.5 7.0 %collective-permute-start.11 = (bf16[256,384]{1,0:T(8,128)(2,1)S(1)}, bf16[256,384]{1,0:T(8,128)(2,1)S(1)}, u32[]{:S(2)}, u32[]{:S(2)}) collective-permute-start(bf16[256,384]{1,0:T(8,128)(2,1)S(1)} %collective-permute-done.7.right), channel_id=1, source_target_pairs={{0,2},{2,4},{4,6},{6,0},{1,3},{3,5},{5,7},{7,1},{8,10},{10,12},{12... | collective-permute-start | bytes 589832 | tf_op jit(solution)/shard_map/ppermute | solution.py:409

commit v11 on v5

--- a/solution.py
+++ b/solution.py
@@ -400,21 +400,19 @@
     )(phase, opened, *operands)
 
 
-def near_kernel(lat, own_0, own_1, right_0, right_1, left_0, left_1, w_own, w_right, w_left, total):
+def near_kernel(r, lat, own, right, left, w_own, w_right, w_left, total):
+    rows = total.shape[0]
+    sums = lat[r * rows : (r + 1) * rows].astype(F32)
+    for a, w in ((own, w_own), (right, w_right), (left, w_left)):
+        sums = sums + jnp.dot(a[...], w[...], preferred_element_type=F32)
+    total[...] = sums
+
+
+def far_kernel(total_0, total_1, first, second, w, out):
     half = ROWS // 2
-    for r, parts in enumerate(((own_0, right_0, left_0), (own_1, right_1, left_1))):
+    for r, (total, part) in enumerate(((total_0, first), (total_1, second))):
         at = slice(r * half, (r + 1) * half)
-        sums = lat[at].astype(F32)
-        for a, w in zip(parts, (w_own, w_right, w_left)):
-            sums = sums + jnp.dot(a[...], w[...], preferred_element_type=F32)
-        total[at] = sums
-
-
-def far_kernel(total, first, second, w, out):
-    half = ROWS // 2
-    for r, part in enumerate((first, second)):
-        at = slice(r * half, (r + 1) * half)
-        out[at] = (total[at] + jnp.dot(part[...], w[...], preferred_element_type=F32)).astype(BF16)
+        out[at] = (total[...] + jnp.dot(part[...], w[...], preferred_element_type=F32)).astype(BF16)
 
 
 def moved(x, axis, by):
@@ -487,20 +485,25 @@
     right = [moved(piece, "mp", 1) for piece in halves]
     left = [moved(piece, "mp", -1) for piece in halves]
     right[1], left[1] = lax.optimization_barrier((right[1], left[1]))
-    far_1, far_2 = moved(right[0], "mp", 1), moved(left[1], "mp", -1)
-    total = vmem_call(
-        near_kernel,
-        shape((ROWS, share), F32),
-        "near_projection",
-        6 * ROWS * COLS * share,
-        (own_columns, *halves, *right, *left, *weights[:3]),
-    )
+    far_2 = moved(left[1], "mp", -1)
+    totals = [None, None]
+    for r in (1, 0):
+        totals[r] = vmem_call(
+            functools.partial(near_kernel, r),
+            shape((ROWS // 2, share), F32),
+            f"near_projection_{r}",
+            3 * ROWS * COLS * share,
+            (own_columns, halves[r], right[r], left[r], *weights[:3]),
+        )
+        if r == 1:
+            right[0], totals[1] = lax.optimization_barrier((right[0], totals[1]))
+            far_1 = moved(right[0], "mp", 1)
     return vmem_call(
         far_kernel,
         shape((ROWS, share), BF16),
         "far_projection",
         2 * ROWS * COLS * share,
-        (total, far_1, far_2, weights[3]),
+        (*totals, far_1, far_2, weights[3]),
     )
 
 

time: 78 us -> 78.6 us (level); the launches traced: 76.6 us -> 78.2 us
  waiting for transfers between devices: 11.3 us -> 15.9 us
  starting transfers between devices: 35.2 us -> 32.1 us
    ppermute x9, waiting for transfers between devices: 6.22 us -> 10.9 us  [moved(): return lax.ppermute(x, axis, [(i, (i + by) % size) for i in range(size)])]
    ppermute x9, starting transfers between devices: 15.1 us -> 11.5 us  [moved(): return lax.ppermute(x, axis, [(i, (i + by) % size) for i in range(size)])]
    pallas_call x6 -> x7, Pallas kernels: 3.89 us -> 4.06 us  [vmem_call(): pl.pallas_call(kernel, out_shape=outs, in_specs=specs, out_specs=out_spec...]
  transfers between devices with their start and end apart: 15 -> 15, of which waited for: 5 -> 8; matrix products, arithmetic and copies ran while one was open for 5% -> 5% of each run, Pallas kernels for 22% -> 22%
where the time goes in v11:
time: 78.6 us; the launch traced here: 78.2 us
  starting transfers between devices  32.1 us (41%)
  Pallas kernels  26 us (33%)
  waiting for transfers between devices  15.9 us (20%)
  local copies, waits for them, and re-layouts  4.01 us (5%)
    ppermute x4, starting transfers between devices, swapped(): lax.ppermute(x, axis, [(i, i ^ bit) for i in range(lax.axis_size(axis))])  12 us
    pallas_call x3, Pallas kernels, call_on_hbm(): pl.pallas_call(kernel, out_shape=outs, in_specs=[pl.BlockSpec(memory_spac...  11.7 us
    ppermute x9, starting transfers between devices, moved(): return lax.ppermute(x, axis, [(i, (i + by) % size) for i in range(size)])  11.5 us
    ppermute x9, waiting for transfers between devices, moved(): return lax.ppermute(x, axis, [(i, (i + by) % size) for i in range(size)])  10.9 us
    pallas_call x2, Pallas kernels, attention(): pl.pallas_call(functools.partial(attend_kernel, r), out_shape=shape((half...  5.5 us
    pallas_call x1, Pallas kernels, tails(): pl.pallas_call(tail_kernel, out_shape=shape((PARTS, PAYLOAD, COLS), BF16)...  4.7 us
    all_to_all x1, starting transfers between devices, local(): arrived = lax.all_to_all(payload, PLANE, 0, 0, tiled=True)  4.48 us
    all_to_all x1, starting transfers between devices, local(): memory = lax.all_to_all(memory, PLANE, 0, 0, tiled=True)  4.09 us
  transfers between devices with their start and end apart: 15, of which 8 were waited for; matrix products, arithmetic and copies ran while one was open for 5% of the time, Pallas kernels for 22%

profile of v11, /device:TPU:32, one launch (start us, length us, event | category | flops | bytes accessed | tf_op | source)
XLA Modules:
  0.0 78.2 jit_solution(14301560056176980519)
XLA Ops:
  0.0 4.7 %tail_projection.1.payload.tail_rows = bf16[8,72,384]{2,1,0:T(8,128)(2,1)} custom-call(s32[1]{0:T(128)} %bitcast.phase, f32[2,3]{1,0:T(2,128)} %bitcast.10, bf16[512,2560]{1,0:T(8,128)(2,1)} %lat.4, bf16[3,2560,384]{2,1,0:T(8,128)(2,1)} %bitcast.5), custom_call_target="tpu_custom_call" | custom-call | flops 1006632960 | bytes 5500000 | tf_op jit(solution)/shard_map/tail_projection/pallas_call | solution.py:105
  4.7 4.5 %all-to-all-start = ((bf16[8,72,384]{2,1,0:T(8,128)(2,1)}), bf16[8,72,384]{2,1,0:T(8,128)(2,1)S(1)}, u32[]{:S(2)}, u32[]{:S(2)}) async-start(bf16[8,72,384]{2,1,0:T(8,128)(2,1)} %tail_projection.1.payload.tail_rows), calls=%async_computation | async-start | bytes 884736 | tf_op jit(solution)/shard_map/all_to_all | solution.py:435
  9.2 2.6 %constant_dynamic-slice_fusion.1 = (bf16[384,640]{1,0:T(8,128)(2,1)}, bf16[384,640]{1,0:T(8,128)(2,1)}, bf16[384,640]{1,0:T(8,128)(2,1)}, bf16[384,640]{1,0:T(8,128)(2,1)S(1)}) fusion(bf16[384,2560]{1,0:T(8,128)(2,1)} %param.8, s32[]{:T(128)S(6)} %select_n.21, s32[]{:T(128)S(6)} %select_n.20, s32[]{:T(128)S(6)} %select_n.19, s32[]{:T(128)S(6)} %select_n.18), kind=kLoop, calls=%fused_computation.2 | loop fusion | bytes 3932176 | tf_op jit(solution)/shard_map/dynamic_slice | solution.py:440
  11.8 3.0 %collective-permute-start.6 = (bf16[384,640]{1,0:T(8,128)(2,1)}, bf16[384,640]{1,0:T(8,128)(2,1)S(1)}, u32[]{:S(2)}, u32[]{:S(2)}) collective-permute-start(bf16[384,640]{1,0:T(8,128)(2,1)} %get-tuple-element.69), channel_id=1, source_target_pairs={{0,4},{2,6},{4,0},{6,2},{1,5},{3,7},{5,1},{7,3},{8,12},{10,14},{12... | collective-permute-start | bytes 1474568 | tf_op jit(solution)/shard_map/ppermute | solution.py:420
  14.8 1.1 %collective-permute-start.5 = (bf16[384,640]{1,0:T(8,128)(2,1)}, bf16[384,640]{1,0:T(8,128)(2,1)S(1)}, u32[]{:S(2)}, u32[]{:S(2)}) collective-permute-start(bf16[384,640]{1,0:T(8,128)(2,1)} %get-tuple-element.70), channel_id=1, source_target_pairs={{0,6},{2,0},{4,2},{6,4},{1,7},{3,1},{5,3},{7,5},{8,14},{10,8},{12,... | collective-permute-start | bytes 1474568 | tf_op jit(solution)/shard_map/ppermute | solution.py:420
  16.0 0.9 %collective-permute-start.4 = (bf16[384,640]{1,0:T(8,128)(2,1)}, bf16[384,640]{1,0:T(8,128)(2,1)S(1)}, u32[]{:S(2)}, u32[]{:S(2)}) collective-permute-start(bf16[384,640]{1,0:T(8,128)(2,1)} %get-tuple-element.71), channel_id=1, source_target_pairs={{0,2},{2,4},{4,6},{6,0},{1,3},{3,5},{5,7},{7,1},{8,10},{10,12},{12... | collective-permute-start | bytes 1474568 | tf_op jit(solution)/shard_map/ppermute | solution.py:420
  16.9 1.2 %all-to-all-done.arrived = bf16[8,72,384]{2,1,0:T(8,128)(2,1)S(1)} async-done(((bf16[8,72,384]{2,1,0:T(8,128)(2,1)}), bf16[8,72,384]{2,1,0:T(8,128)(2,1)S(1)}, u32[]{:S(2)}, u32[]{:S(2)}) %all-to-all-start) | async-done | bytes 442400 | tf_op jit(solution)/shard_map/all_to_all | solution.py:435
  18.0 0.2 plane_total.1
  18.2 0.9 %collective-permute-start = (bf16[72,384]{1,0:T(8,128)(2,1)S(1)}, bf16[72,384]{1,0:T(8,128)(2,1)S(1)}, u32[]{:S(2)}, u32[]{:S(2)}) collective-permute-start(bf16[72,384]{1,0:T(8,128)(2,1)S(1)} %get-tuple-element.40), channel_id=1, source_target_pairs={{0,32},{32,0},{64,96},{96,64},{128,160},{160,128},{192,224},{224,1... | collective-permute-start | bytes 165896 | tf_op jit(solution)/shard_map/ppermute | solution.py:424
  19.1 1.1 %constant_dynamic-slice_fusion.lat = bf16[512,640]{1,0:T(8,128)(2,1)S(1)} fusion(bf16[512,2560]{1,0:T(8,128)(2,1)} %lat.4, s32[]{:T(128)S(6)} %select_n.22), kind=kLoop, calls=%fused_computation.1 | loop fusion | bytes 1310724 | tf_op jit(solution)/shard_map/dynamic_slice | solution.py:452
  20.2 2.3 %collective-permute-done.got_1 = bf16[72,384]{1,0:T(8,128)(2,1)S(1)} collective-permute-done((bf16[72,384]{1,0:T(8,128)(2,1)S(1)}, bf16[72,384]{1,0:T(8,128)(2,1)S(1)}, u32[]{:S(2)}, u32[]{:S(2)}) %collective-permute-start) | collective-permute-done | bytes 55328 | tf_op jit(solution)/shard_map/ppermute | solution.py:424
  22.6 3.4 %collective-permute-start.1 = (bf16[72,384]{1,0:T(8,128)(2,1)S(1)}, bf16[72,384]{1,0:T(8,128)(2,1)S(1)}, u32[]{:S(2)}, u32[]{:S(2)}) collective-permute-start(bf16[72,384]{1,0:T(8,128)(2,1)S(1)} %through_1.1), channel_id=1, source_target_pairs={{0,64},{32,96},{64,0},{96,32},{128,192},{160,224},{192,128},{224,1... | collective-permute-start | bytes 165896 | tf_op jit(solution)/shard_map/ppermute | solution.py:424
  25.9 3.5 %head_values.1.values = bf16[256,384]{1,0:T(8,128)(2,1)} custom-call(s32[1]{0:T(128)} %bitcast.3.z.after, bf16[512,2560]{1,0:T(8,128)(2,1)} %lat.4, bf16[3,2560,384]{2,1,0:T(8,128)(2,1)} %bitcast.6), custom_call_target="tpu_custom_call" | custom-call | flops 503316480 | bytes 3300000 | tf_op jit(solution)/shard_map/head_values/pallas_call | solution.py:126
  29.4 0.0 collective-permute-done.1.got_2
  29.4 0.1 through_3.1
  29.5 0.0 copy-start.3
  29.5 4.3 %collective-permute-start.2 = (bf16[64,384]{1,0:T(8,128)(2,1)S(1)}, bf16[64,384]{1,0:T(8,128)(2,1)S(1)}, u32[]{:S(2)}, u32[]{:S(2)}) collective-permute-start(bf16[64,384]{1,0:T(8,128)(2,1)S(1)} %through_3.1), channel_id=1, source_target_pairs={{0,224},{32,192},{64,160},{96,128},{128,96},{160,64},{192,32},{224... | collective-permute-start | bytes 147464 | tf_op jit(solution)/shard_map/ppermute | solution.py:424
  33.8 3.6 %head_keys.1 = (bf16[256,384]{1,0:T(8,128)(2,1)}, bf16[64,384]{1,0:T(8,128)(2,1)}) custom-call(s32[1]{0:T(128)} %bitcast.phase, bf16[512,2560]{1,0:T(8,128)(2,1)} %lat.4, bf16[3,2560,384]{2,1,0:T(8,128)(2,1)} %bitcast.7, bf16[256,384]{1,0:T(8,128)(2,1)} %head_values.1.values, bf16[8,72,384]{2,1,0:T(8,128)(2,1)} %tail_projection.1.payload.tail_rows), custom_call_target="tpu_custom_call" | custom-call | flops 503316480 | bytes 3300000 | tf_op jit(solution)/shard_map/head_keys/pallas_call | solution.py:126
  37.5 0.0 collective-permute-done.2.got_4
  37.5 1.0 %section_memory.1 = bf16[8,64,384]{2,1,0:T(8,128)(2,1)} custom-call(s32[1]{0:T(128)} %bitcast.3.z.after, bf16[72,384]{1,0:T(8,128)(2,1)S(1)} %collective-permute-done.got_1, bf16[72,384]{1,0:T(8,128)(2,1)S(1)} %collective-permute-done.1.got_2, bf16[64,384]{1,0:T(8,128)(2,1)S(1)} %collective-permute-done.2.got_4, bf16[8,72,384]{2,1,0:T(8,128)(2,1)S(1)} %all-to-all-done.arrived), custom_call_target="tpu_custom_call" | custom-call | flops 1000000 | bytes 602116 | tf_op jit(solution)/shard_map/section_memory/pallas_call | solution.py:220
  38.4 4.1 %all-to-all-start.1 = ((bf16[8,64,384]{2,1,0:T(8,128)(2,1)}), bf16[8,64,384]{2,1,0:T(8,128)(2,1)}, u32[]{:S(2)}, u32[]{:S(2)}) async-start(bf16[8,64,384]{2,1,0:T(8,128)(2,1)} %section_memory.1), calls=%async_computation.1 | async-start | bytes 786432 | tf_op jit(solution)/shard_map/all_to_all | solution.py:471
  42.5 0.0 copy-done.3
  42.5 0.1 pad_dynamic-slice_fusion
  42.6 0.0 copy-start
  42.6 0.0 copy-start.1
  42.6 0.0 copy-start.2
  42.6 3.5 %collective-permute-start.3 = (bf16[64,384]{1,0:T(8,128)(2,1)}, bf16[64,384]{1,0:T(8,128)(2,1)S(1)}, u32[]{:S(2)}, u32[]{:S(2)}) collective-permute-start(bf16[64,384]{1,0:T(8,128)(2,1)} %get-tuple-element.57), channel_id=1, source_target_pairs={{0,1},{1,0},{2,3},{3,2},{4,5},{5,4},{6,7},{7,6},{8,9},{9,8},{10,11... | collective-permute-start | bytes 147464 | tf_op jit(solution)/shard_map/ppermute | solution.py:424
  46.1 4.6 %query_projection.1.q = bf16[512,384]{1,0:T(8,128)(2,1)} custom-call(s32[1]{0:T(128)} %bitcast.3.z.after, bf16[512,2560]{1,0:T(8,128)(2,1)} %lat.4, bf16[3,2560,384]{2,1,0:T(8,128)(2,1)} %bitcast.8), custom_call_target="tpu_custom_call" | custom-call | flops 1006632960 | bytes 4600000 | tf_op jit(solution)/shard_map/query_projection/pallas_call | solution.py:126
  50.7 0.0 collective-permute-done.6.w
  50.7 0.0 collective-permute-done.5.w_left
  50.7 0.0 collective-permute-done.4.w_right
  50.8 0.1 all-to-all-done.1.memory_in
  50.9 1.5 %collective-permute-done.3.halo = bf16[64,384]{1,0:T(8,128)(2,1)S(1)} collective-permute-done((bf16[64,384]{1,0:T(8,128)(2,1)}, bf16[64,384]{1,0:T(8,128)(2,1)S(1)}, u32[]{:S(2)}, u32[]{:S(2)}) %collective-permute-start.3) | collective-permute-done | bytes 49184 | tf_op jit(solution)/shard_map/ppermute | solution.py:424
  52.4 0.1 broadcast_in_dim.2.columns_in
  52.5 0.0 copy-done
  52.6 0.0 copy-done.1
  52.6 0.0 copy-done.2
  52.6 2.8 %attention_1.1.own = bf16[256,384]{1,0:T(8,128)(2,1)S(1)} custom-call(s32[1]{0:T(128)} %bitcast.phase, s32[1,17]{1,0:T(1,128)S(1)} %copy-done.2, bf16[512,384]{1,0:T(8,128)(2,1)} %query_projection.1.q, bf16[256,384]{1,0:T(8,128)(2,1)S(1)} %copy-done.1, bf16[256,384]{1,0:T(8,128)(2,1)S(1)} %copy-done, bf16[8,72,384]{2,1,0:T(8,128)(2,1)} %tail_projection.1.payload.tail_rows, ...), custom_call_target="tpu_custom_call" | custom-call | flops 402653184 | bytes 1500000 | tf_op jit(solution)/shard_map/attention_1/pallas_call | solution.py:378
  55.3 3.0 %collective-permute-start.9 = (bf16[256,384]{1,0:T(8,128)(2,1)S(1)}, bf16[256,384]{1,0:T(8,128)(2,1)S(1)}, u32[]{:S(2)}, u32[]{:S(2)}) collective-permute-start(bf16[256,384]{1,0:T(8,128)(2,1)S(1)} %attention_1.1.own), channel_id=1, source_target_pairs={{0,6},{2,0},{4,2},{6,4},{1,7},{3,1},{5,3},{7,5},{8,14},{10,8},{12,... | collective-permute-start | bytes 589832 | tf_op jit(solution)/shard_map/ppermute | solution.py:420
  58.4 0.0 collective-permute-start.8
  58.4 2.7 %attention_0.1.own = bf16[256,384]{1,0:T(8,128)(2,1)S(1)} custom-call(s32[1]{0:T(128)} %bitcast.phase, s32[1,17]{1,0:T(1,128)S(1)} %copy-done.2, bf16[512,384]{1,0:T(8,128)(2,1)} %query_projection.1.q, bf16[256,384]{1,0:T(8,128)(2,1)S(1)} %copy-done.1, bf16[256,384]{1,0:T(8,128)(2,1)S(1)} %copy-done, bf16[8,72,384]{2,1,0:T(8,128)(2,1)} %tail_projection.1.payload.tail_rows, ...), custom_call_target="tpu_custom_call" | custom-call | flops 402653184 | bytes 1500000 | tf_op jit(solution)/shard_map/attention_0/pallas_call | solution.py:378
  61.1 0.8 collective-permute-start.7
  61.9 2.6 %collective-permute-start.10 = (bf16[256,384]{1,0:T(8,128)(2,1)S(1)}, bf16[256,384]{1,0:T(8,128)(2,1)S(1)}, u32[]{:S(2)}, u32[]{:S(2)}) collective-permute-start(bf16[256,384]{1,0:T(8,128)(2,1)S(1)} %attention_0.1.own), channel_id=1, source_target_pairs={{0,6},{2,0},{4,2},{6,4},{1,7},{3,1},{5,3},{7,5},{8,14},{10,8},{12,... | collective-permute-start | bytes 589832 | tf_op jit(solution)/shard_map/ppermute | solution.py:420
  64.5 0.0 collective-permute-done.9.left
  64.5 2.6 %collective-permute-done.8.right = bf16[256,384]{1,0:T(8,128)(2,1)S(1)} collective-permute-done((bf16[256,384]{1,0:T(8,128)(2,1)S(1)}, bf16[256,384]{1,0:T(8,128)(2,1)S(1)}, u32[]{:S(2)}, u32[]{:S(2)}) %collective-permute-start.8) | collective-permute-done | bytes 196640 | tf_op jit(solution)/shard_map/ppermute | solution.py:420
  67.1 0.0 collective-permute-start.12
  67.1 0.7 near_projection_1.1.total_1
  67.8 2.1 %collective-permute-done.7.right = bf16[256,384]{1,0:T(8,128)(2,1)S(1)} collective-permute-done((bf16[256,384]{1,0:T(8,128)(2,1)S(1)}, bf16[256,384]{1,0:T(8,128)(2,1)S(1)}, u32[]{:S(2)}, u32[]{:S(2)}) %collective-permute-start.7) | collective-permute-done | bytes 196640 | tf_op jit(solution)/shard_map/ppermute | solution.py:420
  69.9 0.0 collective-permute-start.11
  70.0 0.0 collective-permute-done.10.left
  70.0 0.7 near_projection_0.1.total_0
  70.7 2.1 %collective-permute-done.12.second = bf16[256,384]{1,0:T(8,128)(2,1)S(1)} collective-permute-done((bf16[256,384]{1,0:T(8,128)(2,1)S(1)}, bf16[256,384]{1,0:T(8,128)(2,1)S(1)}, u32[]{:S(2)}, u32[]{:S(2)}) %collective-permute-start.12) | collective-permute-done | bytes 196640 | tf_op jit(solution)/shard_map/ppermute | solution.py:420
  72.8 4.1 %collective-permute-done.11.first = bf16[256,384]{1,0:T(8,128)(2,1)S(1)} collective-permute-done((bf16[256,384]{1,0:T(8,128)(2,1)S(1)}, bf16[256,384]{1,0:T(8,128)(2,1)S(1)}, u32[]{:S(2)}, u32[]{:S(2)}) %collective-permute-start.11) | collective-permute-done | bytes 196640 | tf_op jit(solution)/shard_map/ppermute | solution.py:420
  76.8 1.4 %far_projection.1 = bf16[512,640]{1,0:T(8,128)(2,1)} custom-call(f32[256,640]{1,0:T(8,128)S(1)} %near_projection_0.1.total_0, f32[256,640]{1,0:T(8,128)S(1)} %near_projection_1.1.total_1, bf16[256,384]{1,0:T(8,128)(2,1)S(1)} %collective-permute-done.11.first, bf16[256,384]{1,0:T(8,128)(2,1)S(1)} %collective-permute-done.12.second, ...), custom_call_target="tpu_custom_call" | custom-call | flops 251658240 | bytes 2195456 | tf_op jit(solution)/shard_map/far_projection/pallas_call | solution.py:220
  (2 shorter events, 0.0 us)
Async XLA Ops:
  4.7 13.3 %all-to-all-start = ((bf16[8,72,384]{2,1,0:T(8,128)(2,1)}), bf16[8,72,384]{2,1,0:T(8,128)(2,1)S(1)}, u32[]{:S(2)}, u32[]{:S(2)}) async-start(bf16[8,72,384]{2,1,0:T(8,128)(2,1)} %tail_projection.1.payload.tail_rows), calls=%async_computation | async-start | bytes 884736 | tf_op jit(solution)/shard_map/all_to_all | solution.py:435
  11.8 38.9 %collective-permute-start.6 = (bf16[384,640]{1,0:T(8,128)(2,1)}, bf16[384,640]{1,0:T(8,128)(2,1)S(1)}, u32[]{:S(2)}, u32[]{:S(2)}) collective-permute-start(bf16[384,640]{1,0:T(8,128)(2,1)} %get-tuple-element.69), channel_id=1, source_target_pairs={{0,4},{2,6},{4,0},{6,2},{1,5},{3,7},{5,1},{7,3},{8,12},{10,14},{12... | collective-permute-start | bytes 1474568 | tf_op jit(solution)/shard_map/ppermute | solution.py:420
  14.8 35.9 %collective-permute-start.5 = (bf16[384,640]{1,0:T(8,128)(2,1)}, bf16[384,640]{1,0:T(8,128)(2,1)S(1)}, u32[]{:S(2)}, u32[]{:S(2)}) collective-permute-start(bf16[384,640]{1,0:T(8,128)(2,1)} %get-tuple-element.70), channel_id=1, source_target_pairs={{0,6},{2,0},{4,2},{6,4},{1,7},{3,1},{5,3},{7,5},{8,14},{10,8},{12,... | collective-permute-start | bytes 1474568 | tf_op jit(solution)/shard_map/ppermute | solution.py:420
  16.0 34.8 %collective-permute-start.4 = (bf16[384,640]{1,0:T(8,128)(2,1)}, bf16[384,640]{1,0:T(8,128)(2,1)S(1)}, u32[]{:S(2)}, u32[]{:S(2)}) collective-permute-start(bf16[384,640]{1,0:T(8,128)(2,1)} %get-tuple-element.71), channel_id=1, source_target_pairs={{0,2},{2,4},{4,6},{6,0},{1,3},{3,5},{5,7},{7,1},{8,10},{10,12},{12... | collective-permute-start | bytes 1474568 | tf_op jit(solution)/shard_map/ppermute | solution.py:420
  18.2 4.3 %collective-permute-start = (bf16[72,384]{1,0:T(8,128)(2,1)S(1)}, bf16[72,384]{1,0:T(8,128)(2,1)S(1)}, u32[]{:S(2)}, u32[]{:S(2)}) collective-permute-start(bf16[72,384]{1,0:T(8,128)(2,1)S(1)} %get-tuple-element.40), channel_id=1, source_target_pairs={{0,32},{32,0},{64,96},{96,64},{128,160},{160,128},{192,224},{224,1... | collective-permute-start | bytes 165896 | tf_op jit(solution)/shard_map/ppermute | solution.py:424
  22.6 6.8 %collective-permute-start.1 = (bf16[72,384]{1,0:T(8,128)(2,1)S(1)}, bf16[72,384]{1,0:T(8,128)(2,1)S(1)}, u32[]{:S(2)}, u32[]{:S(2)}) collective-permute-start(bf16[72,384]{1,0:T(8,128)(2,1)S(1)} %through_1.1), channel_id=1, source_target_pairs={{0,64},{32,96},{64,0},{96,32},{128,192},{160,224},{192,128},{224,1... | collective-permute-start | bytes 165896 | tf_op jit(solution)/shard_map/ppermute | solution.py:424
  29.5 13.1 %copy-start.3 = (s32[1,1024]{1,0:T(1,128)S(1)}, s32[1,1024]{1,0:T(1,128)}, u32[]{:S(2)}) copy-start(s32[1,1024]{1,0:T(1,128)} %param.10) | copy-start | bytes 12292
  29.5 8.0 %collective-permute-start.2 = (bf16[64,384]{1,0:T(8,128)(2,1)S(1)}, bf16[64,384]{1,0:T(8,128)(2,1)S(1)}, u32[]{:S(2)}, u32[]{:S(2)}) collective-permute-start(bf16[64,384]{1,0:T(8,128)(2,1)S(1)} %through_3.1), channel_id=1, source_target_pairs={{0,224},{32,192},{64,160},{96,128},{128,96},{160,64},{192,32},{224... | collective-permute-start | bytes 147464 | tf_op jit(solution)/shard_map/ppermute | solution.py:424
  38.4 12.5 %all-to-all-start.1 = ((bf16[8,64,384]{2,1,0:T(8,128)(2,1)}), bf16[8,64,384]{2,1,0:T(8,128)(2,1)}, u32[]{:S(2)}, u32[]{:S(2)}) async-start(bf16[8,64,384]{2,1,0:T(8,128)(2,1)} %section_memory.1), calls=%async_computation.1 | async-start | bytes 786432 | tf_op jit(solution)/shard_map/all_to_all | solution.py:471
  42.6 9.9 %copy-start = (bf16[256,384]{1,0:T(8,128)(2,1)S(1)}, bf16[256,384]{1,0:T(8,128)(2,1)}, u32[]{:S(2)}) copy-start(bf16[256,384]{1,0:T(8,128)(2,1)} %head_values.1.values) | copy-start | bytes 589828
  42.6 9.9 %copy-start.1 = (bf16[256,384]{1,0:T(8,128)(2,1)S(1)}, bf16[256,384]{1,0:T(8,128)(2,1)}, u32[]{:S(2)}) copy-start(bf16[256,384]{1,0:T(8,128)(2,1)} %get-tuple-element.56.head_keys) | copy-start | bytes 589828
  42.6 9.9 %copy-start.2 = (s32[1,17]{1,0:T(1,128)S(1)}, s32[1,17]{1,0:T(1,128)}, u32[]{:S(2)}) copy-start(s32[1,17]{1,0:T(1,128)} %opened.3) | copy-start | bytes 208
  42.6 9.8 %collective-permute-start.3 = (bf16[64,384]{1,0:T(8,128)(2,1)}, bf16[64,384]{1,0:T(8,128)(2,1)S(1)}, u32[]{:S(2)}, u32[]{:S(2)}) collective-permute-start(bf16[64,384]{1,0:T(8,128)(2,1)} %get-tuple-element.57), channel_id=1, source_target_pairs={{0,1},{1,0},{2,3},{3,2},{4,5},{5,4},{6,7},{7,6},{8,9},{9,8},{10,11... | collective-permute-start | bytes 147464 | tf_op jit(solution)/shard_map/ppermute | solution.py:424
  55.3 9.2 %collective-permute-start.9 = (bf16[256,384]{1,0:T(8,128)(2,1)S(1)}, bf16[256,384]{1,0:T(8,128)(2,1)S(1)}, u32[]{:S(2)}, u32[]{:S(2)}) collective-permute-start(bf16[256,384]{1,0:T(8,128)(2,1)S(1)} %attention_1.1.own), channel_id=1, source_target_pairs={{0,6},{2,0},{4,2},{6,4},{1,7},{3,1},{5,3},{7,5},{8,14},{10,8},{12,... | collective-permute-start | bytes 589832 | tf_op jit(solution)/shard_map/ppermute | solution.py:420
  58.4 8.7 %collective-permute-start.8 = (bf16[256,384]{1,0:T(8,128)(2,1)S(1)}, bf16[256,384]{1,0:T(8,128)(2,1)S(1)}, u32[]{:S(2)}, u32[]{:S(2)}) collective-permute-start(bf16[256,384]{1,0:T(8,128)(2,1)S(1)} %attention_1.1.own), channel_id=1, source_target_pairs={{0,2},{2,4},{4,6},{6,0},{1,3},{3,5},{5,7},{7,1},{8,10},{10,12},{12... | collective-permute-start | bytes 589832 | tf_op jit(solution)/shard_map/ppermute | solution.py:420
  61.1 8.8 %collective-permute-start.7 = (bf16[256,384]{1,0:T(8,128)(2,1)S(1)}, bf16[256,384]{1,0:T(8,128)(2,1)S(1)}, u32[]{:S(2)}, u32[]{:S(2)}) collective-permute-start(bf16[256,384]{1,0:T(8,128)(2,1)S(1)} %attention_0.1.own), channel_id=1, source_target_pairs={{0,2},{2,4},{4,6},{6,0},{1,3},{3,5},{5,7},{7,1},{8,10},{10,12},{12... | collective-permute-start | bytes 589832 | tf_op jit(solution)/shard_map/ppermute | solution.py:420
  61.9 8.1 %collective-permute-start.10 = (bf16[256,384]{1,0:T(8,128)(2,1)S(1)}, bf16[256,384]{1,0:T(8,128)(2,1)S(1)}, u32[]{:S(2)}, u32[]{:S(2)}) collective-permute-start(bf16[256,384]{1,0:T(8,128)(2,1)S(1)} %attention_0.1.own), channel_id=1, source_target_pairs={{0,6},{2,0},{4,2},{6,4},{1,7},{3,1},{5,3},{7,5},{8,14},{10,8},{12,... | collective-permute-start | bytes 589832 | tf_op jit(solution)/shard_map/ppermute | solution.py:420
  67.1 5.7 %collective-permute-start.12 = (bf16[256,384]{1,0:T(8,128)(2,1)S(1)}, bf16[256,384]{1,0:T(8,128)(2,1)S(1)}, u32[]{:S(2)}, u32[]{:S(2)}) collective-permute-start(bf16[256,384]{1,0:T(8,128)(2,1)S(1)} %collective-permute-done.9.left), channel_id=1, source_target_pairs={{0,6},{2,0},{4,2},{6,4},{1,7},{3,1},{5,3},{7,5},{8,14},{10,8},{12,... | collective-permute-start | bytes 589832 | tf_op jit(solution)/shard_map/ppermute | solution.py:420
  69.9 6.9 %collective-permute-start.11 = (bf16[256,384]{1,0:T(8,128)(2,1)S(1)}, bf16[256,384]{1,0:T(8,128)(2,1)S(1)}, u32[]{:S(2)}, u32[]{:S(2)}) collective-permute-start(bf16[256,384]{1,0:T(8,128)(2,1)S(1)} %collective-permute-done.7.right), channel_id=1, source_target_pairs={{0,2},{2,4},{4,6},{6,0},{1,3},{3,5},{5,7},{7,1},{8,10},{10,12},{12... | collective-permute-start | bytes 589832 | tf_op jit(solution)/shard_map/ppermute | solution.py:420
